TPU v7x, 32 devices: a whole 2x2x4 slice. The times are simulated.
32 devices in a mesh: dp: 4 (over y, x), expert: 8 (over z, core).
Axes of the slice: x: 2, y: 2, z: 4, core: 2. Of those that a mesh axis runs over, the one named last changes fastest.
Arguments:
- tokens: bfloat16 [256, 2560], P(('dp', 'expert')), may hold values from -6 to 6
- routes: int32 [256, 6], P(('dp', 'expert')), may hold values from 0 to 7, all different within a row; in each aligned block of 8 rows (0 to 7, 8 to 15, ...) at most 7 rows name the same one
- router: float32 [2560, 8], replicated, may hold values from -0.125 to 0.125
- w_gate: bfloat16 [2560, 8192], P(None, 'expert'), may hold values from -0.125 to 0.125
- w_up: bfloat16 [2560, 8192], P(None, 'expert'), may hold values from -0.125 to 0.125
- w_down: bfloat16 [2560, 8192], P(None, 'expert'), may hold values from -0.1875 to 0.1875
- cotangent: bfloat16 [256, 2560], P(('dp', 'expert')), may hold values from -6 to 6
Outputs:
- mixed: bfloat16 [256, 2560], P(('dp', 'expert'))
- grad_tokens: bfloat16 [256, 2560], P(('dp', 'expert'))
- grad_router: float32 [2560, 8], replicated
- grad_gate: float32 [2560, 8192], P('dp', 'expert')
- grad_up: float32 [2560, 8192], P('dp', 'expert')
- grad_down: float32 [2560, 8192], P('dp', 'expert')
Inputs may be any that keep to these rules, and one draw needn't show every extreme that they name: `routes`: each row names 6 different experts. Among the rows of one device no expert is named more than 7 times, and in every draw some expert is named exactly 7 times by the rows of some device.
All inputs are finite; a program needn't handle non-finite values.
Results may differ from a plain program's by a relative error of at most 0.02.
Values may be sent and summed in bfloat16 or wider, within the bound.
No kernel may reach another device: no remote copies, remote signals or barrier semaphores. Data moves between devices by JAX's collectives and lax.ppermute only.
A program may use at most 128 MiB of HBM per device.

v0:
```python
import jax
import jax.numpy as jnp
from jax import lax
from jax.sharding import PartitionSpec as P


def expert_hidden(inputs, gate_matrix, up_matrix):
    gate_pre = jnp.dot(inputs, gate_matrix, preferred_element_type=jnp.float32)
    up_pre = jnp.dot(inputs, up_matrix, preferred_element_type=jnp.float32)
    hidden = (jax.nn.silu(gate_pre) * up_pre).astype(jnp.bfloat16)
    return (gate_pre, up_pre, hidden)


def expert_backward(slot_grad, gate_pre, up_pre, gate_matrix, up_matrix, down_matrix):
    hidden_grad = jnp.dot(slot_grad, down_matrix, preferred_element_type=jnp.float32)
    sigma = jax.nn.sigmoid(gate_pre)
    gate_grad = (hidden_grad * up_pre * sigma * (1.0 + gate_pre * (1.0 - sigma))).astype(
        jnp.bfloat16
    )
    up_grad = (hidden_grad * gate_pre * sigma).astype(jnp.bfloat16)
    contract = (((1,), (1,)), ((), ()))
    input_grad = lax.dot_general(
        gate_grad, gate_matrix, contract, preferred_element_type=jnp.float32
    )
    input_grad = input_grad + lax.dot_general(
        up_grad, up_matrix, contract, preferred_element_type=jnp.float32
    )
    return (gate_grad, up_grad, input_grad.astype(jnp.bfloat16))


def return_grads(input_part):
    return lax.all_to_all(input_part, "expert", split_axis=0, concat_axis=0, tiled=True)


def local(tokens, routes, router, w_gate, w_up, w_down, cotangent):
    features = tokens.shape[1]
    experts = router.shape[1]
    fanout = routes.shape[1]
    tok_count = tokens.shape[0]
    hidden_units = w_gate.shape[1]
    sharing = lax.axis_size("expert") // experts
    capacity = min(tok_count, 5 * fanout * tok_count // (4 * experts))
    highest = lax.Precision.HIGHEST
    tokens_wide = tokens.astype(jnp.float32)
    logits = jnp.dot(tokens_wide, router, precision=highest)
    expert_ids = jnp.arange(experts, dtype=jnp.int32)
    choose = routes[:, :, None] == expert_ids[None, None, :]
    choose_f = choose.astype(jnp.float32)
    picked = jnp.sum(choose_f * logits[:, None, :], axis=2)
    affinity = jax.nn.sigmoid(picked)
    denominator = jnp.sum(affinity, axis=1, keepdims=True)
    gate_values = affinity / denominator
    choose_i = choose.astype(jnp.int32)
    per_token = jnp.sum(choose_i, axis=1)
    before = jnp.cumsum(per_token, axis=0) - per_token
    position = jnp.sum(choose_i * before[:, None, :], axis=2)
    slot_ids = jnp.arange(capacity, dtype=jnp.int32)
    placed = choose_f[:, :, :, None] * (
        position[:, :, None, None] == slot_ids[None, None, None, :]
    ).astype(jnp.float32)
    slot_table = jnp.sum(placed, axis=1)
    gate_table = jnp.einsum("tkec,tk->tec", placed, gate_values)
    table_narrow = slot_table.astype(jnp.bfloat16)
    outgoing = jnp.einsum(
        "tec,td->ecd", table_narrow, tokens, preferred_element_type=jnp.float32
    ).astype(jnp.bfloat16)
    outgoing_all = jnp.repeat(outgoing, sharing, axis=0)

    def merge_parts(parts):
        wide_parts = parts.astype(jnp.float32)
        return jnp.sum(wide_parts.reshape(experts, sharing, capacity, features), axis=1)

    received = lax.all_to_all(outgoing_all, "expert", split_axis=0, concat_axis=0, tiled=True)
    sources, item_count, _ = received.shape
    expert_rows = received.reshape(sources * item_count, features)
    gate_pre, up_pre, hidden = expert_hidden(expert_rows, w_gate, w_up)
    output = lax.dot_general(
        hidden, w_down, (((1,), (1,)), ((), ())), preferred_element_type=jnp.float32
    )
    output = output.astype(jnp.bfloat16).reshape(sources, item_count, features)
    returned = lax.all_to_all(output, "expert", split_axis=0, concat_axis=0, tiled=True)
    returned, rows_kept, gate_kept, up_kept, hidden_kept = (
        returned,
        received,
        gate_pre.reshape(sources, item_count, hidden_units),
        up_pre.reshape(sources, item_count, hidden_units),
        hidden.reshape(sources, item_count, hidden_units),
    )
    expert_out = merge_parts(returned).astype(jnp.bfloat16)
    expert_wide = lax.optimization_barrier(expert_out).astype(jnp.float32)
    mixed = jnp.einsum("tec,ecd->td", gate_table, expert_wide).astype(jnp.bfloat16)
    grad_slots = jnp.einsum(
        "tec,td->ecd", table_narrow, cotangent, preferred_element_type=jnp.float32
    ).astype(jnp.bfloat16)
    slot_pull = jnp.sum(grad_slots.astype(jnp.float32) * expert_wide, axis=2)
    expert_pull = jnp.einsum("tec,ec->te", slot_table, slot_pull)
    gate_pull = jnp.sum(choose_f * expert_pull[:, None, :], axis=2)
    mean_pull = jnp.sum(gate_values * gate_pull, axis=1, keepdims=True)
    logit_grad = (gate_pull - mean_pull) / denominator * affinity * (1.0 - affinity)
    per_logit = jnp.sum(choose_f * logit_grad[:, :, None], axis=1)
    router_part = jnp.dot(tokens_wide.T, per_logit, precision=highest)
    grad_router = lax.psum(router_part, ("dp", "expert"))
    slot_gate = jnp.sum(gate_table, axis=0)
    grad_outgoing = (slot_gate[:, :, None] * grad_slots.astype(jnp.float32)).astype(jnp.bfloat16)
    grad_outgoing_all = jnp.repeat(grad_outgoing, sharing, axis=0)
    row_items = lax.all_to_all(outgoing_all, "expert", split_axis=0, concat_axis=0, tiled=True)
    grad_items = lax.all_to_all(
        grad_outgoing_all, "expert", split_axis=0, concat_axis=0, tiled=True
    )
    sources, item_count, _ = row_items.shape
    expert_rows = row_items.reshape(-1, features)
    grad_rows = grad_items.reshape(-1, features)
    gate_pre, up_pre, hidden = expert_hidden(expert_rows, w_gate, w_up)
    backward_gate_grad, backward_up_grad, input_part = expert_backward(
        grad_rows, gate_pre, up_pre, w_gate, w_up, w_down
    )
    input_back = return_grads(input_part.reshape(sources, item_count, features))
    input_back, rows_again, grads_again, hidden_again, gate_again, up_again = (
        input_back,
        row_items,
        grad_items,
        hidden.reshape(sources, item_count, hidden_units),
        backward_gate_grad.reshape(sources, item_count, hidden_units),
        backward_up_grad.reshape(sources, item_count, hidden_units),
    )
    rows_flat = rows_again.reshape(-1, features)
    grad_flat = grads_again.reshape(-1, features)
    hidden_flat = hidden_again.reshape(-1, hidden_units)
    gate_grad = gate_again.reshape(-1, hidden_units)
    up_grad = up_again.reshape(-1, hidden_units)
    contract = (((0,), (0,)), ((), ()))
    part_gate = lax.dot_general(rows_flat, gate_grad, contract, preferred_element_type=jnp.float32)
    part_up = lax.dot_general(rows_flat, up_grad, contract, preferred_element_type=jnp.float32)
    part_down = lax.dot_general(
        grad_flat, hidden_flat, contract, preferred_element_type=jnp.float32
    )
    summed = lax.psum_scatter(
        jnp.concatenate([part_gate, part_up, part_down], axis=1).astype(jnp.bfloat16),
        "dp",
        scatter_dimension=0,
        tiled=True,
    ).astype(jnp.float32)
    grad_gate = summed[:, :hidden_units]
    grad_up = summed[:, hidden_units : 2 * hidden_units]
    grad_down = summed[:, 2 * hidden_units :]
    input_grad = merge_parts(input_back).astype(jnp.bfloat16)
    input_wide = lax.optimization_barrier(input_grad).astype(jnp.float32)
    router_back = lax.dot_general(per_logit, router, (((1,), (1,)), ((), ())), precision=highest)
    grad_tokens = (jnp.einsum("tec,ecd->td", slot_table, input_wide) + router_back).astype(
        jnp.bfloat16
    )
    return (mixed, grad_tokens, grad_router, grad_gate, grad_up, grad_down)


def solution(mesh):
    return jax.shard_map(
        local,
        mesh=mesh,
        in_specs=(
            P(("dp", "expert"), None),
            P(("dp", "expert"), None),
            P(),
            P(None, "expert"),
            P(None, "expert"),
            P(None, "expert"),
            P(("dp", "expert"), None),
        ),
        out_specs=(
            P(("dp", "expert"), None),
            P(("dp", "expert"), None),
            P(),
            P("dp", "expert"),
            P("dp", "expert"),
            P("dp", "expert"),
        ),
        check_vma=False,
    )
```

profile of v0, /device:TPU:0, one launch (start us, length us, event | category | flops | bytes accessed | tf_op | source)
XLA Modules:
  0.0 332.7 jit_solution(13056168883937794117)
XLA Ops:
  8.0 0.0 copy-start
  8.0 0.8 copy.39
  8.8 0.1 convert_reduce_fusion
  8.9 0.1 fusion.13
  9.0 0.2 select_reduce_fusion.3
  9.3 0.1 fusion.10
  9.4 1.0 convolution_convert_fusion.5
  10.4 0.1 copy.42
  10.5 17.3 %all_to_all.21 = bf16[8,7,2560]{2,1,0:T(8,128)(2,1)S(1)} all-to-all(bf16[8,7,2560]{2,1,0:T(8,128)(2,1)S(1)} %copy.42), channel_id=1, replica_groups=mesh['dp'=4,'expert'=8] {'expert'}, dimensions={0} | all-to-all | bytes 573440 | tf_op jit(solution)/shard_map/all_to_all | solution.py:73
  27.8 0.1 reshape.102
  27.9 0.0 slice-start.1
  27.9 3.6 %fusion.22 = f32[56,1024]{1,0:T(8,128)S(1)} fusion(bf16[56,2560]{1,0:T(8,128)(2,1)S(1)} %reshape.102, bf16[2560,1024]{1,0:T(8,128)(2,1)} %param.10), kind=kOutput, calls=%fused_computation.54 | convolution fusion | flops 293601280 | bytes 5758976 | tf_op jit(solution)/shard_map/dot_general | solution.py:8
  31.6 0.0 copy-start.1
  31.6 0.0 copy-start.2
  31.6 3.5 %multiply_convert_fusion.3 = (bf16[56,1024]{1,0:T(8,128)(2,1)S(1)}, f32[56,1024]{1,0:T(8,128)S(1)}) fusion(f32[56,1024]{1,0:T(8,128)S(1)} %fusion.22, bf16[56,2560]{1,0:T(8,128)(2,1)S(1)} %reshape.102, bf16[2560,1024]{1,0:T(8,128)(2,1)} %param.11), kind=kOutput, calls=%fused_computation.24 | convolution fusion | flops 293945344 | bytes 6103040 | tf_op jit(solution)/shard_map/dot_general | solution.py:9
  35.1 0.0 slice-done
  35.1 0.0 slice-done.1
  35.1 1.7 convolution_convert_fusion.4
  36.8 0.8 reshape.103
  37.7 3.4 %all-to-all-start.1 = ((bf16[8,7,2560]{2,1,0:T(8,128)(2,1)}), bf16[8,7,2560]{2,1,0:T(8,128)(2,1)S(1)}, u32[]{:S(2)}, u32[]{:S(2)}) async-start(bf16[8,7,2560]{2,1,0:T(8,128)(2,1)} %reshape.103), calls=%async_computation.1 | async-start | bytes 655360 | tf_op jit(solution)/shard_map/all_to_all | solution.py:81
  41.1 0.0 reduce-scatter.4.cloned.1.call-start
  41.2 0.0 copy-done
  41.2 0.1 fusion.21
  41.3 0.2 broadcast_multiply_fusion
  41.5 10.7 %all-to-all-done.1 = bf16[8,7,2560]{2,1,0:T(8,128)(2,1)S(1)} async-done(((bf16[8,7,2560]{2,1,0:T(8,128)(2,1)}), bf16[8,7,2560]{2,1,0:T(8,128)(2,1)S(1)}, u32[]{:S(2)}, u32[]{:S(2)}) %all-to-all-start.1) | async-done | bytes 286752 | tf_op jit(solution)/shard_map/all_to_all | solution.py:81
  52.2 0.0 copy-done.2
  52.2 0.4 multiply_reduce_fusion
  52.6 0.2 select_reduce_fusion.1
  52.8 0.1 copy.53
  52.9 0.2 fusion.6
  53.1 0.1 multiply_convert_fusion
  53.2 0.1 copy.45
  53.3 0.0 slice-start.2
  53.3 13.7 %all_to_all.22 = bf16[8,7,2560]{2,1,0:T(8,128)(2,1)S(1)} all-to-all(bf16[8,7,2560]{2,1,0:T(8,128)(2,1)S(1)} %copy.45), channel_id=1, replica_groups=mesh['dp'=4,'expert'=8] {'expert'}, dimensions={0} | all-to-all | bytes 573440 | tf_op jit(solution)/shard_map/all_to_all | solution.py:107
  66.9 0.1 reshape.104
  67.1 0.0 slice-start.3
  67.1 1.6 convolution_convert_fusion
  68.6 0.6 slice-done.3
  69.2 1.1 multiply_convert_fusion.1
  70.3 1.6 convolution_convert_fusion.1
  71.9 1.6 convolution_convert_fusion.2
  73.4 33.9 %pad_maximum_fusion = bf16[2560,3072]{0,1:T(8,128)(2,1)} fusion(bf16[2560,1024]{0,1:T(8,128)(2,1)S(1)} %convolution_convert_fusion, bf16[2560,1024]{0,1:T(8,128)(2,1)S(1)} %convolution_convert_fusion.1, bf16[2560,1024]{0,1:T(8,128)(2,1)S(1)} %convolution_convert_fusion.2), kind=kLoop, calls=%fused_computation | loop fusion | flops 47185920 | bytes 31457280 | tf_op jit(solution)/shard_map/concatenate | solution.py:138
  107.3 20.7 %copy.62 = bf16[2560,3072]{1,0:T(8,128)(2,1)} copy(bf16[2560,3072]{0,1:T(8,128)(2,1)} %pad_maximum_fusion) | data formatting | bytes 31457280
  128.0 0.0 reduce-scatter.4.cloned.1.call-update
  128.1 4.2 %fusion.23 = f32[56,2560]{1,0:T(8,128)S(1)} fusion(bf16[56,1024]{1,0:T(8,128)(2,1)S(1)} %get-tuple-element.36, bf16[2560,1024]{1,0:T(8,128)(2,1)} %param.10), kind=kOutput, calls=%fused_computation.55 | convolution fusion | flops 293601280 | bytes 5931008 | tf_op jit(solution)/shard_map/dot_general | solution.py:22
  132.3 5.4 %fusion = bf16[56,2560]{1,0:T(8,128)(2,1)S(1)} fusion(f32[56,2560]{1,0:T(8,128)S(1)} %fusion.23, bf16[56,1024]{1,0:T(8,128)(2,1)S(1)} %get-tuple-element.35, bf16[2560,1024]{1,0:T(8,128)(2,1)} %param.11), kind=kOutput, calls=%fused_computation.5 | convolution fusion | flops 293888000 | bytes 6217728 | tf_op jit(solution)/shard_map/dot_general | solution.py:25
  137.7 0.8 reshape.105
  138.5 3.4 %all-to-all-start.3 = ((bf16[8,7,2560]{2,1,0:T(8,128)(2,1)}), bf16[8,7,2560]{2,1,0:T(8,128)(2,1)S(1)}, u32[]{:S(2)}, u32[]{:S(2)}) async-start(bf16[8,7,2560]{2,1,0:T(8,128)(2,1)} %reshape.105), calls=%async_computation.3 | async-start | bytes 655360 | tf_op jit(solution)/shard_map/all_to_all | solution.py:32
  141.9 0.3 all-reduce.2.cloned.1.call-start
  142.2 0.1 select_reduce_fusion
  142.3 0.9 convolution_bitcast_fusion
  143.2 0.0 all-reduce.2.cloned.1.call-update
  143.2 0.9 fusion.2
  144.1 8.9 %all-to-all-done.3 = bf16[8,7,2560]{2,1,0:T(8,128)(2,1)S(1)} async-done(((bf16[8,7,2560]{2,1,0:T(8,128)(2,1)}), bf16[8,7,2560]{2,1,0:T(8,128)(2,1)S(1)}, u32[]{:S(2)}, u32[]{:S(2)}) %all-to-all-start.3) | async-done | bytes 286752 | tf_op jit(solution)/shard_map/all_to_all | solution.py:32
  153.0 0.3 convolution_bitcast_fusion.1
  153.3 0.8 fusion.3
  154.1 119.9 %reduce-scatter.4.cloned.1.call-done = bf16[640,3072]{1,0:T(8,128)(2,1)} async-done(((bf16[2560,3072]{1,0:T(8,128)(2,1)}), bf16[640,3072]{1,0:T(8,128)(2,1)}) %reduce-scatter.4.cloned.1.call-update) | async-done | bytes 3932176
  274.0 6.3 %copy.63 = bf16[640,3072]{0,1:T(8,128)(2,1)} copy(bf16[640,3072]{1,0:T(8,128)(2,1)} %reduce-scatter.4.cloned.1.call-done) | data formatting | bytes 7864320
  280.3 5.0 %fusion.20 = (f32[640,1024]{0,1:T(8,128)}, f32[640,1024]{0,1:T(8,128)}, f32[640,1024]{0,1:T(8,128)S(1)}) fusion(bf16[640,3072]{0,1:T(8,128)(2,1)} %copy.63), kind=kLoop, calls=%fused_computation.52 | loop fusion | bytes 15728640 | tf_op jit(solution)/shard_map/slice | solution.py:145
  285.3 3.2 copy.51
  288.5 3.2 copy.50
  291.7 2.1 copy.49
  293.8 29.9 %all-reduce.2.cloned.1.call-done = f32[2560,8]{0,1:T(8,128)} async-done(((f32[2560,8]{0,1:T(8,128)}), f32[2560,8]{0,1:T(8,128)}) %all-reduce.2.cloned.1.call-update) | async-done | bytes 81936 | tf_op jit(solution)/shard_map/psum | solution.py:102
  323.7 1.5 copy.80
  (14 shorter events, 0.1 us)
Async XLA Ops:
  8.0 33.2 %copy-start = (f32[2560,8]{0,1:T(8,128)S(1)}, f32[2560,8]{0,1:T(8,128)}, u32[]{:S(2)}) copy-start(f32[2560,8]{0,1:T(8,128)} %param.9) | copy-start | bytes 245764
  27.8 7.3 %slice-start = ((s8[5242880]{0:T(1024)(128)(4,1)}), s8[1048576]{0:T(1024)(128)(4,1)S(1)}, s32[]{:S(2)}) async-start(s8[5242880]{0:T(1024)(128)(4,1)} %bitcast.52), calls=%async_computation.7 | async-start | bytes 2097152
  27.9 7.2 %slice-start.1 = ((s8[5242880]{0:T(1024)(128)(4,1)}), s8[4194304]{0:T(1024)(128)(4,1)S(1)}, s32[]{:S(2)}) async-start(s8[5242880]{0:T(1024)(128)(4,1)} %bitcast.52), calls=%async_computation.8 | async-start | bytes 8388608
  31.6 9.6 %copy-start.1 = (bf16[8,2560]{1,0:T(8,128)(2,1)S(1)}, bf16[8,2560]{1,0:T(8,128)(2,1)}, u32[]{:S(2)}) copy-start(bf16[8,2560]{1,0:T(8,128)(2,1)} %param.7) | copy-start | bytes 122884
  31.6 20.6 %copy-start.2 = (bf16[8,2560]{1,0:T(8,128)(2,1)S(1)}, bf16[8,2560]{1,0:T(8,128)(2,1)}, u32[]{:S(2)}) copy-start(bf16[8,2560]{1,0:T(8,128)(2,1)} %param.13) | copy-start | bytes 122884
  37.7 14.5 %all-to-all-start.1 = ((bf16[8,7,2560]{2,1,0:T(8,128)(2,1)}), bf16[8,7,2560]{2,1,0:T(8,128)(2,1)S(1)}, u32[]{:S(2)}, u32[]{:S(2)}) async-start(bf16[8,7,2560]{2,1,0:T(8,128)(2,1)} %reshape.103), calls=%async_computation.1 | async-start | bytes 655360 | tf_op jit(solution)/shard_map/all_to_all | solution.py:81
  41.1 232.9 %reduce-scatter.4.cloned.1.call-start = ((), (), s32[]{:S(2)}) async-start(), calls=%async_computation.6 | async-start | bytes 19660800
  53.3 15.4 %slice-start.2 = ((s8[5242880]{0:T(1024)(128)(4,1)}), s8[1048576]{0:T(1024)(128)(4,1)S(1)}, s32[]{:S(2)}) async-start(s8[5242880]{0:T(1024)(128)(4,1)} %bitcast.54), calls=%async_computation.9 | async-start | bytes 2097152
  67.1 2.2 slice-start.3
  138.5 14.5 %all-to-all-start.3 = ((bf16[8,7,2560]{2,1,0:T(8,128)(2,1)}), bf16[8,7,2560]{2,1,0:T(8,128)(2,1)S(1)}, u32[]{:S(2)}, u32[]{:S(2)}) async-start(bf16[8,7,2560]{2,1,0:T(8,128)(2,1)} %reshape.105), calls=%async_computation.3 | async-start | bytes 655360 | tf_op jit(solution)/shard_map/all_to_all | solution.py:32
  141.9 181.7 %all-reduce.2.cloned.1.call-start = ((), (), s32[]{:S(2)}) async-start(), calls=%async_computation.5 | async-start | bytes 163840 | tf_op jit(solution)/shard_map/psum | solution.py:102
Sparse Core Ops, SparseCore 0:
  128.1 145.8 reduce-scatter.3
Sparse Core Ops, SparseCore 1:
  148.6 175.1 all-reduce.1
where the time goes:
time: 335 us; the launch traced here: 333 us
  waiting for transfers between devices  169 us (50%)
  local copies, waits for them, and re-layouts  45.6 us (14%)
  other arithmetic  35.1 us (10%)
  blocking collectives  30.9 us (9%)
  matrix products  28.8 us (9%)
  between operations  15.7 us (5%)
  starting transfers between devices  7.17 us (2%)
    unnamed x3, waiting for transfers between devices  120 us
    unnamed x21, local copies, waits for them, and re-layouts  38.4 us
    concatenate x1, other arithmetic, local(): jnp.concatenate([part_gate, part_up, part_down], axis=1)  33.9 us
    psum x1, waiting for transfers between devices, local(): grad_router = lax.psum(router_part, ('dp', 'expert'))  29.9 us
    all_to_all x1, blocking collectives, local(): lax.all_to_all(outgoing_all, 'expert', split_axis=0, concat_axis=0, tiled...  17.3 us
    all_to_all x1, blocking collectives, local(): lax.all_to_all(grad_outgoing_all, 'expert', split_axis=0, concat_axis=0,...  13.7 us
    all_to_all x1, waiting for transfers between devices, local(): lax.all_to_all(output, 'expert', split_axis=0, concat_axis=0, tiled=True)  10.7 us
    all_to_all x1, waiting for transfers between devices, return_grads(): lax.all_to_all(input_part, 'expert', split_axis=0, concat_axis=0, tiled=T...  8.87 us
  transfers between devices with their start and end apart: 4, of which 4 were waited for; matrix products, arithmetic and copies ran while one was open for 10% of the time, Pallas kernels for 0%

commit v1 on v0

v1 whole, which is shorter than its diff:
```python
import jax
import jax.numpy as jnp
from jax import lax
from jax.sharding import PartitionSpec as P

F32 = jnp.float32
BF16 = jnp.bfloat16
LANES = 128
GATHER_BYTES = 8 << 20


def swap(x, axis, mask):
    count = lax.axis_size(axis)
    return lax.ppermute(x, axis, [(i, i ^ mask) for i in range(count)])


def ordered(stack, index):
    count = stack.shape[0]
    rest = stack.shape[1:]
    bit = 1
    while bit < count:
        halves = stack.reshape((count // (2 * bit), 2, bit) + rest)
        flipped = (index // bit) % 2 == 1
        stack = jnp.where(flipped, halves[:, ::-1], halves).reshape((count,) + rest)
        bit *= 2
    return stack


def exact_dot(left, right, contract):
    parts = []
    rest = right
    for _ in range(3):
        part = lax.reduce_precision(rest, 8, 7)
        parts.append(part.astype(BF16))
        rest = rest - part
    return sum(
        lax.dot_general(left, part, contract, preferred_element_type=F32) for part in parts[::-1]
    )


def gates_of(rows, chosen, router):
    experts = router.shape[1]
    logits = exact_dot(rows, router, (((1,), (0,)), ((), ())))
    ids = jnp.arange(experts, dtype=BF16)
    picked = jnp.any(chosen[:, :, None] == ids[None, None, :], axis=1)
    affinity = jnp.where(picked, jax.nn.sigmoid(logits), 0.0)
    denominator = jnp.sum(affinity, axis=1, keepdims=True)
    return picked, affinity, denominator, affinity / denominator


def forward(rows, w_gate, w_up):
    gate_pre = jnp.dot(rows, w_gate, preferred_element_type=F32)
    up_pre = jnp.dot(rows, w_up, preferred_element_type=F32)
    sigma = jax.nn.sigmoid(gate_pre)
    return gate_pre, up_pre, sigma


def hidden_grads(slot_grad, gate_pre, up_pre, sigma, w_down):
    hidden_grad = jnp.dot(slot_grad, w_down, preferred_element_type=F32)
    gate_grad = (hidden_grad * up_pre * sigma * (1.0 + gate_pre * (1.0 - sigma))).astype(BF16)
    up_grad = (hidden_grad * gate_pre * sigma).astype(BF16)
    return gate_grad, up_grad


def local(tokens, routes, router, w_gate, w_up, w_down, cotangent):
    tok_count, features = tokens.shape
    experts = router.shape[1]
    fanout = routes.shape[1]
    hidden_units = w_gate.shape[1]
    devices = lax.axis_size("expert")
    groups = lax.axis_size("dp")
    sharing = devices // experts
    chips = devices // 2
    group_rows = devices * tok_count
    me = lax.axis_index("expert")
    group = lax.axis_index("dp")
    core, chip = me % 2, me // 2
    own_expert = me // sharing
    whole = groups * group_rows * features * 4 <= GATHER_BYTES

    def over_chips(x):
        return ordered(jnp.stack([x] + [swap(x, "expert", 2 * m) for m in range(1, chips)]), chip)

    def both_cores(x):
        pair = ordered(jnp.stack([x, swap(x, "expert", 1)]), core)
        return jnp.swapaxes(pair, 0, 1).reshape(-1, x.shape[-1])

    def over_groups(x):
        return [swap(x, "dp", m) for m in range(1, groups)]

    routes_wide = jnp.pad(routes.astype(BF16), ((0, 0), (0, LANES - fanout)))
    message = jnp.concatenate([tokens, routes_wide], axis=1)
    message_core = over_chips(message)
    grads_core = over_chips(cotangent)
    own_message = both_cores(message_core)
    own_cot = both_cores(grads_core)

    rows = own_message[:, :features]
    picked, affinity, denominator, gates = gates_of(
        rows, own_message[:, features : features + fanout], router
    )

    def own_column(table):
        return lax.dynamic_slice_in_dim(table, own_expert, 1, axis=1)

    slot_gate = own_column(gates)
    gate_pre, up_pre, sigma = forward(rows, w_gate, w_up)
    hidden = (gate_pre * sigma * up_pre).astype(BF16)
    output = lax.dot_general(hidden, w_down, (((1,), (1,)), ((), ())), preferred_element_type=F32)
    cot_wide = own_cot.astype(F32)
    pull = jnp.sum(cot_wide * output, axis=1)
    mixed_part = (slot_gate * output).astype(BF16)
    slot_grad = (slot_gate * cot_wide).astype(BF16)
    gate_grad, up_grad = hidden_grads(slot_grad, gate_pre, up_pre, sigma, w_down)
    contract = (((1,), (1,)), ((), ()))
    input_part = (
        lax.dot_general(gate_grad, w_gate, contract, preferred_element_type=F32)
        + lax.dot_general(up_grad, w_up, contract, preferred_element_type=F32)
    ).astype(BF16)

    def give_back(part):
        parts = part.reshape(chips, 2, tok_count, -1)
        keep = lax.dynamic_index_in_dim(parts, core, 1, keepdims=False).astype(F32)
        send = lax.dynamic_index_in_dim(parts, 1 - core, 1, keepdims=False)
        summed = (keep + swap(send, "expert", 1).astype(F32)).astype(BF16)
        total = lax.dynamic_index_in_dim(summed, chip, 0, keepdims=False).astype(F32)
        for m in range(1, chips):
            piece = lax.dynamic_index_in_dim(summed, chip ^ m, 0, keepdims=False)
            total = total + swap(piece, "expert", 2 * m).astype(F32)
        return total

    mixed = give_back(mixed_part).astype(BF16)
    input_sum = give_back(input_part)

    pulls = both_cores(over_chips(pull[None, :]))
    pulls = jnp.sum(pulls.reshape(experts, sharing, group_rows), axis=1).T
    mean_pull = jnp.sum(gates * pulls, axis=1, keepdims=True)
    logit_grad = (pulls - mean_pull) / denominator * affinity * (1.0 - affinity)
    logit_grad = jnp.where(picked, logit_grad, 0.0)
    own_logit = lax.dynamic_slice_in_dim(logit_grad, me * tok_count, tok_count, axis=0)
    router_back = lax.dot_general(
        own_logit, router, (((1,), (1,)), ((), ())), precision=lax.Precision.HIGHEST
    )
    grad_tokens = (input_sum + router_back).astype(BF16)

    first = (((0,), (0,)), ((), ()))
    if whole:
        far_rows, far_slot, far_gate, far_up, far_hidden = [], [], [], [], []
        far_message = over_groups(message_core)
        far_cot = over_groups(grads_core)
        far_message = jnp.concatenate([both_cores(x) for x in far_message], axis=0)
        far_cot = jnp.concatenate([both_cores(x) for x in far_cot], axis=0)
        far_rows = far_message[:, :features]
        far_gates = gates_of(far_rows, far_message[:, features : features + fanout], router)[3]
        far_pre, far_up, far_sigma = forward(far_rows, w_gate, w_up)
        far_hidden = (far_pre * far_sigma * far_up).astype(BF16)
        far_slot = (own_column(far_gates) * far_cot.astype(F32)).astype(BF16)
        far_gate_grad, far_up_grad = hidden_grads(far_slot, far_pre, far_up, far_sigma, w_down)
        width = features // groups

        def cut(x):
            return lax.dynamic_slice_in_dim(x, group * width, width, axis=1)

        all_rows = jnp.concatenate([rows, far_rows])
        rows_cut = cut(all_rows)
        slot_cut = cut(jnp.concatenate([slot_grad, far_slot]))
        grad_gate = lax.dot_general(
            rows_cut, jnp.concatenate([gate_grad, far_gate_grad]), first, preferred_element_type=F32
        )
        grad_up = lax.dot_general(
            rows_cut, jnp.concatenate([up_grad, far_up_grad]), first, preferred_element_type=F32
        )
        grad_down = lax.dot_general(
            slot_cut, jnp.concatenate([hidden, far_hidden]), first, preferred_element_type=F32
        )
        logit_all = jnp.stack([logit_grad] + over_groups(logit_grad))
        logit_all = ordered(logit_all, group).reshape(-1, experts)
        in_order = ordered(all_rows.reshape(groups, group_rows, features), group)
        grad_router = exact_dot(in_order.reshape(-1, features), logit_all, first)
    else:
        grad_router = lax.psum(
            exact_dot(tokens, own_logit, first), ("dp", "expert")
        )
        parts = [
            lax.dot_general(left, right, first, preferred_element_type=F32)
            for left, right in ((rows, gate_grad), (rows, up_grad), (slot_grad, hidden))
        ]
        summed = lax.psum_scatter(
            jnp.concatenate(parts, axis=1).astype(BF16), "dp", scatter_dimension=0, tiled=True
        ).astype(F32)
        grad_gate, grad_up, grad_down = jnp.split(summed, 3, axis=1)
    return (mixed, grad_tokens, grad_router, grad_gate, grad_up, grad_down)


def solution(mesh):
    return jax.shard_map(
        local,
        mesh=mesh,
        in_specs=(
            P(("dp", "expert"), None),
            P(("dp", "expert"), None),
            P(),
            P(None, "expert"),
            P(None, "expert"),
            P(None, "expert"),
            P(("dp", "expert"), None),
        ),
        out_specs=(
            P(("dp", "expert"), None),
            P(("dp", "expert"), None),
            P(),
            P("dp", "expert"),
            P("dp", "expert"),
            P("dp", "expert"),
        ),
        check_vma=False,
    )
```

time: 335 us -> 104 us (0.31)
  waiting for transfers between devices: 169 us -> 15.4 us
  local copies, waits for them, and re-layouts: 45.6 us -> 5.38 us
  blocking collectives: 30.9 us -> 0 us
  starting transfers between devices: 7.17 us -> 35.4 us
  other arithmetic: 35.1 us -> 10.8 us
  between operations: 15.7 us -> 1.31 us
  matrix products: 28.8 us -> 35 us
    unnamed x3 -> x0, waiting for transfers between devices: 120 us -> none
    ppermute x0 -> x35, starting transfers between devices: none -> 35.4 us  [swap(): return lax.ppermute(x, axis, [(i, i ^ mask) for i in range(count)])]
    unnamed x21 -> x54, local copies, waits for them, and re-layouts: 38.4 us -> 3.5 us
    concatenate x1 -> x2, other arithmetic: 33.9 us -> 0.17 us  [the longest x1 0.09 us: local(): all_rows = jnp.concatenate([rows, far_rows])]
    all_to_all x2 -> x0, blocking collectives: 30.9 us -> none  [the longest x1 17.3 us: local(): lax.all_to_all(outgoing_all, 'expert', split_axis=0, concat_axis=0, tiled...]
    psum x1 -> x0, waiting for transfers between devices: 29.9 us -> none  [local(): grad_router = lax.psum(router_part, ('dp', 'expert'))]
    all_to_all x2 -> x0, waiting for transfers between devices: 19.6 us -> none  [the longest x1 10.7 us: local(): lax.all_to_all(output, 'expert', split_axis=0, concat_axis=0, tiled=True)]
    ppermute x0 -> x35, waiting for transfers between devices: none -> 15.4 us  [swap(): return lax.ppermute(x, axis, [(i, i ^ mask) for i in range(count)])]
  transfers between devices with their start and end apart: 4 -> 35, of which waited for: 4 -> 10; matrix products, arithmetic and copies ran while one was open for 10% -> 44% of each run, Pallas kernels for 0% -> 0%
where the time goes in v1:
time: 104 us; the launch traced here: 103 us
  starting transfers between devices  35.4 us (34%)
  matrix products  35 us (34%)
  waiting for transfers between devices  15.4 us (15%)
  other arithmetic  10.8 us (10%)
  local copies, waits for them, and re-layouts  5.38 us (5%)
  between operations  1.31 us (1%)
    ppermute x35, starting transfers between devices, swap(): return lax.ppermute(x, axis, [(i, i ^ mask) for i in range(count)])  35.4 us
    ppermute x35, waiting for transfers between devices, swap(): return lax.ppermute(x, axis, [(i, i ^ mask) for i in range(count)])  15.4 us
    dot_general x2, matrix products, hidden_grads(): hidden_grad = jnp.dot(slot_grad, w_down, preferred_element_type=F32)  7.6 us
    dot_general x9, matrix products, exact_dot(): lax.dot_general(left, part, contract, preferred_element_type=F32)  5.75 us
    dot_general x1, matrix products, local(): lax.dot_general(gate_grad, w_gate, contract, preferred_element_type=F32)  4.29 us
    unnamed x54, local copies, waits for them, and re-layouts  3.5 us
    dot_general x2, matrix products, forward(): gate_pre = jnp.dot(rows, w_gate, preferred_element_type=F32)  3.28 us
    another operation x9, other arithmetic, both_cores(): pair = ordered(jnp.stack([x, swap(x, 'expert', 1)]), core)  3.19 us
  transfers between devices with their start and end apart: 35, of which 10 were waited for; matrix products, arithmetic and copies ran while one was open for 44% of the time, Pallas kernels for 0%

profile of v1, /device:TPU:0, one launch (start us, length us, event | category | flops | bytes accessed | tf_op | source)
XLA Modules:
  0.0 103.3 jit_solution(17577102660834909756)
XLA Ops:
  0.6 3.1 %collective-permute-start.8 = (bf16[8,2560]{1,0:T(8,128)(2,1)}, bf16[8,2560]{1,0:T(8,128)(2,1)S(1)}, u32[]{:S(2)}, u32[]{:S(2)}) collective-permute-start(bf16[8,2560]{1,0:T(8,128)(2,1)} %param.13), channel_id=1, source_target_pairs={{0,2},{1,3},{2,0},{3,1},{4,6},{5,7},{6,4},{7,5},{8,10},{9,11},{10,... | collective-permute-start | bytes 122888 | tf_op jit(solution)/shard_map/ppermute | solution.py:14
  3.7 2.5 %collective-permute-start.10 = (bf16[8,2560]{1,0:T(8,128)(2,1)}, bf16[8,2560]{1,0:T(8,128)(2,1)S(1)}, u32[]{:S(2)}, u32[]{:S(2)}) collective-permute-start(bf16[8,2560]{1,0:T(8,128)(2,1)} %param.13), channel_id=1, source_target_pairs={{0,6},{1,7},{2,4},{3,5},{4,2},{5,3},{6,0},{7,1},{8,14},{9,15},{10,... | collective-permute-start | bytes 122888 | tf_op jit(solution)/shard_map/ppermute | solution.py:14
  6.3 0.7 convert_element_type.131
  7.0 0.8 fusion.69
  7.8 2.8 %collective-permute-start.1 = (bf16[8,2688]{1,0:T(8,128)(2,1)S(1)}, bf16[8,2688]{1,0:T(8,128)(2,1)S(1)}, u32[]{:S(2)}, u32[]{:S(2)}) collective-permute-start(bf16[8,2688]{1,0:T(8,128)(2,1)S(1)} %get-tuple-element.20), channel_id=1, source_target_pairs={{0,4},{1,5},{2,6},{3,7},{4,0},{5,1},{6,2},{7,3},{8,12},{9,13},{10,... | collective-permute-start | bytes 129032 | tf_op jit(solution)/shard_map/ppermute | solution.py:14
  10.6 0.7 collective-permute-start
  11.3 0.9 collective-permute-start.2
  12.5 0.8 pad_maximum_fusion.11
  13.3 0.7 reverse_select_fusion.12
  14.0 2.4 %collective-permute-start.33 = (bf16[4,8,2560]{2,1,0:T(8,128)(2,1)}, bf16[4,8,2560]{2,1,0:T(8,128)(2,1)}, u32[]{:S(2)}, u32[]{:S(2)}) collective-permute-start(bf16[4,8,2560]{2,1,0:T(8,128)(2,1)} %bitcast.27), channel_id=1, source_target_pairs={{0,24},{8,16},{16,8},{24,0},{1,25},{9,17},{17,9},{25,1},{2,26},{10... | collective-permute-start | bytes 491528 | tf_op jit(solution)/shard_map/ppermute | solution.py:14
  16.4 0.5 collective-permute-start.31
  17.2 0.4 collective-permute-start.3
  17.7 0.9 collective-permute-done.11
  18.6 1.1 %pad_maximum_fusion.6 = bf16[2,4,8,2560]{3,2,1,0:T(8,128)(2,1)S(1)} fusion(bf16[1,4,8,2560]{3,2,1,0:T(8,128)(2,1)S(1)} %bitcast.220, bf16[1,4,8,2560]{3,2,1,0:T(8,128)(2,1)} %bitcast.26), kind=kLoop, calls=%fused_computation.73 | loop fusion | flops 163840 | bytes 655360 | tf_op jit(solution)/shard_map/stack | solution.py:85
  20.0 1.1 %fusion.72 = f32[64,1024]{1,0:T(8,128)S(1)} fusion(bf16[2560,1024]{1,0:T(8,128)(2,1)S(1)} %copy-done, bf16[64,2688]{1,0:T(8,128)(2,1)S(1)} %bitcast.182), kind=kOutput, calls=%fused_computation.158 | convolution fusion | flops 335544320 | bytes 5832704 | tf_op jit(solution)/shard_map/dot_general | solution.py:52
  21.0 1.2 %copy-done.1 = bf16[2560,1024]{1,0:T(8,128)(2,1)S(1)} copy-done((bf16[2560,1024]{1,0:T(8,128)(2,1)S(1)}, bf16[2560,1024]{1,0:T(8,128)(2,1)}, u32[]{:S(2)}) %copy-start.1) | copy-done | bytes 5242904
  22.3 1.1 %multiply_convert_fusion.7 = (bf16[64,1024]{1,0:T(8,128)(2,1)S(1)}, f32[64,1024]{1,0:T(8,128)S(1)}) fusion(f32[64,1024]{1,0:T(8,128)S(1)} %fusion.72, bf16[2560,1024]{1,0:T(8,128)(2,1)S(1)} %copy-done.1, bf16[64,2688]{1,0:T(8,128)(2,1)S(1)} %bitcast.183), kind=kOutput, calls=%fused_computation.83 | convolution fusion | flops 335937536 | bytes 6225920 | tf_op jit(solution)/shard_map/dot_general | solution.py:53
  23.8 1.8 %fusion.16 = (f32[64]{0:T(128)S(1)}, f32[64,2560]{1,0:T(8,128)S(1)}) fusion(f32[4,2,8,2560]{3,2,1,0:T(8,128)S(1)} %copy.46, bf16[64,1024]{1,0:T(8,128)(2,1)S(1)} %get-tuple-element.26, bf16[2560,1024]{1,0:T(8,128)(2,1)S(1)} %bitcast.176), kind=kOutput, calls=%fused_computation.39 | convolution fusion | flops 335871936 | bytes 6684928 | tf_op jit(solution)/shard_map/dot_general | solution.py:109
  25.6 2.6 %collective-permute-start.18 = (f32[1,64]{1,0:T(1,128)S(1)}, f32[1,64]{1,0:T(1,128)S(1)}, u32[]{:S(2)}, u32[]{:S(2)}) collective-permute-start(f32[1,64]{1,0:T(1,128)S(1)} %bitcast.243), channel_id=1, source_target_pairs={{0,6},{1,7},{2,4},{3,5},{4,2},{5,3},{6,0},{7,1},{8,14},{9,15},{10,... | collective-permute-start | bytes 776 | tf_op jit(solution)/shard_map/ppermute | solution.py:14
  28.2 1.9 %collective-permute-start.16 = (f32[1,64]{1,0:T(1,128)S(1)}, f32[1,64]{1,0:T(1,128)S(1)}, u32[]{:S(2)}, u32[]{:S(2)}) collective-permute-start(f32[1,64]{1,0:T(1,128)S(1)} %bitcast.245), channel_id=1, source_target_pairs={{0,2},{1,3},{2,0},{3,1},{4,6},{5,7},{6,4},{7,5},{8,10},{9,11},{10,... | collective-permute-start | bytes 776 | tf_op jit(solution)/shard_map/ppermute | solution.py:14
  30.6 0.4 collective-permute-done.18
  31.0 1.6 %collective-permute-done.17 = f32[1,64]{1,0:T(1,128)S(1)} collective-permute-done((f32[1,64]{1,0:T(1,128)S(1)}, f32[1,64]{1,0:T(1,128)S(1)}, u32[]{:S(2)}, u32[]{:S(2)}) %collective-permute-start.17) | collective-permute-done | bytes 288 | tf_op jit(solution)/shard_map/ppermute | solution.py:14
  33.0 0.9 collective-permute-done.19
  34.0 1.6 %collective-permute-start.28 = (f32[64,8]{0,1:T(8,128)S(1)}, f32[64,8]{0,1:T(8,128)S(1)}, u32[]{:S(2)}, u32[]{:S(2)}) collective-permute-start(f32[64,8]{0,1:T(8,128)S(1)} %multiply_select_fusion), channel_id=1, source_target_pairs={{0,24},{8,16},{16,8},{24,0},{1,25},{9,17},{17,9},{25,1},{2,26},{10... | collective-permute-start | bytes 6152 | tf_op jit(solution)/shard_map/ppermute | solution.py:14
  35.6 0.5 collective-permute-start.27
  36.1 1.5 %collective-permute-start.26 = (f32[64,8]{0,1:T(8,128)S(1)}, f32[64,8]{0,1:T(8,128)S(1)}, u32[]{:S(2)}, u32[]{:S(2)}) collective-permute-start(f32[64,8]{0,1:T(8,128)S(1)} %multiply_select_fusion), channel_id=1, source_target_pairs={{0,8},{8,0},{16,24},{24,16},{1,9},{9,1},{17,25},{25,17},{2,10},{10... | collective-permute-start | bytes 6152 | tf_op jit(solution)/shard_map/ppermute | solution.py:14
  37.7 3.8 %multiply_convert_fusion.5 = (bf16[64,1024]{1,0:T(8,128)(2,1)S(1)}, bf16[64,1024]{1,0:T(8,128)(2,1)S(1)}) fusion(f32[64,1024]{1,0:T(8,128)S(1)} %fusion.72, f32[64,1024]{1,0:T(8,128)S(1)} %get-tuple-element.27, bf16[64,2560]{1,0:T(8,128)(2,1)S(1)} %get-tuple-element.24, bf16[2560,1024]{1,0:T(8,128)(2,1)} %param.12), kind=kOutput, calls=%fused_computation.81 | convolution fusion | flops 336396288 | bytes 6356992 | tf_op jit(solution)/shard_map/dot_general | solution.py:59
  41.6 4.3 %fusion.88 = f32[64,2560]{1,0:T(8,128)S(1)} fusion(bf16[64,1024]{1,0:T(8,128)(2,1)S(1)} %get-tuple-element.12, bf16[2560,1024]{1,0:T(8,128)(2,1)} %param.10), kind=kOutput, calls=%fused_computation.172 | convolution fusion | flops 335544320 | bytes 6029312 | tf_op jit(solution)/shard_map/dot_general | solution.py:117
  45.9 1.7 %fusion = bf16[64,2560]{1,0:T(8,128)(2,1)S(1)} fusion(f32[64,2560]{1,0:T(8,128)S(1)} %fusion.88, bf16[64,1024]{1,0:T(8,128)(2,1)S(1)} %get-tuple-element.11, bf16[2560,1024]{1,0:T(8,128)(2,1)S(1)} %bitcast.178), kind=kOutput, calls=%fused_computation.1 | convolution fusion | flops 335872000 | bytes 6356992 | tf_op jit(solution)/shard_map/dot_general | solution.py:118
  47.7 0.6 collective-permute-start.29
  48.3 2.4 %collective-permute-start.24 = (bf16[4,8,2688]{2,1,0:T(8,128)(2,1)S(1)}, bf16[4,8,2688]{2,1,0:T(8,128)(2,1)S(1)}, u32[]{:S(2)}, u32[]{:S(2)}) collective-permute-start(bf16[4,8,2688]{2,1,0:T(8,128)(2,1)S(1)} %bitcast.204), channel_id=1, source_target_pairs={{0,24},{8,16},{16,8},{24,0},{1,25},{9,17},{17,9},{25,1},{2,26},{10... | collective-permute-start | bytes 516104 | tf_op jit(solution)/shard_map/ppermute | solution.py:14
  50.7 0.5 collective-permute-start.22
  51.3 0.6 collective-permute-start.20
  51.9 0.6 fusion.56
  52.5 2.6 %collective-permute-done.29 = bf16[4,8,2560]{2,1,0:T(8,128)(2,1)S(1)} collective-permute-done((bf16[4,8,2560]{2,1,0:T(8,128)(2,1)}, bf16[4,8,2560]{2,1,0:T(8,128)(2,1)S(1)}, u32[]{:S(2)}, u32[]{:S(2)}) %collective-permute-start.29) | collective-permute-done | bytes 163872 | tf_op jit(solution)/shard_map/ppermute | solution.py:14
  55.1 4.6 %collective-permute-done.24 = bf16[4,8,2688]{2,1,0:T(8,128)(2,1)S(1)} collective-permute-done((bf16[4,8,2688]{2,1,0:T(8,128)(2,1)S(1)}, bf16[4,8,2688]{2,1,0:T(8,128)(2,1)S(1)}, u32[]{:S(2)}, u32[]{:S(2)}) %collective-permute-start.24) | collective-permute-done | bytes 172064 | tf_op jit(solution)/shard_map/ppermute | solution.py:14
  59.7 0.5 collective-permute-start.25
  60.2 0.5 collective-permute-done.20
  60.8 0.5 collective-permute-start.21
  61.3 0.9 pad_maximum_fusion.9
  62.4 0.9 pad_maximum_fusion.8
  63.4 0.6 collective-permute-start.12
  64.0 0.8 reverse_select_fusion.8
  64.9 0.6 dynamic-slice_bitcast_fusion.7
  65.6 1.0 collective-permute-start.5
  66.5 2.5 %collective-permute-start.7 = (bf16[8,2560]{1,0:T(8,128)(2,1)}, bf16[8,2560]{1,0:T(8,128)(2,1)}, u32[]{:S(2)}, u32[]{:S(2)}) collective-permute-start(bf16[8,2560]{1,0:T(8,128)(2,1)} %get-tuple-element.17), channel_id=1, source_target_pairs={{0,6},{1,7},{2,4},{3,5},{4,2},{5,3},{6,0},{7,1},{8,14},{9,15},{10,... | collective-permute-start | bytes 122888 | tf_op jit(solution)/shard_map/ppermute | solution.py:14
  69.1 0.7 dynamic-slice_bitcast_fusion.4
  69.9 1.9 %collective-permute-start.13 = (bf16[8,2560]{1,0:T(8,128)(2,1)}, bf16[8,2560]{1,0:T(8,128)(2,1)S(1)}, u32[]{:S(2)}, u32[]{:S(2)}) collective-permute-start(bf16[8,2560]{1,0:T(8,128)(2,1)} %get-tuple-element.13), channel_id=1, source_target_pairs={{0,2},{1,3},{2,0},{3,1},{4,6},{5,7},{6,4},{7,5},{8,10},{9,11},{10,... | collective-permute-start | bytes 122888 | tf_op jit(solution)/shard_map/ppermute | solution.py:14
  72.1 2.6 %collective-permute-start.15 = (bf16[8,2560]{1,0:T(8,128)(2,1)}, bf16[8,2560]{1,0:T(8,128)(2,1)}, u32[]{:S(2)}, u32[]{:S(2)}) collective-permute-start(bf16[8,2560]{1,0:T(8,128)(2,1)} %get-tuple-element.14), channel_id=1, source_target_pairs={{0,6},{1,7},{2,4},{3,5},{4,2},{5,3},{6,0},{7,1},{8,14},{9,15},{10,... | collective-permute-start | bytes 122888 | tf_op jit(solution)/shard_map/ppermute | solution.py:14
  74.9 0.7 copy-done.12
  75.7 1.0 fusion.65
  76.6 2.2 %fusion.79 = f32[192,1024]{1,0:T(8,128)} fusion(bf16[2560,1024]{1,0:T(8,128)(2,1)S(1)} %bitcast.174, bf16[192,2688]{1,0:T(8,128)(2,1)S(1)} %pad_maximum_fusion.1), kind=kOutput, calls=%fused_computation.163 | convolution fusion | flops 1006632960 | bytes 7012352 | tf_op jit(solution)/shard_map/dot_general | solution.py:52
  79.0 1.3 %convolution_add_fusion.2 = f32[192,8]{0,1:T(8,128)S(1)} fusion(f32[192,8]{0,1:T(8,128)} %fusion.65, f32[2560,8]{0,1:T(8,128)} %param.9, bf16[192,2688]{1,0:T(8,128)(2,1)S(1)} %pad_maximum_fusion.1), kind=kOutput, calls=%fused_computation.23 | convolution fusion | flops 7947776 | bytes 1077248 | tf_op jit(solution)/shard_map/dot_general | solution.py:37
  80.3 1.3 %fusion.87 = (f32[192]{0:T(256)S(1)}, f32[192,8]{0,1:T(8,128)S(1)}) fusion(pred[192,8]{0,1:T(8,128)(4,1)S(1)} %compare_reduce_fusion, f32[192,8]{0,1:T(8,128)S(1)} %convolution_add_fusion.2, f32[2560,8]{0,1:T(8,128)} %param.9, bf16[192,2688]{1,0:T(8,128)(2,1)S(1)} %pad_maximum_fusion.1), kind=kOutput, calls=%fused_computation.171 | convolution fusion | flops 7914304 | bytes 1082112 | tf_op jit(solution)/shard_map/dot_general | solution.py:37
  81.9 3.8 %fusion.89 = f32[192,1024]{1,0:T(8,128)S(1)} fusion(bf16[192,2560]{1,0:T(8,128)(2,1)S(1)} %multiply_convert_fusion, bf16[2560,1024]{1,0:T(8,128)(2,1)} %param.12), kind=kOutput, calls=%fused_computation.173 | convolution fusion | flops 1006632960 | bytes 7012352 | tf_op jit(solution)/shard_map/dot_general | solution.py:59
  86.3 0.6 slice-done.7
  87.2 1.6 %multiply_convert_fusion.1 = (bf16[192,1024]{1,0:T(8,128)(2,1)S(1)}, bf16[192,1024]{1,0:T(8,128)(2,1)S(1)}, bf16[192,1024]{1,0:T(8,128)(2,1)S(1)}) fusion(f32[192,1024]{1,0:T(8,128)S(1)} %copy-done.18, f32[192,1024]{1,0:T(8,128)S(1)} %fusion.89, bf16[2560,1024]{1,0:T(8,128)(2,1)S(1)} %bitcast.180, bf16[192,2688]{1,0:T(8,128)(2,1)S(1)} %pad_maximum_fusion.1), kind=kOutput, calls=%fused_computation.32 | convolution fusion | flops 1009778688 | bytes 8978432 | tf_op jit(solution)/shard_map/dot_general | solution.py:53
  88.8 2.0 %fusion.25 = f32[640,1024]{1,0:T(8,128)} fusion(bf16[192,1024]{1,0:T(8,128)(2,1)S(1)} %get-tuple-element.8, bf16[64,1024]{1,0:T(8,128)(2,1)S(1)} %get-tuple-element.26, s32[]{:T(128)S(6)} %select_n.318, bf16[64,2560]{1,0:T(8,128)(2,1)S(1)} %get-tuple-element.24, bf16[192,2560]{1,0:T(8,128)(2,1)S(1)} %multiply_convert_fusion), kind=kOutput, calls=%fused_computation.50 | convolution fusion | flops 337248256 | bytes 4456452 | tf_op jit(solution)/shard_map/dot_general | solution.py:173
  90.9 2.0 %fusion.17 = f32[640,1024]{1,0:T(8,128)} fusion(bf16[192,1024]{1,0:T(8,128)(2,1)S(1)} %get-tuple-element.9, bf16[64,1024]{1,0:T(8,128)(2,1)S(1)} %copy-done.6, s32[]{:T(128)S(6)} %select_n.318, bf16[192,2560]{1,0:T(8,128)(2,1)S(1)} %slice.18, bf16[64,2560]{1,0:T(8,128)(2,1)S(1)} %slice.17), kind=kOutput, calls=%fused_computation.42 | convolution fusion | flops 337248256 | bytes 4456452 | tf_op jit(solution)/shard_map/dot_general | solution.py:167
  93.6 1.0 fusion.1
  94.6 2.0 %fusion.21 = f32[640,1024]{1,0:T(8,128)} fusion(bf16[192,1024]{1,0:T(8,128)(2,1)S(1)} %get-tuple-element.10, bf16[64,1024]{1,0:T(8,128)(2,1)S(1)} %copy-done.4, s32[]{:T(128)S(6)} %select_n.318, bf16[192,2560]{1,0:T(8,128)(2,1)S(1)} %slice.18, bf16[64,2560]{1,0:T(8,128)(2,1)S(1)} %slice.17), kind=kOutput, calls=%fused_computation.46 | convolution fusion | flops 337248256 | bytes 4456452 | tf_op jit(solution)/shard_map/dot_general | solution.py:170
  96.6 1.5 %fusion.50 = bf16[8,2560]{1,0:T(8,128)(2,1)} fusion(bf16[8,2560]{1,0:T(8,128)(2,1)} %collective-permute-done.7, bf16[8,2560]{1,0:T(8,128)(2,1)} %collective-permute-done.6, bf16[8,2560]{1,0:T(8,128)(2,1)} %collective-permute-done.5, bf16[4,8,2560]{2,1,0:T(8,128)(2,1)} %copy-done.10, s32[]{:T(128)S(6)} %select_n.286), kind=kLoop, calls=%fused_computation.111 | loop fusion | flops 163840 | bytes 204804 | tf_op jit(solution)/shard_map/convert_element_type | solution.py:132
  98.1 3.4 %collective-permute-done.14 = bf16[8,2560]{1,0:T(8,128)(2,1)S(1)} collective-permute-done((bf16[8,2560]{1,0:T(8,128)(2,1)S(1)}, bf16[8,2560]{1,0:T(8,128)(2,1)S(1)}, u32[]{:S(2)}, u32[]{:S(2)}) %collective-permute-start.14) | collective-permute-done | bytes 40992 | tf_op jit(solution)/shard_map/ppermute | solution.py:14
  101.5 1.8 %fusion.47 = bf16[8,2560]{1,0:T(8,128)(2,1)} fusion(bf16[8,2560]{1,0:T(8,128)(2,1)} %collective-permute-done.15, bf16[8,2560]{1,0:T(8,128)(2,1)S(1)} %collective-permute-done.14, bf16[8,2560]{1,0:T(8,128)(2,1)S(1)} %collective-permute-done.13, bf16[4,8,2560]{2,1,0:T(8,128)(2,1)} %copy-done.9, s32[]{:T(128)S(6)} %select_n.286, ...), kind=kOutput, calls=%fused_computation.107 | convolution fusion | flops 2150400 | bytes 288776 | tf_op jit(solution)/shard_map/dot_general | solution.py:141
  (151 shorter events, 5.4 us)
Async XLA Ops:
  0.6 10.6 %collective-permute-start.8 = (bf16[8,2560]{1,0:T(8,128)(2,1)}, bf16[8,2560]{1,0:T(8,128)(2,1)S(1)}, u32[]{:S(2)}, u32[]{:S(2)}) collective-permute-start(bf16[8,2560]{1,0:T(8,128)(2,1)} %param.13), channel_id=1, source_target_pairs={{0,2},{1,3},{2,0},{3,1},{4,6},{5,7},{6,4},{7,5},{8,10},{9,11},{10,... | collective-permute-start | bytes 122888 | tf_op jit(solution)/shard_map/ppermute | solution.py:14
  3.7 8.5 %collective-permute-start.10 = (bf16[8,2560]{1,0:T(8,128)(2,1)}, bf16[8,2560]{1,0:T(8,128)(2,1)S(1)}, u32[]{:S(2)}, u32[]{:S(2)}) collective-permute-start(bf16[8,2560]{1,0:T(8,128)(2,1)} %param.13), channel_id=1, source_target_pairs={{0,6},{1,7},{2,4},{3,5},{4,2},{5,3},{6,0},{7,1},{8,14},{9,15},{10,... | collective-permute-start | bytes 122888 | tf_op jit(solution)/shard_map/ppermute | solution.py:14
  6.2 6.3 %collective-permute-start.9 = (bf16[8,2560]{1,0:T(8,128)(2,1)}, bf16[8,2560]{1,0:T(8,128)(2,1)S(1)}, u32[]{:S(2)}, u32[]{:S(2)}) collective-permute-start(bf16[8,2560]{1,0:T(8,128)(2,1)} %param.13), channel_id=1, source_target_pairs={{0,4},{1,5},{2,6},{3,7},{4,0},{5,1},{6,2},{7,3},{8,12},{9,13},{10,... | collective-permute-start | bytes 122888 | tf_op jit(solution)/shard_map/ppermute | solution.py:14
  7.8 9.2 %collective-permute-start.1 = (bf16[8,2688]{1,0:T(8,128)(2,1)S(1)}, bf16[8,2688]{1,0:T(8,128)(2,1)S(1)}, u32[]{:S(2)}, u32[]{:S(2)}) collective-permute-start(bf16[8,2688]{1,0:T(8,128)(2,1)S(1)} %get-tuple-element.20), channel_id=1, source_target_pairs={{0,4},{1,5},{2,6},{3,7},{4,0},{5,1},{6,2},{7,3},{8,12},{9,13},{10,... | collective-permute-start | bytes 129032 | tf_op jit(solution)/shard_map/ppermute | solution.py:14
  10.6 6.4 %collective-permute-start = (bf16[8,2688]{1,0:T(8,128)(2,1)S(1)}, bf16[8,2688]{1,0:T(8,128)(2,1)S(1)}, u32[]{:S(2)}, u32[]{:S(2)}) collective-permute-start(bf16[8,2688]{1,0:T(8,128)(2,1)S(1)} %get-tuple-element.20), channel_id=1, source_target_pairs={{0,2},{1,3},{2,0},{3,1},{4,6},{5,7},{6,4},{7,5},{8,10},{9,11},{10,... | collective-permute-start | bytes 129032 | tf_op jit(solution)/shard_map/ppermute | solution.py:14
  11.3 5.8 %collective-permute-start.2 = (bf16[8,2688]{1,0:T(8,128)(2,1)S(1)}, bf16[8,2688]{1,0:T(8,128)(2,1)S(1)}, u32[]{:S(2)}, u32[]{:S(2)}) collective-permute-start(bf16[8,2688]{1,0:T(8,128)(2,1)S(1)} %get-tuple-element.20), channel_id=1, source_target_pairs={{0,6},{1,7},{2,4},{3,5},{4,2},{5,3},{6,0},{7,1},{8,14},{9,15},{10,... | collective-permute-start | bytes 129032 | tf_op jit(solution)/shard_map/ppermute | solution.py:14
  14.0 37.3 %collective-permute-start.33 = (bf16[4,8,2560]{2,1,0:T(8,128)(2,1)}, bf16[4,8,2560]{2,1,0:T(8,128)(2,1)}, u32[]{:S(2)}, u32[]{:S(2)}) collective-permute-start(bf16[4,8,2560]{2,1,0:T(8,128)(2,1)} %bitcast.27), channel_id=1, source_target_pairs={{0,24},{8,16},{16,8},{24,0},{1,25},{9,17},{17,9},{25,1},{2,26},{10... | collective-permute-start | bytes 491528 | tf_op jit(solution)/shard_map/ppermute | solution.py:14
  16.4 35.4 %collective-permute-start.31 = (bf16[4,8,2560]{2,1,0:T(8,128)(2,1)}, bf16[4,8,2560]{2,1,0:T(8,128)(2,1)}, u32[]{:S(2)}, u32[]{:S(2)}) collective-permute-start(bf16[4,8,2560]{2,1,0:T(8,128)(2,1)} %bitcast.27), channel_id=1, source_target_pairs={{0,16},{8,24},{16,0},{24,8},{1,17},{9,25},{17,1},{25,9},{2,18},{10... | collective-permute-start | bytes 491528 | tf_op jit(solution)/shard_map/ppermute | solution.py:14
  17.0 1.6 %collective-permute-start.11 = (bf16[4,8,2560]{2,1,0:T(8,128)(2,1)}, bf16[4,8,2560]{2,1,0:T(8,128)(2,1)S(1)}, u32[]{:S(2)}, u32[]{:S(2)}) collective-permute-start(bf16[4,8,2560]{2,1,0:T(8,128)(2,1)} %bitcast.27), channel_id=1, source_target_pairs={{0,1},{1,0},{2,3},{3,2},{4,5},{5,4},{6,7},{7,6},{8,9},{9,8},{10,11... | collective-permute-start | bytes 491528 | tf_op jit(solution)/shard_map/ppermute | solution.py:14
  17.1 2.8 %copy-start = (bf16[2560,1024]{1,0:T(8,128)(2,1)S(1)}, bf16[2560,1024]{1,0:T(8,128)(2,1)}, u32[]{:S(2)}) copy-start(bf16[2560,1024]{1,0:T(8,128)(2,1)} %param.10) | copy-start | bytes 15728644
  17.2 2.7 %copy-start.7 = (bf16[1,2,2,8,2688]{4,3,2,1,0:T(8,128)(2,1)}, bf16[1,2,2,8,2688]{4,3,2,1,0:T(8,128)(2,1)S(1)}, u32[]{:S(2)}) copy-start(bf16[1,2,2,8,2688]{4,3,2,1,0:T(8,128)(2,1)S(1)} %reverse_select_fusion.10) | copy-start | bytes 516100
  17.2 2.5 %collective-permute-start.3 = (bf16[4,8,2688]{2,1,0:T(8,128)(2,1)S(1)}, bf16[4,8,2688]{2,1,0:T(8,128)(2,1)S(1)}, u32[]{:S(2)}, u32[]{:S(2)}) collective-permute-start(bf16[4,8,2688]{2,1,0:T(8,128)(2,1)S(1)} %bitcast.202), channel_id=1, source_target_pairs={{0,1},{1,0},{2,3},{3,2},{4,5},{5,4},{6,7},{7,6},{8,9},{9,8},{10,11... | collective-permute-start | bytes 516104 | tf_op jit(solution)/shard_map/ppermute | solution.py:14
  19.8 2.5 %copy-start.1 = (bf16[2560,1024]{1,0:T(8,128)(2,1)S(1)}, bf16[2560,1024]{1,0:T(8,128)(2,1)}, u32[]{:S(2)}) copy-start(bf16[2560,1024]{1,0:T(8,128)(2,1)} %param.11) | copy-start | bytes 15728644
  19.8 3.7 %slice-start.2 = ((s8[5242880]{0:T(1024)(128)(4,1)}), s8[4194304]{0:T(1024)(128)(4,1)S(1)}, s32[]{:S(2)}) async-start(s8[5242880]{0:T(1024)(128)(4,1)} %bitcast.175), calls=%async_computation.2 | async-start | bytes 8388608
  20.0 3.8 %slice-start.3 = ((s8[5242880]{0:T(1024)(128)(4,1)}), s8[1048576]{0:T(1024)(128)(4,1)S(1)}, s32[]{:S(2)}) async-start(s8[5242880]{0:T(1024)(128)(4,1)} %bitcast.175), calls=%async_computation.3 | async-start | bytes 2097152
  23.8 6.3 %copy-start.11 = (f32[2560,8]{0,1:T(8,128)S(1)}, f32[2560,8]{0,1:T(8,128)}, u32[]{:S(2)}) copy-start(f32[2560,8]{0,1:T(8,128)} %param.9) | copy-start | bytes 245764
  25.6 5.4 %collective-permute-start.18 = (f32[1,64]{1,0:T(1,128)S(1)}, f32[1,64]{1,0:T(1,128)S(1)}, u32[]{:S(2)}, u32[]{:S(2)}) collective-permute-start(f32[1,64]{1,0:T(1,128)S(1)} %bitcast.243), channel_id=1, source_target_pairs={{0,6},{1,7},{2,4},{3,5},{4,2},{5,3},{6,0},{7,1},{8,14},{9,15},{10,... | collective-permute-start | bytes 776 | tf_op jit(solution)/shard_map/ppermute | solution.py:14
  28.2 4.4 %collective-permute-start.17 = (f32[1,64]{1,0:T(1,128)S(1)}, f32[1,64]{1,0:T(1,128)S(1)}, u32[]{:S(2)}, u32[]{:S(2)}) collective-permute-start(f32[1,64]{1,0:T(1,128)S(1)} %bitcast.244), channel_id=1, source_target_pairs={{0,4},{1,5},{2,6},{3,7},{4,0},{5,1},{6,2},{7,3},{8,12},{9,13},{10,... | collective-permute-start | bytes 776 | tf_op jit(solution)/shard_map/ppermute | solution.py:14
  28.2 4.4 %collective-permute-start.16 = (f32[1,64]{1,0:T(1,128)S(1)}, f32[1,64]{1,0:T(1,128)S(1)}, u32[]{:S(2)}, u32[]{:S(2)}) collective-permute-start(f32[1,64]{1,0:T(1,128)S(1)} %bitcast.245), channel_id=1, source_target_pairs={{0,2},{1,3},{2,0},{3,1},{4,6},{5,7},{6,4},{7,5},{8,10},{9,11},{10,... | collective-permute-start | bytes 776 | tf_op jit(solution)/shard_map/ppermute | solution.py:14
  32.7 1.2 %collective-permute-start.19 = (f32[4,1,64]{2,0,1:T(4,128)S(1)}, f32[4,1,64]{2,0,1:T(4,128)S(1)}, u32[]{:S(2)}, u32[]{:S(2)}) collective-permute-start(f32[4,1,64]{2,0,1:T(4,128)S(1)} %bitcast.232), channel_id=1, source_target_pairs={{0,1},{1,0},{2,3},{3,2},{4,5},{5,4},{6,7},{7,6},{8,9},{9,8},{10,11... | collective-permute-start | bytes 3080 | tf_op jit(solution)/shard_map/ppermute | solution.py:14
  34.0 13.6 %collective-permute-start.28 = (f32[64,8]{0,1:T(8,128)S(1)}, f32[64,8]{0,1:T(8,128)S(1)}, u32[]{:S(2)}, u32[]{:S(2)}) collective-permute-start(f32[64,8]{0,1:T(8,128)S(1)} %multiply_select_fusion), channel_id=1, source_target_pairs={{0,24},{8,16},{16,8},{24,0},{1,25},{9,17},{17,9},{25,1},{2,26},{10... | collective-permute-start | bytes 6152 | tf_op jit(solution)/shard_map/ppermute | solution.py:14
  35.6 12.7 %collective-permute-start.27 = (f32[64,8]{0,1:T(8,128)S(1)}, f32[64,8]{0,1:T(8,128)S(1)}, u32[]{:S(2)}, u32[]{:S(2)}) collective-permute-start(f32[64,8]{0,1:T(8,128)S(1)} %multiply_select_fusion), channel_id=1, source_target_pairs={{0,16},{8,24},{16,0},{24,8},{1,17},{9,25},{17,1},{25,9},{2,18},{10... | collective-permute-start | bytes 6152 | tf_op jit(solution)/shard_map/ppermute | solution.py:14
  36.1 14.6 %collective-permute-start.26 = (f32[64,8]{0,1:T(8,128)S(1)}, f32[64,8]{0,1:T(8,128)S(1)}, u32[]{:S(2)}, u32[]{:S(2)}) collective-permute-start(f32[64,8]{0,1:T(8,128)S(1)} %multiply_select_fusion), channel_id=1, source_target_pairs={{0,8},{8,0},{16,24},{24,16},{1,9},{9,1},{17,25},{25,17},{2,10},{10... | collective-permute-start | bytes 6152 | tf_op jit(solution)/shard_map/ppermute | solution.py:14
  37.6 8.3 %slice-start.4 = ((s8[5242880]{0:T(1024)(128)(4,1)}), s8[4194304]{0:T(1024)(128)(4,1)S(1)}, s32[]{:S(2)}) async-start(s8[5242880]{0:T(1024)(128)(4,1)} %bitcast.177), calls=%async_computation.4 | async-start | bytes 8388608
  37.7 8.2 %slice-start.5 = ((s8[5242880]{0:T(1024)(128)(4,1)}), s8[1048576]{0:T(1024)(128)(4,1)S(1)}, s32[]{:S(2)}) async-start(s8[5242880]{0:T(1024)(128)(4,1)} %bitcast.177), calls=%async_computation.5 | async-start | bytes 2097152
  41.5 4.3 %copy-start.5 = (bf16[64,1024]{1,0:T(8,128)(2,1)}, bf16[64,1024]{1,0:T(8,128)(2,1)S(1)}, u32[]{:S(2)}) copy-start(bf16[64,1024]{1,0:T(8,128)(2,1)S(1)} %get-tuple-element.12) | copy-start | bytes 393220
  41.5 4.3 %copy-start.3 = (bf16[64,1024]{1,0:T(8,128)(2,1)}, bf16[64,1024]{1,0:T(8,128)(2,1)S(1)}, u32[]{:S(2)}) copy-start(bf16[64,1024]{1,0:T(8,128)(2,1)S(1)} %get-tuple-element.11) | copy-start | bytes 393220
  45.9 2.4 %copy-start.8 = (bf16[1,2,2,8,2688]{4,3,2,1,0:T(8,128)(2,1)S(1)}, bf16[1,2,2,8,2688]{4,3,2,1,0:T(8,128)(2,1)}, u32[]{:S(2)}) copy-start(bf16[1,2,2,8,2688]{4,3,2,1,0:T(8,128)(2,1)} %copy-done.7) | copy-start | bytes 516100
  47.7 7.4 %collective-permute-start.29 = (bf16[4,8,2560]{2,1,0:T(8,128)(2,1)}, bf16[4,8,2560]{2,1,0:T(8,128)(2,1)S(1)}, u32[]{:S(2)}, u32[]{:S(2)}) collective-permute-start(bf16[4,8,2560]{2,1,0:T(8,128)(2,1)} %bitcast.27), channel_id=1, source_target_pairs={{0,8},{8,0},{16,24},{24,16},{1,9},{9,1},{17,25},{25,17},{2,10},{10... | collective-permute-start | bytes 491528 | tf_op jit(solution)/shard_map/ppermute | solution.py:14
  48.3 11.4 %collective-permute-start.24 = (bf16[4,8,2688]{2,1,0:T(8,128)(2,1)S(1)}, bf16[4,8,2688]{2,1,0:T(8,128)(2,1)S(1)}, u32[]{:S(2)}, u32[]{:S(2)}) collective-permute-start(bf16[4,8,2688]{2,1,0:T(8,128)(2,1)S(1)} %bitcast.204), channel_id=1, source_target_pairs={{0,24},{8,16},{16,8},{24,0},{1,25},{9,17},{17,9},{25,1},{2,26},{10... | collective-permute-start | bytes 516104 | tf_op jit(solution)/shard_map/ppermute | solution.py:14
  50.7 9.0 %collective-permute-start.22 = (bf16[4,8,2688]{2,1,0:T(8,128)(2,1)S(1)}, bf16[4,8,2688]{2,1,0:T(8,128)(2,1)S(1)}, u32[]{:S(2)}, u32[]{:S(2)}) collective-permute-start(bf16[4,8,2688]{2,1,0:T(8,128)(2,1)S(1)} %bitcast.205), channel_id=1, source_target_pairs={{0,16},{8,24},{16,0},{24,8},{1,17},{9,25},{17,1},{25,9},{2,18},{10... | collective-permute-start | bytes 516104 | tf_op jit(solution)/shard_map/ppermute | solution.py:14
  51.3 9.5 %collective-permute-start.20 = (bf16[4,8,2688]{2,1,0:T(8,128)(2,1)S(1)}, bf16[4,8,2688]{2,1,0:T(8,128)(2,1)S(1)}, u32[]{:S(2)}, u32[]{:S(2)}) collective-permute-start(bf16[4,8,2688]{2,1,0:T(8,128)(2,1)S(1)} %bitcast.206), channel_id=1, source_target_pairs={{0,8},{8,0},{16,24},{24,16},{1,9},{9,1},{17,25},{25,17},{2,10},{10... | collective-permute-start | bytes 516104 | tf_op jit(solution)/shard_map/ppermute | solution.py:14
  51.9 8.9 %collective-permute-start.34 = (bf16[4,8,2560]{2,1,0:T(8,128)(2,1)}, bf16[4,8,2560]{2,1,0:T(8,128)(2,1)S(1)}, u32[]{:S(2)}, u32[]{:S(2)}) collective-permute-start(bf16[4,8,2560]{2,1,0:T(8,128)(2,1)} %collective-permute-done.33), channel_id=1, source_target_pairs={{0,1},{1,0},{2,3},{3,2},{4,5},{5,4},{6,7},{7,6},{8,9},{9,8},{10,11... | collective-permute-start | bytes 491528 | tf_op jit(solution)/shard_map/ppermute | solution.py:14
  55.1 7.2 %collective-permute-start.32 = (bf16[4,8,2560]{2,1,0:T(8,128)(2,1)}, bf16[4,8,2560]{2,1,0:T(8,128)(2,1)S(1)}, u32[]{:S(2)}, u32[]{:S(2)}) collective-permute-start(bf16[4,8,2560]{2,1,0:T(8,128)(2,1)} %collective-permute-done.31), channel_id=1, source_target_pairs={{0,1},{1,0},{2,3},{3,2},{4,5},{5,4},{6,7},{7,6},{8,9},{9,8},{10,11... | collective-permute-start | bytes 491528 | tf_op jit(solution)/shard_map/ppermute | solution.py:14
  59.7 3.7 %collective-permute-start.30 = (bf16[4,8,2560]{2,1,0:T(8,128)(2,1)S(1)}, bf16[4,8,2560]{2,1,0:T(8,128)(2,1)S(1)}, u32[]{:S(2)}, u32[]{:S(2)}) collective-permute-start(bf16[4,8,2560]{2,1,0:T(8,128)(2,1)S(1)} %collective-permute-done.29), channel_id=1, source_target_pairs={{0,1},{1,0},{2,3},{3,2},{4,5},{5,4},{6,7},{7,6},{8,9},{9,8},{10,11... | collective-permute-start | bytes 491528 | tf_op jit(solution)/shard_map/ppermute | solution.py:14
  59.7 10.1 %collective-permute-start.25 = (bf16[4,8,2688]{2,1,0:T(8,128)(2,1)S(1)}, bf16[4,8,2688]{2,1,0:T(8,128)(2,1)S(1)}, u32[]{:S(2)}, u32[]{:S(2)}) collective-permute-start(bf16[4,8,2688]{2,1,0:T(8,128)(2,1)S(1)} %collective-permute-done.24), channel_id=1, source_target_pairs={{0,1},{1,0},{2,3},{3,2},{4,5},{5,4},{6,7},{7,6},{8,9},{9,8},{10,11... | collective-permute-start | bytes 516104 | tf_op jit(solution)/shard_map/ppermute | solution.py:14
  60.8 9.2 %collective-permute-start.23 = (bf16[4,8,2688]{2,1,0:T(8,128)(2,1)S(1)}, bf16[4,8,2688]{2,1,0:T(8,128)(2,1)S(1)}, u32[]{:S(2)}, u32[]{:S(2)}) collective-permute-start(bf16[4,8,2688]{2,1,0:T(8,128)(2,1)S(1)} %collective-permute-done.22), channel_id=1, source_target_pairs={{0,1},{1,0},{2,3},{3,2},{4,5},{5,4},{6,7},{7,6},{8,9},{9,8},{10,11... | collective-permute-start | bytes 516104 | tf_op jit(solution)/shard_map/ppermute | solution.py:14
  60.8 11.3 %collective-permute-start.21 = (bf16[4,8,2688]{2,1,0:T(8,128)(2,1)S(1)}, bf16[4,8,2688]{2,1,0:T(8,128)(2,1)S(1)}, u32[]{:S(2)}, u32[]{:S(2)}) collective-permute-start(bf16[4,8,2688]{2,1,0:T(8,128)(2,1)S(1)} %collective-permute-done.20), channel_id=1, source_target_pairs={{0,1},{1,0},{2,3},{3,2},{4,5},{5,4},{6,7},{7,6},{8,9},{9,8},{10,11... | collective-permute-start | bytes 516104 | tf_op jit(solution)/shard_map/ppermute | solution.py:14
  62.3 2.5 %collective-permute-start.4 = (bf16[4,8,2560]{2,1,0:T(8,128)(2,1)S(1)}, bf16[4,8,2560]{2,1,0:T(8,128)(2,1)S(1)}, u32[]{:S(2)}, u32[]{:S(2)}) collective-permute-start(bf16[4,8,2560]{2,1,0:T(8,128)(2,1)S(1)} %dynamic-slice_bitcast_fusion.1), channel_id=1, source_target_pairs={{0,1},{1,0},{2,3},{3,2},{4,5},{5,4},{6,7},{7,6},{8,9},{9,8},{10,11... | collective-permute-start | bytes 491528 | tf_op jit(solution)/shard_map/ppermute | solution.py:14
  63.4 3.1 %collective-permute-start.12 = (bf16[4,8,2560]{2,1,0:T(8,128)(2,1)S(1)}, bf16[4,8,2560]{2,1,0:T(8,128)(2,1)S(1)}, u32[]{:S(2)}, u32[]{:S(2)}) collective-permute-start(bf16[4,8,2560]{2,1,0:T(8,128)(2,1)S(1)} %dynamic-slice_bitcast_fusion), channel_id=1, source_target_pairs={{0,1},{1,0},{2,3},{3,2},{4,5},{5,4},{6,7},{7,6},{8,9},{9,8},{10,11... | collective-permute-start | bytes 491528 | tf_op jit(solution)/shard_map/ppermute | solution.py:14
  64.0 12.7 %slice-start = ((s8[5242880]{0:T(1024)(128)(4,1)}), s8[4194304]{0:T(1024)(128)(4,1)S(1)}, s32[]{:S(2)}) async-start(s8[5242880]{0:T(1024)(128)(4,1)} %bitcast.173), calls=%async_computation | async-start | bytes 8388608
  64.9 1.6 %copy-start.10 = (bf16[4,8,2560]{2,1,0:T(8,128)(2,1)}, bf16[4,8,2560]{2,1,0:T(8,128)(2,1)S(1)}, u32[]{:S(2)}) copy-start(bf16[4,8,2560]{2,1,0:T(8,128)(2,1)S(1)} %fusion.38) | copy-start | bytes 491524
  65.6 31.0 %collective-permute-start.5 = (bf16[8,2560]{1,0:T(8,128)(2,1)}, bf16[8,2560]{1,0:T(8,128)(2,1)}, u32[]{:S(2)}, u32[]{:S(2)}) collective-permute-start(bf16[8,2560]{1,0:T(8,128)(2,1)} %get-tuple-element.16), channel_id=1, source_target_pairs={{0,2},{1,3},{2,0},{3,1},{4,6},{5,7},{6,4},{7,5},{8,10},{9,11},{10,... | collective-permute-start | bytes 122888 | tf_op jit(solution)/shard_map/ppermute | solution.py:14
  66.5 30.1 %collective-permute-start.7 = (bf16[8,2560]{1,0:T(8,128)(2,1)}, bf16[8,2560]{1,0:T(8,128)(2,1)}, u32[]{:S(2)}, u32[]{:S(2)}) collective-permute-start(bf16[8,2560]{1,0:T(8,128)(2,1)} %get-tuple-element.17), channel_id=1, source_target_pairs={{0,6},{1,7},{2,4},{3,5},{4,2},{5,3},{6,0},{7,1},{8,14},{9,15},{10,... | collective-permute-start | bytes 122888 | tf_op jit(solution)/shard_map/ppermute | solution.py:14
  69.1 0.7 copy-start.9
  69.8 26.8 %collective-permute-start.6 = (bf16[8,2560]{1,0:T(8,128)(2,1)}, bf16[8,2560]{1,0:T(8,128)(2,1)}, u32[]{:S(2)}, u32[]{:S(2)}) collective-permute-start(bf16[8,2560]{1,0:T(8,128)(2,1)} %get-tuple-element.18), channel_id=1, source_target_pairs={{0,4},{1,5},{2,6},{3,7},{4,0},{5,1},{6,2},{7,3},{8,12},{9,13},{10,... | collective-permute-start | bytes 122888 | tf_op jit(solution)/shard_map/ppermute | solution.py:14
  69.9 28.2 %collective-permute-start.13 = (bf16[8,2560]{1,0:T(8,128)(2,1)}, bf16[8,2560]{1,0:T(8,128)(2,1)S(1)}, u32[]{:S(2)}, u32[]{:S(2)}) collective-permute-start(bf16[8,2560]{1,0:T(8,128)(2,1)} %get-tuple-element.13), channel_id=1, source_target_pairs={{0,2},{1,3},{2,0},{3,1},{4,6},{5,7},{6,4},{7,5},{8,10},{9,11},{10,... | collective-permute-start | bytes 122888 | tf_op jit(solution)/shard_map/ppermute | solution.py:14
  72.0 4.6 %slice-start.1 = ((s8[5242880]{0:T(1024)(128)(4,1)}), s8[1048576]{0:T(1024)(128)(4,1)S(1)}, s32[]{:S(2)}) async-start(s8[5242880]{0:T(1024)(128)(4,1)} %bitcast.173), calls=%async_computation.1 | async-start | bytes 2097152
  72.1 26.0 %collective-permute-start.15 = (bf16[8,2560]{1,0:T(8,128)(2,1)}, bf16[8,2560]{1,0:T(8,128)(2,1)}, u32[]{:S(2)}, u32[]{:S(2)}) collective-permute-start(bf16[8,2560]{1,0:T(8,128)(2,1)} %get-tuple-element.14), channel_id=1, source_target_pairs={{0,6},{1,7},{2,4},{3,5},{4,2},{5,3},{6,0},{7,1},{8,14},{9,15},{10,... | collective-permute-start | bytes 122888 | tf_op jit(solution)/shard_map/ppermute | solution.py:14
  74.8 0.9 copy-start.12
  79.0 2.6 %copy-start.2 = (bf16[2,4,8,2560]{3,2,0,1:T(8,128)(2,1)S(1)}, bf16[2,4,8,2560]{3,2,0,1:T(8,128)(2,1)}, u32[]{:S(2)}) copy-start(bf16[2,4,8,2560]{3,2,0,1:T(8,128)(2,1)} %reverse_select_fusion.8) | copy-start | bytes 983044
  81.9 4.4 %slice-start.6 = ((s8[5242880]{0:T(1024)(128)(4,1)}), s8[4194304]{0:T(1024)(128)(4,1)S(1)}, s32[]{:S(2)}) async-start(s8[5242880]{0:T(1024)(128)(4,1)} %bitcast.179), calls=%async_computation.6 | async-start | bytes 8388608
  85.7 1.2 %slice-start.7 = ((s8[5242880]{0:T(1024)(128)(4,1)}), s8[1048576]{0:T(1024)(128)(4,1)S(1)}, s32[]{:S(2)}) async-start(s8[5242880]{0:T(1024)(128)(4,1)} %bitcast.179), calls=%async_computation.7 | async-start | bytes 2097152
  85.8 1.4 %copy-start.18 = (f32[192,1024]{1,0:T(8,128)S(1)}, f32[192,1024]{1,0:T(8,128)}, u32[]{:S(2)}) copy-start(f32[192,1024]{1,0:T(8,128)} %fusion.79) | copy-start | bytes 2359300
  88.8 2.0 %copy-start.6 = (bf16[64,1024]{1,0:T(8,128)(2,1)S(1)}, bf16[64,1024]{1,0:T(8,128)(2,1)}, u32[]{:S(2)}) copy-start(bf16[64,1024]{1,0:T(8,128)(2,1)} %copy-done.5) | copy-start | bytes 393220
  90.9 2.0 %copy-start.17 = (bf16[2,2,64,8]{2,3,1,0:T(8,128)(2,1)S(1)}, bf16[2,2,64,8]{2,3,1,0:T(8,128)(2,1)}, u32[]{:S(2)}) copy-start(bf16[2,2,64,8]{2,3,1,0:T(8,128)(2,1)} %get-tuple-element.23) | copy-start | bytes 12292
  90.9 2.4 %copy-start.16 = (bf16[2,2,64,8]{2,3,1,0:T(8,128)(2,1)S(1)}, bf16[2,2,64,8]{2,3,1,0:T(8,128)(2,1)}, u32[]{:S(2)}) copy-start(bf16[2,2,64,8]{2,3,1,0:T(8,128)(2,1)} %get-tuple-element.22) | copy-start | bytes 12292
  92.9 0.7 copy-start.15
  92.9 1.7 %copy-start.4 = (bf16[64,1024]{1,0:T(8,128)(2,1)S(1)}, bf16[64,1024]{1,0:T(8,128)(2,1)}, u32[]{:S(2)}) copy-start(bf16[64,1024]{1,0:T(8,128)(2,1)} %copy-done.3) | copy-start | bytes 393220
  94.6 2.0 %copy-start.14 = (bf16[8,2560]{1,0:T(8,128)(2,1)S(1)}, bf16[8,2560]{1,0:T(8,128)(2,1)}, u32[]{:S(2)}) copy-start(bf16[8,2560]{1,0:T(8,128)(2,1)} %get-tuple-element.15) | copy-start | bytes 122884
  94.6 6.9 %copy-start.13 = (f32[2560,8]{0,1:T(8,128)S(1)}, f32[2560,8]{0,1:T(8,128)}, u32[]{:S(2)}) copy-start(f32[2560,8]{0,1:T(8,128)} %param.9) | copy-start | bytes 245764
  96.6 4.9 %collective-permute-start.14 = (bf16[8,2560]{1,0:T(8,128)(2,1)S(1)}, bf16[8,2560]{1,0:T(8,128)(2,1)S(1)}, u32[]{:S(2)}, u32[]{:S(2)}) collective-permute-start(bf16[8,2560]{1,0:T(8,128)(2,1)S(1)} %copy-done.14), channel_id=1, source_target_pairs={{0,4},{1,5},{2,6},{3,7},{4,0},{5,1},{6,2},{7,3},{8,12},{9,13},{10,... | collective-permute-start | bytes 122888 | tf_op jit(solution)/shard_map/ppermute | solution.py:14

commit v2 on v1

v2 whole, which is shorter than its diff:
```python
import jax
import jax.numpy as jnp
from jax import lax
from jax.sharding import PartitionSpec as P

F32 = jnp.float32
BF16 = jnp.bfloat16
LANES = 128
GATHER_BYTES = 8 << 20


def swap(x, axis, mask):
    count = lax.axis_size(axis)
    return lax.ppermute(x, axis, [(i, i ^ mask) for i in range(count)])


def exact_dot(left, right, contract):
    parts = []
    rest = right
    for _ in range(3):
        part = lax.reduce_precision(rest, 8, 7)
        parts.append(part.astype(BF16))
        rest = rest - part
    return sum(
        lax.dot_general(left, part, contract, preferred_element_type=F32) for part in parts[::-1]
    )


def gates_of(rows, chosen, router):
    experts = router.shape[1]
    logits = exact_dot(rows, router, (((1,), (0,)), ((), ())))
    ids = jnp.arange(experts, dtype=BF16)
    picked = jnp.any(chosen[:, :, None] == ids[None, None, :], axis=1)
    affinity = jnp.where(picked, jax.nn.sigmoid(logits), 0.0)
    denominator = jnp.sum(affinity, axis=1, keepdims=True)
    return picked, affinity, denominator, affinity / denominator


def local(tokens, routes, router, w_gate, w_up, w_down, cotangent):
    tok_count, features = tokens.shape
    experts = router.shape[1]
    fanout = routes.shape[1]
    hidden_units = w_gate.shape[1]
    devices = lax.axis_size("expert")
    groups = lax.axis_size("dp")
    sharing = devices // experts
    chips = devices // 2
    group_rows = devices * tok_count
    me = lax.axis_index("expert")
    group = lax.axis_index("dp")
    core, chip = me % 2, me // 2
    own_expert = me // sharing
    whole = groups * group_rows * features * 4 <= GATHER_BYTES

    def over_chips(x):
        out = jnp.zeros((chips,) + x.shape, x.dtype)
        for m in range(chips):
            piece = x if m == 0 else swap(x, "expert", 2 * m)
            out = lax.dynamic_update_index_in_dim(out, piece, chip ^ m, 0)
        return out

    def over_cores(x):
        other = swap(x, "expert", 1)
        return jnp.where(core == 0, jnp.stack([x, other]), jnp.stack([other, x]))

    routes_wide = jnp.pad(routes.astype(BF16), ((0, 0), (0, LANES - fanout)))
    message = jnp.concatenate([tokens, cotangent, routes_wide], axis=1)
    width = message.shape[1]
    by_chip = over_chips(message)
    by_core = over_cores(by_chip)
    own = by_core.reshape(group_rows, width)

    def own_column(table):
        return lax.dynamic_slice_in_dim(table, own_expert, 1, axis=1)

    def backward_rows(batch):
        rows = batch[:, :features]
        cot = batch[:, features : 2 * features]
        tables = gates_of(rows, batch[:, 2 * features : 2 * features + fanout], router)
        slot_gate = own_column(tables[3])
        gate_pre = jnp.dot(rows, w_gate, preferred_element_type=F32)
        up_pre = jnp.dot(rows, w_up, preferred_element_type=F32)
        sigma = jax.nn.sigmoid(gate_pre)
        silu = gate_pre * sigma
        hidden = silu * up_pre
        raw = jnp.dot(cot, w_down, preferred_element_type=F32)
        pull = jnp.sum(hidden * raw, axis=1)
        hidden_grad = slot_gate * raw
        gate_grad = (hidden_grad * up_pre * sigma * (1.0 + gate_pre * (1.0 - sigma))).astype(BF16)
        up_grad = (hidden_grad * silu).astype(BF16)
        gated = (slot_gate * hidden).astype(BF16)
        return rows, cot, tables, gate_grad, up_grad, gated, pull

    rows, cot, tables, gate_grad, up_grad, gated, pull = backward_rows(own)
    contract = (((1,), (1,)), ((), ()))
    mixed_part = lax.dot_general(gated, w_down, contract, preferred_element_type=F32)
    input_part = lax.dot_general(
        gate_grad, w_gate, contract, preferred_element_type=F32
    ) + lax.dot_general(up_grad, w_up, contract, preferred_element_type=F32)
    part = jnp.concatenate([mixed_part.astype(BF16), input_part.astype(BF16)], axis=1)
    part = part.reshape(2, chips, tok_count, 2 * features)
    keep = lax.dynamic_index_in_dim(part, core, 0, keepdims=False).astype(F32)
    send = lax.dynamic_index_in_dim(part, 1 - core, 0, keepdims=False)
    summed = (keep + swap(send, "expert", 1).astype(F32)).astype(BF16)
    total = lax.dynamic_index_in_dim(summed, chip, 0, keepdims=False).astype(F32)
    for m in range(1, chips):
        piece = lax.dynamic_index_in_dim(summed, chip ^ m, 0, keepdims=False)
        total = total + swap(piece, "expert", 2 * m).astype(F32)
    mixed = total[:, :features].astype(BF16)
    input_sum = total[:, features:]

    def logit_grads(pull, tables):
        picked, affinity, denominator, gates = tables
        pulls = over_cores(over_chips(pull))
        pulls = jnp.swapaxes(pulls, 0, 1).reshape(experts, sharing, -1)
        pulls = jnp.sum(pulls, axis=1).T
        mean_pull = jnp.sum(gates * pulls, axis=1, keepdims=True)
        grads = (pulls - mean_pull) / denominator * affinity * (1.0 - affinity)
        return jnp.where(picked, grads, 0.0)

    first = (((0,), (0,)), ((), ()))
    place = core * chips + chip
    if whole:
        by_group = jnp.zeros((groups,) + by_chip.shape, BF16)
        for m in range(groups):
            piece = by_chip if m == 0 else swap(by_chip, "dp", m)
            by_group = lax.dynamic_update_index_in_dim(by_group, piece, group ^ m, 0)
        batch = over_cores(by_group).reshape(-1, width)
        rows, cot, tables, gate_grad, up_grad, gated, pull = backward_rows(batch)
        portion = features // groups
        rows_cut = lax.dynamic_slice_in_dim(rows, group * portion, portion, axis=1)
        cot_cut = lax.dynamic_slice_in_dim(cot, group * portion, portion, axis=1)
        grad_gate, grad_up, grad_down = [
            lax.dot_general(left, right, first, preferred_element_type=F32)
            for left, right in ((rows_cut, gate_grad), (rows_cut, up_grad), (cot_cut, gated))
        ]
        logit_grad = logit_grads(pull, tables)
        grad_router = exact_dot(rows, logit_grad, first)
        place = (core * groups + group) * chips + chip
    else:
        logit_grad = logit_grads(pull, tables)
        own_logit = lax.dynamic_slice_in_dim(logit_grad, place * tok_count, tok_count, axis=0)
        grad_router = lax.psum(exact_dot(tokens, own_logit, first), ("dp", "expert"))
        parts = [
            lax.dot_general(left, right, first, preferred_element_type=F32)
            for left, right in ((rows, gate_grad), (rows, up_grad), (cot, gated))
        ]
        summed = lax.psum_scatter(
            jnp.concatenate(parts, axis=1).astype(BF16), "dp", scatter_dimension=0, tiled=True
        ).astype(F32)
        grad_gate, grad_up, grad_down = jnp.split(summed, 3, axis=1)
    own_logit = lax.dynamic_slice_in_dim(logit_grad, place * tok_count, tok_count, axis=0)
    router_back = lax.dot_general(
        own_logit, router, (((1,), (1,)), ((), ())), precision=lax.Precision.HIGHEST
    )
    grad_tokens = (input_sum + router_back).astype(BF16)
    return (mixed, grad_tokens, grad_router, grad_gate, grad_up, grad_down)


def solution(mesh):
    return jax.shard_map(
        local,
        mesh=mesh,
        in_specs=(
            P(("dp", "expert"), None),
            P(("dp", "expert"), None),
            P(),
            P(None, "expert"),
            P(None, "expert"),
            P(None, "expert"),
            P(("dp", "expert"), None),
        ),
        out_specs=(
            P(("dp", "expert"), None),
            P(("dp", "expert"), None),
            P(),
            P("dp", "expert"),
            P("dp", "expert"),
            P("dp", "expert"),
        ),
        check_vma=False,
    )
```

time: 104 us -> 83.4 us (0.80)
  starting transfers between devices: 35.4 us -> 18.4 us
  other arithmetic: 10.8 us -> 6.69 us
    ppermute x35 -> x16, starting transfers between devices: 35.4 us -> 18.4 us  [swap(): return lax.ppermute(x, axis, [(i, i ^ mask) for i in range(count)])]
    another operation x21 -> x0, other arithmetic: 5.96 us -> none  [the longest x9 3.19 us: both_cores(): pair = ordered(jnp.stack([x, swap(x, 'expert', 1)]), core)]
    dot_general x10, matrix products: 21.5 us -> 26.8 us  [the longest x3 10.8 us: local(): lax.dot_general(left, right, first, preferred_element_type=F32)]
    dot_general x1, matrix products: 4.29 us -> 1.71 us  [local(): lax.dot_general(gate_grad, w_gate, contract, preferred_element_type=F32)]
    dot_general x9, matrix products: 5.75 us -> 3.39 us  [exact_dot(): lax.dot_general(left, part, contract, preferred_element_type=F32)]
    slice x5 -> x6, local copies, waits for them, and re-layouts: 0.27 us -> 2.51 us  [the longest x1 1.67 us: backward_rows(): cot = batch[:, features:2 * features]]
    convert_element_type x6 -> x1, other arithmetic: 2 us -> 0.08 us  [local(): summed = (keep + swap(send, 'expert', 1).astype(F32)).astype(BF16)]
    select_n x7 -> x3, other arithmetic: 1.6 us -> 3.17 us  [the longest x2 3.16 us: over_cores(): return jnp.where(core == 0, jnp.stack([x, other]), jnp.stack([other, x]))]
  transfers between devices with their start and end apart: 35 -> 16, of which waited for: 10 -> 8; matrix products, arithmetic and copies ran while one was open for 44% -> 21% of each run, Pallas kernels for 0% -> 0%
where the time goes in v2:
time: 83.4 us; the launch traced here: 82.9 us
  matrix products  34.6 us (41%)
  starting transfers between devices  18.4 us (22%)
  waiting for transfers between devices  16.2 us (19%)
  other arithmetic  6.69 us (8%)
  local copies, waits for them, and re-layouts  5.91 us (7%)
  between operations  1.12 us (1%)
    ppermute x16, starting transfers between devices, swap(): return lax.ppermute(x, axis, [(i, i ^ mask) for i in range(count)])  18.4 us
    ppermute x16, waiting for transfers between devices, swap(): return lax.ppermute(x, axis, [(i, i ^ mask) for i in range(count)])  16.2 us
    dot_general x3, matrix products, local(): lax.dot_general(left, right, first, preferred_element_type=F32)  10.8 us
    dot_general x2, matrix products, backward_rows(): gate_pre = jnp.dot(rows, w_gate, preferred_element_type=F32)  7.92 us
    dot_general x2, matrix products, backward_rows(): raw = jnp.dot(cot, w_down, preferred_element_type=F32)  3.77 us
    dot_general x9, matrix products, exact_dot(): lax.dot_general(left, part, contract, preferred_element_type=F32)  3.39 us
    select_n x2, other arithmetic, over_cores(): return jnp.where(core == 0, jnp.stack([x, other]), jnp.stack([other, x]))  3.16 us
    unnamed x32, local copies, waits for them, and re-layouts  2.83 us
  transfers between devices with their start and end apart: 16, of which 8 were waited for; matrix products, arithmetic and copies ran while one was open for 21% of the time, Pallas kernels for 0%

profile of v2, /device:TPU:0, one launch (start us, length us, event | category | flops | bytes accessed | tf_op | source)
XLA Modules:
  0.0 82.9 jit_solution(4379245235606319863)
XLA Ops:
  0.6 0.7 convert_element_type.81
  1.4 0.8 fusion.38
  2.2 4.0 %collective-permute-start.1 = (bf16[8,5248]{1,0:T(8,128)(2,1)S(1)}, bf16[8,5248]{1,0:T(8,128)(2,1)S(1)}, u32[]{:S(2)}, u32[]{:S(2)}) collective-permute-start(bf16[8,5248]{1,0:T(8,128)(2,1)S(1)} %fusion.38), channel_id=1, source_target_pairs={{0,4},{1,5},{2,6},{3,7},{4,0},{5,1},{6,2},{7,3},{8,12},{9,13},{10,... | collective-permute-start | bytes 251912 | tf_op jit(solution)/shard_map/ppermute | solution.py:14
  6.2 1.6 %collective-permute-start = (bf16[8,5248]{1,0:T(8,128)(2,1)S(1)}, bf16[8,5248]{1,0:T(8,128)(2,1)S(1)}, u32[]{:S(2)}, u32[]{:S(2)}) collective-permute-start(bf16[8,5248]{1,0:T(8,128)(2,1)S(1)} %fusion.38), channel_id=1, source_target_pairs={{0,2},{1,3},{2,0},{3,1},{4,6},{5,7},{6,4},{7,5},{8,10},{9,11},{10,... | collective-permute-start | bytes 251912 | tf_op jit(solution)/shard_map/ppermute | solution.py:14
  7.8 0.8 bitcast_dynamic-update-slice_fusion.6
  8.7 2.1 %collective-permute-done = bf16[8,5248]{1,0:T(8,128)(2,1)S(1)} collective-permute-done((bf16[8,5248]{1,0:T(8,128)(2,1)S(1)}, bf16[8,5248]{1,0:T(8,128)(2,1)S(1)}, u32[]{:S(2)}, u32[]{:S(2)}) %collective-permute-start) | collective-permute-done | bytes 84000 | tf_op jit(solution)/shard_map/ppermute | solution.py:14
  10.9 3.2 %collective-permute-done.2 = bf16[8,5248]{1,0:T(8,128)(2,1)S(1)} collective-permute-done((bf16[8,5248]{1,0:T(8,128)(2,1)S(1)}, bf16[8,5248]{1,0:T(8,128)(2,1)S(1)}, u32[]{:S(2)}, u32[]{:S(2)}) %collective-permute-start.2) | collective-permute-done | bytes 84000 | tf_op jit(solution)/shard_map/ppermute | solution.py:14
  14.1 2.6 %collective-permute-start.10 = (bf16[4,8,5248]{2,1,0:T(8,128)(2,1)S(1)}, bf16[4,8,5248]{2,1,0:T(8,128)(2,1)S(1)}, u32[]{:S(2)}, u32[]{:S(2)}) collective-permute-start(bf16[4,8,5248]{2,1,0:T(8,128)(2,1)S(1)} %bitcast_dynamic-update-slice_fusion.3), channel_id=1, source_target_pairs={{0,24},{8,16},{16,8},{24,0},{1,25},{9,17},{17,9},{25,1},{2,26},{10... | collective-permute-start | bytes 1007624 | tf_op jit(solution)/shard_map/ppermute | solution.py:14
  16.7 0.5 collective-permute-start.9
  17.2 0.5 collective-permute-start.8
  17.7 0.1 broadcast_in_dim.68
  17.8 1.5 %collective-permute-done.3 = bf16[4,8,5248]{2,1,0:T(8,128)(2,1)S(1)} collective-permute-done((bf16[4,8,5248]{2,1,0:T(8,128)(2,1)S(1)}, bf16[4,8,5248]{2,1,0:T(8,128)(2,1)S(1)}, u32[]{:S(2)}, u32[]{:S(2)}) %collective-permute-start.3) | collective-permute-done | bytes 335904 | tf_op jit(solution)/shard_map/ppermute | solution.py:14
  19.3 0.1 maximum_select_fusion.1
  19.4 0.2 fusion.30
  19.6 0.2 convolution_add_fusion.6
  19.8 0.1 copy.16
  20.0 0.0 copy-start
  20.0 3.7 %fusion.26 = f32[64,1024]{1,0:T(8,128)S(1)} fusion(bf16[2560,1024]{1,0:T(8,128)(2,1)} %param.10, bf16[64,5248]{1,0:T(8,128)(2,1)S(1)} %bitcast.89), kind=kOutput, calls=%fused_computation.52 | convolution fusion | flops 335544320 | bytes 5832704 | tf_op jit(solution)/shard_map/dot_general | solution.py:81
  23.7 0.3 copy-done
  24.0 1.0 %fusion.24 = f32[64,1024]{1,0:T(8,128)S(1)} fusion(bf16[2560,1024]{1,0:T(8,128)(2,1)S(1)} %copy-done, bf16[64,5248]{1,0:T(8,128)(2,1)S(1)} %bitcast.90), kind=kOutput, calls=%fused_computation.50 | convolution fusion | flops 335544320 | bytes 5832704 | tf_op jit(solution)/shard_map/dot_general | solution.py:82
  25.1 0.0 slice-start
  25.1 0.2 fusion.81
  25.3 1.2 %copy-done.1 = bf16[2560,1024]{1,0:T(8,128)(2,1)S(1)} copy-done((bf16[2560,1024]{1,0:T(8,128)(2,1)S(1)}, bf16[2560,1024]{1,0:T(8,128)(2,1)}, u32[]{:S(2)}) %copy-start.1) | copy-done | bytes 5242904
  26.5 1.0 %convolution_multiply_fusion = f32[64,1024]{1,0:T(8,128)S(1)} fusion(bf16[2560,1024]{1,0:T(8,128)(2,1)S(1)} %copy-done.1, bf16[64,5248]{1,0:T(8,128)(2,1)S(1)} %bitcast.92, f32[64]{0:T(128)S(1)} %fusion.59), kind=kOutput, calls=%fused_computation.6 | convolution fusion | flops 335609856 | bytes 5833216 | tf_op jit(solution)/shard_map/dot_general | solution.py:86
  27.5 1.7 %convolution_convert_fusion = bf16[64,2560]{1,0:T(8,128)(2,1)S(1)} fusion(bf16[2560,1024]{1,0:T(8,128)(2,1)S(1)} %copy-done.1, f32[64,1024]{1,0:T(8,128)S(1)} %fusion.24, f32[64]{0:T(128)S(1)} %fusion.59, f32[64,1024]{1,0:T(8,128)S(1)} %fusion.26), kind=kOutput, calls=%fused_computation.2 | convolution fusion | flops 336166912 | bytes 6095104 | tf_op jit(solution)/shard_map/dot_general | solution.py:96
  29.3 1.7 %fusion.35 = f32[64,2560]{1,0:T(8,128)S(1)} fusion(bf16[2560,1024]{1,0:T(8,128)(2,1)S(1)} %bitcast.69, f32[64,1024]{1,0:T(8,128)S(1)} %fusion.26, f32[64,1024]{1,0:T(8,128)S(1)} %convolution_multiply_fusion, f32[64,1024]{1,0:T(8,128)S(1)} %fusion.24), kind=kOutput, calls=%fused_computation.63 | convolution fusion | flops 336199680 | bytes 6684672 | tf_op jit(solution)/shard_map/dot_general | solution.py:97
  31.0 1.7 %fusion = bf16[64,2560]{1,0:T(8,128)(2,1)S(1)} fusion(f32[64,2560]{1,0:T(8,128)S(1)} %fusion.35, bf16[2560,1024]{1,0:T(8,128)(2,1)S(1)} %copy-done, f32[64,1024]{1,0:T(8,128)S(1)} %convolution_multiply_fusion, f32[64,1024]{1,0:T(8,128)S(1)} %fusion.26), kind=kOutput, calls=%fused_computation.1 | convolution fusion | flops 336265216 | bytes 6750208 | tf_op jit(solution)/shard_map/dot_general | solution.py:99
  32.8 0.2 collective-permute-start.4
  33.2 0.4 collective-permute-start.11
  33.6 0.9 %collective-permute-done.4 = bf16[4,8,5120]{2,1,0:T(8,128)(2,1)S(1)} collective-permute-done((bf16[4,8,5120]{2,1,0:T(8,128)(2,1)S(1)}, bf16[4,8,5120]{2,1,0:T(8,128)(2,1)S(1)}, u32[]{:S(2)}, u32[]{:S(2)}) %collective-permute-start.4) | collective-permute-done | bytes 327712 | tf_op jit(solution)/shard_map/ppermute | solution.py:14
  34.5 0.1 fusion.12
  34.6 0.8 collective-permute-start.5
  35.4 3.4 %collective-permute-start.7 = (bf16[8,5120]{1,0:T(8,128)(2,1)S(1)}, bf16[8,5120]{1,0:T(8,128)(2,1)S(1)}, u32[]{:S(2)}, u32[]{:S(2)}) collective-permute-start(bf16[8,5120]{1,0:T(8,128)(2,1)S(1)} %get-tuple-element.11), channel_id=1, source_target_pairs={{0,6},{1,7},{2,4},{3,5},{4,2},{5,3},{6,0},{7,1},{8,14},{9,15},{10,... | collective-permute-start | bytes 245768 | tf_op jit(solution)/shard_map/ppermute | solution.py:14
  38.8 0.4 collective-permute-done.5
  39.2 4.7 %collective-permute-done.7 = bf16[8,5120]{1,0:T(8,128)(2,1)S(1)} collective-permute-done((bf16[8,5120]{1,0:T(8,128)(2,1)S(1)}, bf16[8,5120]{1,0:T(8,128)(2,1)S(1)}, u32[]{:S(2)}, u32[]{:S(2)}) %collective-permute-start.7) | collective-permute-done | bytes 81952 | tf_op jit(solution)/shard_map/ppermute | solution.py:14
  43.9 2.6 %collective-permute-done.6 = bf16[8,5120]{1,0:T(8,128)(2,1)} collective-permute-done((bf16[8,5120]{1,0:T(8,128)(2,1)S(1)}, bf16[8,5120]{1,0:T(8,128)(2,1)}, u32[]{:S(2)}, u32[]{:S(2)}) %collective-permute-start.6) | collective-permute-done | bytes 81952 | tf_op jit(solution)/shard_map/ppermute | solution.py:14
  46.5 0.9 %fusion.34 = f32[8,5120]{1,0:T(8,128)S(1)} fusion(bf16[8,5120]{1,0:T(8,128)(2,1)S(1)} %collective-permute-done.7, bf16[8,5120]{1,0:T(8,128)(2,1)} %collective-permute-done.6, bf16[8,5120]{1,0:T(8,128)(2,1)S(1)} %collective-permute-done.5, bf16[4,8,5120]{2,1,0:T(8,128)(2,1)S(1)} %fusion.12, s32[]{:T(128)S(6)} %select_n.112), kind=kLoop, calls=%fused_computation.62 | loop fusion | flops 286720 | bytes 491524 | tf_op jit(solution)/shard_map/add | solution.py:108
  47.5 0.6 slice.75
  48.1 1.1 %copy-done.3 = bf16[4,4,8,5248]{3,2,1,0:T(8,128)(2,1)} copy-done((bf16[4,4,8,5248]{3,2,1,0:T(8,128)(2,1)}, bf16[4,4,8,5248]{3,2,1,0:T(8,128)(2,1)S(1)}, u32[]{:S(2)}) %copy-start.3) | copy-done | bytes 1343512
  49.2 3.0 %maximum_select_fusion = bf16[2,4,4,8,5248]{4,3,2,1,0:T(8,128)(2,1)S(1)} fusion(bf16[1,4,4,8,5248]{4,3,2,1,0:T(8,128)(2,1)} %bitcast.96, bf16[1,4,4,8,5248]{4,3,2,1,0:T(8,128)(2,1)} %bitcast.85, pred[]{:T(512)S(6)} %eq.16), kind=kLoop, calls=%fused_computation.5 | loop fusion | flops 4030464 | bytes 5373953 | tf_op jit(solution)/shard_map/jit(_where)/select_n | solution.py:64
  52.2 0.0 slice-start.2
  52.2 0.4 fusion.52
  52.7 0.0 slice-start.3
  52.7 0.0 slice-start.4
  52.7 4.2 %fusion.78 = f32[256,1024]{1,0:T(8,128)S(1)} fusion(bf16[2560,1024]{1,0:T(8,128)(2,1)} %param.10, bf16[256,5248]{1,0:T(8,128)(2,1)S(1)} %bitcast.76), kind=kOutput, calls=%fused_computation.127 | convolution fusion | flops 1342177280 | bytes 7602176 | tf_op jit(solution)/shard_map/dot_general | solution.py:81
  57.0 0.0 slice-start.5
  57.0 1.6 %fusion.76 = f32[256,1024]{1,0:T(8,128)S(1)} fusion(bf16[2560,1024]{1,0:T(8,128)(2,1)S(1)} %bitcast.71, bf16[256,5248]{1,0:T(8,128)(2,1)S(1)} %bitcast.77), kind=kOutput, calls=%fused_computation.125 | convolution fusion | flops 1342177280 | bytes 7602176 | tf_op jit(solution)/shard_map/dot_general | solution.py:82
  58.6 0.1 slice-done.5
  58.8 2.7 %multiply_reduce_fusion = (f32[256]{0:T(256)S(1)}, f32[256,1024]{1,0:T(8,128)}) fusion(f32[256,1024]{1,0:T(8,128)S(1)} %fusion.76, f32[256,1024]{1,0:T(8,128)S(1)} %fusion.78, bf16[2560,1024]{1,0:T(8,128)(2,1)S(1)} %bitcast.73, bf16[256,5248]{1,0:T(8,128)(2,1)S(1)} %bitcast.78), kind=kOutput, calls=%fused_computation.24 | convolution fusion | flops 1344012032 | bytes 9700352 | tf_op jit(solution)/shard_map/dot_general | solution.py:86
  61.5 1.6 %collective-permute-start.14 = (f32[256]{0:T(256)S(1)}, f32[256]{0:T(256)S(1)}, u32[]{:S(2)}, u32[]{:S(2)}) collective-permute-start(f32[256]{0:T(256)S(1)} %get-tuple-element.15), channel_id=1, source_target_pairs={{0,6},{1,7},{2,4},{3,5},{4,2},{5,3},{6,0},{7,1},{8,14},{9,15},{10,... | collective-permute-start | bytes 3080 | tf_op jit(solution)/shard_map/ppermute | solution.py:14
  63.1 2.7 %collective-permute-start.12 = (f32[256]{0:T(256)S(1)}, f32[256]{0:T(256)S(1)}, u32[]{:S(2)}, u32[]{:S(2)}) collective-permute-start(f32[256]{0:T(256)S(1)} %get-tuple-element.15), channel_id=1, source_target_pairs={{0,2},{1,3},{2,0},{3,1},{4,6},{5,7},{6,4},{7,5},{8,10},{9,11},{10,... | collective-permute-start | bytes 3080 | tf_op jit(solution)/shard_map/ppermute | solution.py:14
  65.9 1.7 %fusion.80 = (bf16[256,2560]{1,0:T(8,128)(2,1)}, bf16[256,2560]{1,0:T(8,128)(2,1)}) fusion(bf16[256,5248]{1,0:T(8,128)(2,1)S(1)} %bitcast.79), kind=kLoop, calls=%fused_computation.129 | loop fusion | bytes 5242880 | tf_op jit(solution)/shard_map/slice | solution.py:78
  67.6 0.4 convolution_add_fusion.4
  68.0 0.1 copy.17
  68.3 0.1 collective-permute-start.15
  68.4 0.5 fusion.82
  68.9 0.7 collective-permute-done.15
  69.7 4.4 %fusion.17 = f32[640,1024]{1,0:T(8,128)} fusion(f32[256,1024]{1,0:T(8,128)} %copy-done.5, f32[256,1024]{1,0:T(8,128)} %copy-done.7, f32[256,1024]{1,0:T(8,128)} %get-tuple-element.16, f32[256]{0:T(256)S(1)} %bitcast.102, bf16[256,2560]{1,0:T(8,128)(2,1)} %get-tuple-element.9, s32[]{:T(128)S(6)} %select_n.134), kind=kOutput, calls=%fused_computation.35 | convolution fusion | flops 338427904 | bytes 6095876 | tf_op jit(solution)/shard_map/dot_general | solution.py:134
  74.1 3.2 %fusion.13 = f32[640,1024]{1,0:T(8,128)} fusion(f32[256,1024]{1,0:T(8,128)S(1)} %copy-done.9, f32[256]{0:T(256)S(1)} %bitcast.103, bf16[256,2560]{1,0:T(8,128)(2,1)} %get-tuple-element.9, s32[]{:T(128)S(6)} %select_n.134, f32[256,1024]{1,0:T(8,128)S(1)} %copy-done.6), kind=kOutput, calls=%fused_computation.31 | convolution fusion | flops 337379328 | bytes 5047300 | tf_op jit(solution)/shard_map/dot_general | solution.py:134
  77.3 0.3 fusion.57
  77.6 1.0 %fusion.41 = bf16[8,2560]{1,0:T(8,128)(2,1)} fusion(f32[8,5120]{1,0:T(8,128)S(1)} %fusion.34, f32[2560,8]{0,1:T(8,128)S(1)} %copy-done.4, f32[256,8]{0,1:T(8,128)S(1)} %fusion.51, s32[]{:T(128)S(6)} %select_n.133), kind=kOutput, calls=%fused_computation.78 | convolution fusion | flops 2007040 | bytes 208900 | tf_op jit(solution)/shard_map/dot_general | solution.py:153
  78.6 0.3 convolution_add_fusion.2
  78.8 0.9 %convolution_add_fusion.1 = f32[2560,8]{0,1:T(8,128)} fusion(f32[2560,8]{0,1:T(8,128)S(1)} %convolution_add_fusion.2, f32[256,8]{0,1:T(8,128)S(1)} %fusion.51, bf16[256,5248]{1,0:T(8,128)(2,1)S(1)} %bitcast.84), kind=kOutput, calls=%fused_computation.3 | convolution fusion | flops 10510336 | bytes 1482752 | tf_op jit(solution)/shard_map/dot_general | solution.py:25
  79.8 3.2 %fusion.14 = f32[640,1024]{1,0:T(8,128)} fusion(f32[256]{0:T(256)S(1)} %bitcast.104, f32[256,1024]{1,0:T(8,128)S(1)} %copy-done.8, bf16[256,2560]{1,0:T(8,128)(2,1)} %get-tuple-element.8, s32[]{:T(128)S(6)} %select_n.134, f32[256,1024]{1,0:T(8,128)S(1)} %copy-done.6), kind=kOutput, calls=%fused_computation.32 | convolution fusion | flops 337379328 | bytes 5047300 | tf_op jit(solution)/shard_map/dot_general | solution.py:134
  (66 shorter events, 0.7 us)
Async XLA Ops:
  0.6 18.8 %copy-start.4 = (f32[2560,8]{0,1:T(8,128)S(1)}, f32[2560,8]{0,1:T(8,128)}, u32[]{:S(2)}) copy-start(f32[2560,8]{0,1:T(8,128)} %param.9) | copy-start | bytes 245764
  2.2 8.7 %collective-permute-start.1 = (bf16[8,5248]{1,0:T(8,128)(2,1)S(1)}, bf16[8,5248]{1,0:T(8,128)(2,1)S(1)}, u32[]{:S(2)}, u32[]{:S(2)}) collective-permute-start(bf16[8,5248]{1,0:T(8,128)(2,1)S(1)} %fusion.38), channel_id=1, source_target_pairs={{0,4},{1,5},{2,6},{3,7},{4,0},{5,1},{6,2},{7,3},{8,12},{9,13},{10,... | collective-permute-start | bytes 251912 | tf_op jit(solution)/shard_map/ppermute | solution.py:14
  6.2 4.6 %collective-permute-start = (bf16[8,5248]{1,0:T(8,128)(2,1)S(1)}, bf16[8,5248]{1,0:T(8,128)(2,1)S(1)}, u32[]{:S(2)}, u32[]{:S(2)}) collective-permute-start(bf16[8,5248]{1,0:T(8,128)(2,1)S(1)} %fusion.38), channel_id=1, source_target_pairs={{0,2},{1,3},{2,0},{3,1},{4,6},{5,7},{6,4},{7,5},{8,10},{9,11},{10,... | collective-permute-start | bytes 251912 | tf_op jit(solution)/shard_map/ppermute | solution.py:14
  7.8 6.3 %collective-permute-start.2 = (bf16[8,5248]{1,0:T(8,128)(2,1)S(1)}, bf16[8,5248]{1,0:T(8,128)(2,1)S(1)}, u32[]{:S(2)}, u32[]{:S(2)}) collective-permute-start(bf16[8,5248]{1,0:T(8,128)(2,1)S(1)} %fusion.38), channel_id=1, source_target_pairs={{0,6},{1,7},{2,4},{3,5},{4,2},{5,3},{6,0},{7,1},{8,14},{9,15},{10,... | collective-permute-start | bytes 251912 | tf_op jit(solution)/shard_map/ppermute | solution.py:14
  14.1 19.0 %collective-permute-start.10 = (bf16[4,8,5248]{2,1,0:T(8,128)(2,1)S(1)}, bf16[4,8,5248]{2,1,0:T(8,128)(2,1)S(1)}, u32[]{:S(2)}, u32[]{:S(2)}) collective-permute-start(bf16[4,8,5248]{2,1,0:T(8,128)(2,1)S(1)} %bitcast_dynamic-update-slice_fusion.3), channel_id=1, source_target_pairs={{0,24},{8,16},{16,8},{24,0},{1,25},{9,17},{17,9},{25,1},{2,26},{10... | collective-permute-start | bytes 1007624 | tf_op jit(solution)/shard_map/ppermute | solution.py:14
  16.7 16.4 %collective-permute-start.9 = (bf16[4,8,5248]{2,1,0:T(8,128)(2,1)S(1)}, bf16[4,8,5248]{2,1,0:T(8,128)(2,1)S(1)}, u32[]{:S(2)}, u32[]{:S(2)}) collective-permute-start(bf16[4,8,5248]{2,1,0:T(8,128)(2,1)S(1)} %bitcast_dynamic-update-slice_fusion.3), channel_id=1, source_target_pairs={{0,16},{8,24},{16,0},{24,8},{1,17},{9,25},{17,1},{25,9},{2,18},{10... | collective-permute-start | bytes 1007624 | tf_op jit(solution)/shard_map/ppermute | solution.py:14
  17.2 15.8 %collective-permute-start.8 = (bf16[4,8,5248]{2,1,0:T(8,128)(2,1)S(1)}, bf16[4,8,5248]{2,1,0:T(8,128)(2,1)S(1)}, u32[]{:S(2)}, u32[]{:S(2)}) collective-permute-start(bf16[4,8,5248]{2,1,0:T(8,128)(2,1)S(1)} %bitcast_dynamic-update-slice_fusion.3), channel_id=1, source_target_pairs={{0,8},{8,0},{16,24},{24,16},{1,9},{9,1},{17,25},{25,17},{2,10},{10... | collective-permute-start | bytes 1007624 | tf_op jit(solution)/shard_map/ppermute | solution.py:14
  17.7 1.6 %collective-permute-start.3 = (bf16[4,8,5248]{2,1,0:T(8,128)(2,1)S(1)}, bf16[4,8,5248]{2,1,0:T(8,128)(2,1)S(1)}, u32[]{:S(2)}, u32[]{:S(2)}) collective-permute-start(bf16[4,8,5248]{2,1,0:T(8,128)(2,1)S(1)} %bitcast_dynamic-update-slice_fusion.3), channel_id=1, source_target_pairs={{0,1},{1,0},{2,3},{3,2},{4,5},{5,4},{6,7},{7,6},{8,9},{9,8},{10,11... | collective-permute-start | bytes 1007624 | tf_op jit(solution)/shard_map/ppermute | solution.py:14
  20.0 4.0 %copy-start = (bf16[2560,1024]{1,0:T(8,128)(2,1)S(1)}, bf16[2560,1024]{1,0:T(8,128)(2,1)}, u32[]{:S(2)}) copy-start(bf16[2560,1024]{1,0:T(8,128)(2,1)} %param.11) | copy-start | bytes 15728644
  24.0 2.5 %copy-start.1 = (bf16[2560,1024]{1,0:T(8,128)(2,1)S(1)}, bf16[2560,1024]{1,0:T(8,128)(2,1)}, u32[]{:S(2)}) copy-start(bf16[2560,1024]{1,0:T(8,128)(2,1)} %param.12) | copy-start | bytes 15728644
  25.1 4.2 %slice-start = ((s8[5242880]{0:T(1024)(128)(4,1)}), s8[4194304]{0:T(1024)(128)(4,1)S(1)}, s32[]{:S(2)}) async-start(s8[5242880]{0:T(1024)(128)(4,1)} %bitcast.68), calls=%async_computation | async-start | bytes 8388608
  26.5 2.8 %slice-start.1 = ((s8[5242880]{0:T(1024)(128)(4,1)}), s8[1048576]{0:T(1024)(128)(4,1)S(1)}, s32[]{:S(2)}) async-start(s8[5242880]{0:T(1024)(128)(4,1)} %bitcast.68), calls=%async_computation.1 | async-start | bytes 2097152
  32.8 1.7 %collective-permute-start.4 = (bf16[4,8,5120]{2,1,0:T(8,128)(2,1)S(1)}, bf16[4,8,5120]{2,1,0:T(8,128)(2,1)S(1)}, u32[]{:S(2)}, u32[]{:S(2)}) collective-permute-start(bf16[4,8,5120]{2,1,0:T(8,128)(2,1)S(1)} %dynamic-slice_bitcast_fusion), channel_id=1, source_target_pairs={{0,1},{1,0},{2,3},{3,2},{4,5},{5,4},{6,7},{7,6},{8,9},{9,8},{10,11... | collective-permute-start | bytes 983048 | tf_op jit(solution)/shard_map/ppermute | solution.py:14
  33.2 14.9 %copy-start.2 = (bf16[4,4,8,5248]{3,2,1,0:T(8,128)(2,1)}, bf16[4,4,8,5248]{3,2,1,0:T(8,128)(2,1)S(1)}, u32[]{:S(2)}) copy-start(bf16[4,4,8,5248]{3,2,1,0:T(8,128)(2,1)S(1)} %bitcast_dynamic-update-slice_fusion) | copy-start | bytes 4030468
  33.2 14.9 %collective-permute-start.11 = (bf16[4,4,8,5248]{3,2,1,0:T(8,128)(2,1)S(1)}, bf16[4,4,8,5248]{3,2,1,0:T(8,128)(2,1)S(1)}, u32[]{:S(2)}, u32[]{:S(2)}) collective-permute-start(bf16[4,4,8,5248]{3,2,1,0:T(8,128)(2,1)S(1)} %bitcast_dynamic-update-slice_fusion), channel_id=1, source_target_pairs={{0,1},{1,0},{2,3},{3,2},{4,5},{5,4},{6,7},{7,6},{8,9},{9,8},{10,11... | collective-permute-start | bytes 4030472 | tf_op jit(solution)/shard_map/ppermute | solution.py:14
  34.6 4.6 %collective-permute-start.5 = (bf16[8,5120]{1,0:T(8,128)(2,1)S(1)}, bf16[8,5120]{1,0:T(8,128)(2,1)S(1)}, u32[]{:S(2)}, u32[]{:S(2)}) collective-permute-start(bf16[8,5120]{1,0:T(8,128)(2,1)S(1)} %get-tuple-element.10), channel_id=1, source_target_pairs={{0,2},{1,3},{2,0},{3,1},{4,6},{5,7},{6,4},{7,5},{8,10},{9,11},{10,... | collective-permute-start | bytes 245768 | tf_op jit(solution)/shard_map/ppermute | solution.py:14
  35.4 8.5 %collective-permute-start.7 = (bf16[8,5120]{1,0:T(8,128)(2,1)S(1)}, bf16[8,5120]{1,0:T(8,128)(2,1)S(1)}, u32[]{:S(2)}, u32[]{:S(2)}) collective-permute-start(bf16[8,5120]{1,0:T(8,128)(2,1)S(1)} %get-tuple-element.11), channel_id=1, source_target_pairs={{0,6},{1,7},{2,4},{3,5},{4,2},{5,3},{6,0},{7,1},{8,14},{9,15},{10,... | collective-permute-start | bytes 245768 | tf_op jit(solution)/shard_map/ppermute | solution.py:14
  38.8 7.7 %collective-permute-start.6 = (bf16[8,5120]{1,0:T(8,128)(2,1)S(1)}, bf16[8,5120]{1,0:T(8,128)(2,1)}, u32[]{:S(2)}, u32[]{:S(2)}) collective-permute-start(bf16[8,5120]{1,0:T(8,128)(2,1)S(1)} %get-tuple-element.12), channel_id=1, source_target_pairs={{0,4},{1,5},{2,6},{3,7},{4,0},{5,1},{6,2},{7,3},{8,12},{9,13},{10,... | collective-permute-start | bytes 245768 | tf_op jit(solution)/shard_map/ppermute | solution.py:14
  48.1 1.1 %copy-start.3 = (bf16[4,4,8,5248]{3,2,1,0:T(8,128)(2,1)}, bf16[4,4,8,5248]{3,2,1,0:T(8,128)(2,1)S(1)}, u32[]{:S(2)}) copy-start(bf16[4,4,8,5248]{3,2,1,0:T(8,128)(2,1)S(1)} %collective-permute-done.11) | copy-start | bytes 4030468
  52.2 4.7 %slice-start.2 = ((s8[5242880]{0:T(1024)(128)(4,1)}), s8[4194304]{0:T(1024)(128)(4,1)S(1)}, s32[]{:S(2)}) async-start(s8[5242880]{0:T(1024)(128)(4,1)} %bitcast.70), calls=%async_computation.2 | async-start | bytes 8388608
  52.7 4.3 %slice-start.3 = ((s8[5242880]{0:T(1024)(128)(4,1)}), s8[1048576]{0:T(1024)(128)(4,1)S(1)}, s32[]{:S(2)}) async-start(s8[5242880]{0:T(1024)(128)(4,1)} %bitcast.70), calls=%async_computation.3 | async-start | bytes 2097152
  52.7 5.9 %slice-start.4 = ((s8[5242880]{0:T(1024)(128)(4,1)}), s8[4194304]{0:T(1024)(128)(4,1)S(1)}, s32[]{:S(2)}) async-start(s8[5242880]{0:T(1024)(128)(4,1)} %bitcast.72), calls=%async_computation.4 | async-start | bytes 8388608
  57.0 1.6 %copy-start.5 = (f32[256,1024]{1,0:T(8,128)}, f32[256,1024]{1,0:T(8,128)S(1)}, u32[]{:S(2)}) copy-start(f32[256,1024]{1,0:T(8,128)S(1)} %fusion.78) | copy-start | bytes 3145732
  57.0 1.8 %slice-start.5 = ((s8[5242880]{0:T(1024)(128)(4,1)}), s8[1048576]{0:T(1024)(128)(4,1)S(1)}, s32[]{:S(2)}) async-start(s8[5242880]{0:T(1024)(128)(4,1)} %bitcast.72), calls=%async_computation.5 | async-start | bytes 2097152
  58.8 2.7 %copy-start.7 = (f32[256,1024]{1,0:T(8,128)}, f32[256,1024]{1,0:T(8,128)S(1)}, u32[]{:S(2)}) copy-start(f32[256,1024]{1,0:T(8,128)S(1)} %fusion.76) | copy-start | bytes 3145732
  61.5 6.8 %collective-permute-start.14 = (f32[256]{0:T(256)S(1)}, f32[256]{0:T(256)S(1)}, u32[]{:S(2)}, u32[]{:S(2)}) collective-permute-start(f32[256]{0:T(256)S(1)} %get-tuple-element.15), channel_id=1, source_target_pairs={{0,6},{1,7},{2,4},{3,5},{4,2},{5,3},{6,0},{7,1},{8,14},{9,15},{10,... | collective-permute-start | bytes 3080 | tf_op jit(solution)/shard_map/ppermute | solution.py:14
  63.1 5.1 %collective-permute-start.13 = (f32[256]{0:T(256)S(1)}, f32[256]{0:T(256)S(1)}, u32[]{:S(2)}, u32[]{:S(2)}) collective-permute-start(f32[256]{0:T(256)S(1)} %get-tuple-element.15), channel_id=1, source_target_pairs={{0,4},{1,5},{2,6},{3,7},{4,0},{5,1},{6,2},{7,3},{8,12},{9,13},{10,... | collective-permute-start | bytes 3080 | tf_op jit(solution)/shard_map/ppermute | solution.py:14
  63.1 5.0 %collective-permute-start.12 = (f32[256]{0:T(256)S(1)}, f32[256]{0:T(256)S(1)}, u32[]{:S(2)}, u32[]{:S(2)}) collective-permute-start(f32[256]{0:T(256)S(1)} %get-tuple-element.15), channel_id=1, source_target_pairs={{0,2},{1,3},{2,0},{3,1},{4,6},{5,7},{6,4},{7,5},{8,10},{9,11},{10,... | collective-permute-start | bytes 3080 | tf_op jit(solution)/shard_map/ppermute | solution.py:14
  68.3 1.2 %collective-permute-start.15 = (f32[4,256]{1,0:T(4,128)S(1)}, f32[4,256]{1,0:T(4,128)S(1)}, u32[]{:S(2)}, u32[]{:S(2)}) collective-permute-start(f32[4,256]{1,0:T(4,128)S(1)} %dynamic_update_slice.50), channel_id=1, source_target_pairs={{0,1},{1,0},{2,3},{3,2},{4,5},{5,4},{6,7},{7,6},{8,9},{9,8},{10,11... | collective-permute-start | bytes 12296 | tf_op jit(solution)/shard_map/ppermute | solution.py:14
  69.7 4.5 %copy-start.6 = (f32[256,1024]{1,0:T(8,128)S(1)}, f32[256,1024]{1,0:T(8,128)}, u32[]{:S(2)}) copy-start(f32[256,1024]{1,0:T(8,128)} %copy-done.5) | copy-start | bytes 3145732
  69.7 4.5 %copy-start.9 = (f32[256,1024]{1,0:T(8,128)S(1)}, f32[256,1024]{1,0:T(8,128)}, u32[]{:S(2)}) copy-start(f32[256,1024]{1,0:T(8,128)} %get-tuple-element.16) | copy-start | bytes 3145732
  77.3 2.5 %copy-start.8 = (f32[256,1024]{1,0:T(8,128)S(1)}, f32[256,1024]{1,0:T(8,128)}, u32[]{:S(2)}) copy-start(f32[256,1024]{1,0:T(8,128)} %copy-done.7) | copy-start | bytes 3145732

commit v3 on v2

v3 whole, which is shorter than its diff:
```python
import jax
import jax.numpy as jnp
from jax import lax
from jax.experimental import pallas as pl
from jax.experimental.pallas import tpu as pltpu
from jax.sharding import PartitionSpec as P

F32 = jnp.float32
BF16 = jnp.bfloat16
LANES = 128
STEP = 256
GATHER_BYTES = 8 << 20
VMEM_LIMIT = 24 << 20
HIGHEST = lax.Precision.HIGHEST
LAST = (((1,), (1,)), ((), ()))
FIRST = (((0,), (0,)), ((), ()))
IN_VMEM = pl.BlockSpec(memory_space=pltpu.VMEM)
IN_SMEM = pl.BlockSpec(memory_space=pltpu.SMEM)


def dot(left, right, contract=(((1,), (0,)), ((), ()))):
    return lax.dot_general(left, right, contract, preferred_element_type=F32)


def swap(x, axis, mask):
    count = lax.axis_size(axis)
    return lax.ppermute(x, axis, [(i, i ^ mask) for i in range(count)])


def three_parts(x):
    parts = []
    for _ in range(3):
        part = lax.reduce_precision(x, 8, 7)
        parts.append(part.astype(BF16))
        x = x - part
    return parts


def exact_dot(left, right, contract):
    return sum(dot(left, part, contract) for part in three_parts(right)[::-1])


def gates_of(rows, chosen, router):
    logits = exact_dot(rows, router, (((1,), (0,)), ((), ())))
    picked = chosen > 0.5
    affinity = jnp.where(picked, jax.nn.sigmoid(logits), 0.0)
    denominator = jnp.sum(affinity, axis=1, keepdims=True)
    return picked, affinity, denominator, affinity / denominator


def place_rows(x_ref, core, mine_ref, theirs_ref):
    half = mine_ref.shape[0]
    x_ref[pl.ds(pl.multiple_of(core * half, half), half), :] = mine_ref[...]
    x_ref[pl.ds(pl.multiple_of((1 - core) * half, half), half), :] = theirs_ref[...]


def gate_tables(x_ref, parts_ref, features, experts):
    logits = dot(parts_ref[...], x_ref[:, :features], LAST)
    logits = logits[2 * experts :] + logits[experts : 2 * experts] + logits[:experts]
    unit = lax.broadcasted_iota(jnp.int32, (experts, LANES), 0) == lax.broadcasted_iota(
        jnp.int32, (experts, LANES), 1
    )
    picked = dot(unit.astype(BF16), x_ref[:, 2 * features :], LAST) > 0.5
    affinity = jnp.where(picked, 1.0 / (1.0 + jnp.exp(-logits)), 0.0)
    denominator = jnp.sum(affinity, axis=0, keepdims=True)
    return affinity, denominator, affinity / denominator


def slot_gates(gates, expert):
    own = lax.broadcasted_iota(jnp.int32, (gates.shape[0], LANES), 0) == expert
    return lax.dot_general(
        gates, own.astype(F32), FIRST, precision=HIGHEST, preferred_element_type=F32
    )


def hidden_step(start, x_ref, slot_gate, w_gate_ref, w_up_ref, w_down_ref, grads, pull_ref):
    features = w_gate_ref.shape[0]
    at = pl.ds(pl.multiple_of(start, STEP), STEP)
    gate_pre = dot(x_ref[:, :features], w_gate_ref[:, at])
    up_pre = dot(x_ref[:, :features], w_up_ref[:, at])
    raw = dot(x_ref[:, features : 2 * features], w_down_ref[:, at])
    sigma = 1.0 / (1.0 + jnp.exp(-gate_pre))
    silu = gate_pre * sigma
    hidden = silu * up_pre
    slot = jnp.tile(slot_gate, (1, STEP // LANES))
    hidden_grad = slot * raw
    gate_grad_ref, up_grad_ref, gated_ref = grads
    gate_grad = hidden_grad * up_pre * sigma * (1.0 + gate_pre * (1.0 - sigma))
    gate_grad_ref[:, at] = gate_grad.astype(BF16)
    up_grad_ref[:, at] = (hidden_grad * silu).astype(BF16)
    gated_ref[:, at] = (slot * hidden).astype(BF16)
    if pull_ref is not None:
        pulled = hidden * raw
        for lane in range(0, STEP, LANES):
            pull_ref[...] += pulled[:, lane : lane + LANES]


def own_kernel(
    at_ref, mine_ref, theirs_ref, parts_ref, w_gate_ref, w_up_ref, w_down_ref,
    keep_ref, send_ref, x_ref, gate_grad_ref, up_grad_ref, gated_ref, back_ref,
):
    features, hidden_units = w_gate_ref.shape
    experts = parts_ref.shape[0] // 3
    core = at_ref[0]
    place_rows(x_ref, core, mine_ref, theirs_ref)
    gates = gate_tables(x_ref, parts_ref, features, experts)[2]
    slot_gate = slot_gates(gates, at_ref[1])
    grads = (gate_grad_ref, up_grad_ref, gated_ref)

    @pl.loop(0, hidden_units // STEP)
    def _(i):
        hidden_step(
            i * STEP, x_ref, slot_gate, w_gate_ref, w_up_ref, w_down_ref, grads, None
        )

    @pl.loop(0, features // STEP)
    def _(i):
        at = pl.ds(pl.multiple_of(i * STEP, STEP), STEP)
        later = pl.ds(pl.multiple_of(features + i * STEP, STEP), STEP)
        back_ref[:, at] = dot(gated_ref[...], w_down_ref[at, :], LAST).astype(BF16)
        back = dot(gate_grad_ref[...], w_gate_ref[at, :], LAST)
        back_ref[:, later] = (back + dot(up_grad_ref[...], w_up_ref[at, :], LAST)).astype(BF16)

    half = keep_ref.shape[0]
    keep_ref[...] = back_ref[pl.ds(pl.multiple_of(core * half, half), half), :]
    send_ref[...] = back_ref[pl.ds(pl.multiple_of((1 - core) * half, half), half), :]


def all_kernel(
    at_ref, mine_ref, theirs_ref, parts_ref, w_gate_ref, w_up_ref, w_down_ref,
    x_ref, gate_grad_ref, up_grad_ref, gated_ref, pull_ref, table_ref, sums_ref,
):
    features, hidden_units = w_gate_ref.shape
    experts = parts_ref.shape[0] // 3
    place_rows(x_ref, at_ref[0], mine_ref, theirs_ref)
    affinity, denominator, gates = gate_tables(x_ref, parts_ref, features, experts)
    table_ref[0] = affinity
    table_ref[1] = gates
    table_ref[2] = jnp.broadcast_to(denominator, affinity.shape)
    slot_gate = slot_gates(gates, at_ref[1])
    sums_ref[...] = jnp.zeros_like(sums_ref)
    grads = (gate_grad_ref, up_grad_ref, gated_ref)

    @pl.loop(0, hidden_units // STEP)
    def _(i):
        hidden_step(
            i * STEP, x_ref, slot_gate, w_gate_ref, w_up_ref, w_down_ref, grads, sums_ref
        )

    ones = jnp.ones((pull_ref.shape[0], LANES), F32)
    pull_ref[...] = lax.dot_general(
        ones, sums_ref[...], LAST, precision=HIGHEST, preferred_element_type=F32
    )


def weight_kernel(
    at_ref, x_ref, gate_grad_ref, up_grad_ref, gated_ref, gate_ref, up_ref, down_ref,
    gate_out, up_out, down_out, sems,
):
    features = (x_ref.shape[1] - LANES) // 2
    portion = gate_ref.shape[0]
    first = at_ref[2] * portion
    copies = []
    for k, row in enumerate(range(0, portion, LANES)):
        at = pl.ds(pl.multiple_of(first + row, LANES), LANES)
        later = pl.ds(pl.multiple_of(features + first + row, LANES), LANES)
        rows, cot = x_ref[:, at].T, x_ref[:, later].T
        here = pl.ds(row, LANES)
        for j, (left, right, out, target) in enumerate(
            (
                (rows, gate_grad_ref, gate_out, gate_ref),
                (rows, up_grad_ref, up_out, up_ref),
                (cot, gated_ref, down_out, down_ref),
            )
        ):
            out[here, :] = dot(left, right[...])
            copy = pltpu.make_async_copy(out.at[here, :], target.at[here, :], sems.at[k, j])
            copy.start()
            copies.append(copy)
    for copy in copies:
        copy.wait()


def last_kernel(
    at_ref, x_ref, table_ref, pulls_ref, router_ref, back_refs,
    mixed_ref, tokens_ref, router_grad_ref,
):
    experts, features = router_ref.shape
    affinity, gates, denominator = table_ref[0], table_ref[1], table_ref[2]
    pulls = pulls_ref[...]
    mean_pull = jnp.sum(gates * pulls, axis=0, keepdims=True)
    grads = (pulls - mean_pull) / denominator * affinity * (1.0 - affinity)
    rest, parts = grads, []
    for _ in range(3):
        parts.append(rest.astype(BF16).astype(F32))
        rest = rest - parts[-1]
    stacked = jnp.concatenate(parts, axis=0).astype(BF16)
    total = dot(stacked, x_ref[:, :features])
    router_grad_ref[...] = (
        total[2 * experts :] + total[experts : 2 * experts] + total[:experts]
    )
    count = mixed_ref.shape[0]
    shape = (count, pulls.shape[1])
    row = lax.broadcasted_iota(jnp.int32, shape, 0) + at_ref[3] * count
    own = (lax.broadcasted_iota(jnp.int32, shape, 1) == row).astype(F32)
    own_grads = lax.dot_general(own, grads, LAST, precision=HIGHEST, preferred_element_type=F32)
    back = jnp.dot(own_grads, router_ref[...], precision=HIGHEST, preferred_element_type=F32)
    summed = sum(ref[...].astype(F32) for ref in back_refs)
    mixed_ref[...] = summed[:, :features].astype(BF16)
    tokens_ref[...] = (summed[:, features:] + back).astype(BF16)


def call(kernel, out_shape, in_specs, out_specs, scratch, flops, moved):
    return pl.pallas_call(
        kernel,
        out_shape=out_shape,
        in_specs=in_specs,
        out_specs=out_specs,
        scratch_shapes=scratch,
        compiler_params=pltpu.CompilerParams(vmem_limit_bytes=VMEM_LIMIT),
        cost_estimate=pl.CostEstimate(flops=flops, bytes_accessed=moved, transcendentals=0),
    )


def local(tokens, routes, router, w_gate, w_up, w_down, cotangent):
    tok_count, features = tokens.shape
    experts = router.shape[1]
    hidden_units = w_gate.shape[1]
    devices = lax.axis_size("expert")
    groups = lax.axis_size("dp")
    sharing = devices // experts
    chips = devices // 2
    group_rows = devices * tok_count
    me = lax.axis_index("expert")
    group = lax.axis_index("dp")
    core, chip = me % 2, me // 2
    own_expert = me // sharing
    whole = groups * group_rows * features * 4 <= GATHER_BYTES

    def over_chips(x):
        out = jnp.zeros((chips,) + x.shape, x.dtype)
        for m in range(chips):
            piece = x if m == 0 else swap(x, "expert", 2 * m)
            out = lax.dynamic_update_index_in_dim(out, piece, chip ^ m, 0)
        return out

    def over_cores(x):
        other = swap(x, "expert", 1)
        return jnp.where(core == 0, jnp.stack([x, other]), jnp.stack([other, x]))

    ids = jnp.arange(LANES, dtype=jnp.int32)
    picked_wide = jnp.any(routes[:, :, None] == ids[None, None, :], axis=1).astype(BF16)
    message = jnp.concatenate([tokens, cotangent, picked_wide], axis=1)
    width = message.shape[1]
    by_chip = over_chips(message)
    if whole:
        return kernels_plan(
            by_chip, router, w_gate, w_up, w_down, over_chips, over_cores,
            groups, chips, tok_count, core, chip, group, own_expert,
        )

    own = over_cores(by_chip).reshape(group_rows, width)
    rows, cot = own[:, :features], own[:, features : 2 * features]
    picked, affinity, denominator, gates = gates_of(
        rows, own[:, 2 * features : 2 * features + experts], router
    )
    slot_gate = lax.dynamic_slice_in_dim(gates, own_expert, 1, axis=1)
    gate_pre = dot(rows, w_gate)
    up_pre = dot(rows, w_up)
    sigma = jax.nn.sigmoid(gate_pre)
    silu = gate_pre * sigma
    hidden = silu * up_pre
    raw = dot(cot, w_down)
    pull = jnp.sum(hidden * raw, axis=1)
    hidden_grad = slot_gate * raw
    gate_grad = (hidden_grad * up_pre * sigma * (1.0 + gate_pre * (1.0 - sigma))).astype(BF16)
    up_grad = (hidden_grad * silu).astype(BF16)
    gated = (slot_gate * hidden).astype(BF16)
    mixed_part = dot(gated, w_down, LAST)
    input_part = dot(gate_grad, w_gate, LAST) + dot(up_grad, w_up, LAST)
    part = jnp.concatenate([mixed_part.astype(BF16), input_part.astype(BF16)], axis=1)
    part = part.reshape(2, chips, tok_count, 2 * features)
    keep = lax.dynamic_index_in_dim(part, core, 0, keepdims=False)
    send = lax.dynamic_index_in_dim(part, 1 - core, 0, keepdims=False)
    total = sum(x.astype(F32) for x in give_back(keep, send, chips, chip))
    pulls = over_cores(over_chips(pull))
    pulls = jnp.swapaxes(pulls, 0, 1).reshape(experts, sharing, -1)
    pulls = jnp.sum(pulls, axis=1).T
    mean_pull = jnp.sum(gates * pulls, axis=1, keepdims=True)
    logit_grad = (pulls - mean_pull) / denominator * affinity * (1.0 - affinity)
    logit_grad = jnp.where(picked, logit_grad, 0.0)
    place = core * chips + chip
    own_logit = lax.dynamic_slice_in_dim(logit_grad, place * tok_count, tok_count, axis=0)
    grad_router = lax.psum(exact_dot(tokens, own_logit, FIRST), ("dp", "expert"))
    router_back = lax.dot_general(own_logit, router, LAST, precision=HIGHEST)
    parts = [
        dot(left, right, FIRST)
        for left, right in ((rows, gate_grad), (rows, up_grad), (cot, gated))
    ]
    summed = lax.psum_scatter(
        jnp.concatenate(parts, axis=1).astype(BF16), "dp", scatter_dimension=0, tiled=True
    ).astype(F32)
    grad_gate, grad_up, grad_down = jnp.split(summed, 3, axis=1)
    mixed = total[:, :features].astype(BF16)
    grad_tokens = (total[:, features:] + router_back).astype(BF16)
    return (mixed, grad_tokens, grad_router, grad_gate, grad_up, grad_down)


def give_back(keep, send, chips, chip):
    summed = (keep.astype(F32) + swap(send, "expert", 1).astype(F32)).astype(BF16)
    total = [lax.dynamic_index_in_dim(summed, chip, 0, keepdims=False)]
    for m in range(1, chips):
        piece = lax.dynamic_index_in_dim(summed, chip ^ m, 0, keepdims=False)
        total.append(swap(piece, "expert", 2 * m))
    return total


def kernels_plan(
    by_chip, router, w_gate, w_up, w_down, over_chips, over_cores,
    groups, chips, tok_count, core, chip, group, own_expert,
):
    features, experts = router.shape
    hidden_units = w_gate.shape[1]
    width = by_chip.shape[-1]
    half = chips * tok_count
    group_rows = 2 * half
    count = groups * group_rows
    portion = features // groups
    place = (core * groups + group) * chips + chip
    at = jnp.stack([core, own_expert, group, place]).astype(jnp.int32)
    router_t = router.T
    parts = jnp.concatenate(three_parts(router_t), axis=0)
    weights = [
        pltpu.with_memory_space_constraint(w, pltpu.VMEM) for w in (w_gate, w_up, w_down)
    ]
    grad_scratch = [pltpu.VMEM((group_rows, hidden_units), BF16)] * 3
    matrix = 2 * features * hidden_units

    theirs = swap(by_chip, "expert", 1)
    keep, send = call(
        own_kernel,
        [jax.ShapeDtypeStruct((half, 2 * features), BF16)] * 2,
        [IN_SMEM] + [IN_VMEM] * 6,
        [IN_VMEM] * 2,
        [pltpu.VMEM((group_rows, width), BF16)]
        + grad_scratch
        + [pltpu.VMEM((group_rows, 2 * features), BF16)],
        6 * matrix * group_rows,
        6 * matrix,
    )(at, by_chip.reshape(half, width), theirs.reshape(half, width), parts, *weights)
    by_group = jnp.zeros((groups,) + by_chip.shape, BF16)
    for m in range(groups):
        piece = by_chip if m == 0 else swap(by_chip, "dp", m)
        by_group = lax.dynamic_update_index_in_dim(by_group, piece, group ^ m, 0)
    theirs = swap(by_group, "expert", 1)
    back = give_back(
        keep.reshape(chips, tok_count, -1), send.reshape(chips, tok_count, -1), chips, chip
    )

    grads = [pltpu.VMEM((count, hidden_units), BF16)] * 3
    x, gate_grad, up_grad, gated, pull, tables = call(
        all_kernel,
        [pltpu.VMEM((count, width), BF16)]
        + grads
        + [
            jax.ShapeDtypeStruct((8, count), F32),
            pltpu.VMEM((3, experts, count), F32),
        ],
        [IN_SMEM] + [IN_VMEM] * 6,
        [IN_VMEM] * 6,
        [pltpu.VMEM((count, LANES), F32)],
        3 * matrix * count,
        3 * matrix,
    )(at, by_group.reshape(groups * half, width), theirs.reshape(groups * half, width), parts, *weights)
    pulls = over_cores(over_chips(pull[0]))
    pulls = jnp.swapaxes(pulls, 0, 1).reshape(experts, count)
    blocks = portion // LANES
    result = jax.ShapeDtypeStruct((portion, hidden_units), F32)
    grad_gate, grad_up, grad_down = call(
        weight_kernel,
        [result] * 3,
        [IN_SMEM] + [IN_VMEM] * 4,
        [pl.BlockSpec(memory_space=pl.ANY)] * 3,
        [pltpu.VMEM((portion, hidden_units), F32)] * 3 + [pltpu.SemaphoreType.DMA((blocks, 3))],
        6 * portion * hidden_units * count,
        12 * portion * hidden_units,
    )(at, x, gate_grad, up_grad, gated)
    rows = jax.ShapeDtypeStruct((tok_count, features), BF16)
    mixed, grad_tokens, router_grad = call(
        last_kernel,
        [rows, rows, jax.ShapeDtypeStruct((experts, features), F32)],
        [IN_SMEM] + [IN_VMEM] * 4 + [[IN_VMEM] * chips],
        [IN_VMEM] * 3,
        [],
        6 * experts * features * count,
        2 * features * count,
    )(at, x, tables, pulls, router_t, back)
    return (mixed, grad_tokens, router_grad.T, grad_gate, grad_up, grad_down)


def solution(mesh):
    return jax.shard_map(
        local,
        mesh=mesh,
        in_specs=(
            P(("dp", "expert"), None),
            P(("dp", "expert"), None),
            P(),
            P(None, "expert"),
            P(None, "expert"),
            P(None, "expert"),
            P(("dp", "expert"), None),
        ),
        out_specs=(
            P(("dp", "expert"), None),
            P(("dp", "expert"), None),
            P(),
            P("dp", "expert"),
            P("dp", "expert"),
            P("dp", "expert"),
        ),
        check_vma=False,
    )
```

time: 83.4 us -> 78.6 us (0.942)
  matrix products: 34.6 us -> 0 us
  Pallas kernels: 0 us -> 23.9 us
  local copies, waits for them, and re-layouts: 5.91 us -> 25.3 us
  waiting for transfers between devices: 16.2 us -> 5.11 us
  other arithmetic: 6.69 us -> 3.78 us
    dot_general x22 -> x0, matrix products: 34.6 us -> none  [the longest x3 10.8 us: local(): lax.dot_general(left, right, first, preferred_element_type=F32)]
    pallas_call x0 -> x4, Pallas kernels: none -> 23.9 us  [the longest x1 10.6 us: kernels_plan(): call(own_kernel, [jax.ShapeDtypeStruct((half, 2 * features), BF16)] * 2,...]
    unnamed x32 -> x31, local copies, waits for them, and re-layouts: 2.83 us -> 24.2 us
    ppermute x16, waiting for transfers between devices: 16.2 us -> 5.11 us  [swap(): return lax.ppermute(x, axis, [(i, i ^ mask) for i in range(count)])]
    select_n x3 -> x0, other arithmetic: 3.17 us -> none  [the longest x2 3.16 us: over_cores(): return jnp.where(core == 0, jnp.stack([x, other]), jnp.stack([other, x]))]
    slice x6 -> x1, local copies, waits for them, and re-layouts: 2.51 us -> 0.01 us  [kernels_plan(): pulls = over_cores(over_chips(pull[0]))]
    convert_element_type x2 -> x3, other arithmetic: 0.8 us -> 1.97 us  [the longest x1 1.05 us: give_back(): (keep.astype(F32) + swap(send, 'expert', 1).astype(F32)).astype(BF16)]
    add x1 -> x0, other arithmetic: 0.93 us -> none  [local(): total = total + swap(piece, 'expert', 2 * m).astype(F32)]
  transfers between devices with their start and end apart: 16 -> 16, of which waited for: 8 -> 3; matrix products, arithmetic and copies ran while one was open for 21% -> 5% of each run, Pallas kernels for 0% -> 19%
where the time goes in v3:
time: 78.6 us; the launch traced here: 77.8 us
  local copies, waits for them, and re-layouts  25.3 us (32%)
  Pallas kernels  23.9 us (30%)
  starting transfers between devices  18.8 us (24%)
  waiting for transfers between devices  5.11 us (7%)
  other arithmetic  3.78 us (5%)
  between operations  0.91 us (1%)
    unnamed x31, local copies, waits for them, and re-layouts  24.2 us
    ppermute x16, starting transfers between devices, swap(): return lax.ppermute(x, axis, [(i, i ^ mask) for i in range(count)])  18.8 us
    pallas_call x1, Pallas kernels, kernels_plan(): call(own_kernel, [jax.ShapeDtypeStruct((half, 2 * features), BF16)] * 2,...  10.6 us
    pallas_call x1, Pallas kernels, kernels_plan(): call(all_kernel, [pltpu.VMEM((count, width), BF16)] + grads + [jax.ShapeD...  7.1 us
    ppermute x16, waiting for transfers between devices, swap(): return lax.ppermute(x, axis, [(i, i ^ mask) for i in range(count)])  5.11 us
    pallas_call x1, Pallas kernels, kernels_plan(): call(weight_kernel, [result] * 3, [IN_SMEM] + [IN_VMEM] * 4, [pl.BlockSpe...  4.06 us
    pallas_call x1, Pallas kernels, kernels_plan(): call(last_kernel, [rows, rows, jax.ShapeDtypeStruct((experts, features),...  2.19 us
  transfers between devices with their start and end apart: 16, of which 3 were waited for; matrix products, arithmetic and copies ran while one was open for 5% of the time, Pallas kernels for 19%

profile of v3, /device:TPU:0, one launch (start us, length us, event | category | flops | bytes accessed | tf_op | source)
XLA Modules:
  0.0 77.8 jit_solution(10133478773245789410)
XLA Ops:
  0.6 0.8 copy.13
  1.4 0.1 fusion.3
  1.5 0.8 %pad_maximum_fusion.1 = bf16[8,5248]{1,0:T(8,128)(2,1)S(1)} fusion(bf16[8,128]{1,0:T(8,128)(2,1)S(1)} %convert_element_type.24, bf16[8,2560]{1,0:T(8,128)(2,1)} %param.13, bf16[8,2560]{1,0:T(8,128)(2,1)} %param.7), kind=kLoop, calls=%fused_computation.11 | loop fusion | flops 251904 | bytes 167936 | tf_op jit(solution)/shard_map/concatenate | solution.py:253
  2.3 4.0 %collective-permute-start.1 = (bf16[8,5248]{1,0:T(8,128)(2,1)S(1)}, bf16[8,5248]{1,0:T(8,128)(2,1)S(1)}, u32[]{:S(2)}, u32[]{:S(2)}) collective-permute-start(bf16[8,5248]{1,0:T(8,128)(2,1)S(1)} %pad_maximum_fusion.1), channel_id=1, source_target_pairs={{0,4},{1,5},{2,6},{3,7},{4,0},{5,1},{6,2},{7,3},{8,12},{9,13},{10,... | collective-permute-start | bytes 251912 | tf_op jit(solution)/shard_map/ppermute | solution.py:27
  6.3 1.6 %collective-permute-start = (bf16[8,5248]{1,0:T(8,128)(2,1)S(1)}, bf16[8,5248]{1,0:T(8,128)(2,1)S(1)}, u32[]{:S(2)}, u32[]{:S(2)}) collective-permute-start(bf16[8,5248]{1,0:T(8,128)(2,1)S(1)} %pad_maximum_fusion.1), channel_id=1, source_target_pairs={{0,2},{1,3},{2,0},{3,1},{4,6},{5,7},{6,4},{7,5},{8,10},{9,11},{10,... | collective-permute-start | bytes 251912 | tf_op jit(solution)/shard_map/ppermute | solution.py:27
  7.9 0.0 collective-permute-start.2
  7.9 0.9 %reduce-precision_convert_fusion.1 = (bf16[8,2560]{1,0:T(8,128)(2,1)S(1)}, bf16[8,2560]{1,0:T(8,128)(2,1)S(1)}, bf16[8,2560]{1,0:T(8,128)(2,1)S(1)}) fusion(f32[2560,8]{0,1:T(8,128)} %param.9), kind=kLoop, calls=%fused_computation.10 | loop fusion | flops 163840 | bytes 204800 | tf_op jit(solution)/shard_map/convert_element_type | solution.py:34
  8.9 0.8 %bitcast_dynamic-update-slice_fusion.7 = bf16[4,8,5248]{2,1,0:T(8,128)(2,1)S(1)} fusion(bf16[4,8,5248]{2,1,0:T(8,128)(2,1)S(1)} %broadcast_in_dim.49, s32[]{:T(128)S(6)} %select_n.58, bf16[8,128]{1,0:T(8,128)(2,1)S(1)} %convert_element_type.24, bf16[8,2560]{1,0:T(8,128)(2,1)} %param.13, bf16[8,2560]{1,0:T(8,128)(2,1)} %param.7), kind=kLoop, calls=%fused_computation.15 | loop fusion | flops 251904 | bytes 167940 | tf_op jit(solution)/shard_map/jit(dynamic_update_index_in_dim)/dynamic_update_slice | solution.py:244
  9.7 0.1 pad_add_fusion.at_ref
  9.8 1.2 %collective-permute-done = bf16[8,5248]{1,0:T(8,128)(2,1)S(1)} collective-permute-done((bf16[8,5248]{1,0:T(8,128)(2,1)S(1)}, bf16[8,5248]{1,0:T(8,128)(2,1)S(1)}, u32[]{:S(2)}, u32[]{:S(2)}) %collective-permute-start) | collective-permute-done | bytes 84000 | tf_op jit(solution)/shard_map/ppermute | solution.py:27
  11.0 0.0 collective-permute-done.1
  11.0 3.2 %collective-permute-done.2 = bf16[8,5248]{1,0:T(8,128)(2,1)S(1)} collective-permute-done((bf16[8,5248]{1,0:T(8,128)(2,1)S(1)}, bf16[8,5248]{1,0:T(8,128)(2,1)S(1)}, u32[]{:S(2)}, u32[]{:S(2)}) %collective-permute-start.2) | collective-permute-done | bytes 84000 | tf_op jit(solution)/shard_map/ppermute | solution.py:27
  14.2 0.1 collective-permute-start.11
  14.3 2.6 %collective-permute-start.5 = (bf16[4,8,5248]{2,1,0:T(8,128)(2,1)S(1)}, bf16[4,8,5248]{2,1,0:T(8,128)(2,1)S(1)}, u32[]{:S(2)}, u32[]{:S(2)}) collective-permute-start(bf16[4,8,5248]{2,1,0:T(8,128)(2,1)S(1)} %bitcast_dynamic-update-slice_fusion.4), channel_id=1, source_target_pairs={{0,24},{8,16},{16,8},{24,0},{1,25},{9,17},{17,9},{25,1},{2,26},{10... | collective-permute-start | bytes 1007624 | tf_op jit(solution)/shard_map/ppermute | solution.py:27
  16.9 0.5 collective-permute-start.4
  17.4 0.5 collective-permute-start.3
  17.9 0.1 broadcast_in_dim.48
  18.0 0.0 collective-permute-done.11
  18.0 0.0 copy-start
  18.0 2.5 %copy-done = bf16[2560,1024]{1,0:T(8,128)(2,1)S(1)} copy-done((bf16[2560,1024]{1,0:T(8,128)(2,1)S(1)}, bf16[2560,1024]{1,0:T(8,128)(2,1)}, u32[]{:S(2)}) %copy-start) | copy-done | bytes 5242904
  20.5 0.0 copy-start.2
  20.5 2.5 %copy-done.2 = bf16[2560,1024]{1,0:T(8,128)(2,1)S(1)} copy-done((bf16[2560,1024]{1,0:T(8,128)(2,1)S(1)}, bf16[2560,1024]{1,0:T(8,128)(2,1)}, u32[]{:S(2)}) %copy-start.2) | copy-done | bytes 5242904
  23.0 0.0 copy-start.4
  23.0 2.5 %copy-done.4 = bf16[2560,1024]{1,0:T(8,128)(2,1)S(1)} copy-done((bf16[2560,1024]{1,0:T(8,128)(2,1)S(1)}, bf16[2560,1024]{1,0:T(8,128)(2,1)}, u32[]{:S(2)}) %copy-start.4) | copy-done | bytes 5242904
  25.5 10.6 %shard_map.119 = (bf16[32,5120]{1,0:T(8,128)(2,1)S(1)}, bf16[32,5120]{1,0:T(8,128)(2,1)S(1)}) custom-call(s32[4]{0:T(128)S(1)} %pad_add_fusion.at_ref, bf16[32,5248]{1,0:T(8,128)(2,1)S(1)} %bitcast.48, bf16[32,5248]{1,0:T(8,128)(2,1)S(1)} %bitcast.50, bf16[24,2560]{1,0:T(8,128)(2,1)S(1)} %pad_maximum_fusion.parts_ref, bf16[2560,1024]{1,0:T(8,128)(2,1)S(1)} %copy-done, ...), custom_call_target="tpu_custom_call" | custom-call | flops 2013265920 | bytes 31457280 | tf_op jit(solution)/shard_map/pallas_call | solution.py:340
  36.1 0.1 collective-permute-start.12
  36.2 0.0 collective-permute-done.3
  36.2 0.0 collective-permute-done.4
  36.3 0.0 collective-permute-done.5
  36.3 0.5 collective-permute-start.6
  36.9 1.1 %copy-done.6 = bf16[4,4,8,5248]{3,2,1,0:T(8,128)(2,1)} copy-done((bf16[4,4,8,5248]{3,2,1,0:T(8,128)(2,1)}, bf16[4,4,8,5248]{3,2,1,0:T(8,128)(2,1)S(1)}, u32[]{:S(2)}) %copy-start.6) | copy-done | bytes 1343512
  37.9 0.0 collective-permute-done.12
  37.9 1.1 %fusion = bf16[4,8,5120]{2,1,0:T(8,128)(2,1)S(1)} fusion(bf16[4,8,5120]{2,1,0:T(8,128)(2,1)} %collective-permute-done.12, bf16[32,5120]{1,0:T(8,128)(2,1)S(1)} %get-tuple-element.23), kind=kLoop, calls=%fused_computation.1 | loop fusion | flops 655360 | bytes 983040 | tf_op jit(solution)/shard_map/convert_element_type | solution.py:310
  39.0 0.7 collective-permute-done.6
  39.7 1.1 %copy-done.8 = bf16[4,4,8,5248]{3,2,1,0:T(8,128)(2,1)} copy-done((bf16[4,4,8,5248]{3,2,1,0:T(8,128)(2,1)}, bf16[4,4,8,5248]{3,2,1,0:T(8,128)(2,1)S(1)}, u32[]{:S(2)}) %copy-start.8) | copy-done | bytes 1343512
  40.8 2.5 %copy-done.1 = bf16[2560,1024]{1,0:T(8,128)(2,1)S(1)} copy-done((bf16[2560,1024]{1,0:T(8,128)(2,1)S(1)}, bf16[2560,1024]{1,0:T(8,128)(2,1)}, u32[]{:S(2)}) %copy-start.1) | copy-done | bytes 5242904
  43.2 2.5 %copy-done.3 = bf16[2560,1024]{1,0:T(8,128)(2,1)S(1)} copy-done((bf16[2560,1024]{1,0:T(8,128)(2,1)S(1)}, bf16[2560,1024]{1,0:T(8,128)(2,1)}, u32[]{:S(2)}) %copy-start.3) | copy-done | bytes 5242904
  45.7 2.5 %copy-done.5 = bf16[2560,1024]{1,0:T(8,128)(2,1)S(1)} copy-done((bf16[2560,1024]{1,0:T(8,128)(2,1)S(1)}, bf16[2560,1024]{1,0:T(8,128)(2,1)}, u32[]{:S(2)}) %copy-start.5) | copy-done | bytes 5242904
  48.2 1.3 %copy-done.7 = bf16[4,4,8,5248]{3,2,1,0:T(8,128)(2,1)S(1)} copy-done((bf16[4,4,8,5248]{3,2,1,0:T(8,128)(2,1)S(1)}, bf16[4,4,8,5248]{3,2,1,0:T(8,128)(2,1)}, u32[]{:S(2)}) %copy-start.7) | copy-done | bytes 1343512
  49.5 1.3 %copy-done.9 = bf16[4,4,8,5248]{3,2,1,0:T(8,128)(2,1)S(1)} copy-done((bf16[4,4,8,5248]{3,2,1,0:T(8,128)(2,1)S(1)}, bf16[4,4,8,5248]{3,2,1,0:T(8,128)(2,1)}, u32[]{:S(2)}) %copy-start.9) | copy-done | bytes 1343512
  50.9 7.1 %shard_map.118 = (bf16[256,5248]{1,0:T(8,128)(2,1)S(1)}, bf16[256,1024]{1,0:T(8,128)(2,1)S(1)}, bf16[256,1024]{1,0:T(8,128)(2,1)S(1)}, bf16[256,1024]{1,0:T(8,12...) custom-call(s32[4]{0:T(128)S(1)} %pad_add_fusion.at_ref, bf16[128,5248]{1,0:T(8,128)(2,1)S(1)} %bitcast.47, ...), custom_call_target="tpu_custom_call" | custom-call | flops 4026531840 | bytes 15728640 | tf_op jit(solution)/shard_map/pallas_call | solution.py:361
  58.0 0.8 %copy-done.10 = bf16[256,1024]{1,0:T(8,128)(2,1)} copy-done((bf16[256,1024]{1,0:T(8,128)(2,1)}, bf16[256,1024]{1,0:T(8,128)(2,1)S(1)}, u32[]{:S(2)}) %copy-start.10) | copy-done | bytes 524312
  58.8 0.8 %copy-done.12 = bf16[256,1024]{1,0:T(8,128)(2,1)} copy-done((bf16[256,1024]{1,0:T(8,128)(2,1)}, bf16[256,1024]{1,0:T(8,128)(2,1)S(1)}, u32[]{:S(2)}) %copy-start.12) | copy-done | bytes 524312
  59.6 2.0 %collective-permute-start.9 = (f32[256]{0:T(256)S(1)}, f32[256]{0:T(256)S(1)}, u32[]{:S(2)}, u32[]{:S(2)}) collective-permute-start(f32[256]{0:T(256)S(1)} %bitcast.53), channel_id=1, source_target_pairs={{0,6},{1,7},{2,4},{3,5},{4,2},{5,3},{6,0},{7,1},{8,14},{9,15},{10,... | collective-permute-start | bytes 3080 | tf_op jit(solution)/shard_map/ppermute | solution.py:27
  61.6 0.6 collective-permute-start.8
  62.2 1.7 %collective-permute-start.7 = (f32[256]{0:T(256)S(1)}, f32[256]{0:T(256)S(1)}, u32[]{:S(2)}, u32[]{:S(2)}) collective-permute-start(f32[256]{0:T(256)S(1)} %bitcast.55), channel_id=1, source_target_pairs={{0,2},{1,3},{2,0},{3,1},{4,6},{5,7},{6,4},{7,5},{8,10},{9,11},{10,... | collective-permute-start | bytes 3080 | tf_op jit(solution)/shard_map/ppermute | solution.py:27
  64.0 0.7 dynamic-slice_bitcast_fusion
  64.7 2.0 %collective-permute-start.15 = (bf16[8,5120]{1,0:T(8,128)(2,1)}, bf16[8,5120]{1,0:T(8,128)(2,1)S(1)}, u32[]{:S(2)}, u32[]{:S(2)}) collective-permute-start(bf16[8,5120]{1,0:T(8,128)(2,1)} %get-tuple-element.34), channel_id=1, source_target_pairs={{0,6},{1,7},{2,4},{3,5},{4,2},{5,3},{6,0},{7,1},{8,14},{9,15},{10,... | collective-permute-start | bytes 245768 | tf_op jit(solution)/shard_map/ppermute | solution.py:27
  66.7 0.0 collective-permute-start.14
  66.7 0.0 collective-permute-done.7
  66.7 2.4 %collective-permute-start.13 = (bf16[8,5120]{1,0:T(8,128)(2,1)}, bf16[8,5120]{1,0:T(8,128)(2,1)}, u32[]{:S(2)}, u32[]{:S(2)}) collective-permute-start(bf16[8,5120]{1,0:T(8,128)(2,1)} %get-tuple-element.36), channel_id=1, source_target_pairs={{0,2},{1,3},{2,0},{3,1},{4,6},{5,7},{6,4},{7,5},{8,10},{9,11},{10,... | collective-permute-start | bytes 245768 | tf_op jit(solution)/shard_map/ppermute | solution.py:27
  69.2 0.0 collective-permute-done.8
  69.2 0.0 collective-permute-done.9
  69.3 0.1 collective-permute-start.10
  69.4 0.0 copy-start.11
  69.4 1.0 %copy-done.11 = bf16[256,1024]{1,0:T(8,128)(2,1)S(1)} copy-done((bf16[256,1024]{1,0:T(8,128)(2,1)S(1)}, bf16[256,1024]{1,0:T(8,128)(2,1)}, u32[]{:S(2)}) %copy-start.11) | copy-done | bytes 524312
  70.4 1.0 %copy-done.13 = bf16[256,1024]{1,0:T(8,128)(2,1)S(1)} copy-done((bf16[256,1024]{1,0:T(8,128)(2,1)S(1)}, bf16[256,1024]{1,0:T(8,128)(2,1)}, u32[]{:S(2)}) %copy-start.13) | copy-done | bytes 524312
  71.4 4.1 %shard_map.121 = (f32[640,1024]{1,0:T(8,128)}, f32[640,1024]{1,0:T(8,128)}, f32[640,1024]{1,0:T(8,128)}) custom-call(s32[4]{0:T(128)S(1)} %pad_add_fusion.at_ref, bf16[256,5248]{1,0:T(8,128)(2,1)S(1)} %get-tuple-element.20.x_ref, bf16[256,1024]{1,0:T(8,128)(2,1)S(1)} %get-tuple-element.28.gate_grad_ref, bf16[256,1024]{1,0:T(8,128)(2,1)S(1)} %copy-done.11, ...), custom_call_target="tpu_custom_call" | custom-call | flops 1006632960 | bytes 7864320 | tf_op jit(solution)/shard_map/pallas_call | solution.py:379
  75.5 0.0 collective-permute-done.10
  75.6 0.0 collective-permute-done.15.back_refs_3_
  75.6 0.0 collective-permute-done.14.back_refs_2_
  75.6 0.0 collective-permute-done.13.back_refs_1_
  75.6 0.0 copy-done.14
  75.6 2.2 %shard_map.120 = (bf16[8,2560]{1,0:T(8,128)(2,1)}, bf16[8,2560]{1,0:T(8,128)(2,1)}, f32[8,2560]{1,0:T(8,128)}) custom-call(s32[4]{0:T(128)S(1)} %pad_add_fusion.at_ref, bf16[256,5248]{1,0:T(8,128)(2,1)S(1)} %get-tuple-element.20.x_ref, f32[3,8,256]{2,1,0:T(8,128)S(1)} %get-tuple-element.21.table_ref, f32[8,256]{1,0:T(8,128)S(1)} %reshape.36.pulls_ref, ...), custom_call_target="tpu_custom_call" | custom-call | flops 31457280 | bytes 1310720 | tf_op jit(solution)/shard_map/pallas_call | solution.py:389
  (31 shorter events, 0.4 us)
Async XLA Ops:
  2.3 8.7 %collective-permute-start.1 = (bf16[8,5248]{1,0:T(8,128)(2,1)S(1)}, bf16[8,5248]{1,0:T(8,128)(2,1)S(1)}, u32[]{:S(2)}, u32[]{:S(2)}) collective-permute-start(bf16[8,5248]{1,0:T(8,128)(2,1)S(1)} %pad_maximum_fusion.1), channel_id=1, source_target_pairs={{0,4},{1,5},{2,6},{3,7},{4,0},{5,1},{6,2},{7,3},{8,12},{9,13},{10,... | collective-permute-start | bytes 251912 | tf_op jit(solution)/shard_map/ppermute | solution.py:27
  6.3 4.6 %collective-permute-start = (bf16[8,5248]{1,0:T(8,128)(2,1)S(1)}, bf16[8,5248]{1,0:T(8,128)(2,1)S(1)}, u32[]{:S(2)}, u32[]{:S(2)}) collective-permute-start(bf16[8,5248]{1,0:T(8,128)(2,1)S(1)} %pad_maximum_fusion.1), channel_id=1, source_target_pairs={{0,2},{1,3},{2,0},{3,1},{4,6},{5,7},{6,4},{7,5},{8,10},{9,11},{10,... | collective-permute-start | bytes 251912 | tf_op jit(solution)/shard_map/ppermute | solution.py:27
  7.9 6.3 %collective-permute-start.2 = (bf16[8,5248]{1,0:T(8,128)(2,1)S(1)}, bf16[8,5248]{1,0:T(8,128)(2,1)S(1)}, u32[]{:S(2)}, u32[]{:S(2)}) collective-permute-start(bf16[8,5248]{1,0:T(8,128)(2,1)S(1)} %pad_maximum_fusion.1), channel_id=1, source_target_pairs={{0,6},{1,7},{2,4},{3,5},{4,2},{5,3},{6,0},{7,1},{8,14},{9,15},{10,... | collective-permute-start | bytes 251912 | tf_op jit(solution)/shard_map/ppermute | solution.py:27
  14.2 3.8 %collective-permute-start.11 = (bf16[4,8,5248]{2,1,0:T(8,128)(2,1)S(1)}, bf16[4,8,5248]{2,1,0:T(8,128)(2,1)S(1)}, u32[]{:S(2)}, u32[]{:S(2)}) collective-permute-start(bf16[4,8,5248]{2,1,0:T(8,128)(2,1)S(1)} %bitcast_dynamic-update-slice_fusion.4), channel_id=1, source_target_pairs={{0,1},{1,0},{2,3},{3,2},{4,5},{5,4},{6,7},{7,6},{8,9},{9,8},{10,11... | collective-permute-start | bytes 1007624 | tf_op jit(solution)/shard_map/ppermute | solution.py:27
  14.3 22.0 %collective-permute-start.5 = (bf16[4,8,5248]{2,1,0:T(8,128)(2,1)S(1)}, bf16[4,8,5248]{2,1,0:T(8,128)(2,1)S(1)}, u32[]{:S(2)}, u32[]{:S(2)}) collective-permute-start(bf16[4,8,5248]{2,1,0:T(8,128)(2,1)S(1)} %bitcast_dynamic-update-slice_fusion.4), channel_id=1, source_target_pairs={{0,24},{8,16},{16,8},{24,0},{1,25},{9,17},{17,9},{25,1},{2,26},{10... | collective-permute-start | bytes 1007624 | tf_op jit(solution)/shard_map/ppermute | solution.py:27
  16.9 19.3 %collective-permute-start.4 = (bf16[4,8,5248]{2,1,0:T(8,128)(2,1)S(1)}, bf16[4,8,5248]{2,1,0:T(8,128)(2,1)S(1)}, u32[]{:S(2)}, u32[]{:S(2)}) collective-permute-start(bf16[4,8,5248]{2,1,0:T(8,128)(2,1)S(1)} %bitcast_dynamic-update-slice_fusion.4), channel_id=1, source_target_pairs={{0,16},{8,24},{16,0},{24,8},{1,17},{9,25},{17,1},{25,9},{2,18},{10... | collective-permute-start | bytes 1007624 | tf_op jit(solution)/shard_map/ppermute | solution.py:27
  17.4 18.8 %collective-permute-start.3 = (bf16[4,8,5248]{2,1,0:T(8,128)(2,1)S(1)}, bf16[4,8,5248]{2,1,0:T(8,128)(2,1)S(1)}, u32[]{:S(2)}, u32[]{:S(2)}) collective-permute-start(bf16[4,8,5248]{2,1,0:T(8,128)(2,1)S(1)} %bitcast_dynamic-update-slice_fusion.4), channel_id=1, source_target_pairs={{0,8},{8,0},{16,24},{24,16},{1,9},{9,1},{17,25},{25,17},{2,10},{10... | collective-permute-start | bytes 1007624 | tf_op jit(solution)/shard_map/ppermute | solution.py:27
  18.0 2.5 %copy-start = (bf16[2560,1024]{1,0:T(8,128)(2,1)S(1)}, bf16[2560,1024]{1,0:T(8,128)(2,1)}, u32[]{:S(2)}) copy-start(bf16[2560,1024]{1,0:T(8,128)(2,1)} %w_gate_ref.3) | copy-start | bytes 15728644
  20.5 2.5 %copy-start.2 = (bf16[2560,1024]{1,0:T(8,128)(2,1)S(1)}, bf16[2560,1024]{1,0:T(8,128)(2,1)}, u32[]{:S(2)}) copy-start(bf16[2560,1024]{1,0:T(8,128)(2,1)} %w_up_ref.3) | copy-start | bytes 15728644
  23.0 2.5 %copy-start.4 = (bf16[2560,1024]{1,0:T(8,128)(2,1)S(1)}, bf16[2560,1024]{1,0:T(8,128)(2,1)}, u32[]{:S(2)}) copy-start(bf16[2560,1024]{1,0:T(8,128)(2,1)} %w_down_ref.3) | copy-start | bytes 15728644
  36.1 1.8 %collective-permute-start.12 = (bf16[4,8,5120]{2,1,0:T(8,128)(2,1)S(1)}, bf16[4,8,5120]{2,1,0:T(8,128)(2,1)}, u32[]{:S(2)}, u32[]{:S(2)}) collective-permute-start(bf16[4,8,5120]{2,1,0:T(8,128)(2,1)S(1)} %bitcast.52), channel_id=1, source_target_pairs={{0,1},{1,0},{2,3},{3,2},{4,5},{5,4},{6,7},{7,6},{8,9},{9,8},{10,11... | collective-permute-start | bytes 983048 | tf_op jit(solution)/shard_map/ppermute | solution.py:27
  36.3 3.4 %collective-permute-start.6 = (bf16[4,4,8,5248]{3,2,1,0:T(8,128)(2,1)S(1)}, bf16[4,4,8,5248]{3,2,1,0:T(8,128)(2,1)S(1)}, u32[]{:S(2)}, u32[]{:S(2)}) collective-permute-start(bf16[4,4,8,5248]{3,2,1,0:T(8,128)(2,1)S(1)} %bitcast_dynamic-update-slice_fusion), channel_id=1, source_target_pairs={{0,1},{1,0},{2,3},{3,2},{4,5},{5,4},{6,7},{7,6},{8,9},{9,8},{10,11... | collective-permute-start | bytes 4030472 | tf_op jit(solution)/shard_map/ppermute | solution.py:27
  36.9 1.1 %copy-start.6 = (bf16[4,4,8,5248]{3,2,1,0:T(8,128)(2,1)}, bf16[4,4,8,5248]{3,2,1,0:T(8,128)(2,1)S(1)}, u32[]{:S(2)}) copy-start(bf16[4,4,8,5248]{3,2,1,0:T(8,128)(2,1)S(1)} %bitcast_dynamic-update-slice_fusion) | copy-start | bytes 4030468
  39.7 1.1 %copy-start.8 = (bf16[4,4,8,5248]{3,2,1,0:T(8,128)(2,1)}, bf16[4,4,8,5248]{3,2,1,0:T(8,128)(2,1)S(1)}, u32[]{:S(2)}) copy-start(bf16[4,4,8,5248]{3,2,1,0:T(8,128)(2,1)S(1)} %collective-permute-done.6) | copy-start | bytes 4030468
  40.8 2.5 %copy-start.1 = (bf16[2560,1024]{1,0:T(8,128)(2,1)S(1)}, bf16[2560,1024]{1,0:T(8,128)(2,1)}, u32[]{:S(2)}) copy-start(bf16[2560,1024]{1,0:T(8,128)(2,1)} %w_gate_ref.3) | copy-start | bytes 15728644
  43.2 2.5 %copy-start.3 = (bf16[2560,1024]{1,0:T(8,128)(2,1)S(1)}, bf16[2560,1024]{1,0:T(8,128)(2,1)}, u32[]{:S(2)}) copy-start(bf16[2560,1024]{1,0:T(8,128)(2,1)} %w_up_ref.3) | copy-start | bytes 15728644
  45.7 2.5 %copy-start.5 = (bf16[2560,1024]{1,0:T(8,128)(2,1)S(1)}, bf16[2560,1024]{1,0:T(8,128)(2,1)}, u32[]{:S(2)}) copy-start(bf16[2560,1024]{1,0:T(8,128)(2,1)} %w_down_ref.3) | copy-start | bytes 15728644
  48.2 1.3 %copy-start.7 = (bf16[4,4,8,5248]{3,2,1,0:T(8,128)(2,1)S(1)}, bf16[4,4,8,5248]{3,2,1,0:T(8,128)(2,1)}, u32[]{:S(2)}) copy-start(bf16[4,4,8,5248]{3,2,1,0:T(8,128)(2,1)} %copy-done.6) | copy-start | bytes 4030468
  49.5 1.3 %copy-start.9 = (bf16[4,4,8,5248]{3,2,1,0:T(8,128)(2,1)S(1)}, bf16[4,4,8,5248]{3,2,1,0:T(8,128)(2,1)}, u32[]{:S(2)}) copy-start(bf16[4,4,8,5248]{3,2,1,0:T(8,128)(2,1)} %copy-done.8) | copy-start | bytes 4030468
  58.0 0.8 %copy-start.10 = (bf16[256,1024]{1,0:T(8,128)(2,1)}, bf16[256,1024]{1,0:T(8,128)(2,1)S(1)}, u32[]{:S(2)}) copy-start(bf16[256,1024]{1,0:T(8,128)(2,1)S(1)} %get-tuple-element.29.up_grad_ref) | copy-start | bytes 1572868
  58.8 0.8 %copy-start.12 = (bf16[256,1024]{1,0:T(8,128)(2,1)}, bf16[256,1024]{1,0:T(8,128)(2,1)S(1)}, u32[]{:S(2)}) copy-start(bf16[256,1024]{1,0:T(8,128)(2,1)S(1)} %get-tuple-element.30.gated_ref) | copy-start | bytes 1572868
  59.6 9.6 %collective-permute-start.9 = (f32[256]{0:T(256)S(1)}, f32[256]{0:T(256)S(1)}, u32[]{:S(2)}, u32[]{:S(2)}) collective-permute-start(f32[256]{0:T(256)S(1)} %bitcast.53), channel_id=1, source_target_pairs={{0,6},{1,7},{2,4},{3,5},{4,2},{5,3},{6,0},{7,1},{8,14},{9,15},{10,... | collective-permute-start | bytes 3080 | tf_op jit(solution)/shard_map/ppermute | solution.py:27
  61.6 7.6 %collective-permute-start.8 = (f32[256]{0:T(256)S(1)}, f32[256]{0:T(256)S(1)}, u32[]{:S(2)}, u32[]{:S(2)}) collective-permute-start(f32[256]{0:T(256)S(1)} %bitcast.54), channel_id=1, source_target_pairs={{0,4},{1,5},{2,6},{3,7},{4,0},{5,1},{6,2},{7,3},{8,12},{9,13},{10,... | collective-permute-start | bytes 3080 | tf_op jit(solution)/shard_map/ppermute | solution.py:27
  62.2 4.5 %collective-permute-start.7 = (f32[256]{0:T(256)S(1)}, f32[256]{0:T(256)S(1)}, u32[]{:S(2)}, u32[]{:S(2)}) collective-permute-start(f32[256]{0:T(256)S(1)} %bitcast.55), channel_id=1, source_target_pairs={{0,2},{1,3},{2,0},{3,1},{4,6},{5,7},{6,4},{7,5},{8,10},{9,11},{10,... | collective-permute-start | bytes 3080 | tf_op jit(solution)/shard_map/ppermute | solution.py:27
  64.7 10.9 %collective-permute-start.15 = (bf16[8,5120]{1,0:T(8,128)(2,1)}, bf16[8,5120]{1,0:T(8,128)(2,1)S(1)}, u32[]{:S(2)}, u32[]{:S(2)}) collective-permute-start(bf16[8,5120]{1,0:T(8,128)(2,1)} %get-tuple-element.34), channel_id=1, source_target_pairs={{0,6},{1,7},{2,4},{3,5},{4,2},{5,3},{6,0},{7,1},{8,14},{9,15},{10,... | collective-permute-start | bytes 245768 | tf_op jit(solution)/shard_map/ppermute | solution.py:27
  66.7 8.9 %collective-permute-start.14 = (bf16[8,5120]{1,0:T(8,128)(2,1)}, bf16[8,5120]{1,0:T(8,128)(2,1)}, u32[]{:S(2)}, u32[]{:S(2)}) collective-permute-start(bf16[8,5120]{1,0:T(8,128)(2,1)} %get-tuple-element.35), channel_id=1, source_target_pairs={{0,4},{1,5},{2,6},{3,7},{4,0},{5,1},{6,2},{7,3},{8,12},{9,13},{10,... | collective-permute-start | bytes 245768 | tf_op jit(solution)/shard_map/ppermute | solution.py:27
  66.7 8.9 %collective-permute-start.13 = (bf16[8,5120]{1,0:T(8,128)(2,1)}, bf16[8,5120]{1,0:T(8,128)(2,1)}, u32[]{:S(2)}, u32[]{:S(2)}) collective-permute-start(bf16[8,5120]{1,0:T(8,128)(2,1)} %get-tuple-element.36), channel_id=1, source_target_pairs={{0,2},{1,3},{2,0},{3,1},{4,6},{5,7},{6,4},{7,5},{8,10},{9,11},{10,... | collective-permute-start | bytes 245768 | tf_op jit(solution)/shard_map/ppermute | solution.py:27
  69.3 6.2 %collective-permute-start.10 = (f32[4,256]{1,0:T(4,128)S(1)}, f32[4,256]{1,0:T(4,128)S(1)}, u32[]{:S(2)}, u32[]{:S(2)}) collective-permute-start(f32[4,256]{1,0:T(4,128)S(1)} %dynamic_update_slice.50), channel_id=1, source_target_pairs={{0,1},{1,0},{2,3},{3,2},{4,5},{5,4},{6,7},{7,6},{8,9},{9,8},{10,11... | collective-permute-start | bytes 12296 | tf_op jit(solution)/shard_map/ppermute | solution.py:27
  69.4 1.0 %copy-start.11 = (bf16[256,1024]{1,0:T(8,128)(2,1)S(1)}, bf16[256,1024]{1,0:T(8,128)(2,1)}, u32[]{:S(2)}) copy-start(bf16[256,1024]{1,0:T(8,128)(2,1)} %copy-done.10) | copy-start | bytes 1572868
  70.4 1.0 %copy-start.13 = (bf16[256,1024]{1,0:T(8,128)(2,1)S(1)}, bf16[256,1024]{1,0:T(8,128)(2,1)}, u32[]{:S(2)}) copy-start(bf16[256,1024]{1,0:T(8,128)(2,1)} %copy-done.12) | copy-start | bytes 1572868
  71.4 4.2 %copy-start.14 = (f32[2560,8]{0,1:T(8,128)S(1)}, f32[2560,8]{0,1:T(8,128)}, u32[]{:S(2)}) copy-start(f32[2560,8]{0,1:T(8,128)} %param.9) | copy-start | bytes 245764

commit v4 on v3

--- a/solution.py
+++ b/solution.py
@@ -10,7 +10,6 @@
 LANES = 128
 STEP = 256
 GATHER_BYTES = 8 << 20
-VMEM_LIMIT = 24 << 20
 HIGHEST = lax.Precision.HIGHEST
 LAST = (((1,), (1,)), ((), ()))
 FIRST = (((0,), (0,)), ((), ()))
@@ -25,6 +24,10 @@
 def swap(x, axis, mask):
     count = lax.axis_size(axis)
     return lax.ppermute(x, axis, [(i, i ^ mask) for i in range(count)])
+
+
+def in_hbm(x):
+    return pltpu.with_memory_space_constraint(x, pltpu.HBM)
 
 
 def three_parts(x):
@@ -95,6 +98,17 @@
             pull_ref[...] += pulled[:, lane : lane + LANES]
 
 
+def load_kernel(_, *refs):
+    count = len(refs) // 2
+    copies = [
+        pltpu.make_async_copy(refs[i], refs[count + i], refs[-1].at[i]) for i in range(count)
+    ]
+    for copy in copies:
+        copy.start()
+    for copy in copies:
+        copy.wait()
+
+
 def own_kernel(
     at_ref, mine_ref, theirs_ref, parts_ref, w_gate_ref, w_up_ref, w_down_ref,
     keep_ref, send_ref, x_ref, gate_grad_ref, up_grad_ref, gated_ref, back_ref,
@@ -154,7 +168,7 @@
 
 
 def weight_kernel(
-    at_ref, x_ref, gate_grad_ref, up_grad_ref, gated_ref, gate_ref, up_ref, down_ref,
+    at_ref, x_ref, gate_grad_ref, up_grad_ref, gated_ref, _, gate_ref, up_ref, down_ref,
     gate_out, up_out, down_out, sems,
 ):
     features = (x_ref.shape[1] - LANES) // 2
@@ -210,14 +224,14 @@
     tokens_ref[...] = (summed[:, features:] + back).astype(BF16)
 
 
-def call(kernel, out_shape, in_specs, out_specs, scratch, flops, moved):
+def call(kernel, out_shape, in_specs, out_specs, scratch, limit, flops, moved):
     return pl.pallas_call(
         kernel,
         out_shape=out_shape,
         in_specs=in_specs,
         out_specs=out_specs,
         scratch_shapes=scratch,
-        compiler_params=pltpu.CompilerParams(vmem_limit_bytes=VMEM_LIMIT),
+        compiler_params=pltpu.CompilerParams(vmem_limit_bytes=limit << 20),
         cost_estimate=pl.CostEstimate(flops=flops, bytes_accessed=moved, transcendentals=0),
     )
 
@@ -255,7 +269,7 @@
     by_chip = over_chips(message)
     if whole:
         return kernels_plan(
-            by_chip, router, w_gate, w_up, w_down, over_chips, over_cores,
+            message, by_chip, router, w_gate, w_up, w_down, over_chips, over_cores,
             groups, chips, tok_count, core, chip, group, own_expert,
         )
 
@@ -282,7 +296,8 @@
     part = part.reshape(2, chips, tok_count, 2 * features)
     keep = lax.dynamic_index_in_dim(part, core, 0, keepdims=False)
     send = lax.dynamic_index_in_dim(part, 1 - core, 0, keepdims=False)
-    total = sum(x.astype(F32) for x in give_back(keep, send, chips, chip))
+    back = give_back(send_back(keep, send, chips, chip))
+    total = sum(x.astype(F32) for x in back)
     pulls = over_cores(over_chips(pull))
     pulls = jnp.swapaxes(pulls, 0, 1).reshape(experts, sharing, -1)
     pulls = jnp.sum(pulls, axis=1).T
@@ -306,17 +321,21 @@
     return (mixed, grad_tokens, grad_router, grad_gate, grad_up, grad_down)
 
 
-def give_back(keep, send, chips, chip):
+def send_back(keep, send, chips, chip):
     summed = (keep.astype(F32) + swap(send, "expert", 1).astype(F32)).astype(BF16)
-    total = [lax.dynamic_index_in_dim(summed, chip, 0, keepdims=False)]
-    for m in range(1, chips):
-        piece = lax.dynamic_index_in_dim(summed, chip ^ m, 0, keepdims=False)
-        total.append(swap(piece, "expert", 2 * m))
-    return total
+    return [
+        lax.dynamic_index_in_dim(summed, chip ^ m, 0, keepdims=False) for m in range(chips)
+    ]
+
+
+def give_back(pieces):
+    return [
+        piece if m == 0 else swap(piece, "expert", 2 * m) for m, piece in enumerate(pieces)
+    ]
 
 
 def kernels_plan(
-    by_chip, router, w_gate, w_up, w_down, over_chips, over_cores,
+    message, by_chip, router, w_gate, w_up, w_down, over_chips, over_cores,
     groups, chips, tok_count, core, chip, group, own_expert,
 ):
     features, experts = router.shape
@@ -330,9 +349,16 @@
     at = jnp.stack([core, own_expert, group, place]).astype(jnp.int32)
     router_t = router.T
     parts = jnp.concatenate(three_parts(router_t), axis=0)
-    weights = [
-        pltpu.with_memory_space_constraint(w, pltpu.VMEM) for w in (w_gate, w_up, w_down)
-    ]
+    weights = call(
+        load_kernel,
+        [pltpu.VMEM(w.shape, w.dtype) for w in (w_gate, w_up, w_down)],
+        [IN_VMEM] + [pl.BlockSpec(memory_space=pltpu.HBM)] * 3,
+        [IN_VMEM] * 3,
+        [pltpu.SemaphoreType.DMA((3,))],
+        2,
+        0,
+        6 * features * hidden_units,
+    )(message[:, 2 * features :], *[in_hbm(w) for w in (w_gate, w_up, w_down)])
     grad_scratch = [pltpu.VMEM((group_rows, hidden_units), BF16)] * 3
     matrix = 2 * features * hidden_units
 
@@ -345,6 +371,7 @@
         [pltpu.VMEM((group_rows, width), BF16)]
         + grad_scratch
         + [pltpu.VMEM((group_rows, 2 * features), BF16)],
+        8,
         6 * matrix * group_rows,
         6 * matrix,
     )(at, by_chip.reshape(half, width), theirs.reshape(half, width), parts, *weights)
@@ -353,9 +380,10 @@
         piece = by_chip if m == 0 else swap(by_chip, "dp", m)
         by_group = lax.dynamic_update_index_in_dim(by_group, piece, group ^ m, 0)
     theirs = swap(by_group, "expert", 1)
-    back = give_back(
+    pieces = send_back(
         keep.reshape(chips, tok_count, -1), send.reshape(chips, tok_count, -1), chips, chip
     )
+    back = give_back(pieces)
 
     grads = [pltpu.VMEM((count, hidden_units), BF16)] * 3
     x, gate_grad, up_grad, gated, pull, tables = call(
@@ -369,9 +397,16 @@
         [IN_SMEM] + [IN_VMEM] * 6,
         [IN_VMEM] * 6,
         [pltpu.VMEM((count, LANES), F32)],
+        8,
         3 * matrix * count,
         3 * matrix,
-    )(at, by_group.reshape(groups * half, width), theirs.reshape(groups * half, width), parts, *weights)
+    )(
+        at,
+        by_group.reshape(groups * half, width),
+        theirs.reshape(groups * half, width),
+        parts,
+        *weights,
+    )
     pulls = over_cores(over_chips(pull[0]))
     pulls = jnp.swapaxes(pulls, 0, 1).reshape(experts, count)
     blocks = portion // LANES
@@ -379,12 +414,13 @@
     grad_gate, grad_up, grad_down = call(
         weight_kernel,
         [result] * 3,
-        [IN_SMEM] + [IN_VMEM] * 4,
+        [IN_SMEM] + [IN_VMEM] * 4 + [[pl.BlockSpec(memory_space=pl.ANY)] * (chips - 1)],
         [pl.BlockSpec(memory_space=pl.ANY)] * 3,
         [pltpu.VMEM((portion, hidden_units), F32)] * 3 + [pltpu.SemaphoreType.DMA((blocks, 3))],
+        14,
         6 * portion * hidden_units * count,
         12 * portion * hidden_units,
-    )(at, x, gate_grad, up_grad, gated)
+    )(at, x, gate_grad, up_grad, gated, back[1:])
     rows = jax.ShapeDtypeStruct((tok_count, features), BF16)
     mixed, grad_tokens, router_grad = call(
         last_kernel,
@@ -392,6 +428,7 @@
         [IN_SMEM] + [IN_VMEM] * 4 + [[IN_VMEM] * chips],
         [IN_VMEM] * 3,
         [],
+        6,
         6 * experts * features * count,
         2 * features * count,
     )(at, x, tables, pulls, router_t, back)

time: 78.6 us -> 70.6 us (0.90)
  local copies, waits for them, and re-layouts: 25.3 us -> 10.7 us
  Pallas kernels: 23.9 us -> 29.1 us
  starting transfers between devices: 18.8 us -> 21 us
  other arithmetic: 3.78 us -> 2.8 us
    unnamed x31 -> x23, local copies, waits for them, and re-layouts: 24.2 us -> 8.22 us
    pallas_call x1 -> x2, Pallas kernels: 4.06 us -> 9.63 us  [the longest x1 5.58 us: kernels_plan(): call(load_kernel, [pltpu.VMEM(w.shape, w.dtype) for w in (w_gate, w_up, w...]
    ppermute x16, starting transfers between devices: 18.8 us -> 21 us  [swap(): return lax.ppermute(x, axis, [(i, i ^ mask) for i in range(count)])]
    dynamic_update_slice x7, local copies, waits for them, and re-layouts: 0.2 us -> 1.52 us  [over_chips(): out = lax.dynamic_update_index_in_dim(out, piece, chip ^ m, 0)]
    convert_element_type x1, other arithmetic: 1.05 us -> 0.08 us  [send_back(): (keep.astype(F32) + swap(send, 'expert', 1).astype(F32)).astype(BF16)]
  transfers between devices with their start and end apart: 16 -> 16, of which waited for: 3 -> 2; matrix products, arithmetic and copies ran while one was open for 5% -> 6% of each run, Pallas kernels for 19% -> 39%
where the time goes in v4:
time: 70.6 us; the launch traced here: 70 us
  Pallas kernels  29.1 us (41%)
  starting transfers between devices  21 us (30%)
  local copies, waits for them, and re-layouts  10.7 us (15%)
  waiting for transfers between devices  5.45 us (8%)
  other arithmetic  2.8 us (4%)
  between operations  0.92 us (1%)
    ppermute x16, starting transfers between devices, swap(): return lax.ppermute(x, axis, [(i, i ^ mask) for i in range(count)])  21 us
    pallas_call x1, Pallas kernels, kernels_plan(): call(own_kernel, [jax.ShapeDtypeStruct((half, 2 * features), BF16)] * 2,...  10.6 us
    unnamed x23, local copies, waits for them, and re-layouts  8.22 us
    pallas_call x1, Pallas kernels, kernels_plan(): call(all_kernel, [pltpu.VMEM((count, width), BF16)] + grads + [jax.ShapeD...  7.1 us
    pallas_call x1, Pallas kernels, kernels_plan(): call(load_kernel, [pltpu.VMEM(w.shape, w.dtype) for w in (w_gate, w_up, w...  5.58 us
    ppermute x16, waiting for transfers between devices, swap(): return lax.ppermute(x, axis, [(i, i ^ mask) for i in range(count)])  5.45 us
    pallas_call x1, Pallas kernels, kernels_plan(): call(weight_kernel, [result] * 3, [IN_SMEM] + [IN_VMEM] * 4 + [[pl.BlockS...  4.05 us
    pallas_call x1, Pallas kernels, kernels_plan(): call(last_kernel, [rows, rows, jax.ShapeDtypeStruct((experts, features),...  1.79 us
  transfers between devices with their start and end apart: 16, of which 2 were waited for; matrix products, arithmetic and copies ran while one was open for 6% of the time, Pallas kernels for 39%

profile of v4, /device:TPU:0, one launch (start us, length us, event | category | flops | bytes accessed | tf_op | source)
XLA Modules:
  0.0 70.0 jit_solution(5741708587901456337)
XLA Ops:
  0.6 0.8 %copy.13 = s32[8,6]{0,1:T(8,128)S(1)} copy(s32[8,6]{1,0:T(8,128)} %param.8) | data formatting | bytes 384 | tf_op args[1]
  1.4 0.1 fusion.3
  1.5 0.8 %pad_maximum_fusion.1 = bf16[8,5248]{1,0:T(8,128)(2,1)S(1)} fusion(bf16[8,128]{1,0:T(8,128)(2,1)S(1)} %convert_element_type.24._, bf16[8,2560]{1,0:T(8,128)(2,1)} %param.13, bf16[8,2560]{1,0:T(8,128)(2,1)} %param.7), kind=kLoop, calls=%fused_computation.11 | loop fusion | flops 251904 | bytes 167936 | tf_op jit(solution)/shard_map/concatenate | solution.py:267
  2.3 3.0 %collective-permute-start = (bf16[8,5248]{1,0:T(8,128)(2,1)S(1)}, bf16[8,5248]{1,0:T(8,128)(2,1)S(1)}, u32[]{:S(2)}, u32[]{:S(2)}) collective-permute-start(bf16[8,5248]{1,0:T(8,128)(2,1)S(1)} %pad_maximum_fusion.1), channel_id=1, source_target_pairs={{0,2},{1,3},{2,0},{3,1},{4,6},{5,7},{6,4},{7,5},{8,10},{9,11},{10,... | collective-permute-start | bytes 251912 | tf_op jit(solution)/shard_map/ppermute | solution.py:26
  5.3 2.6 %collective-permute-start.1 = (bf16[8,5248]{1,0:T(8,128)(2,1)S(1)}, bf16[8,5248]{1,0:T(8,128)(2,1)S(1)}, u32[]{:S(2)}, u32[]{:S(2)}) collective-permute-start(bf16[8,5248]{1,0:T(8,128)(2,1)S(1)} %pad_maximum_fusion.1), channel_id=1, source_target_pairs={{0,4},{1,5},{2,6},{3,7},{4,0},{5,1},{6,2},{7,3},{8,12},{9,13},{10,... | collective-permute-start | bytes 251912 | tf_op jit(solution)/shard_map/ppermute | solution.py:26
  7.9 0.0 collective-permute-start.2
  7.9 0.9 %reduce-precision_convert_fusion.1 = (bf16[8,2560]{1,0:T(8,128)(2,1)S(1)}, bf16[8,2560]{1,0:T(8,128)(2,1)S(1)}, bf16[8,2560]{1,0:T(8,128)(2,1)S(1)}) fusion(f32[2560,8]{0,1:T(8,128)} %param.9), kind=kLoop, calls=%fused_computation.10 | loop fusion | flops 163840 | bytes 204800 | tf_op jit(solution)/shard_map/convert_element_type | solution.py:37
  8.9 0.8 %bitcast_dynamic-update-slice_fusion.7 = bf16[4,8,5248]{2,1,0:T(8,128)(2,1)S(1)} fusion(bf16[4,8,5248]{2,1,0:T(8,128)(2,1)S(1)} %broadcast_in_dim.49, s32[]{:T(128)S(6)} %select_n.58, bf16[8,128]{1,0:T(8,128)(2,1)S(1)} %convert_element_type.24._, bf16[8,2560]{1,0:T(8,128)(2,1)} %param.13, bf16[8,2560]{1,0:T(8,128)(2,1)} %param.7), kind=kLoop, calls=%fused_computation.15 | loop fusion | flops 251904 | bytes 167940 | tf_op jit(solution)/shard_map/jit(dynamic_update_index_in_dim)/dynamic_update_slice | solution.py:258
  9.7 5.6 %shard_map.118 = (bf16[2560,1024]{1,0:T(8,128)(2,1)S(1)}, bf16[2560,1024]{1,0:T(8,128)(2,1)S(1)}, bf16[2560,1024]{1,0:T(8,128)(2,1)S(1)}) custom-call(bf16[8,128]{1,0:T(8,128)(2,1)S(1)} %convert_element_type.24._, bf16[2560,1024]{1,0:T(8,128)(2,1)} %refs_0_.1, bf16[2560,1024]{1,0:T(8,128)(2,1)} %refs_1_.1, bf16[2560,1024]{1,0:T(8,128)(2,1)} %refs_2_.1), custom_call_target="tpu_custom_call" | custom-call | bytes 15728640 | tf_op jit(solution)/shard_map/pallas_call | solution.py:352
  15.3 0.1 pad_add_fusion.at_ref
  15.4 0.0 collective-permute-done
  15.4 0.0 collective-permute-done.1
  15.4 0.0 collective-permute-done.2
  15.5 0.1 collective-permute-start.11
  15.5 1.8 %collective-permute-start.3 = (bf16[4,8,5248]{2,1,0:T(8,128)(2,1)S(1)}, bf16[4,8,5248]{2,1,0:T(8,128)(2,1)S(1)}, u32[]{:S(2)}, u32[]{:S(2)}) collective-permute-start(bf16[4,8,5248]{2,1,0:T(8,128)(2,1)S(1)} %bitcast_dynamic-update-slice_fusion.4), channel_id=1, source_target_pairs={{0,8},{8,0},{16,24},{24,16},{1,9},{9,1},{17,25},{25,17},{2,10},{10... | collective-permute-start | bytes 1007624 | tf_op jit(solution)/shard_map/ppermute | solution.py:26
  17.3 1.5 %collective-permute-start.4 = (bf16[4,8,5248]{2,1,0:T(8,128)(2,1)S(1)}, bf16[4,8,5248]{2,1,0:T(8,128)(2,1)S(1)}, u32[]{:S(2)}, u32[]{:S(2)}) collective-permute-start(bf16[4,8,5248]{2,1,0:T(8,128)(2,1)S(1)} %bitcast_dynamic-update-slice_fusion.4), channel_id=1, source_target_pairs={{0,16},{8,24},{16,0},{24,8},{1,17},{9,25},{17,1},{25,9},{2,18},{10... | collective-permute-start | bytes 1007624 | tf_op jit(solution)/shard_map/ppermute | solution.py:26
  18.8 0.3 collective-permute-start.5
  19.1 0.1 broadcast_in_dim.48
  19.2 0.0 collective-permute-done.11
  19.2 10.6 %shard_map.120 = (bf16[32,5120]{1,0:T(8,128)(2,1)S(1)}, bf16[32,5120]{1,0:T(8,128)(2,1)S(1)}) custom-call(s32[4]{0:T(128)S(1)} %pad_add_fusion.at_ref, bf16[32,5248]{1,0:T(8,128)(2,1)S(1)} %bitcast.48, bf16[32,5248]{1,0:T(8,128)(2,1)S(1)} %bitcast.50, bf16[24,2560]{1,0:T(8,128)(2,1)S(1)} %pad_maximum_fusion.parts_ref, ...), custom_call_target="tpu_custom_call" | custom-call | flops 2013265920 | bytes 31457280 | tf_op jit(solution)/shard_map/pallas_call | solution.py:366
  29.8 0.1 collective-permute-start.12
  29.9 0.0 collective-permute-done.3
  30.0 4.5 %collective-permute-done.4 = bf16[4,8,5248]{2,1,0:T(8,128)(2,1)S(1)} collective-permute-done((bf16[4,8,5248]{2,1,0:T(8,128)(2,1)S(1)}, bf16[4,8,5248]{2,1,0:T(8,128)(2,1)S(1)}, u32[]{:S(2)}, u32[]{:S(2)}) %collective-permute-start.4) | collective-permute-done | bytes 335904 | tf_op jit(solution)/shard_map/ppermute | solution.py:26
  34.5 0.0 collective-permute-done.5
  34.6 0.1 collective-permute-start.6
  34.6 0.0 collective-permute-done.12
  34.6 0.1 fusion
  34.7 0.7 %dynamic-slice_bitcast_fusion = (bf16[8,5120]{1,0:T(8,128)(2,1)}, bf16[8,5120]{1,0:T(8,128)(2,1)}, bf16[8,5120]{1,0:T(8,128)(2,1)}, bf16[8,5120]{1,0:T(8,128)(2,1)S(1)}) fusion(bf16[4,8,5120]{2,1,0:T(8,128)(2,1)S(1)} %fusion, s32[]{:T(128)S(6)} %select_n.61, s32[]{:T(128)S(6)} %select_n.60, s32[]{:T(128)S(6)} %select_n.59, s32[]{:T(128)S(6)} %select_n.58), kind=kLoop, calls=%fused_computation.18 | loop fusion | bytes 655376 | tf_op jit(solution)/shard_map/jit(dynamic_index_in_dim)/squeeze | solution.py:327
  35.4 0.7 collective-permute-start.13
  36.1 3.5 %collective-permute-start.14 = (bf16[8,5120]{1,0:T(8,128)(2,1)}, bf16[8,5120]{1,0:T(8,128)(2,1)S(1)}, u32[]{:S(2)}, u32[]{:S(2)}) collective-permute-start(bf16[8,5120]{1,0:T(8,128)(2,1)} %get-tuple-element.41), channel_id=1, source_target_pairs={{0,4},{1,5},{2,6},{3,7},{4,0},{5,1},{6,2},{7,3},{8,12},{9,13},{10,... | collective-permute-start | bytes 245768 | tf_op jit(solution)/shard_map/ppermute | solution.py:26
  39.6 0.2 collective-permute-start.15
  39.8 0.0 collective-permute-done.6
  39.8 7.1 %shard_map.119 = (bf16[256,5248]{1,0:T(8,128)(2,1)S(1)}, bf16[256,1024]{1,0:T(8,128)(2,1)S(1)}, bf16[256,1024]{1,0:T(8,128)(2,1)S(1)}, bf16[256,1024]{1,0:T(8,12...) custom-call(s32[4]{0:T(128)S(1)} %pad_add_fusion.at_ref, bf16[128,5248]{1,0:T(8,128)(2,1)S(1)} %bitcast.47, ...), custom_call_target="tpu_custom_call" | custom-call | flops 4026531840 | bytes 15728640 | tf_op jit(solution)/shard_map/pallas_call | solution.py:389
  46.9 0.0 copy-start
  46.9 0.8 %copy-done = bf16[256,1024]{1,0:T(8,128)(2,1)} copy-done((bf16[256,1024]{1,0:T(8,128)(2,1)}, bf16[256,1024]{1,0:T(8,128)(2,1)S(1)}, u32[]{:S(2)}) %copy-start) | copy-done | bytes 524312
  47.8 0.0 copy-start.2
  47.8 0.8 %copy-done.2 = bf16[256,1024]{1,0:T(8,128)(2,1)} copy-done((bf16[256,1024]{1,0:T(8,128)(2,1)}, bf16[256,1024]{1,0:T(8,128)(2,1)S(1)}, u32[]{:S(2)}) %copy-start.2) | copy-done | bytes 524312
  48.6 0.0 copy-start.8
  48.6 0.6 copy-done.8
  49.2 0.3 collective-permute-start.7
  49.5 3.8 %collective-permute-start.8 = (f32[256]{0:T(256)S(1)}, f32[256]{0:T(256)}, u32[]{:S(2)}, u32[]{:S(2)}) collective-permute-start(f32[256]{0:T(256)S(1)} %bitcast.54), channel_id=1, source_target_pairs={{0,4},{1,5},{2,6},{3,7},{4,0},{5,1},{6,2},{7,3},{8,12},{9,13},{10,... | collective-permute-start | bytes 3080 | tf_op jit(solution)/shard_map/ppermute | solution.py:26
  53.3 0.0 collective-permute-done.7
  53.3 3.0 %collective-permute-start.9 = (f32[256]{0:T(256)S(1)}, f32[256]{0:T(256)S(1)}, u32[]{:S(2)}, u32[]{:S(2)}) collective-permute-start(f32[256]{0:T(256)S(1)} %bitcast.55), channel_id=1, source_target_pairs={{0,6},{1,7},{2,4},{3,5},{4,2},{5,3},{6,0},{7,1},{8,14},{9,15},{10,... | collective-permute-start | bytes 3080 | tf_op jit(solution)/shard_map/ppermute | solution.py:26
  56.3 0.0 copy-done.10
  56.4 0.7 %dynamic_update_slice.48 = f32[4,256]{1,0:T(4,128)S(1)} dynamic-update-slice(f32[4,256]{1,0:T(4,128)S(1)} %dynamic_update_slice.47, f32[1,256]{1,0:T(1,128)} %bitcast.57, s32[]{:T(128)S(6)} %select_n.59, s32[]{:T(128)} %constant.83.clone.1) | dynamic-update-slice | bytes 2052 | tf_op jit(solution)/shard_map/jit(dynamic_update_index_in_dim)/dynamic_update_slice | solution.py:258
  57.1 0.0 collective-permute-done.8
  57.1 0.7 dynamic_update_slice.49
  57.8 0.9 %collective-permute-done.9 = f32[256]{0:T(256)S(1)} collective-permute-done((f32[256]{0:T(256)S(1)}, f32[256]{0:T(256)S(1)}, u32[]{:S(2)}, u32[]{:S(2)}) %collective-permute-start.9) | collective-permute-done | bytes 1056 | tf_op jit(solution)/shard_map/ppermute | solution.py:26
  58.7 0.1 collective-permute-start.10
  58.8 0.0 collective-permute-done.13.back_refs_1_.__0_
  58.8 0.0 collective-permute-done.14.back_refs_2_.__1_
  58.8 0.0 collective-permute-done.15.back_refs_3_.__2_
  58.8 0.0 copy-start.5
  58.9 0.6 copy-done.5
  59.5 1.0 %copy-done.1 = bf16[256,1024]{1,0:T(8,128)(2,1)S(1)} copy-done((bf16[256,1024]{1,0:T(8,128)(2,1)S(1)}, bf16[256,1024]{1,0:T(8,128)(2,1)}, u32[]{:S(2)}) %copy-start.1) | copy-done | bytes 524312
  60.5 1.0 %copy-done.3 = bf16[256,1024]{1,0:T(8,128)(2,1)S(1)} copy-done((bf16[256,1024]{1,0:T(8,128)(2,1)S(1)}, bf16[256,1024]{1,0:T(8,128)(2,1)}, u32[]{:S(2)}) %copy-start.3) | copy-done | bytes 524312
  61.6 0.9 %copy-done.6 = bf16[8,5120]{1,0:T(8,128)(2,1)S(1)} copy-done((bf16[8,5120]{1,0:T(8,128)(2,1)S(1)}, bf16[8,5120]{1,0:T(8,128)(2,1)}, u32[]{:S(2)}) %copy-start.6) | copy-done | bytes 81944
  62.5 4.1 %shard_map.122 = (f32[640,1024]{1,0:T(8,128)}, f32[640,1024]{1,0:T(8,128)}, f32[640,1024]{1,0:T(8,128)}) custom-call(s32[4]{0:T(128)S(1)} %pad_add_fusion.at_ref, bf16[256,5248]{1,0:T(8,128)(2,1)S(1)} %get-tuple-element.26.x_ref, bf16[256,1024]{1,0:T(8,128)(2,1)S(1)} %get-tuple-element.34.gate_grad_ref, bf16[256,1024]{1,0:T(8,128)(2,1)S(1)} %copy-done.1, ...), custom_call_target="tpu_custom_call" | custom-call | flops 1006632960 | bytes 7864320 | tf_op jit(solution)/shard_map/pallas_call | solution.py:414
  66.5 0.0 collective-permute-done.10
  66.6 0.0 copy-done.4
  66.6 0.0 copy-start.7
  66.6 0.9 %copy-done.7 = bf16[8,5120]{1,0:T(8,128)(2,1)S(1)} copy-done((bf16[8,5120]{1,0:T(8,128)(2,1)S(1)}, bf16[8,5120]{1,0:T(8,128)(2,1)}, u32[]{:S(2)}) %copy-start.7) | copy-done | bytes 81944
  67.5 0.7 %copy-done.9 = f32[3,8,256]{2,1,0:T(8,128)S(1)} copy-done((f32[3,8,256]{2,1,0:T(8,128)S(1)}, f32[3,8,256]{2,1,0:T(8,128)}, u32[]{:S(2)}) %copy-start.9) | copy-done | bytes 24600
  68.2 1.8 %shard_map.121 = (bf16[8,2560]{1,0:T(8,128)(2,1)}, bf16[8,2560]{1,0:T(8,128)(2,1)}, f32[8,2560]{1,0:T(8,128)}) custom-call(s32[4]{0:T(128)S(1)} %pad_add_fusion.at_ref, bf16[256,5248]{1,0:T(8,128)(2,1)S(1)} %get-tuple-element.26.x_ref, f32[3,8,256]{2,1,0:T(8,128)S(1)} %copy-done.9, f32[8,256]{1,0:T(8,128)S(1)} %reshape.36.pulls_ref, f32[8,2560]{1,0:T(8,128)S(1)} %bitcast.51, ...), custom_call_target="tpu_custom_call" | custom-call | flops 31457280 | bytes 1310720 | tf_op jit(solution)/shard_map/pallas_call | solution.py:425
  (24 shorter events, 0.4 us)
Async XLA Ops:
  2.3 13.1 %collective-permute-start = (bf16[8,5248]{1,0:T(8,128)(2,1)S(1)}, bf16[8,5248]{1,0:T(8,128)(2,1)S(1)}, u32[]{:S(2)}, u32[]{:S(2)}) collective-permute-start(bf16[8,5248]{1,0:T(8,128)(2,1)S(1)} %pad_maximum_fusion.1), channel_id=1, source_target_pairs={{0,2},{1,3},{2,0},{3,1},{4,6},{5,7},{6,4},{7,5},{8,10},{9,11},{10,... | collective-permute-start | bytes 251912 | tf_op jit(solution)/shard_map/ppermute | solution.py:26
  5.3 10.1 %collective-permute-start.1 = (bf16[8,5248]{1,0:T(8,128)(2,1)S(1)}, bf16[8,5248]{1,0:T(8,128)(2,1)S(1)}, u32[]{:S(2)}, u32[]{:S(2)}) collective-permute-start(bf16[8,5248]{1,0:T(8,128)(2,1)S(1)} %pad_maximum_fusion.1), channel_id=1, source_target_pairs={{0,4},{1,5},{2,6},{3,7},{4,0},{5,1},{6,2},{7,3},{8,12},{9,13},{10,... | collective-permute-start | bytes 251912 | tf_op jit(solution)/shard_map/ppermute | solution.py:26
  7.9 7.5 %collective-permute-start.2 = (bf16[8,5248]{1,0:T(8,128)(2,1)S(1)}, bf16[8,5248]{1,0:T(8,128)(2,1)S(1)}, u32[]{:S(2)}, u32[]{:S(2)}) collective-permute-start(bf16[8,5248]{1,0:T(8,128)(2,1)S(1)} %pad_maximum_fusion.1), channel_id=1, source_target_pairs={{0,6},{1,7},{2,4},{3,5},{4,2},{5,3},{6,0},{7,1},{8,14},{9,15},{10,... | collective-permute-start | bytes 251912 | tf_op jit(solution)/shard_map/ppermute | solution.py:26
  15.5 3.8 %collective-permute-start.11 = (bf16[4,8,5248]{2,1,0:T(8,128)(2,1)S(1)}, bf16[4,8,5248]{2,1,0:T(8,128)(2,1)S(1)}, u32[]{:S(2)}, u32[]{:S(2)}) collective-permute-start(bf16[4,8,5248]{2,1,0:T(8,128)(2,1)S(1)} %bitcast_dynamic-update-slice_fusion.4), channel_id=1, source_target_pairs={{0,1},{1,0},{2,3},{3,2},{4,5},{5,4},{6,7},{7,6},{8,9},{9,8},{10,11... | collective-permute-start | bytes 1007624 | tf_op jit(solution)/shard_map/ppermute | solution.py:26
  15.5 14.4 %collective-permute-start.3 = (bf16[4,8,5248]{2,1,0:T(8,128)(2,1)S(1)}, bf16[4,8,5248]{2,1,0:T(8,128)(2,1)S(1)}, u32[]{:S(2)}, u32[]{:S(2)}) collective-permute-start(bf16[4,8,5248]{2,1,0:T(8,128)(2,1)S(1)} %bitcast_dynamic-update-slice_fusion.4), channel_id=1, source_target_pairs={{0,8},{8,0},{16,24},{24,16},{1,9},{9,1},{17,25},{25,17},{2,10},{10... | collective-permute-start | bytes 1007624 | tf_op jit(solution)/shard_map/ppermute | solution.py:26
  17.3 17.2 %collective-permute-start.4 = (bf16[4,8,5248]{2,1,0:T(8,128)(2,1)S(1)}, bf16[4,8,5248]{2,1,0:T(8,128)(2,1)S(1)}, u32[]{:S(2)}, u32[]{:S(2)}) collective-permute-start(bf16[4,8,5248]{2,1,0:T(8,128)(2,1)S(1)} %bitcast_dynamic-update-slice_fusion.4), channel_id=1, source_target_pairs={{0,16},{8,24},{16,0},{24,8},{1,17},{9,25},{17,1},{25,9},{2,18},{10... | collective-permute-start | bytes 1007624 | tf_op jit(solution)/shard_map/ppermute | solution.py:26
  18.8 15.7 %collective-permute-start.5 = (bf16[4,8,5248]{2,1,0:T(8,128)(2,1)S(1)}, bf16[4,8,5248]{2,1,0:T(8,128)(2,1)S(1)}, u32[]{:S(2)}, u32[]{:S(2)}) collective-permute-start(bf16[4,8,5248]{2,1,0:T(8,128)(2,1)S(1)} %bitcast_dynamic-update-slice_fusion.4), channel_id=1, source_target_pairs={{0,24},{8,16},{16,8},{24,0},{1,25},{9,17},{17,9},{25,1},{2,26},{10... | collective-permute-start | bytes 1007624 | tf_op jit(solution)/shard_map/ppermute | solution.py:26
  29.8 4.8 %collective-permute-start.12 = (bf16[4,8,5120]{2,1,0:T(8,128)(2,1)S(1)}, bf16[4,8,5120]{2,1,0:T(8,128)(2,1)S(1)}, u32[]{:S(2)}, u32[]{:S(2)}) collective-permute-start(bf16[4,8,5120]{2,1,0:T(8,128)(2,1)S(1)} %bitcast.52), channel_id=1, source_target_pairs={{0,1},{1,0},{2,3},{3,2},{4,5},{5,4},{6,7},{7,6},{8,9},{9,8},{10,11... | collective-permute-start | bytes 983048 | tf_op jit(solution)/shard_map/ppermute | solution.py:26
  34.6 5.3 %collective-permute-start.6 = (bf16[4,4,8,5248]{3,2,1,0:T(8,128)(2,1)S(1)}, bf16[4,4,8,5248]{3,2,1,0:T(8,128)(2,1)S(1)}, u32[]{:S(2)}, u32[]{:S(2)}) collective-permute-start(bf16[4,4,8,5248]{3,2,1,0:T(8,128)(2,1)S(1)} %bitcast_dynamic-update-slice_fusion), channel_id=1, source_target_pairs={{0,1},{1,0},{2,3},{3,2},{4,5},{5,4},{6,7},{7,6},{8,9},{9,8},{10,11... | collective-permute-start | bytes 4030472 | tf_op jit(solution)/shard_map/ppermute | solution.py:26
  35.4 23.4 %collective-permute-start.13 = (bf16[8,5120]{1,0:T(8,128)(2,1)}, bf16[8,5120]{1,0:T(8,128)(2,1)S(1)}, u32[]{:S(2)}, u32[]{:S(2)}) collective-permute-start(bf16[8,5120]{1,0:T(8,128)(2,1)} %get-tuple-element.42), channel_id=1, source_target_pairs={{0,2},{1,3},{2,0},{3,1},{4,6},{5,7},{6,4},{7,5},{8,10},{9,11},{10,... | collective-permute-start | bytes 245768 | tf_op jit(solution)/shard_map/ppermute | solution.py:26
  36.1 22.7 %collective-permute-start.14 = (bf16[8,5120]{1,0:T(8,128)(2,1)}, bf16[8,5120]{1,0:T(8,128)(2,1)S(1)}, u32[]{:S(2)}, u32[]{:S(2)}) collective-permute-start(bf16[8,5120]{1,0:T(8,128)(2,1)} %get-tuple-element.41), channel_id=1, source_target_pairs={{0,4},{1,5},{2,6},{3,7},{4,0},{5,1},{6,2},{7,3},{8,12},{9,13},{10,... | collective-permute-start | bytes 245768 | tf_op jit(solution)/shard_map/ppermute | solution.py:26
  39.6 19.2 %collective-permute-start.15 = (bf16[8,5120]{1,0:T(8,128)(2,1)}, bf16[8,5120]{1,0:T(8,128)(2,1)S(1)}, u32[]{:S(2)}, u32[]{:S(2)}) collective-permute-start(bf16[8,5120]{1,0:T(8,128)(2,1)} %get-tuple-element.40), channel_id=1, source_target_pairs={{0,6},{1,7},{2,4},{3,5},{4,2},{5,3},{6,0},{7,1},{8,14},{9,15},{10,... | collective-permute-start | bytes 245768 | tf_op jit(solution)/shard_map/ppermute | solution.py:26
  46.9 0.8 %copy-start = (bf16[256,1024]{1,0:T(8,128)(2,1)}, bf16[256,1024]{1,0:T(8,128)(2,1)S(1)}, u32[]{:S(2)}) copy-start(bf16[256,1024]{1,0:T(8,128)(2,1)S(1)} %get-tuple-element.35.up_grad_ref) | copy-start | bytes 1572868
  47.8 0.8 %copy-start.2 = (bf16[256,1024]{1,0:T(8,128)(2,1)}, bf16[256,1024]{1,0:T(8,128)(2,1)S(1)}, u32[]{:S(2)}) copy-start(bf16[256,1024]{1,0:T(8,128)(2,1)S(1)} %get-tuple-element.36.gated_ref) | copy-start | bytes 1572868
  48.6 0.6 copy-start.8
  49.2 4.2 %collective-permute-start.7 = (f32[256]{0:T(256)S(1)}, f32[256]{0:T(256)S(1)}, u32[]{:S(2)}, u32[]{:S(2)}) collective-permute-start(f32[256]{0:T(256)S(1)} %bitcast.53), channel_id=1, source_target_pairs={{0,2},{1,3},{2,0},{3,1},{4,6},{5,7},{6,4},{7,5},{8,10},{9,11},{10,... | collective-permute-start | bytes 3080 | tf_op jit(solution)/shard_map/ppermute | solution.py:26
  49.5 7.6 %collective-permute-start.8 = (f32[256]{0:T(256)S(1)}, f32[256]{0:T(256)}, u32[]{:S(2)}, u32[]{:S(2)}) collective-permute-start(f32[256]{0:T(256)S(1)} %bitcast.54), channel_id=1, source_target_pairs={{0,4},{1,5},{2,6},{3,7},{4,0},{5,1},{6,2},{7,3},{8,12},{9,13},{10,... | collective-permute-start | bytes 3080 | tf_op jit(solution)/shard_map/ppermute | solution.py:26
  53.3 3.0 %copy-start.10 = (f32[256]{0:T(256)}, f32[256]{0:T(256)S(1)}, u32[]{:S(2)}) copy-start(f32[256]{0:T(256)S(1)} %collective-permute-done.7) | copy-start | bytes 3076
  53.3 5.4 %collective-permute-start.9 = (f32[256]{0:T(256)S(1)}, f32[256]{0:T(256)S(1)}, u32[]{:S(2)}, u32[]{:S(2)}) collective-permute-start(f32[256]{0:T(256)S(1)} %bitcast.55), channel_id=1, source_target_pairs={{0,6},{1,7},{2,4},{3,5},{4,2},{5,3},{6,0},{7,1},{8,14},{9,15},{10,... | collective-permute-start | bytes 3080 | tf_op jit(solution)/shard_map/ppermute | solution.py:26
  58.7 7.8 %collective-permute-start.10 = (f32[4,256]{1,0:T(4,128)S(1)}, f32[4,256]{1,0:T(4,128)S(1)}, u32[]{:S(2)}, u32[]{:S(2)}) collective-permute-start(f32[4,256]{1,0:T(4,128)S(1)} %dynamic_update_slice.50), channel_id=1, source_target_pairs={{0,1},{1,0},{2,3},{3,2},{4,5},{5,4},{6,7},{7,6},{8,9},{9,8},{10,11... | collective-permute-start | bytes 12296 | tf_op jit(solution)/shard_map/ppermute | solution.py:26
  58.8 0.6 copy-start.5
  59.5 1.0 %copy-start.1 = (bf16[256,1024]{1,0:T(8,128)(2,1)S(1)}, bf16[256,1024]{1,0:T(8,128)(2,1)}, u32[]{:S(2)}) copy-start(bf16[256,1024]{1,0:T(8,128)(2,1)} %copy-done) | copy-start | bytes 1572868
  60.5 1.0 %copy-start.3 = (bf16[256,1024]{1,0:T(8,128)(2,1)S(1)}, bf16[256,1024]{1,0:T(8,128)(2,1)}, u32[]{:S(2)}) copy-start(bf16[256,1024]{1,0:T(8,128)(2,1)} %copy-done.2) | copy-start | bytes 1572868
  61.6 0.9 %copy-start.6 = (bf16[8,5120]{1,0:T(8,128)(2,1)S(1)}, bf16[8,5120]{1,0:T(8,128)(2,1)}, u32[]{:S(2)}) copy-start(bf16[8,5120]{1,0:T(8,128)(2,1)} %copy-done.5) | copy-start | bytes 245764
  62.5 4.1 %copy-start.4 = (f32[2560,8]{0,1:T(8,128)S(1)}, f32[2560,8]{0,1:T(8,128)}, u32[]{:S(2)}) copy-start(f32[2560,8]{0,1:T(8,128)} %param.9) | copy-start | bytes 245764
  66.6 0.9 %copy-start.7 = (bf16[8,5120]{1,0:T(8,128)(2,1)S(1)}, bf16[8,5120]{1,0:T(8,128)(2,1)}, u32[]{:S(2)}) copy-start(bf16[8,5120]{1,0:T(8,128)(2,1)} %copy-done.5) | copy-start | bytes 245764
  67.5 0.7 %copy-start.9 = (f32[3,8,256]{2,1,0:T(8,128)S(1)}, f32[3,8,256]{2,1,0:T(8,128)}, u32[]{:S(2)}) copy-start(f32[3,8,256]{2,1,0:T(8,128)} %copy-done.8) | copy-start | bytes 73732

commit v5 on v4

v5 whole, which is shorter than its diff:
```python
import jax
import jax.numpy as jnp
from jax import lax
from jax.experimental import pallas as pl
from jax.experimental.pallas import tpu as pltpu
from jax.sharding import PartitionSpec as P

F32 = jnp.float32
BF16 = jnp.bfloat16
LANES = 128
STEP = 256
GATHER_BYTES = 8 << 20
HIGHEST = lax.Precision.HIGHEST
LAST = (((1,), (1,)), ((), ()))
FIRST = (((0,), (0,)), ((), ()))
IN_VMEM = pl.BlockSpec(memory_space=pltpu.VMEM)
IN_SMEM = pl.BlockSpec(memory_space=pltpu.SMEM)


def dot(left, right, contract=(((1,), (0,)), ((), ()))):
    return lax.dot_general(left, right, contract, preferred_element_type=F32)


def swap(x, axis, mask):
    count = lax.axis_size(axis)
    return lax.ppermute(x, axis, [(i, i ^ mask) for i in range(count)])


def in_hbm(x):
    return pltpu.with_memory_space_constraint(x, pltpu.HBM)


def three_parts(x):
    parts = []
    for _ in range(3):
        part = lax.reduce_precision(x, 8, 7)
        parts.append(part.astype(BF16))
        x = x - part
    return parts


def exact_dot(left, right, contract):
    return sum(dot(left, part, contract) for part in three_parts(right)[::-1])


def gates_of(rows, chosen, router):
    logits = exact_dot(rows, router, (((1,), (0,)), ((), ())))
    picked = chosen > 0.5
    affinity = jnp.where(picked, jax.nn.sigmoid(logits), 0.0)
    denominator = jnp.sum(affinity, axis=1, keepdims=True)
    return picked, affinity, denominator, affinity / denominator


def place_rows(x_ref, first, core, mine_ref, theirs_ref):
    half = mine_ref.shape[0]
    x_ref[pl.ds(pl.multiple_of(first + core * half, half), half), :] = mine_ref[...]
    x_ref[pl.ds(pl.multiple_of(first + (1 - core) * half, half), half), :] = theirs_ref[...]


def gate_tables(x, parts_ref, experts):
    features = parts_ref.shape[1]
    logits = dot(parts_ref[...], x[:, :features], LAST)
    logits = logits[2 * experts :] + logits[experts : 2 * experts] + logits[:experts]
    unit = lax.broadcasted_iota(jnp.int32, (experts, LANES), 0) == lax.broadcasted_iota(
        jnp.int32, (experts, LANES), 1
    )
    picked = dot(unit.astype(BF16), x[:, 2 * features :], LAST) > 0.5
    affinity = jnp.where(picked, 1.0 / (1.0 + jnp.exp(-logits)), 0.0)
    denominator = jnp.sum(affinity, axis=0, keepdims=True)
    return affinity, denominator, affinity / denominator


def slot_gates(gates, expert):
    own = lax.broadcasted_iota(jnp.int32, (gates.shape[0], LANES), 0) == expert
    return lax.dot_general(
        gates, own.astype(F32), FIRST, precision=HIGHEST, preferred_element_type=F32
    )


def hidden_step(at, x, slot_gate, w_gate_ref, w_up_ref, w_down_ref):
    features = w_gate_ref.shape[0]
    gate_pre = dot(x[:, :features], w_gate_ref[:, at])
    up_pre = dot(x[:, :features], w_up_ref[:, at])
    raw = dot(x[:, features : 2 * features], w_down_ref[:, at])
    sigma = 1.0 / (1.0 + jnp.exp(-gate_pre))
    silu = gate_pre * sigma
    hidden = silu * up_pre
    slot = jnp.tile(slot_gate, (1, STEP // LANES))
    hidden_grad = slot * raw
    gate_grad = hidden_grad * up_pre * sigma * (1.0 + gate_pre * (1.0 - sigma))
    grads = (gate_grad, hidden_grad * silu, slot * hidden)
    return [grad.astype(BF16) for grad in grads], hidden * raw


def load_kernel(_, *refs):
    count = len(refs) // 2
    copies = [
        pltpu.make_async_copy(refs[i], refs[count + i], refs[-1].at[i]) for i in range(count)
    ]
    for copy in copies:
        copy.start()
    for copy in copies:
        copy.wait()


def order_kernel(at_ref, piece_refs, out_ref):
    for m, ref in enumerate(piece_refs):
        out_ref[at_ref[3] ^ m] = ref[...]


def own_kernel(
    at_ref, mine_ref, theirs_ref, parts_ref, w_gate_ref, w_up_ref, w_down_ref,
    keep_ref, send_ref, gate_grad_ref, up_grad_ref, gated_ref, pull_ref, table_ref,
    x_ref, back_ref,
):
    features, hidden_units = w_gate_ref.shape
    experts = parts_ref.shape[0] // 3
    core = at_ref[0]
    place_rows(x_ref, 0, core, mine_ref, theirs_ref)
    affinity, denominator, gates = gate_tables(x_ref, parts_ref, experts)
    table_ref[0] = affinity
    table_ref[1] = gates
    table_ref[2] = jnp.broadcast_to(denominator, affinity.shape)
    slot_gate = slot_gates(gates, at_ref[1])
    pulls = jnp.zeros(slot_gate.shape, F32)
    for start in range(0, hidden_units, STEP):
        at = pl.ds(start, STEP)
        grads, pulled = hidden_step(at, x_ref, slot_gate, w_gate_ref, w_up_ref, w_down_ref)
        gate_grad_ref[:, at], up_grad_ref[:, at], gated_ref[:, at] = grads
        pulls += sum(pulled[:, lane : lane + LANES] for lane in range(0, STEP, LANES))
    ones = jnp.ones((pull_ref.shape[0], LANES), F32)
    pull_ref[...] = lax.dot_general(
        ones, pulls, LAST, precision=HIGHEST, preferred_element_type=F32
    )
    for start in range(0, features, STEP):
        at = pl.ds(start, STEP)
        later = pl.ds(features + start, STEP)
        back_ref[:, at] = dot(gated_ref[...], w_down_ref[at, :], LAST).astype(BF16)
        back = dot(gate_grad_ref[...], w_gate_ref[at, :], LAST)
        back_ref[:, later] = (back + dot(up_grad_ref[...], w_up_ref[at, :], LAST)).astype(BF16)

    half = keep_ref.shape[0]
    keep_ref[...] = back_ref[pl.ds(pl.multiple_of(core * half, half), half), :]
    send_ref[...] = back_ref[pl.ds(pl.multiple_of((1 - core) * half, half), half), :]


def pair_kernel(at_ref, keep_ref, other_ref, pull_ref, other_pull_ref, pair_ref, out_refs):
    for m, ref in enumerate(out_refs):
        chip = at_ref[3] ^ m
        ref[...] = (keep_ref[chip].astype(F32) + other_ref[chip].astype(F32)).astype(BF16)
    row = lax.broadcasted_iota(jnp.int32, pull_ref.shape, 0)
    pair_ref[...] = jnp.where(row % 2 == at_ref[0], pull_ref[...], other_pull_ref[...])


def logit_kernel(at_ref, table_ref, pair_refs, out_ref):
    affinity, gates, denominator = table_ref[0], table_ref[1], table_ref[2]
    chip = lax.broadcasted_iota(jnp.int32, affinity.shape, 0) // 2
    pulls = jnp.zeros(affinity.shape, F32)
    for m, ref in enumerate(pair_refs):
        pulls = jnp.where(chip == at_ref[3] ^ m, ref[...], pulls)
    mean_pull = jnp.sum(gates * pulls, axis=0, keepdims=True)
    out_ref[...] = (pulls - mean_pull) / denominator * affinity * (1.0 - affinity)


def weight_kernel(
    at_ref, mine_refs, theirs_refs, parts_ref, w_gate_ref, w_up_ref, w_down_ref,
    own_refs, logit_refs, gate_ref, up_ref, down_ref, router_ref,
    x_ref, turned_ref, grad_refs, out_refs, sems,
):
    features, hidden_units = w_gate_ref.shape
    experts = parts_ref.shape[0] // 3
    portion = gate_ref.shape[0]
    group_rows = own_refs[0].shape[0]
    for m, (mine_ref, theirs_ref) in enumerate(zip(mine_refs, theirs_refs)):
        place_rows(x_ref, m * group_rows, at_ref[0], mine_ref, theirs_ref)
    first = at_ref[2] * portion
    for half in range(2):
        for row in range(0, portion, LANES):
            at = pl.ds(pl.multiple_of(half * features + first + row, LANES), LANES)
            turned_ref[half, row : row + LANES, :] = x_ref[:, at].T
    far = x_ref.at[group_rows:, :]
    slot_gate = slot_gates(gate_tables(far, parts_ref, experts)[2], at_ref[1])
    copies = []
    for step, start in enumerate(range(0, hidden_units, STEP)):
        at = pl.ds(start, STEP)
        grads, _ = hidden_step(at, far, slot_gate, w_gate_ref, w_up_ref, w_down_ref)
        targets = (gate_ref, up_ref, down_ref)
        for j, (own_ref, grad) in enumerate(zip(own_refs, grads)):
            grad_refs[j][:group_rows, at] = own_ref[:, at]
            grad_refs[j][group_rows:, at] = grad
            out_refs[j][:, at] = dot(turned_ref[j // 2], grad_refs[j][:, at])
            copy = pltpu.make_async_copy(
                out_refs[j].at[:, at], targets[j].at[:, at], sems.at[step, j]
            )
            copy.start()
            copies.append(copy)
    totals = []
    for m, ref in enumerate(logit_refs):
        rest, parts = ref[...], []
        for _ in range(3):
            parts.append(rest.astype(BF16).astype(F32))
            rest = rest - parts[-1]
        stacked = jnp.concatenate(parts, axis=0).astype(BF16)
        total = dot(stacked, x_ref[m * group_rows : (m + 1) * group_rows, :features])
        totals.append(total[2 * experts :] + total[experts : 2 * experts] + total[:experts])
    while len(totals) > 1:
        totals = [totals[i] + totals[i + 1] for i in range(0, len(totals), 2)]
    router_ref[...] = totals[0]
    for copy in copies:
        copy.wait()


def last_kernel(at_ref, logit_ref, router_ref, back_refs, mixed_ref, tokens_ref):
    features = router_ref.shape[1]
    count = mixed_ref.shape[0]
    chips = len(back_refs)
    grads = logit_ref[...]
    shape = (count, grads.shape[1])
    row = lax.broadcasted_iota(jnp.int32, shape, 0) + (at_ref[0] * chips + at_ref[3]) * count
    own = (lax.broadcasted_iota(jnp.int32, shape, 1) == row).astype(F32)
    own_grads = lax.dot_general(own, grads, LAST, precision=HIGHEST, preferred_element_type=F32)
    back = jnp.dot(own_grads, router_ref[...], precision=HIGHEST, preferred_element_type=F32)
    summed = sum(ref[...].astype(F32) for ref in back_refs)
    mixed_ref[...] = summed[:, :features].astype(BF16)
    tokens_ref[...] = (summed[:, features:] + back).astype(BF16)


def call(kernel, out_shape, in_specs, out_specs, scratch=(), limit=4, flops=0, moved=1 << 17):
    return pl.pallas_call(
        kernel,
        out_shape=out_shape,
        in_specs=in_specs,
        out_specs=out_specs,
        scratch_shapes=scratch,
        compiler_params=pltpu.CompilerParams(vmem_limit_bytes=limit << 20),
        cost_estimate=pl.CostEstimate(flops=flops, bytes_accessed=moved, transcendentals=0),
    )


def local(tokens, routes, router, w_gate, w_up, w_down, cotangent):
    tok_count, features = tokens.shape
    experts = router.shape[1]
    hidden_units = w_gate.shape[1]
    devices = lax.axis_size("expert")
    groups = lax.axis_size("dp")
    sharing = devices // experts
    chips = devices // 2
    group_rows = devices * tok_count
    me = lax.axis_index("expert")
    group = lax.axis_index("dp")
    core, chip = me % 2, me // 2
    own_expert = me // sharing
    whole = sharing == 1 and groups * group_rows * features * 4 <= GATHER_BYTES

    def over_chips(x):
        out = jnp.zeros((chips,) + x.shape, x.dtype)
        for m in range(chips):
            piece = x if m == 0 else swap(x, "expert", 2 * m)
            out = lax.dynamic_update_index_in_dim(out, piece, chip ^ m, 0)
        return out

    def over_cores(x):
        other = swap(x, "expert", 1)
        return jnp.where(core == 0, jnp.stack([x, other]), jnp.stack([other, x]))

    ids = jnp.arange(LANES, dtype=jnp.int32)
    picked_wide = jnp.any(routes[:, :, None] == ids[None, None, :], axis=1).astype(BF16)
    message = jnp.concatenate([tokens, cotangent, picked_wide], axis=1)
    width = message.shape[1]
    if whole:
        return kernels_plan(message, router, w_gate, w_up, w_down)

    by_chip = over_chips(message)
    own = over_cores(by_chip).reshape(group_rows, width)
    rows, cot = own[:, :features], own[:, features : 2 * features]
    picked, affinity, denominator, gates = gates_of(
        rows, own[:, 2 * features : 2 * features + experts], router
    )
    slot_gate = lax.dynamic_slice_in_dim(gates, own_expert, 1, axis=1)
    gate_pre = dot(rows, w_gate)
    up_pre = dot(rows, w_up)
    sigma = jax.nn.sigmoid(gate_pre)
    silu = gate_pre * sigma
    hidden = silu * up_pre
    raw = dot(cot, w_down)
    pull = jnp.sum(hidden * raw, axis=1)
    hidden_grad = slot_gate * raw
    gate_grad = (hidden_grad * up_pre * sigma * (1.0 + gate_pre * (1.0 - sigma))).astype(BF16)
    up_grad = (hidden_grad * silu).astype(BF16)
    gated = (slot_gate * hidden).astype(BF16)
    mixed_part = dot(gated, w_down, LAST)
    input_part = dot(gate_grad, w_gate, LAST) + dot(up_grad, w_up, LAST)
    part = jnp.concatenate([mixed_part.astype(BF16), input_part.astype(BF16)], axis=1)
    part = part.reshape(2, chips, tok_count, 2 * features)
    keep = lax.dynamic_index_in_dim(part, core, 0, keepdims=False)
    send = lax.dynamic_index_in_dim(part, 1 - core, 0, keepdims=False)
    back = give_back(send_back(keep, send, chips, chip))
    total = sum(x.astype(F32) for x in back)
    pulls = over_cores(over_chips(pull))
    pulls = jnp.swapaxes(pulls, 0, 1).reshape(experts, sharing, -1)
    pulls = jnp.sum(pulls, axis=1).T
    mean_pull = jnp.sum(gates * pulls, axis=1, keepdims=True)
    logit_grad = (pulls - mean_pull) / denominator * affinity * (1.0 - affinity)
    logit_grad = jnp.where(picked, logit_grad, 0.0)
    place = core * chips + chip
    own_logit = lax.dynamic_slice_in_dim(logit_grad, place * tok_count, tok_count, axis=0)
    grad_router = lax.psum(exact_dot(tokens, own_logit, FIRST), ("dp", "expert"))
    router_back = lax.dot_general(own_logit, router, LAST, precision=HIGHEST)
    parts = [
        dot(left, right, FIRST)
        for left, right in ((rows, gate_grad), (rows, up_grad), (cot, gated))
    ]
    summed = lax.psum_scatter(
        jnp.concatenate(parts, axis=1).astype(BF16), "dp", scatter_dimension=0, tiled=True
    ).astype(F32)
    grad_gate, grad_up, grad_down = jnp.split(summed, 3, axis=1)
    mixed = total[:, :features].astype(BF16)
    grad_tokens = (total[:, features:] + router_back).astype(BF16)
    return (mixed, grad_tokens, grad_router, grad_gate, grad_up, grad_down)


def send_back(keep, send, chips, chip):
    summed = (keep.astype(F32) + swap(send, "expert", 1).astype(F32)).astype(BF16)
    return [
        lax.dynamic_index_in_dim(summed, chip ^ m, 0, keepdims=False) for m in range(chips)
    ]


def give_back(pieces):
    return [
        piece if m == 0 else swap(piece, "expert", 2 * m) for m, piece in enumerate(pieces)
    ]


def kernels_plan(message, router, w_gate, w_up, w_down):
    features, experts = router.shape
    hidden_units = w_gate.shape[1]
    tok_count, width = message.shape
    groups = lax.axis_size("dp")
    chips = lax.axis_size("expert") // 2
    me = lax.axis_index("expert")
    half = chips * tok_count
    group_rows = 2 * half
    portion = features // groups
    at = jnp.stack([me % 2, me, lax.axis_index("dp"), me // 2]).astype(jnp.int32)
    router_t = router.T
    parts = jnp.concatenate(three_parts(router_t), axis=0)
    matrix = 2 * features * hidden_units
    weight_kinds = [pltpu.VMEM(w.shape, w.dtype) for w in (w_gate, w_up, w_down)]
    small = jax.ShapeDtypeStruct((experts, group_rows), F32)
    in_hbm_spec = pl.BlockSpec(memory_space=pltpu.HBM)

    pieces = [message] + [swap(message, "expert", 2 * m) for m in range(1, chips)]
    weights = call(
        load_kernel,
        weight_kinds,
        [IN_SMEM] + [in_hbm_spec] * 3,
        [IN_VMEM] * 3,
        [pltpu.SemaphoreType.DMA((3,))],
        moved=3 * matrix,
    )(at, *[in_hbm(w) for w in (w_gate, w_up, w_down)])
    by_chip = call(
        order_kernel,
        jax.ShapeDtypeStruct((chips, tok_count, width), BF16),
        [IN_SMEM, [IN_VMEM] * chips],
        IN_VMEM,
    )(at, pieces)
    mine = [by_chip] + [swap(by_chip, "dp", m) for m in range(1, groups)]
    theirs = [swap(x, "expert", 1) for x in mine]
    mine, theirs = [[x.reshape(half, width) for x in xs] for xs in (mine, theirs)]

    rows = jax.ShapeDtypeStruct((half, 2 * features), BF16)
    grad = jax.ShapeDtypeStruct((group_rows, hidden_units), BF16)
    keep, send, *own, pull, tables = call(
        own_kernel,
        [rows] * 2 + [grad] * 3 + [small, jax.ShapeDtypeStruct((3,) + small.shape, F32)],
        [IN_SMEM] + [IN_VMEM] * 6,
        [IN_VMEM] * 7,
        [pltpu.VMEM((group_rows, width), BF16), pltpu.VMEM((group_rows, 2 * features), BF16)],
        8,
        6 * matrix * group_rows,
        6 * matrix,
    )(at, mine[0], theirs[0], parts, *weights)
    rows = jax.ShapeDtypeStruct((tok_count, 2 * features), BF16)
    keep, send = [x.reshape(chips, tok_count, -1) for x in (keep, send)]
    pair, pieces = call(
        pair_kernel,
        [small, [rows] * chips],
        [IN_SMEM] + [IN_VMEM] * 4,
        [IN_VMEM, [IN_VMEM] * chips],
    )(at, keep, swap(send, "expert", 1), pull, swap(pull, "expert", 1))
    pairs = [pair] + [swap(pair, "expert", 2 * m) for m in range(1, chips)]
    back = give_back(pieces)
    logit = call(
        logit_kernel, small, [IN_SMEM, IN_VMEM, [IN_VMEM] * chips], IN_VMEM
    )(at, tables, pairs)
    logits = [logit] + [swap(logit, "dp", m) for m in range(1, groups)]

    count = groups * group_rows
    result = jax.ShapeDtypeStruct((portion, hidden_units), F32)
    grad_gate, grad_up, grad_down, router_grad = call(
        weight_kernel,
        [result] * 3 + [jax.ShapeDtypeStruct((experts, features), F32)],
        [IN_SMEM, [IN_VMEM] * groups, [IN_VMEM] * groups]
        + [IN_VMEM] * 4
        + [[IN_VMEM] * 3, [IN_VMEM] * groups],
        [pl.BlockSpec(memory_space=pl.ANY)] * 3 + [IN_VMEM],
        [
            pltpu.VMEM((count, width), BF16),
            pltpu.VMEM((2, portion, count), BF16),
            [pltpu.VMEM((count, hidden_units), BF16)] * 3,
            [pltpu.VMEM((portion, hidden_units), F32)] * 3,
            pltpu.SemaphoreType.DMA((hidden_units // STEP, 3)),
        ],
        20,
        3 * matrix * count + 6 * portion * hidden_units * count,
        3 * matrix + 12 * portion * hidden_units,
    )(at, mine, theirs, parts, *weights, own, logits)
    rows = jax.ShapeDtypeStruct((tok_count, features), BF16)
    mixed, grad_tokens = call(
        last_kernel,
        [rows] * 2,
        [IN_SMEM] + [IN_VMEM] * 2 + [[IN_VMEM] * chips],
        [IN_VMEM] * 2,
    )(at, logit, router_t, back)
    return (mixed, grad_tokens, router_grad.T, grad_gate, grad_up, grad_down)


def solution(mesh):
    return jax.shard_map(
        local,
        mesh=mesh,
        in_specs=(
            P(("dp", "expert"), None),
            P(("dp", "expert"), None),
            P(),
            P(None, "expert"),
            P(None, "expert"),
            P(None, "expert"),
            P(("dp", "expert"), None),
        ),
        out_specs=(
            P(("dp", "expert"), None),
            P(("dp", "expert"), None),
            P(),
            P("dp", "expert"),
            P("dp", "expert"),
            P("dp", "expert"),
        ),
        check_vma=False,
    )
```

time: 70.6 us -> 68.7 us (0.973)
  local copies, waits for them, and re-layouts: 10.7 us -> 0.77 us
  waiting for transfers between devices: 5.45 us -> 13.9 us
  starting transfers between devices: 21 us -> 24 us
  Pallas kernels: 29.1 us -> 27.1 us
  other arithmetic: 2.8 us -> 1.89 us
    ppermute x16 -> x21, waiting for transfers between devices: 5.45 us -> 13.9 us  [swap(): return lax.ppermute(x, axis, [(i, i ^ mask) for i in range(count)])]
    unnamed x23 -> x3, local copies, waits for them, and re-layouts: 8.22 us -> 0.77 us
    ppermute x16 -> x21, starting transfers between devices: 21 us -> 24 us  [swap(): return lax.ppermute(x, axis, [(i, i ^ mask) for i in range(count)])]
    pallas_call x5 -> x7, Pallas kernels: 29.1 us -> 27.1 us  [the longest x1 9.01 us: kernels_plan(): call(weight_kernel, [result] * 3 + [jax.ShapeDtypeStruct((experts, featur...]
    dynamic_update_slice x11 -> x0, local copies, waits for them, and re-layouts: 1.66 us -> none  [the longest x7 1.52 us: over_chips(): out = lax.dynamic_update_index_in_dim(out, piece, chip ^ m, 0)]
    dynamic_update_slice x1 -> x0, other arithmetic: 0.82 us -> none  [over_chips(): out = lax.dynamic_update_index_in_dim(out, piece, chip ^ m, 0)]
    squeeze x1 -> x0, local copies, waits for them, and re-layouts: 0.71 us -> none  [send_back(): lax.dynamic_index_in_dim(summed, chip ^ m, 0, keepdims=False)]
  transfers between devices with their start and end apart: 16 -> 21, of which waited for: 2 -> 6; matrix products, arithmetic and copies ran while one was open for 6% -> 1% of each run, Pallas kernels for 39% -> 36%
where the time goes in v5:
time: 68.7 us; the launch traced here: 68.4 us
  Pallas kernels  27.1 us (39%)
  starting transfers between devices  24 us (35%)
  waiting for transfers between devices  13.9 us (20%)
  other arithmetic  1.89 us (3%)
  between operations  0.78 us (1%)
  local copies, waits for them, and re-layouts  0.77 us (1%)
    ppermute x21, starting transfers between devices, swap(): return lax.ppermute(x, axis, [(i, i ^ mask) for i in range(count)])  24 us
    ppermute x21, waiting for transfers between devices, swap(): return lax.ppermute(x, axis, [(i, i ^ mask) for i in range(count)])  13.9 us
    pallas_call x1, Pallas kernels, kernels_plan(): call(weight_kernel, [result] * 3 + [jax.ShapeDtypeStruct((experts, featur...  9.01 us
    pallas_call x1, Pallas kernels, kernels_plan(): call(own_kernel, [rows] * 2 + [grad] * 3 + [small, jax.ShapeDtypeStruct((...  8.6 us
    pallas_call x1, Pallas kernels, kernels_plan(): call(load_kernel, weight_kinds, [IN_SMEM] + [in_hbm_spec] * 3, [IN_VMEM]...  6.12 us
    pallas_call x1, Pallas kernels, kernels_plan(): call(last_kernel, [rows] * 2, [IN_SMEM] + [IN_VMEM] * 2 + [[IN_VMEM] * ch...  1.61 us
  transfers between devices with their start and end apart: 21, of which 6 were waited for; matrix products, arithmetic and copies ran while one was open for 1% of the time, Pallas kernels for 36%

profile of v5, /device:TPU:0, one launch (start us, length us, event | category | flops | bytes accessed | tf_op | source)
XLA Modules:
  0.0 68.4 jit_solution(6435188474532755043)
XLA Ops:
  0.6 0.8 %copy.13 = s32[8,6]{0,1:T(8,128)S(1)} copy(s32[8,6]{1,0:T(8,128)} %param.8) | data formatting | bytes 384 | tf_op args[1]
  1.4 0.1 fusion.2
  1.5 0.8 %pad_maximum_fusion.1.piece_refs_0_ = bf16[8,5248]{1,0:T(8,128)(2,1)S(1)} fusion(bf16[8,128]{1,0:T(8,128)(2,1)S(1)} %convert_element_type.12, bf16[8,2560]{1,0:T(8,128)(2,1)} %param.13, bf16[8,2560]{1,0:T(8,128)(2,1)} %param.7), kind=kLoop, calls=%fused_computation.5 | loop fusion | flops 251904 | bytes 167936 | tf_op jit(solution)/shard_map/concatenate | solution.py:268
  2.3 3.0 %collective-permute-start = (bf16[8,5248]{1,0:T(8,128)(2,1)S(1)}, bf16[8,5248]{1,0:T(8,128)(2,1)S(1)}, u32[]{:S(2)}, u32[]{:S(2)}) collective-permute-start(bf16[8,5248]{1,0:T(8,128)(2,1)S(1)} %pad_maximum_fusion.1.piece_refs_0_), channel_id=1, source_target_pairs={{0,2},{1,3},{2,0},{3,1},{4,6},{5,7},{6,4},{7,5},{8,10},{9,11},{10,... | collective-permute-start | bytes 251912 | tf_op jit(solution)/shard_map/ppermute | solution.py:26
  5.3 2.6 %collective-permute-start.1 = (bf16[8,5248]{1,0:T(8,128)(2,1)S(1)}, bf16[8,5248]{1,0:T(8,128)(2,1)S(1)}, u32[]{:S(2)}, u32[]{:S(2)}) collective-permute-start(bf16[8,5248]{1,0:T(8,128)(2,1)S(1)} %pad_maximum_fusion.1.piece_refs_0_), channel_id=1, source_target_pairs={{0,4},{1,5},{2,6},{3,7},{4,0},{5,1},{6,2},{7,3},{8,12},{9,13},{10,... | collective-permute-start | bytes 251912 | tf_op jit(solution)/shard_map/ppermute | solution.py:26
  7.9 0.0 collective-permute-start.2
  7.9 0.9 %reduce-precision_convert_fusion.1 = (bf16[8,2560]{1,0:T(8,128)(2,1)S(1)}, bf16[8,2560]{1,0:T(8,128)(2,1)S(1)}, bf16[8,2560]{1,0:T(8,128)(2,1)S(1)}) fusion(f32[2560,8]{0,1:T(8,128)} %param.9), kind=kLoop, calls=%fused_computation.4 | loop fusion | flops 163840 | bytes 204800 | tf_op jit(solution)/shard_map/convert_element_type | solution.py:37
  8.8 0.1 pad_add_fusion.at_ref._
  8.9 0.0 collective-permute-done.piece_refs_1_
  8.9 5.7 %collective-permute-done.1.piece_refs_2_ = bf16[8,5248]{1,0:T(8,128)(2,1)S(1)} collective-permute-done((bf16[8,5248]{1,0:T(8,128)(2,1)S(1)}, bf16[8,5248]{1,0:T(8,128)(2,1)S(1)}, u32[]{:S(2)}, u32[]{:S(2)}) %collective-permute-start.1) | collective-permute-done | bytes 84000 | tf_op jit(solution)/shard_map/ppermute | solution.py:26
  14.7 0.0 collective-permute-done.2.piece_refs_3_
  14.7 0.6 shard_map.118
  15.2 0.1 collective-permute-start.3
  15.3 1.6 %collective-permute-start.12 = (bf16[4,8,5248]{2,1,0:T(8,128)(2,1)S(1)}, bf16[4,8,5248]{2,1,0:T(8,128)(2,1)S(1)}, u32[]{:S(2)}, u32[]{:S(2)}) collective-permute-start(bf16[4,8,5248]{2,1,0:T(8,128)(2,1)S(1)} %shard_map.118), channel_id=1, source_target_pairs={{0,8},{8,0},{16,24},{24,16},{1,9},{9,1},{17,25},{25,17},{2,10},{10... | collective-permute-start | bytes 1007624 | tf_op jit(solution)/shard_map/ppermute | solution.py:26
  16.9 1.5 %collective-permute-start.13 = (bf16[4,8,5248]{2,1,0:T(8,128)(2,1)S(1)}, bf16[4,8,5248]{2,1,0:T(8,128)(2,1)S(1)}, u32[]{:S(2)}, u32[]{:S(2)}) collective-permute-start(bf16[4,8,5248]{2,1,0:T(8,128)(2,1)S(1)} %shard_map.118), channel_id=1, source_target_pairs={{0,16},{8,24},{16,0},{24,8},{1,17},{9,25},{17,1},{25,9},{2,18},{10... | collective-permute-start | bytes 1007624 | tf_op jit(solution)/shard_map/ppermute | solution.py:26
  18.4 0.5 collective-permute-start.14
  18.9 6.1 %shard_map.119 = (bf16[2560,1024]{1,0:T(8,128)(2,1)S(1)}, bf16[2560,1024]{1,0:T(8,128)(2,1)S(1)}, bf16[2560,1024]{1,0:T(8,128)(2,1)S(1)}) custom-call(s32[4]{0:T(128)S(1)} %pad_add_fusion.at_ref._, bf16[2560,1024]{1,0:T(8,128)(2,1)} %refs_0_.1, bf16[2560,1024]{1,0:T(8,128)(2,1)} %refs_1_.1, bf16[2560,1024]{1,0:T(8,128)(2,1)} %refs_2_.1), custom_call_target="tpu_custom_call" | custom-call | bytes 15728640 | tf_op jit(solution)/shard_map/pallas_call | solution.py:354
  25.0 0.0 collective-permute-done.3
  25.0 8.6 %shard_map.120 = (bf16[32,5120]{1,0:T(8,128)(2,1)S(1)}, bf16[32,5120]{1,0:T(8,128)(2,1)S(1)}, bf16[64,1024]{1,0:T(8,128)(2,1)S(1)}, bf16[64,1024]{1,0:T(8,128)(2...) custom-call(s32[4]{0:T(128)S(1)} %pad_add_fusion.at_ref._, ...), custom_call_target="tpu_custom_call" | custom-call | flops 2013265920 | bytes 31457280 | tf_op jit(solution)/shard_map/pallas_call | solution.py:374
  33.6 0.1 collective-permute-start.4
  33.7 0.0 collective-permute-done.12
  33.7 0.5 collective-permute-start.15
  34.2 0.0 collective-permute-done.13
  34.2 0.1 collective-permute-start.16
  34.3 0.0 collective-permute-done.14
  34.3 0.4 collective-permute-start.17
  34.7 0.1 collective-permute-start.5
  34.8 2.0 %collective-permute-done.5.other_pull_ref = f32[8,64]{1,0:T(8,128)S(1)} collective-permute-done((f32[8,64]{1,0:T(8,128)S(1)}, f32[8,64]{1,0:T(8,128)S(1)}, u32[]{:S(2)}, u32[]{:S(2)}) %collective-permute-start.5) | collective-permute-done | bytes 2080 | tf_op jit(solution)/shard_map/ppermute | solution.py:26
  36.8 0.0 collective-permute-done.4.other_ref
  36.8 0.6 shard_map.121
  37.4 1.5 %collective-permute-start.6 = (f32[8,64]{1,0:T(8,128)S(1)}, f32[8,64]{1,0:T(8,128)S(1)}, u32[]{:S(2)}, u32[]{:S(2)}) collective-permute-start(f32[8,64]{1,0:T(8,128)S(1)} %get-tuple-element.34.pair_refs_0_), channel_id=1, source_target_pairs={{0,2},{1,3},{2,0},{3,1},{4,6},{5,7},{6,4},{7,5},{8,10},{9,11},{10,... | collective-permute-start | bytes 6152 | tf_op jit(solution)/shard_map/ppermute | solution.py:26
  38.9 1.6 %collective-permute-start.7 = (f32[8,64]{1,0:T(8,128)S(1)}, f32[8,64]{1,0:T(8,128)S(1)}, u32[]{:S(2)}, u32[]{:S(2)}) collective-permute-start(f32[8,64]{1,0:T(8,128)S(1)} %get-tuple-element.34.pair_refs_0_), channel_id=1, source_target_pairs={{0,4},{1,5},{2,6},{3,7},{4,0},{5,1},{6,2},{7,3},{8,12},{9,13},{10,... | collective-permute-start | bytes 6152 | tf_op jit(solution)/shard_map/ppermute | solution.py:26
  40.5 0.6 collective-permute-done.6.pair_refs_1_
  41.1 2.5 %collective-permute-start.8 = (f32[8,64]{1,0:T(8,128)S(1)}, f32[8,64]{1,0:T(8,128)S(1)}, u32[]{:S(2)}, u32[]{:S(2)}) collective-permute-start(f32[8,64]{1,0:T(8,128)S(1)} %get-tuple-element.34.pair_refs_0_), channel_id=1, source_target_pairs={{0,6},{1,7},{2,4},{3,5},{4,2},{5,3},{6,0},{7,1},{8,14},{9,15},{10,... | collective-permute-start | bytes 6152 | tf_op jit(solution)/shard_map/ppermute | solution.py:26
  43.6 0.0 collective-permute-done.7.pair_refs_2_
  43.6 2.9 %collective-permute-done.8.pair_refs_3_ = f32[8,64]{1,0:T(8,128)S(1)} collective-permute-done((f32[8,64]{1,0:T(8,128)S(1)}, f32[8,64]{1,0:T(8,128)S(1)}, u32[]{:S(2)}, u32[]{:S(2)}) %collective-permute-start.8) | collective-permute-done | bytes 2080 | tf_op jit(solution)/shard_map/ppermute | solution.py:26
  46.5 0.6 shard_map.122.logit_ref.logit_refs_0_
  47.1 1.6 %collective-permute-start.18 = (f32[8,64]{1,0:T(8,128)S(1)}, f32[8,64]{1,0:T(8,128)S(1)}, u32[]{:S(2)}, u32[]{:S(2)}) collective-permute-start(f32[8,64]{1,0:T(8,128)S(1)} %shard_map.122.logit_ref.logit_refs_0_), channel_id=1, source_target_pairs={{0,8},{8,0},{16,24},{24,16},{1,9},{9,1},{17,25},{25,17},{2,10},{10... | collective-permute-start | bytes 6152 | tf_op jit(solution)/shard_map/ppermute | solution.py:26
  48.6 1.5 %collective-permute-start.19 = (f32[8,64]{1,0:T(8,128)S(1)}, f32[8,64]{1,0:T(8,128)S(1)}, u32[]{:S(2)}, u32[]{:S(2)}) collective-permute-start(f32[8,64]{1,0:T(8,128)S(1)} %shard_map.122.logit_ref.logit_refs_0_), channel_id=1, source_target_pairs={{0,16},{8,24},{16,0},{24,8},{1,17},{9,25},{17,1},{25,9},{2,18},{10... | collective-permute-start | bytes 6152 | tf_op jit(solution)/shard_map/ppermute | solution.py:26
  50.1 0.6 collective-permute-done.18.logit_refs_1_
  50.7 2.5 %collective-permute-start.20 = (f32[8,64]{1,0:T(8,128)S(1)}, f32[8,64]{1,0:T(8,128)S(1)}, u32[]{:S(2)}, u32[]{:S(2)}) collective-permute-start(f32[8,64]{1,0:T(8,128)S(1)} %shard_map.122.logit_ref.logit_refs_0_), channel_id=1, source_target_pairs={{0,24},{8,16},{16,8},{24,0},{1,25},{9,17},{17,9},{25,1},{2,26},{10... | collective-permute-start | bytes 6152 | tf_op jit(solution)/shard_map/ppermute | solution.py:26
  53.2 0.0 collective-permute-done.19.logit_refs_2_
  53.2 0.0 collective-permute-start.9
  53.2 2.0 %collective-permute-done.20.logit_refs_3_ = f32[8,64]{1,0:T(8,128)S(1)} collective-permute-done((f32[8,64]{1,0:T(8,128)S(1)}, f32[8,64]{1,0:T(8,128)S(1)}, u32[]{:S(2)}, u32[]{:S(2)}) %collective-permute-start.20) | collective-permute-done | bytes 2080 | tf_op jit(solution)/shard_map/ppermute | solution.py:26
  55.2 1.0 %collective-permute-start.10 = (bf16[8,5120]{1,0:T(8,128)(2,1)S(1)}, bf16[8,5120]{1,0:T(8,128)(2,1)S(1)}, u32[]{:S(2)}, u32[]{:S(2)}) collective-permute-start(bf16[8,5120]{1,0:T(8,128)(2,1)S(1)} %get-tuple-element.37), channel_id=1, source_target_pairs={{0,4},{1,5},{2,6},{3,7},{4,0},{5,1},{6,2},{7,3},{8,12},{9,13},{10,... | collective-permute-start | bytes 245768 | tf_op jit(solution)/shard_map/ppermute | solution.py:26
  56.2 0.0 collective-permute-done.15
  56.2 1.5 %collective-permute-start.11 = (bf16[8,5120]{1,0:T(8,128)(2,1)S(1)}, bf16[8,5120]{1,0:T(8,128)(2,1)S(1)}, u32[]{:S(2)}, u32[]{:S(2)}) collective-permute-start(bf16[8,5120]{1,0:T(8,128)(2,1)S(1)} %get-tuple-element.38), channel_id=1, source_target_pairs={{0,6},{1,7},{2,4},{3,5},{4,2},{5,3},{6,0},{7,1},{8,14},{9,15},{10,... | collective-permute-start | bytes 245768 | tf_op jit(solution)/shard_map/ppermute | solution.py:26
  57.7 0.0 collective-permute-done.16
  57.7 0.0 collective-permute-done.17
  57.7 0.0 copy-start
  57.7 9.0 %shard_map.124 = (f32[640,1024]{1,0:T(8,128)}, f32[640,1024]{1,0:T(8,128)}, f32[640,1024]{1,0:T(8,128)}, f32[8,2560]{1,0:T(8,128)}) custom-call(s32[4]{0:T(128)S(1)} %pad_add_fusion.at_ref._, bf16[32,5248]{1,0:T(8,128)(2,1)S(1)} %bitcast.20, bf16[32,5248]{1,0:T(8,128)(2,1)S(1)} %bitcast.23, bf16[32,5248]{1,0:T(8,128)(2,1)S(1)} %bitcast.24, ...), custom_call_target="tpu_custom_call" | custom-call | flops 5033164800 | bytes 23592960 | tf_op jit(solution)/shard_map/pallas_call | solution.py:401
  66.8 0.0 collective-permute-done.9.back_refs_1_
  66.8 0.0 collective-permute-done.10.back_refs_2_
  66.8 0.0 collective-permute-done.11.back_refs_3_
  66.8 0.0 copy-done
  66.8 1.6 %shard_map.123 = (bf16[8,2560]{1,0:T(8,128)(2,1)}, bf16[8,2560]{1,0:T(8,128)(2,1)}) custom-call(s32[4]{0:T(128)S(1)} %pad_add_fusion.at_ref._, f32[8,64]{1,0:T(8,128)S(1)} %shard_map.122.logit_ref.logit_refs_0_, f32[8,2560]{1,0:T(8,128)S(1)} %bitcast.29, bf16[8,5120]{1,0:T(8,128)(2,1)S(1)} %get-tuple-element.35.back_refs_0_, ...), custom_call_target="tpu_custom_call" | custom-call | bytes 131072 | tf_op jit(solution)/shard_map/pallas_call | solution.py:420
  (2 shorter events, 0.0 us)
Async XLA Ops:
  2.3 6.6 %collective-permute-start = (bf16[8,5248]{1,0:T(8,128)(2,1)S(1)}, bf16[8,5248]{1,0:T(8,128)(2,1)S(1)}, u32[]{:S(2)}, u32[]{:S(2)}) collective-permute-start(bf16[8,5248]{1,0:T(8,128)(2,1)S(1)} %pad_maximum_fusion.1.piece_refs_0_), channel_id=1, source_target_pairs={{0,2},{1,3},{2,0},{3,1},{4,6},{5,7},{6,4},{7,5},{8,10},{9,11},{10,... | collective-permute-start | bytes 251912 | tf_op jit(solution)/shard_map/ppermute | solution.py:26
  5.3 9.3 %collective-permute-start.1 = (bf16[8,5248]{1,0:T(8,128)(2,1)S(1)}, bf16[8,5248]{1,0:T(8,128)(2,1)S(1)}, u32[]{:S(2)}, u32[]{:S(2)}) collective-permute-start(bf16[8,5248]{1,0:T(8,128)(2,1)S(1)} %pad_maximum_fusion.1.piece_refs_0_), channel_id=1, source_target_pairs={{0,4},{1,5},{2,6},{3,7},{4,0},{5,1},{6,2},{7,3},{8,12},{9,13},{10,... | collective-permute-start | bytes 251912 | tf_op jit(solution)/shard_map/ppermute | solution.py:26
  7.9 6.8 %collective-permute-start.2 = (bf16[8,5248]{1,0:T(8,128)(2,1)S(1)}, bf16[8,5248]{1,0:T(8,128)(2,1)S(1)}, u32[]{:S(2)}, u32[]{:S(2)}) collective-permute-start(bf16[8,5248]{1,0:T(8,128)(2,1)S(1)} %pad_maximum_fusion.1.piece_refs_0_), channel_id=1, source_target_pairs={{0,6},{1,7},{2,4},{3,5},{4,2},{5,3},{6,0},{7,1},{8,14},{9,15},{10,... | collective-permute-start | bytes 251912 | tf_op jit(solution)/shard_map/ppermute | solution.py:26
  15.2 9.8 %collective-permute-start.3 = (bf16[4,8,5248]{2,1,0:T(8,128)(2,1)S(1)}, bf16[4,8,5248]{2,1,0:T(8,128)(2,1)S(1)}, u32[]{:S(2)}, u32[]{:S(2)}) collective-permute-start(bf16[4,8,5248]{2,1,0:T(8,128)(2,1)S(1)} %shard_map.118), channel_id=1, source_target_pairs={{0,1},{1,0},{2,3},{3,2},{4,5},{5,4},{6,7},{7,6},{8,9},{9,8},{10,11... | collective-permute-start | bytes 1007624 | tf_op jit(solution)/shard_map/ppermute | solution.py:26
  15.3 18.4 %collective-permute-start.12 = (bf16[4,8,5248]{2,1,0:T(8,128)(2,1)S(1)}, bf16[4,8,5248]{2,1,0:T(8,128)(2,1)S(1)}, u32[]{:S(2)}, u32[]{:S(2)}) collective-permute-start(bf16[4,8,5248]{2,1,0:T(8,128)(2,1)S(1)} %shard_map.118), channel_id=1, source_target_pairs={{0,8},{8,0},{16,24},{24,16},{1,9},{9,1},{17,25},{25,17},{2,10},{10... | collective-permute-start | bytes 1007624 | tf_op jit(solution)/shard_map/ppermute | solution.py:26
  16.9 17.3 %collective-permute-start.13 = (bf16[4,8,5248]{2,1,0:T(8,128)(2,1)S(1)}, bf16[4,8,5248]{2,1,0:T(8,128)(2,1)S(1)}, u32[]{:S(2)}, u32[]{:S(2)}) collective-permute-start(bf16[4,8,5248]{2,1,0:T(8,128)(2,1)S(1)} %shard_map.118), channel_id=1, source_target_pairs={{0,16},{8,24},{16,0},{24,8},{1,17},{9,25},{17,1},{25,9},{2,18},{10... | collective-permute-start | bytes 1007624 | tf_op jit(solution)/shard_map/ppermute | solution.py:26
  18.4 15.9 %collective-permute-start.14 = (bf16[4,8,5248]{2,1,0:T(8,128)(2,1)S(1)}, bf16[4,8,5248]{2,1,0:T(8,128)(2,1)S(1)}, u32[]{:S(2)}, u32[]{:S(2)}) collective-permute-start(bf16[4,8,5248]{2,1,0:T(8,128)(2,1)S(1)} %shard_map.118), channel_id=1, source_target_pairs={{0,24},{8,16},{16,8},{24,0},{1,25},{9,17},{17,9},{25,1},{2,26},{10... | collective-permute-start | bytes 1007624 | tf_op jit(solution)/shard_map/ppermute | solution.py:26
  33.6 3.1 %collective-permute-start.4 = (bf16[4,8,5120]{2,1,0:T(8,128)(2,1)S(1)}, bf16[4,8,5120]{2,1,0:T(8,128)(2,1)S(1)}, u32[]{:S(2)}, u32[]{:S(2)}) collective-permute-start(bf16[4,8,5120]{2,1,0:T(8,128)(2,1)S(1)} %bitcast.31), channel_id=1, source_target_pairs={{0,1},{1,0},{2,3},{3,2},{4,5},{5,4},{6,7},{7,6},{8,9},{9,8},{10,11... | collective-permute-start | bytes 983048 | tf_op jit(solution)/shard_map/ppermute | solution.py:26
  33.7 22.5 %collective-permute-start.15 = (bf16[4,8,5248]{2,1,0:T(8,128)(2,1)S(1)}, bf16[4,8,5248]{2,1,0:T(8,128)(2,1)S(1)}, u32[]{:S(2)}, u32[]{:S(2)}) collective-permute-start(bf16[4,8,5248]{2,1,0:T(8,128)(2,1)S(1)} %collective-permute-done.12), channel_id=1, source_target_pairs={{0,1},{1,0},{2,3},{3,2},{4,5},{5,4},{6,7},{7,6},{8,9},{9,8},{10,11... | collective-permute-start | bytes 1007624 | tf_op jit(solution)/shard_map/ppermute | solution.py:26
  34.2 23.5 %collective-permute-start.16 = (bf16[4,8,5248]{2,1,0:T(8,128)(2,1)S(1)}, bf16[4,8,5248]{2,1,0:T(8,128)(2,1)S(1)}, u32[]{:S(2)}, u32[]{:S(2)}) collective-permute-start(bf16[4,8,5248]{2,1,0:T(8,128)(2,1)S(1)} %collective-permute-done.13), channel_id=1, source_target_pairs={{0,1},{1,0},{2,3},{3,2},{4,5},{5,4},{6,7},{7,6},{8,9},{9,8},{10,11... | collective-permute-start | bytes 1007624 | tf_op jit(solution)/shard_map/ppermute | solution.py:26
  34.3 23.4 %collective-permute-start.17 = (bf16[4,8,5248]{2,1,0:T(8,128)(2,1)S(1)}, bf16[4,8,5248]{2,1,0:T(8,128)(2,1)S(1)}, u32[]{:S(2)}, u32[]{:S(2)}) collective-permute-start(bf16[4,8,5248]{2,1,0:T(8,128)(2,1)S(1)} %collective-permute-done.14), channel_id=1, source_target_pairs={{0,1},{1,0},{2,3},{3,2},{4,5},{5,4},{6,7},{7,6},{8,9},{9,8},{10,11... | collective-permute-start | bytes 1007624 | tf_op jit(solution)/shard_map/ppermute | solution.py:26
  34.7 2.0 %collective-permute-start.5 = (f32[8,64]{1,0:T(8,128)S(1)}, f32[8,64]{1,0:T(8,128)S(1)}, u32[]{:S(2)}, u32[]{:S(2)}) collective-permute-start(f32[8,64]{1,0:T(8,128)S(1)} %get-tuple-element.33.pull_ref), channel_id=1, source_target_pairs={{0,1},{1,0},{2,3},{3,2},{4,5},{5,4},{6,7},{7,6},{8,9},{9,8},{10,11... | collective-permute-start | bytes 6152 | tf_op jit(solution)/shard_map/ppermute | solution.py:26
  37.4 3.7 %collective-permute-start.6 = (f32[8,64]{1,0:T(8,128)S(1)}, f32[8,64]{1,0:T(8,128)S(1)}, u32[]{:S(2)}, u32[]{:S(2)}) collective-permute-start(f32[8,64]{1,0:T(8,128)S(1)} %get-tuple-element.34.pair_refs_0_), channel_id=1, source_target_pairs={{0,2},{1,3},{2,0},{3,1},{4,6},{5,7},{6,4},{7,5},{8,10},{9,11},{10,... | collective-permute-start | bytes 6152 | tf_op jit(solution)/shard_map/ppermute | solution.py:26
  38.9 4.6 %collective-permute-start.7 = (f32[8,64]{1,0:T(8,128)S(1)}, f32[8,64]{1,0:T(8,128)S(1)}, u32[]{:S(2)}, u32[]{:S(2)}) collective-permute-start(f32[8,64]{1,0:T(8,128)S(1)} %get-tuple-element.34.pair_refs_0_), channel_id=1, source_target_pairs={{0,4},{1,5},{2,6},{3,7},{4,0},{5,1},{6,2},{7,3},{8,12},{9,13},{10,... | collective-permute-start | bytes 6152 | tf_op jit(solution)/shard_map/ppermute | solution.py:26
  41.1 5.4 %collective-permute-start.8 = (f32[8,64]{1,0:T(8,128)S(1)}, f32[8,64]{1,0:T(8,128)S(1)}, u32[]{:S(2)}, u32[]{:S(2)}) collective-permute-start(f32[8,64]{1,0:T(8,128)S(1)} %get-tuple-element.34.pair_refs_0_), channel_id=1, source_target_pairs={{0,6},{1,7},{2,4},{3,5},{4,2},{5,3},{6,0},{7,1},{8,14},{9,15},{10,... | collective-permute-start | bytes 6152 | tf_op jit(solution)/shard_map/ppermute | solution.py:26
  47.1 3.7 %collective-permute-start.18 = (f32[8,64]{1,0:T(8,128)S(1)}, f32[8,64]{1,0:T(8,128)S(1)}, u32[]{:S(2)}, u32[]{:S(2)}) collective-permute-start(f32[8,64]{1,0:T(8,128)S(1)} %shard_map.122.logit_ref.logit_refs_0_), channel_id=1, source_target_pairs={{0,8},{8,0},{16,24},{24,16},{1,9},{9,1},{17,25},{25,17},{2,10},{10... | collective-permute-start | bytes 6152 | tf_op jit(solution)/shard_map/ppermute | solution.py:26
  48.6 4.6 %collective-permute-start.19 = (f32[8,64]{1,0:T(8,128)S(1)}, f32[8,64]{1,0:T(8,128)S(1)}, u32[]{:S(2)}, u32[]{:S(2)}) collective-permute-start(f32[8,64]{1,0:T(8,128)S(1)} %shard_map.122.logit_ref.logit_refs_0_), channel_id=1, source_target_pairs={{0,16},{8,24},{16,0},{24,8},{1,17},{9,25},{17,1},{25,9},{2,18},{10... | collective-permute-start | bytes 6152 | tf_op jit(solution)/shard_map/ppermute | solution.py:26
  50.7 4.5 %collective-permute-start.20 = (f32[8,64]{1,0:T(8,128)S(1)}, f32[8,64]{1,0:T(8,128)S(1)}, u32[]{:S(2)}, u32[]{:S(2)}) collective-permute-start(f32[8,64]{1,0:T(8,128)S(1)} %shard_map.122.logit_ref.logit_refs_0_), channel_id=1, source_target_pairs={{0,24},{8,16},{16,8},{24,0},{1,25},{9,17},{17,9},{25,1},{2,26},{10... | collective-permute-start | bytes 6152 | tf_op jit(solution)/shard_map/ppermute | solution.py:26
  53.2 13.6 %collective-permute-start.9 = (bf16[8,5120]{1,0:T(8,128)(2,1)S(1)}, bf16[8,5120]{1,0:T(8,128)(2,1)S(1)}, u32[]{:S(2)}, u32[]{:S(2)}) collective-permute-start(bf16[8,5120]{1,0:T(8,128)(2,1)S(1)} %get-tuple-element.36), channel_id=1, source_target_pairs={{0,2},{1,3},{2,0},{3,1},{4,6},{5,7},{6,4},{7,5},{8,10},{9,11},{10,... | collective-permute-start | bytes 245768 | tf_op jit(solution)/shard_map/ppermute | solution.py:26
  55.2 11.5 %collective-permute-start.10 = (bf16[8,5120]{1,0:T(8,128)(2,1)S(1)}, bf16[8,5120]{1,0:T(8,128)(2,1)S(1)}, u32[]{:S(2)}, u32[]{:S(2)}) collective-permute-start(bf16[8,5120]{1,0:T(8,128)(2,1)S(1)} %get-tuple-element.37), channel_id=1, source_target_pairs={{0,4},{1,5},{2,6},{3,7},{4,0},{5,1},{6,2},{7,3},{8,12},{9,13},{10,... | collective-permute-start | bytes 245768 | tf_op jit(solution)/shard_map/ppermute | solution.py:26
  56.2 10.5 %collective-permute-start.11 = (bf16[8,5120]{1,0:T(8,128)(2,1)S(1)}, bf16[8,5120]{1,0:T(8,128)(2,1)S(1)}, u32[]{:S(2)}, u32[]{:S(2)}) collective-permute-start(bf16[8,5120]{1,0:T(8,128)(2,1)S(1)} %get-tuple-element.38), channel_id=1, source_target_pairs={{0,6},{1,7},{2,4},{3,5},{4,2},{5,3},{6,0},{7,1},{8,14},{9,15},{10,... | collective-permute-start | bytes 245768 | tf_op jit(solution)/shard_map/ppermute | solution.py:26
  57.7 9.1 %copy-start = (f32[2560,8]{0,1:T(8,128)S(1)}, f32[2560,8]{0,1:T(8,128)}, u32[]{:S(2)}) copy-start(f32[2560,8]{0,1:T(8,128)} %param.9) | copy-start | bytes 245764

commit v6 on v5

--- a/solution.py
+++ b/solution.py
@@ -103,7 +103,24 @@
         copy.wait()
 
 
-def order_kernel(at_ref, piece_refs, out_ref):
+def message_kernel(tokens_hbm, cot_hbm, routes_hbm, out_ref, tokens_ref, cot_ref, routes_ref, sems):
+    count, features = tokens_ref.shape
+    pairs = ((tokens_hbm, tokens_ref), (cot_hbm, cot_ref), (routes_hbm, routes_ref))
+    copies = [pltpu.make_async_copy(*pair, sems.at[i]) for i, pair in enumerate(pairs)]
+    for copy in copies:
+        copy.start()
+    for copy in copies:
+        copy.wait()
+    out_ref[:, :features] = tokens_ref[...]
+    out_ref[:, features : 2 * features] = cot_ref[...]
+    ids = lax.broadcasted_iota(jnp.int32, (count, LANES), 1)
+    picked = jnp.zeros((count, LANES), F32)
+    for k in range(routes_ref.shape[1]):
+        picked += (routes_ref[:, k : k + 1] == ids).astype(F32)
+    out_ref[:, 2 * features :] = picked.astype(BF16)
+
+
+def order_kernel(at_ref, piece_refs, _, out_ref):
     for m, ref in enumerate(piece_refs):
         out_ref[at_ref[3] ^ m] = ref[...]
 
@@ -144,32 +161,51 @@
     send_ref[...] = back_ref[pl.ds(pl.multiple_of((1 - core) * half, half), half), :]
 
 
-def pair_kernel(at_ref, keep_ref, other_ref, pull_ref, other_pull_ref, pair_ref, out_refs):
+def parts_of(x):
+    parts = []
+    for _ in range(3):
+        parts.append(x.astype(BF16).astype(F32))
+        x = x - parts[-1]
+    return parts
+
+
+def pair_kernel(at_ref, keep_ref, other_ref, pull_ref, other_pull_ref, *out_refs):
+    features = keep_ref.shape[2]
+    group_rows = pull_ref.shape[1]
+    row = lax.broadcasted_iota(jnp.int32, pull_ref.shape, 0)
+    pulls = jnp.where(row % 2 == at_ref[0], pull_ref[...], other_pull_ref[...])
+    large, middle, low = parts_of(pulls)
+    pulls = jnp.where(row < 2, large, jnp.where(row < 4, middle, low))
+    tail = jnp.concatenate([pulls, jnp.zeros((row.shape[0], LANES - group_rows), F32)], axis=1)
     for m, ref in enumerate(out_refs):
         chip = at_ref[3] ^ m
-        ref[...] = (keep_ref[chip].astype(F32) + other_ref[chip].astype(F32)).astype(BF16)
-    row = lax.broadcasted_iota(jnp.int32, pull_ref.shape, 0)
-    pair_ref[...] = jnp.where(row % 2 == at_ref[0], pull_ref[...], other_pull_ref[...])
-
-
-def logit_kernel(at_ref, table_ref, pair_refs, out_ref):
+        both = keep_ref[chip].astype(F32) + other_ref[chip].astype(F32)
+        ref[:, :features] = both.astype(BF16)
+        ref[:, features:] = tail.astype(BF16)
+
+
+def logit_kernel(at_ref, table_ref, back_refs, _, out_ref):
     affinity, gates, denominator = table_ref[0], table_ref[1], table_ref[2]
-    chip = lax.broadcasted_iota(jnp.int32, affinity.shape, 0) // 2
+    row = lax.broadcasted_iota(jnp.int32, affinity.shape, 0)
+    width = back_refs[0].shape[1]
     pulls = jnp.zeros(affinity.shape, F32)
-    for m, ref in enumerate(pair_refs):
-        pulls = jnp.where(chip == at_ref[3] ^ m, ref[...], pulls)
+    for m, ref in enumerate(back_refs):
+        tail = ref[:, width - LANES :].astype(F32)[:, : affinity.shape[1]]
+        first = tail[0:1] + (tail[2:3] + tail[4:5])
+        second = tail[1:2] + (tail[3:4] + tail[5:6])
+        pulls = jnp.where(row // 2 == at_ref[3] ^ m, jnp.where(row % 2 == 0, first, second), pulls)
     mean_pull = jnp.sum(gates * pulls, axis=0, keepdims=True)
     out_ref[...] = (pulls - mean_pull) / denominator * affinity * (1.0 - affinity)
 
 
-def weight_kernel(
-    at_ref, mine_refs, theirs_refs, parts_ref, w_gate_ref, w_up_ref, w_down_ref,
-    own_refs, logit_refs, gate_ref, up_ref, down_ref, router_ref,
-    x_ref, turned_ref, grad_refs, out_refs, sems,
+def far_kernel(
+    at_ref, mine_refs, theirs_refs, parts_ref, w_gate_ref, w_up_ref, w_down_ref, own_refs,
+    gate_grad_ref, up_grad_ref, gated_ref, turned_ref, x_ref,
 ):
     features, hidden_units = w_gate_ref.shape
     experts = parts_ref.shape[0] // 3
-    portion = gate_ref.shape[0]
+    grad_refs = (gate_grad_ref, up_grad_ref, gated_ref)
+    portion = turned_ref.shape[1]
     group_rows = own_refs[0].shape[0]
     for m, (mine_ref, theirs_ref) in enumerate(zip(mine_refs, theirs_refs)):
         place_rows(x_ref, m * group_rows, at_ref[0], mine_ref, theirs_ref)
@@ -180,41 +216,40 @@
             turned_ref[half, row : row + LANES, :] = x_ref[:, at].T
     far = x_ref.at[group_rows:, :]
     slot_gate = slot_gates(gate_tables(far, parts_ref, experts)[2], at_ref[1])
-    copies = []
-    for step, start in enumerate(range(0, hidden_units, STEP)):
+    for start in range(0, hidden_units, STEP):
         at = pl.ds(start, STEP)
         grads, _ = hidden_step(at, far, slot_gate, w_gate_ref, w_up_ref, w_down_ref)
-        targets = (gate_ref, up_ref, down_ref)
-        for j, (own_ref, grad) in enumerate(zip(own_refs, grads)):
-            grad_refs[j][:group_rows, at] = own_ref[:, at]
-            grad_refs[j][group_rows:, at] = grad
-            out_refs[j][:, at] = dot(turned_ref[j // 2], grad_refs[j][:, at])
+        for grad_ref, own_ref, grad in zip(grad_refs, own_refs, grads):
+            grad_ref[:group_rows, at] = own_ref[:, at]
+            grad_ref[group_rows:, at] = grad
+
+
+def weight_kernel(turned_ref, grad_refs, _, gate_ref, up_ref, down_ref, out_refs, sems):
+    target_refs = (gate_ref, up_ref, down_ref)
+    copies = []
+    for step, start in enumerate(range(0, grad_refs[0].shape[1], STEP)):
+        at = pl.ds(start, STEP)
+        for j, (grad_ref, out_ref, target_ref) in enumerate(
+            zip(grad_refs, out_refs, target_refs)
+        ):
+            out_ref[:, at] = dot(turned_ref[j // 2], grad_ref[:, at])
             copy = pltpu.make_async_copy(
-                out_refs[j].at[:, at], targets[j].at[:, at], sems.at[step, j]
+                out_ref.at[:, at], target_ref.at[:, at], sems.at[step, j]
             )
             copy.start()
             copies.append(copy)
-    totals = []
-    for m, ref in enumerate(logit_refs):
-        rest, parts = ref[...], []
-        for _ in range(3):
-            parts.append(rest.astype(BF16).astype(F32))
-            rest = rest - parts[-1]
-        stacked = jnp.concatenate(parts, axis=0).astype(BF16)
-        total = dot(stacked, x_ref[m * group_rows : (m + 1) * group_rows, :features])
-        totals.append(total[2 * experts :] + total[experts : 2 * experts] + total[:experts])
-    while len(totals) > 1:
-        totals = [totals[i] + totals[i + 1] for i in range(0, len(totals), 2)]
-    router_ref[...] = totals[0]
     for copy in copies:
         copy.wait()
 
 
-def last_kernel(at_ref, logit_ref, router_ref, back_refs, mixed_ref, tokens_ref):
-    features = router_ref.shape[1]
+def last_kernel(
+    at_ref, mine_refs, theirs_refs, logit_refs, router_ref, back_refs,
+    mixed_ref, tokens_ref, router_grad_ref, x_ref,
+):
+    experts, features = router_ref.shape
     count = mixed_ref.shape[0]
     chips = len(back_refs)
-    grads = logit_ref[...]
+    grads = logit_refs[0][...]
     shape = (count, grads.shape[1])
     row = lax.broadcasted_iota(jnp.int32, shape, 0) + (at_ref[0] * chips + at_ref[3]) * count
     own = (lax.broadcasted_iota(jnp.int32, shape, 1) == row).astype(F32)
@@ -222,7 +257,24 @@
     back = jnp.dot(own_grads, router_ref[...], precision=HIGHEST, preferred_element_type=F32)
     summed = sum(ref[...].astype(F32) for ref in back_refs)
     mixed_ref[...] = summed[:, :features].astype(BF16)
-    tokens_ref[...] = (summed[:, features:] + back).astype(BF16)
+    tokens_ref[...] = (summed[:, features : 2 * features] + back).astype(BF16)
+    totals = []
+    group_rows = grads.shape[1]
+    for m, (mine_ref, theirs_ref) in enumerate(zip(mine_refs, theirs_refs)):
+        place_rows(
+            x_ref,
+            m * group_rows,
+            at_ref[0],
+            mine_ref.at[:, :features],
+            theirs_ref.at[:, :features],
+        )
+    for m, logit_ref in enumerate(logit_refs):
+        stacked = jnp.concatenate(parts_of(logit_ref[...]), axis=0).astype(BF16)
+        total = dot(stacked, x_ref[m * group_rows : (m + 1) * group_rows, :])
+        totals.append(total[2 * experts :] + total[experts : 2 * experts] + total[:experts])
+    while len(totals) > 1:
+        totals = [totals[i] + totals[i + 1] for i in range(0, len(totals), 2)]
+    router_grad_ref[...] = totals[0]
 
 
 def call(kernel, out_shape, in_specs, out_specs, scratch=(), limit=4, flops=0, moved=1 << 17):
@@ -250,7 +302,7 @@
     group = lax.axis_index("dp")
     core, chip = me % 2, me // 2
     own_expert = me // sharing
-    whole = sharing == 1 and groups * group_rows * features * 4 <= GATHER_BYTES
+    whole = sharing == 1 and group_rows <= LANES and groups * group_rows * features * 4 <= GATHER_BYTES
 
     def over_chips(x):
         out = jnp.zeros((chips,) + x.shape, x.dtype)
@@ -263,13 +315,13 @@
         other = swap(x, "expert", 1)
         return jnp.where(core == 0, jnp.stack([x, other]), jnp.stack([other, x]))
 
+    if whole:
+        return kernels_plan(tokens, routes, router, w_gate, w_up, w_down, cotangent)
+
     ids = jnp.arange(LANES, dtype=jnp.int32)
     picked_wide = jnp.any(routes[:, :, None] == ids[None, None, :], axis=1).astype(BF16)
     message = jnp.concatenate([tokens, cotangent, picked_wide], axis=1)
     width = message.shape[1]
-    if whole:
-        return kernels_plan(message, router, w_gate, w_up, w_down)
-
     by_chip = over_chips(message)
     own = over_cores(by_chip).reshape(group_rows, width)
     rows, cot = own[:, :features], own[:, features : 2 * features]
@@ -332,10 +384,11 @@
     ]
 
 
-def kernels_plan(message, router, w_gate, w_up, w_down):
+def kernels_plan(tokens, routes, router, w_gate, w_up, w_down, cotangent):
     features, experts = router.shape
     hidden_units = w_gate.shape[1]
-    tok_count, width = message.shape
+    tok_count = tokens.shape[0]
+    width = 2 * features + LANES
     groups = lax.axis_size("dp")
     chips = lax.axis_size("expert") // 2
     me = lax.axis_index("expert")
@@ -350,6 +403,14 @@
     small = jax.ShapeDtypeStruct((experts, group_rows), F32)
     in_hbm_spec = pl.BlockSpec(memory_space=pltpu.HBM)
 
+    sources = (tokens, cotangent, routes)
+    message = call(
+        message_kernel,
+        jax.ShapeDtypeStruct((tok_count, width), BF16),
+        [in_hbm_spec] * 3,
+        IN_VMEM,
+        [pltpu.VMEM(x.shape, x.dtype) for x in sources] + [pltpu.SemaphoreType.DMA((3,))],
+    )(*[in_hbm(x) for x in sources])
     pieces = [message] + [swap(message, "expert", 2 * m) for m in range(1, chips)]
     weights = call(
         load_kernel,
@@ -362,12 +423,11 @@
     by_chip = call(
         order_kernel,
         jax.ShapeDtypeStruct((chips, tok_count, width), BF16),
-        [IN_SMEM, [IN_VMEM] * chips],
+        [IN_SMEM, [IN_VMEM] * chips, pl.BlockSpec(memory_space=pl.ANY)],
         IN_VMEM,
-    )(at, pieces)
+    )(at, pieces, weights[0])
     mine = [by_chip] + [swap(by_chip, "dp", m) for m in range(1, groups)]
-    theirs = [swap(x, "expert", 1) for x in mine]
-    mine, theirs = [[x.reshape(half, width) for x in xs] for xs in (mine, theirs)]
+    theirs = swap(by_chip, "expert", 1)
 
     rows = jax.ShapeDtypeStruct((half, 2 * features), BF16)
     grad = jax.ShapeDtypeStruct((group_rows, hidden_units), BF16)
@@ -380,49 +440,61 @@
         8,
         6 * matrix * group_rows,
         6 * matrix,
-    )(at, mine[0], theirs[0], parts, *weights)
-    rows = jax.ShapeDtypeStruct((tok_count, 2 * features), BF16)
+    )(at, by_chip.reshape(half, width), theirs.reshape(half, width), parts, *weights)
+    rows = jax.ShapeDtypeStruct((tok_count, width), BF16)
     keep, send = [x.reshape(chips, tok_count, -1) for x in (keep, send)]
-    pair, pieces = call(
+    pieces = call(
         pair_kernel,
-        [small, [rows] * chips],
+        [rows] * chips,
         [IN_SMEM] + [IN_VMEM] * 4,
-        [IN_VMEM, [IN_VMEM] * chips],
+        [IN_VMEM] * chips,
     )(at, keep, swap(send, "expert", 1), pull, swap(pull, "expert", 1))
-    pairs = [pair] + [swap(pair, "expert", 2 * m) for m in range(1, chips)]
     back = give_back(pieces)
+    _, *far = lax.optimization_barrier([pieces[0]] + mine[1:])
+    mine = [by_chip] + far
+    theirs = [theirs] + [swap(x, "expert", 1) for x in far]
+    mine, theirs = [[x.reshape(half, width) for x in xs] for xs in (mine, theirs)]
+
+    count = groups * group_rows
+    *grads, turned = call(
+        far_kernel,
+        [pltpu.VMEM((count, hidden_units), BF16)] * 3 + [pltpu.VMEM((2, portion, count), BF16)],
+        [IN_SMEM, [IN_VMEM] * groups, [IN_VMEM] * groups] + [IN_VMEM] * 4 + [[IN_VMEM] * 3],
+        [IN_VMEM] * 4,
+        [pltpu.VMEM((count, width), BF16)],
+        12,
+    )(at, mine, theirs, parts, *weights, own)
     logit = call(
-        logit_kernel, small, [IN_SMEM, IN_VMEM, [IN_VMEM] * chips], IN_VMEM
-    )(at, tables, pairs)
+        logit_kernel,
+        small,
+        [IN_SMEM, IN_VMEM, [IN_VMEM] * chips, pl.BlockSpec(memory_space=pl.ANY)],
+        IN_VMEM,
+    )(at, tables, back, turned)
     logits = [logit] + [swap(logit, "dp", m) for m in range(1, groups)]
-
-    count = groups * group_rows
     result = jax.ShapeDtypeStruct((portion, hidden_units), F32)
-    grad_gate, grad_up, grad_down, router_grad = call(
+    grad_gate, grad_up, grad_down = call(
         weight_kernel,
-        [result] * 3 + [jax.ShapeDtypeStruct((experts, features), F32)],
-        [IN_SMEM, [IN_VMEM] * groups, [IN_VMEM] * groups]
-        + [IN_VMEM] * 4
-        + [[IN_VMEM] * 3, [IN_VMEM] * groups],
-        [pl.BlockSpec(memory_space=pl.ANY)] * 3 + [IN_VMEM],
+        [result] * 3,
+        [IN_VMEM, [IN_VMEM] * 3, pl.BlockSpec(memory_space=pl.ANY)],
+        [pl.BlockSpec(memory_space=pl.ANY)] * 3,
         [
-            pltpu.VMEM((count, width), BF16),
-            pltpu.VMEM((2, portion, count), BF16),
-            [pltpu.VMEM((count, hidden_units), BF16)] * 3,
             [pltpu.VMEM((portion, hidden_units), F32)] * 3,
             pltpu.SemaphoreType.DMA((hidden_units // STEP, 3)),
         ],
-        20,
-        3 * matrix * count + 6 * portion * hidden_units * count,
-        3 * matrix + 12 * portion * hidden_units,
-    )(at, mine, theirs, parts, *weights, own, logits)
+        12,
+        6 * portion * hidden_units * count,
+        12 * portion * hidden_units,
+    )(turned, grads, logit)
     rows = jax.ShapeDtypeStruct((tok_count, features), BF16)
-    mixed, grad_tokens = call(
+    mixed, grad_tokens, router_grad = call(
         last_kernel,
-        [rows] * 2,
-        [IN_SMEM] + [IN_VMEM] * 2 + [[IN_VMEM] * chips],
-        [IN_VMEM] * 2,
-    )(at, logit, router_t, back)
+        [rows] * 2 + [jax.ShapeDtypeStruct((experts, features), F32)],
+        [IN_SMEM]
+        + [[IN_VMEM] * groups] * 3
+        + [IN_VMEM, [IN_VMEM] * chips],
+        [IN_VMEM] * 3,
+        [pltpu.VMEM((count, features), BF16)],
+    )(at, mine, theirs, logits, router_t, back)
     return (mixed, grad_tokens, router_grad.T, grad_gate, grad_up, grad_down)
 
 

time: 68.7 us -> 55.2 us (0.80)
  waiting for transfers between devices: 13.9 us -> 6.58 us
  starting transfers between devices: 24 us -> 18.7 us
  other arithmetic: 1.89 us -> 1 us
  local copies, waits for them, and re-layouts: 0.77 us -> 0.01 us
  Pallas kernels: 27.1 us -> 27.8 us
    ppermute x21 -> x18, waiting for transfers between devices: 13.9 us -> 6.58 us  [swap(): return lax.ppermute(x, axis, [(i, i ^ mask) for i in range(count)])]
    ppermute x21 -> x18, starting transfers between devices: 24 us -> 18.7 us  [swap(): return lax.ppermute(x, axis, [(i, i ^ mask) for i in range(count)])]
    concatenate x1 -> x0, other arithmetic: 0.81 us -> none  [local(): message = jnp.concatenate([tokens, cotangent, picked_wide], axis=1)]
    unnamed x3 -> x2, local copies, waits for them, and re-layouts: 0.77 us -> 0.01 us
    pallas_call x4 -> x6, Pallas kernels: 11.8 us -> 12.5 us  [the longest x1 4.98 us: kernels_plan(): call(far_kernel, [pltpu.VMEM((count, hidden_units), BF16)] * 3 + [pltpu.V...]
  transfers between devices with their start and end apart: 21 -> 18, of which waited for: 6 -> 4; matrix products, arithmetic and copies ran while one was open for 1% -> 2% of each run, Pallas kernels for 36% -> 44%
where the time goes in v6:
time: 55.2 us; the launch traced here: 54.9 us
  Pallas kernels  27.8 us (50%)
  starting transfers between devices  18.7 us (34%)
  waiting for transfers between devices  6.58 us (12%)
  other arithmetic  1 us (2%)
  between operations  0.82 us (1%)
    ppermute x18, starting transfers between devices, swap(): return lax.ppermute(x, axis, [(i, i ^ mask) for i in range(count)])  18.7 us
    pallas_call x1, Pallas kernels, kernels_plan(): call(own_kernel, [rows] * 2 + [grad] * 3 + [small, jax.ShapeDtypeStruct((...  8.65 us
    ppermute x18, waiting for transfers between devices, swap(): return lax.ppermute(x, axis, [(i, i ^ mask) for i in range(count)])  6.58 us
    pallas_call x1, Pallas kernels, kernels_plan(): call(load_kernel, weight_kinds, [IN_SMEM] + [in_hbm_spec] * 3, [IN_VMEM]...  6.11 us
    pallas_call x1, Pallas kernels, kernels_plan(): call(far_kernel, [pltpu.VMEM((count, hidden_units), BF16)] * 3 + [pltpu.V...  4.98 us
    pallas_call x1, Pallas kernels, kernels_plan(): call(weight_kernel, [result] * 3, [IN_VMEM, [IN_VMEM] * 3, pl.BlockSpec(m...  3.58 us
    pallas_call x1, Pallas kernels, kernels_plan(): call(last_kernel, [rows] * 2 + [jax.ShapeDtypeStruct((experts, features),...  1.81 us
  transfers between devices with their start and end apart: 18, of which 4 were waited for; matrix products, arithmetic and copies ran while one was open for 2% of the time, Pallas kernels for 44%

profile of v6, /device:TPU:0, one launch (start us, length us, event | category | flops | bytes accessed | tf_op | source)
XLA Modules:
  0.0 54.9 jit_solution(16771338482118255548)
XLA Ops:
  0.6 0.9 %shard_map.118.piece_refs_0_ = bf16[8,5248]{1,0:T(8,128)(2,1)S(1)} custom-call(bf16[8,2560]{1,0:T(8,128)(2,1)} %tokens_hbm.1, bf16[8,2560]{1,0:T(8,128)(2,1)} %cot_hbm.1, s32[8,6]{1,0:T(8,128)} %routes_hbm.1), custom_call_target="tpu_custom_call" | custom-call | bytes 131072 | tf_op jit(solution)/shard_map/pallas_call | solution.py:407
  1.5 5.1 %collective-permute-start.2 = (bf16[8,5248]{1,0:T(8,128)(2,1)S(1)}, bf16[8,5248]{1,0:T(8,128)(2,1)S(1)}, u32[]{:S(2)}, u32[]{:S(2)}) collective-permute-start(bf16[8,5248]{1,0:T(8,128)(2,1)S(1)} %shard_map.118.piece_refs_0_), channel_id=1, source_target_pairs={{0,6},{1,7},{2,4},{3,5},{4,2},{5,3},{6,0},{7,1},{8,14},{9,15},{10,... | collective-permute-start | bytes 251912 | tf_op jit(solution)/shard_map/ppermute | solution.py:26
  6.7 0.0 collective-permute-start.1
  6.7 0.6 %collective-permute-start = (bf16[8,5248]{1,0:T(8,128)(2,1)S(1)}, bf16[8,5248]{1,0:T(8,128)(2,1)S(1)}, u32[]{:S(2)}, u32[]{:S(2)}) collective-permute-start(bf16[8,5248]{1,0:T(8,128)(2,1)S(1)} %shard_map.118.piece_refs_0_), channel_id=1, source_target_pairs={{0,2},{1,3},{2,0},{3,1},{4,6},{5,7},{6,4},{7,5},{8,10},{9,11},{10,... | collective-permute-start | bytes 251912 | tf_op jit(solution)/shard_map/ppermute | solution.py:26
  7.3 0.9 %reduce-precision_convert_fusion.1 = (bf16[8,2560]{1,0:T(8,128)(2,1)S(1)}, bf16[8,2560]{1,0:T(8,128)(2,1)S(1)}, bf16[8,2560]{1,0:T(8,128)(2,1)S(1)}) fusion(f32[2560,8]{0,1:T(8,128)} %param.9), kind=kLoop, calls=%fused_computation.4 | loop fusion | flops 163840 | bytes 204800 | tf_op jit(solution)/shard_map/convert_element_type | solution.py:37
  8.2 0.1 pad_add_fusion._.at_ref
  8.3 6.1 %shard_map.119 = (bf16[2560,1024]{1,0:T(8,128)(2,1)S(1)}, bf16[2560,1024]{1,0:T(8,128)(2,1)S(1)}, bf16[2560,1024]{1,0:T(8,128)(2,1)S(1)}) custom-call(s32[4]{0:T(128)S(1)} %pad_add_fusion._.at_ref, bf16[2560,1024]{1,0:T(8,128)(2,1)} %refs_0_.1, bf16[2560,1024]{1,0:T(8,128)(2,1)} %refs_1_.1, bf16[2560,1024]{1,0:T(8,128)(2,1)} %refs_2_.1), custom_call_target="tpu_custom_call" | custom-call | bytes 15728640 | tf_op jit(solution)/shard_map/pallas_call | solution.py:415
  14.4 0.0 collective-permute-done.2.piece_refs_3_
  14.4 0.0 collective-permute-done.1.piece_refs_2_
  14.5 0.0 collective-permute-done.piece_refs_1_
  14.5 0.6 %shard_map.120 = bf16[4,8,5248]{2,1,0:T(8,128)(2,1)S(1)} custom-call(s32[4]{0:T(128)S(1)} %pad_add_fusion._.at_ref, bf16[8,5248]{1,0:T(8,128)(2,1)S(1)} %shard_map.118.piece_refs_0_, bf16[8,5248]{1,0:T(8,128)(2,1)S(1)} %collective-permute-done.piece_refs_1_, bf16[8,5248]{1,0:T(8,128)(2,1)S(1)} %collective-permute-done.1.piece_refs_2_, ...), custom_call_target="tpu_custom_call" | custom-call | bytes 131072 | tf_op jit(solution)/shard_map/pallas_call | solution.py:423
  15.0 0.1 collective-permute-start.3
  15.1 2.7 %collective-permute-start.8 = (bf16[4,8,5248]{2,1,0:T(8,128)(2,1)S(1)}, bf16[4,8,5248]{2,1,0:T(8,128)(2,1)S(1)}, u32[]{:S(2)}, u32[]{:S(2)}) collective-permute-start(bf16[4,8,5248]{2,1,0:T(8,128)(2,1)S(1)} %shard_map.120), channel_id=1, source_target_pairs={{0,24},{8,16},{16,8},{24,0},{1,25},{9,17},{17,9},{25,1},{2,26},{10... | collective-permute-start | bytes 1007624 | tf_op jit(solution)/shard_map/ppermute | solution.py:26
  17.8 0.5 collective-permute-start.7
  18.3 0.4 collective-permute-start.6
  18.7 0.0 collective-permute-done.3
  18.7 8.6 %shard_map.121 = (bf16[32,5120]{1,0:T(8,128)(2,1)S(1)}, bf16[32,5120]{1,0:T(8,128)(2,1)S(1)}, bf16[64,1024]{1,0:T(8,128)(2,1)S(1)}, bf16[64,1024]{1,0:T(8,128)(2...) custom-call(s32[4]{0:T(128)S(1)} %pad_add_fusion._.at_ref, ...), custom_call_target="tpu_custom_call" | custom-call | flops 2013265920 | bytes 31457280 | tf_op jit(solution)/shard_map/pallas_call | solution.py:434
  27.4 0.1 collective-permute-start.4
  27.4 0.5 collective-permute-start.5
  27.9 1.1 %collective-permute-done.5.other_pull_ref = f32[8,64]{1,0:T(8,128)S(1)} collective-permute-done((f32[8,64]{1,0:T(8,128)S(1)}, f32[8,64]{1,0:T(8,128)S(1)}, u32[]{:S(2)}, u32[]{:S(2)}) %collective-permute-start.5) | collective-permute-done | bytes 2080 | tf_op jit(solution)/shard_map/ppermute | solution.py:26
  29.1 0.0 collective-permute-done.4.other_ref
  29.1 0.6 %shard_map.122 = (bf16[8,5248]{1,0:T(8,128)(2,1)S(1)}, bf16[8,5248]{1,0:T(8,128)(2,1)S(1)}, bf16[8,5248]{1,0:T(8,128)(2,1)S(1)}, bf16[8,5248]{1,0:T(8,128)(2,1)S(1)}) custom-call(s32[4]{0:T(128)S(1)} %pad_add_fusion._.at_ref, bf16[4,8,5120]{2,1,0:T(8,128)(2,1)S(1)} %bitcast.37, bf16[4,8,5120]{2,1,0:T(8,128)(2,1)S(1)} %collective-permute-done.4.other_ref, ...), custom_call_target="tpu_custom_call" | custom-call | bytes 131072 | tf_op jit(solution)/shard_map/pallas_call | solution.py:446
  29.7 0.0 collective-permute-done.8
  29.7 3.9 %collective-permute-done.7 = bf16[4,8,5248]{2,1,0:T(8,128)(2,1)S(1)} collective-permute-done((bf16[4,8,5248]{2,1,0:T(8,128)(2,1)S(1)}, bf16[4,8,5248]{2,1,0:T(8,128)(2,1)S(1)}, u32[]{:S(2)}, u32[]{:S(2)}) %collective-permute-start.7) | collective-permute-done | bytes 335904 | tf_op jit(solution)/shard_map/ppermute | solution.py:26
  33.6 0.2 collective-permute-done.6
  33.8 0.0 collective-permute-start.9
  33.8 0.5 collective-permute-start.10
  34.3 0.0 collective-permute-start.11
  34.3 1.2 %collective-permute-start.12 = (bf16[8,5248]{1,0:T(8,128)(2,1)S(1)}, bf16[8,5248]{1,0:T(8,128)(2,1)S(1)}, u32[]{:S(2)}, u32[]{:S(2)}) collective-permute-start(bf16[8,5248]{1,0:T(8,128)(2,1)S(1)} %get-tuple-element.44), channel_id=1, source_target_pairs={{0,2},{1,3},{2,0},{3,1},{4,6},{5,7},{6,4},{7,5},{8,10},{9,11},{10,... | collective-permute-start | bytes 251912 | tf_op jit(solution)/shard_map/ppermute | solution.py:26
  35.6 2.9 %collective-permute-start.13 = (bf16[8,5248]{1,0:T(8,128)(2,1)S(1)}, bf16[8,5248]{1,0:T(8,128)(2,1)S(1)}, u32[]{:S(2)}, u32[]{:S(2)}) collective-permute-start(bf16[8,5248]{1,0:T(8,128)(2,1)S(1)} %get-tuple-element.45), channel_id=1, source_target_pairs={{0,4},{1,5},{2,6},{3,7},{4,0},{5,1},{6,2},{7,3},{8,12},{9,13},{10,... | collective-permute-start | bytes 251912 | tf_op jit(solution)/shard_map/ppermute | solution.py:26
  38.5 0.0 collective-permute-done.9
  38.5 0.6 %collective-permute-start.14 = (bf16[8,5248]{1,0:T(8,128)(2,1)S(1)}, bf16[8,5248]{1,0:T(8,128)(2,1)S(1)}, u32[]{:S(2)}, u32[]{:S(2)}) collective-permute-start(bf16[8,5248]{1,0:T(8,128)(2,1)S(1)} %get-tuple-element.46), channel_id=1, source_target_pairs={{0,6},{1,7},{2,4},{3,5},{4,2},{5,3},{6,0},{7,1},{8,14},{9,15},{10,... | collective-permute-start | bytes 251912 | tf_op jit(solution)/shard_map/ppermute | solution.py:26
  39.1 0.0 collective-permute-done.10
  39.1 0.0 collective-permute-done.11
  39.1 0.0 copy-start
  39.1 5.0 %shard_map.123 = (bf16[256,1024]{1,0:T(8,128)(2,1)S(1)}, bf16[256,1024]{1,0:T(8,128)(2,1)S(1)}, bf16[256,1024]{1,0:T(8,128)(2,1)S(1)}, bf16[2,640,256]{2,1,0:T(8,128)(2,1)S(1)}) custom-call(s32[4]{0:T(128)S(1)} %pad_add_fusion._.at_ref, bf16[32,5248]{1,0:T(8,128)(2,1)S(1)} %bitcast.20, bf16[32,5248]{1,0:T(8,128)(2,1)S(1)} %bitcast.29, ...), custom_call_target="tpu_custom_call" | custom-call | bytes 131072 | tf_op jit(solution)/shard_map/pallas_call | solution.py:459
  44.1 0.0 collective-permute-done.12.back_refs_1_
  44.1 1.3 %collective-permute-done.13.back_refs_2_ = bf16[8,5248]{1,0:T(8,128)(2,1)S(1)} collective-permute-done((bf16[8,5248]{1,0:T(8,128)(2,1)S(1)}, bf16[8,5248]{1,0:T(8,128)(2,1)S(1)}, u32[]{:S(2)}, u32[]{:S(2)}) %collective-permute-start.13) | collective-permute-done | bytes 84000 | tf_op jit(solution)/shard_map/ppermute | solution.py:26
  45.4 0.0 collective-permute-done.14.back_refs_3_
  45.4 0.6 %shard_map.124.logit_refs_0_._ = f32[8,64]{1,0:T(8,128)S(1)} custom-call(s32[4]{0:T(128)S(1)} %pad_add_fusion._.at_ref, f32[3,8,64]{2,1,0:T(8,128)S(1)} %get-tuple-element.43.table_ref, bf16[8,5248]{1,0:T(8,128)(2,1)S(1)} %get-tuple-element.39.back_refs_0_, bf16[8,5248]{1,0:T(8,128)(2,1)S(1)} %collective-permute-done.12.back_refs_1_, ...), custom_call_target="tpu_custom_call" | custom-call | bytes 131072 | tf_op jit(solution)/shard_map/pallas_call | solution.py:467
  45.9 1.7 %collective-permute-start.17 = (f32[8,64]{1,0:T(8,128)S(1)}, f32[8,64]{1,0:T(8,128)S(1)}, u32[]{:S(2)}, u32[]{:S(2)}) collective-permute-start(f32[8,64]{1,0:T(8,128)S(1)} %shard_map.124.logit_refs_0_._), channel_id=1, source_target_pairs={{0,24},{8,16},{16,8},{24,0},{1,25},{9,17},{17,9},{25,1},{2,26},{10... | collective-permute-start | bytes 6152 | tf_op jit(solution)/shard_map/ppermute | solution.py:26
  47.7 1.3 %collective-permute-start.16 = (f32[8,64]{1,0:T(8,128)S(1)}, f32[8,64]{1,0:T(8,128)S(1)}, u32[]{:S(2)}, u32[]{:S(2)}) collective-permute-start(f32[8,64]{1,0:T(8,128)S(1)} %shard_map.124.logit_refs_0_._), channel_id=1, source_target_pairs={{0,16},{8,24},{16,0},{24,8},{1,17},{9,25},{17,1},{25,9},{2,18},{10... | collective-permute-start | bytes 6152 | tf_op jit(solution)/shard_map/ppermute | solution.py:26
  49.0 0.5 collective-permute-start.15
  49.5 3.6 %shard_map.126 = (f32[640,1024]{1,0:T(8,128)}, f32[640,1024]{1,0:T(8,128)}, f32[640,1024]{1,0:T(8,128)}) custom-call(bf16[2,640,256]{2,1,0:T(8,128)(2,1)S(1)} %get-tuple-element.50._.turned_ref, bf16[256,1024]{1,0:T(8,128)(2,1)S(1)} %get-tuple-element.54.grad_refs_0_, bf16[256,1024]{1,0:T(8,128)(2,1)S(1)} %get-tuple-element.55.grad_refs_1_, ...), custom_call_target="tpu_custom_call" | custom-call | flops 1006632960 | bytes 7864320 | tf_op jit(solution)/shard_map/pallas_call | solution.py:475
  53.1 0.0 collective-permute-done.17.logit_refs_3_
  53.1 0.0 collective-permute-done.16.logit_refs_2_
  53.1 0.0 collective-permute-done.15.logit_refs_1_
  53.1 0.0 copy-done
  53.1 1.8 %shard_map.125 = (bf16[8,2560]{1,0:T(8,128)(2,1)}, bf16[8,2560]{1,0:T(8,128)(2,1)}, f32[8,2560]{1,0:T(8,128)}) custom-call(s32[4]{0:T(128)S(1)} %pad_add_fusion._.at_ref, bf16[32,5248]{1,0:T(8,128)(2,1)S(1)} %bitcast.21, bf16[32,5248]{1,0:T(8,128)(2,1)S(1)} %bitcast.30, bf16[32,5248]{1,0:T(8,128)(2,1)S(1)} %bitcast.28, bf16[32,5248]{1,0:T(8,128)(2,1)S(1)} %bitcast.26, ...), custom_call_target="tpu_custom_call" | custom-call | bytes 131072 | tf_op jit(solution)/shard_map/pallas_call | solution.py:489
  (1 shorter events, 0.0 us)
Async XLA Ops:
  1.5 12.9 %collective-permute-start.2 = (bf16[8,5248]{1,0:T(8,128)(2,1)S(1)}, bf16[8,5248]{1,0:T(8,128)(2,1)S(1)}, u32[]{:S(2)}, u32[]{:S(2)}) collective-permute-start(bf16[8,5248]{1,0:T(8,128)(2,1)S(1)} %shard_map.118.piece_refs_0_), channel_id=1, source_target_pairs={{0,6},{1,7},{2,4},{3,5},{4,2},{5,3},{6,0},{7,1},{8,14},{9,15},{10,... | collective-permute-start | bytes 251912 | tf_op jit(solution)/shard_map/ppermute | solution.py:26
  6.7 7.8 %collective-permute-start.1 = (bf16[8,5248]{1,0:T(8,128)(2,1)S(1)}, bf16[8,5248]{1,0:T(8,128)(2,1)S(1)}, u32[]{:S(2)}, u32[]{:S(2)}) collective-permute-start(bf16[8,5248]{1,0:T(8,128)(2,1)S(1)} %shard_map.118.piece_refs_0_), channel_id=1, source_target_pairs={{0,4},{1,5},{2,6},{3,7},{4,0},{5,1},{6,2},{7,3},{8,12},{9,13},{10,... | collective-permute-start | bytes 251912 | tf_op jit(solution)/shard_map/ppermute | solution.py:26
  6.7 7.8 %collective-permute-start = (bf16[8,5248]{1,0:T(8,128)(2,1)S(1)}, bf16[8,5248]{1,0:T(8,128)(2,1)S(1)}, u32[]{:S(2)}, u32[]{:S(2)}) collective-permute-start(bf16[8,5248]{1,0:T(8,128)(2,1)S(1)} %shard_map.118.piece_refs_0_), channel_id=1, source_target_pairs={{0,2},{1,3},{2,0},{3,1},{4,6},{5,7},{6,4},{7,5},{8,10},{9,11},{10,... | collective-permute-start | bytes 251912 | tf_op jit(solution)/shard_map/ppermute | solution.py:26
  15.0 3.7 %collective-permute-start.3 = (bf16[4,8,5248]{2,1,0:T(8,128)(2,1)S(1)}, bf16[4,8,5248]{2,1,0:T(8,128)(2,1)S(1)}, u32[]{:S(2)}, u32[]{:S(2)}) collective-permute-start(bf16[4,8,5248]{2,1,0:T(8,128)(2,1)S(1)} %shard_map.120), channel_id=1, source_target_pairs={{0,1},{1,0},{2,3},{3,2},{4,5},{5,4},{6,7},{7,6},{8,9},{9,8},{10,11... | collective-permute-start | bytes 1007624 | tf_op jit(solution)/shard_map/ppermute | solution.py:26
  15.1 14.6 %collective-permute-start.8 = (bf16[4,8,5248]{2,1,0:T(8,128)(2,1)S(1)}, bf16[4,8,5248]{2,1,0:T(8,128)(2,1)S(1)}, u32[]{:S(2)}, u32[]{:S(2)}) collective-permute-start(bf16[4,8,5248]{2,1,0:T(8,128)(2,1)S(1)} %shard_map.120), channel_id=1, source_target_pairs={{0,24},{8,16},{16,8},{24,0},{1,25},{9,17},{17,9},{25,1},{2,26},{10... | collective-permute-start | bytes 1007624 | tf_op jit(solution)/shard_map/ppermute | solution.py:26
  17.8 15.8 %collective-permute-start.7 = (bf16[4,8,5248]{2,1,0:T(8,128)(2,1)S(1)}, bf16[4,8,5248]{2,1,0:T(8,128)(2,1)S(1)}, u32[]{:S(2)}, u32[]{:S(2)}) collective-permute-start(bf16[4,8,5248]{2,1,0:T(8,128)(2,1)S(1)} %shard_map.120), channel_id=1, source_target_pairs={{0,16},{8,24},{16,0},{24,8},{1,17},{9,25},{17,1},{25,9},{2,18},{10... | collective-permute-start | bytes 1007624 | tf_op jit(solution)/shard_map/ppermute | solution.py:26
  18.3 15.5 %collective-permute-start.6 = (bf16[4,8,5248]{2,1,0:T(8,128)(2,1)S(1)}, bf16[4,8,5248]{2,1,0:T(8,128)(2,1)S(1)}, u32[]{:S(2)}, u32[]{:S(2)}) collective-permute-start(bf16[4,8,5248]{2,1,0:T(8,128)(2,1)S(1)} %shard_map.120), channel_id=1, source_target_pairs={{0,8},{8,0},{16,24},{24,16},{1,9},{9,1},{17,25},{25,17},{2,10},{10... | collective-permute-start | bytes 1007624 | tf_op jit(solution)/shard_map/ppermute | solution.py:26
  27.4 1.7 %collective-permute-start.4 = (bf16[4,8,5120]{2,1,0:T(8,128)(2,1)S(1)}, bf16[4,8,5120]{2,1,0:T(8,128)(2,1)S(1)}, u32[]{:S(2)}, u32[]{:S(2)}) collective-permute-start(bf16[4,8,5120]{2,1,0:T(8,128)(2,1)S(1)} %bitcast.39), channel_id=1, source_target_pairs={{0,1},{1,0},{2,3},{3,2},{4,5},{5,4},{6,7},{7,6},{8,9},{9,8},{10,11... | collective-permute-start | bytes 983048 | tf_op jit(solution)/shard_map/ppermute | solution.py:26
  27.4 1.6 %collective-permute-start.5 = (f32[8,64]{1,0:T(8,128)S(1)}, f32[8,64]{1,0:T(8,128)S(1)}, u32[]{:S(2)}, u32[]{:S(2)}) collective-permute-start(f32[8,64]{1,0:T(8,128)S(1)} %get-tuple-element.38.pull_ref), channel_id=1, source_target_pairs={{0,1},{1,0},{2,3},{3,2},{4,5},{5,4},{6,7},{7,6},{8,9},{9,8},{10,11... | collective-permute-start | bytes 6152 | tf_op jit(solution)/shard_map/ppermute | solution.py:26
  33.8 4.7 %collective-permute-start.9 = (bf16[4,8,5248]{2,1,0:T(8,128)(2,1)S(1)}, bf16[4,8,5248]{2,1,0:T(8,128)(2,1)S(1)}, u32[]{:S(2)}, u32[]{:S(2)}) collective-permute-start(bf16[4,8,5248]{2,1,0:T(8,128)(2,1)S(1)} %collective-permute-done.6), channel_id=1, source_target_pairs={{0,1},{1,0},{2,3},{3,2},{4,5},{5,4},{6,7},{7,6},{8,9},{9,8},{10,11... | collective-permute-start | bytes 1007624 | tf_op jit(solution)/shard_map/ppermute | solution.py:26
  33.8 5.2 %collective-permute-start.10 = (bf16[4,8,5248]{2,1,0:T(8,128)(2,1)S(1)}, bf16[4,8,5248]{2,1,0:T(8,128)(2,1)S(1)}, u32[]{:S(2)}, u32[]{:S(2)}) collective-permute-start(bf16[4,8,5248]{2,1,0:T(8,128)(2,1)S(1)} %collective-permute-done.7), channel_id=1, source_target_pairs={{0,1},{1,0},{2,3},{3,2},{4,5},{5,4},{6,7},{7,6},{8,9},{9,8},{10,11... | collective-permute-start | bytes 1007624 | tf_op jit(solution)/shard_map/ppermute | solution.py:26
  34.3 4.7 %collective-permute-start.11 = (bf16[4,8,5248]{2,1,0:T(8,128)(2,1)S(1)}, bf16[4,8,5248]{2,1,0:T(8,128)(2,1)S(1)}, u32[]{:S(2)}, u32[]{:S(2)}) collective-permute-start(bf16[4,8,5248]{2,1,0:T(8,128)(2,1)S(1)} %collective-permute-done.8), channel_id=1, source_target_pairs={{0,1},{1,0},{2,3},{3,2},{4,5},{5,4},{6,7},{7,6},{8,9},{9,8},{10,11... | collective-permute-start | bytes 1007624 | tf_op jit(solution)/shard_map/ppermute | solution.py:26
  34.3 9.7 %collective-permute-start.12 = (bf16[8,5248]{1,0:T(8,128)(2,1)S(1)}, bf16[8,5248]{1,0:T(8,128)(2,1)S(1)}, u32[]{:S(2)}, u32[]{:S(2)}) collective-permute-start(bf16[8,5248]{1,0:T(8,128)(2,1)S(1)} %get-tuple-element.44), channel_id=1, source_target_pairs={{0,2},{1,3},{2,0},{3,1},{4,6},{5,7},{6,4},{7,5},{8,10},{9,11},{10,... | collective-permute-start | bytes 251912 | tf_op jit(solution)/shard_map/ppermute | solution.py:26
  35.6 9.8 %collective-permute-start.13 = (bf16[8,5248]{1,0:T(8,128)(2,1)S(1)}, bf16[8,5248]{1,0:T(8,128)(2,1)S(1)}, u32[]{:S(2)}, u32[]{:S(2)}) collective-permute-start(bf16[8,5248]{1,0:T(8,128)(2,1)S(1)} %get-tuple-element.45), channel_id=1, source_target_pairs={{0,4},{1,5},{2,6},{3,7},{4,0},{5,1},{6,2},{7,3},{8,12},{9,13},{10,... | collective-permute-start | bytes 251912 | tf_op jit(solution)/shard_map/ppermute | solution.py:26
  38.5 6.9 %collective-permute-start.14 = (bf16[8,5248]{1,0:T(8,128)(2,1)S(1)}, bf16[8,5248]{1,0:T(8,128)(2,1)S(1)}, u32[]{:S(2)}, u32[]{:S(2)}) collective-permute-start(bf16[8,5248]{1,0:T(8,128)(2,1)S(1)} %get-tuple-element.46), channel_id=1, source_target_pairs={{0,6},{1,7},{2,4},{3,5},{4,2},{5,3},{6,0},{7,1},{8,14},{9,15},{10,... | collective-permute-start | bytes 251912 | tf_op jit(solution)/shard_map/ppermute | solution.py:26
  39.1 14.0 %copy-start = (f32[2560,8]{0,1:T(8,128)S(1)}, f32[2560,8]{0,1:T(8,128)}, u32[]{:S(2)}) copy-start(f32[2560,8]{0,1:T(8,128)} %param.9) | copy-start | bytes 245764
  45.9 7.1 %collective-permute-start.17 = (f32[8,64]{1,0:T(8,128)S(1)}, f32[8,64]{1,0:T(8,128)S(1)}, u32[]{:S(2)}, u32[]{:S(2)}) collective-permute-start(f32[8,64]{1,0:T(8,128)S(1)} %shard_map.124.logit_refs_0_._), channel_id=1, source_target_pairs={{0,24},{8,16},{16,8},{24,0},{1,25},{9,17},{17,9},{25,1},{2,26},{10... | collective-permute-start | bytes 6152 | tf_op jit(solution)/shard_map/ppermute | solution.py:26
  47.7 5.4 %collective-permute-start.16 = (f32[8,64]{1,0:T(8,128)S(1)}, f32[8,64]{1,0:T(8,128)S(1)}, u32[]{:S(2)}, u32[]{:S(2)}) collective-permute-start(f32[8,64]{1,0:T(8,128)S(1)} %shard_map.124.logit_refs_0_._), channel_id=1, source_target_pairs={{0,16},{8,24},{16,0},{24,8},{1,17},{9,25},{17,1},{25,9},{2,18},{10... | collective-permute-start | bytes 6152 | tf_op jit(solution)/shard_map/ppermute | solution.py:26
  49.0 4.1 %collective-permute-start.15 = (f32[8,64]{1,0:T(8,128)S(1)}, f32[8,64]{1,0:T(8,128)S(1)}, u32[]{:S(2)}, u32[]{:S(2)}) collective-permute-start(f32[8,64]{1,0:T(8,128)S(1)} %shard_map.124.logit_refs_0_._), channel_id=1, source_target_pairs={{0,8},{8,0},{16,24},{24,16},{1,9},{9,1},{17,25},{25,17},{2,10},{10... | collective-permute-start | bytes 6152 | tf_op jit(solution)/shard_map/ppermute | solution.py:26

commit v7 on v6

--- a/solution.py
+++ b/solution.py
@@ -277,7 +277,7 @@
     router_grad_ref[...] = totals[0]
 
 
-def call(kernel, out_shape, in_specs, out_specs, scratch=(), limit=4, flops=0, moved=1 << 17):
+def call(kernel, out_shape, in_specs, out_specs, scratch=(), limit=4):
     return pl.pallas_call(
         kernel,
         out_shape=out_shape,
@@ -285,7 +285,7 @@
         out_specs=out_specs,
         scratch_shapes=scratch,
         compiler_params=pltpu.CompilerParams(vmem_limit_bytes=limit << 20),
-        cost_estimate=pl.CostEstimate(flops=flops, bytes_accessed=moved, transcendentals=0),
+        cost_estimate=pl.CostEstimate(flops=0, bytes_accessed=1, transcendentals=0),
     )
 
 
@@ -398,7 +398,6 @@
     at = jnp.stack([me % 2, me, lax.axis_index("dp"), me // 2]).astype(jnp.int32)
     router_t = router.T
     parts = jnp.concatenate(three_parts(router_t), axis=0)
-    matrix = 2 * features * hidden_units
     weight_kinds = [pltpu.VMEM(w.shape, w.dtype) for w in (w_gate, w_up, w_down)]
     small = jax.ShapeDtypeStruct((experts, group_rows), F32)
     in_hbm_spec = pl.BlockSpec(memory_space=pltpu.HBM)
@@ -418,7 +417,6 @@
         [IN_SMEM] + [in_hbm_spec] * 3,
         [IN_VMEM] * 3,
         [pltpu.SemaphoreType.DMA((3,))],
-        moved=3 * matrix,
     )(at, *[in_hbm(w) for w in (w_gate, w_up, w_down)])
     by_chip = call(
         order_kernel,
@@ -438,8 +436,6 @@
         [IN_VMEM] * 7,
         [pltpu.VMEM((group_rows, width), BF16), pltpu.VMEM((group_rows, 2 * features), BF16)],
         8,
-        6 * matrix * group_rows,
-        6 * matrix,
     )(at, by_chip.reshape(half, width), theirs.reshape(half, width), parts, *weights)
     rows = jax.ShapeDtypeStruct((tok_count, width), BF16)
     keep, send = [x.reshape(chips, tok_count, -1) for x in (keep, send)]
@@ -482,8 +478,6 @@
             pltpu.SemaphoreType.DMA((hidden_units // STEP, 3)),
         ],
         12,
-        6 * portion * hidden_units * count,
-        12 * portion * hidden_units,
     )(turned, grads, logit)
     rows = jax.ShapeDtypeStruct((tok_count, features), BF16)
     mixed, grad_tokens, router_grad = call(

time: 55.2 us -> 53.8 us (0.975)
  waiting for transfers between devices: 6.58 us -> 5.46 us
    ppermute x18, waiting for transfers between devices: 6.58 us -> 5.46 us  [swap(): return lax.ppermute(x, axis, [(i, i ^ mask) for i in range(count)])]
  transfers between devices with their start and end apart: 18 -> 18, of which waited for: 4 -> 5; matrix products, arithmetic and copies ran while one was open for 2% -> 2% of each run, Pallas kernels for 44% -> 45%
where the time goes in v7:
time: 53.8 us; the launch traced here: 53.6 us
  Pallas kernels  27.8 us (52%)
  starting transfers between devices  18.5 us (34%)
  waiting for transfers between devices  5.46 us (10%)
  other arithmetic  0.99 us (2%)
  between operations  0.8 us (1%)
    ppermute x18, starting transfers between devices, swap(): return lax.ppermute(x, axis, [(i, i ^ mask) for i in range(count)])  18.5 us
    pallas_call x1, Pallas kernels, kernels_plan(): call(own_kernel, [rows] * 2 + [grad] * 3 + [small, jax.ShapeDtypeStruct((...  8.64 us
    pallas_call x1, Pallas kernels, kernels_plan(): call(load_kernel, weight_kinds, [IN_SMEM] + [in_hbm_spec] * 3, [IN_VMEM]...  6.11 us
    ppermute x18, waiting for transfers between devices, swap(): return lax.ppermute(x, axis, [(i, i ^ mask) for i in range(count)])  5.46 us
    pallas_call x1, Pallas kernels, kernels_plan(): call(far_kernel, [pltpu.VMEM((count, hidden_units), BF16)] * 3 + [pltpu.V...  4.98 us
    pallas_call x1, Pallas kernels, kernels_plan(): call(weight_kernel, [result] * 3, [IN_VMEM, [IN_VMEM] * 3, pl.BlockSpec(m...  3.57 us
    pallas_call x1, Pallas kernels, kernels_plan(): call(last_kernel, [rows] * 2 + [jax.ShapeDtypeStruct((experts, features),...  1.81 us
  transfers between devices with their start and end apart: 18, of which 5 were waited for; matrix products, arithmetic and copies ran while one was open for 2% of the time, Pallas kernels for 45%

profile of v7, /device:TPU:0, one launch (start us, length us, event | category | flops | bytes accessed | tf_op | source)
XLA Modules:
  0.0 53.6 jit_solution(13337386779459472668)
XLA Ops:
  0.6 0.9 %shard_map.118.piece_refs_0_ = bf16[8,5248]{1,0:T(8,128)(2,1)S(1)} custom-call(bf16[8,2560]{1,0:T(8,128)(2,1)} %tokens_hbm.1, bf16[8,2560]{1,0:T(8,128)(2,1)} %cot_hbm.1, s32[8,6]{1,0:T(8,128)} %routes_hbm.1), custom_call_target="tpu_custom_call" | custom-call | bytes 1 | tf_op jit(solution)/shard_map/pallas_call | solution.py:406
  1.5 5.1 %collective-permute-start.2 = (bf16[8,5248]{1,0:T(8,128)(2,1)S(1)}, bf16[8,5248]{1,0:T(8,128)(2,1)S(1)}, u32[]{:S(2)}, u32[]{:S(2)}) collective-permute-start(bf16[8,5248]{1,0:T(8,128)(2,1)S(1)} %shard_map.118.piece_refs_0_), channel_id=1, source_target_pairs={{0,6},{1,7},{2,4},{3,5},{4,2},{5,3},{6,0},{7,1},{8,14},{9,15},{10,... | collective-permute-start | bytes 251912 | tf_op jit(solution)/shard_map/ppermute | solution.py:26
  6.7 0.0 collective-permute-start.1
  6.7 0.6 %collective-permute-start = (bf16[8,5248]{1,0:T(8,128)(2,1)S(1)}, bf16[8,5248]{1,0:T(8,128)(2,1)S(1)}, u32[]{:S(2)}, u32[]{:S(2)}) collective-permute-start(bf16[8,5248]{1,0:T(8,128)(2,1)S(1)} %shard_map.118.piece_refs_0_), channel_id=1, source_target_pairs={{0,2},{1,3},{2,0},{3,1},{4,6},{5,7},{6,4},{7,5},{8,10},{9,11},{10,... | collective-permute-start | bytes 251912 | tf_op jit(solution)/shard_map/ppermute | solution.py:26
  7.3 0.9 %reduce-precision_convert_fusion.1 = (bf16[8,2560]{1,0:T(8,128)(2,1)S(1)}, bf16[8,2560]{1,0:T(8,128)(2,1)S(1)}, bf16[8,2560]{1,0:T(8,128)(2,1)S(1)}) fusion(f32[2560,8]{0,1:T(8,128)} %param.9), kind=kLoop, calls=%fused_computation.4 | loop fusion | flops 163840 | bytes 204800 | tf_op jit(solution)/shard_map/convert_element_type | solution.py:37
  8.2 0.1 pad_add_fusion._.at_ref
  8.3 6.1 %shard_map.119 = (bf16[2560,1024]{1,0:T(8,128)(2,1)S(1)}, bf16[2560,1024]{1,0:T(8,128)(2,1)S(1)}, bf16[2560,1024]{1,0:T(8,128)(2,1)S(1)}) custom-call(s32[4]{0:T(128)S(1)} %pad_add_fusion._.at_ref, bf16[2560,1024]{1,0:T(8,128)(2,1)} %refs_0_.1, bf16[2560,1024]{1,0:T(8,128)(2,1)} %refs_1_.1, bf16[2560,1024]{1,0:T(8,128)(2,1)} %refs_2_.1), custom_call_target="tpu_custom_call" | custom-call | bytes 1 | tf_op jit(solution)/shard_map/pallas_call | solution.py:414
  14.4 0.0 collective-permute-done.2.piece_refs_3_
  14.4 0.0 collective-permute-done.1.piece_refs_2_
  14.5 0.0 collective-permute-done.piece_refs_1_
  14.5 0.6 %shard_map.120 = bf16[4,8,5248]{2,1,0:T(8,128)(2,1)S(1)} custom-call(s32[4]{0:T(128)S(1)} %pad_add_fusion._.at_ref, bf16[8,5248]{1,0:T(8,128)(2,1)S(1)} %shard_map.118.piece_refs_0_, bf16[8,5248]{1,0:T(8,128)(2,1)S(1)} %collective-permute-done.piece_refs_1_, bf16[8,5248]{1,0:T(8,128)(2,1)S(1)} %collective-permute-done.1.piece_refs_2_, ...), custom_call_target="tpu_custom_call" | custom-call | bytes 1 | tf_op jit(solution)/shard_map/pallas_call | solution.py:421
  15.0 2.7 %collective-permute-start.8 = (bf16[4,8,5248]{2,1,0:T(8,128)(2,1)S(1)}, bf16[4,8,5248]{2,1,0:T(8,128)(2,1)S(1)}, u32[]{:S(2)}, u32[]{:S(2)}) collective-permute-start(bf16[4,8,5248]{2,1,0:T(8,128)(2,1)S(1)} %shard_map.120), channel_id=1, source_target_pairs={{0,24},{8,16},{16,8},{24,0},{1,25},{9,17},{17,9},{25,1},{2,26},{10... | collective-permute-start | bytes 1007624 | tf_op jit(solution)/shard_map/ppermute | solution.py:26
  17.7 0.5 collective-permute-start.7
  18.2 0.4 collective-permute-start.6
  18.6 0.0 collective-permute-start.3
  18.6 1.6 %collective-permute-done.3 = bf16[4,8,5248]{2,1,0:T(8,128)(2,1)S(1)} collective-permute-done((bf16[4,8,5248]{2,1,0:T(8,128)(2,1)S(1)}, bf16[4,8,5248]{2,1,0:T(8,128)(2,1)S(1)}, u32[]{:S(2)}, u32[]{:S(2)}) %collective-permute-start.3) | collective-permute-done | bytes 335904 | tf_op jit(solution)/shard_map/ppermute | solution.py:26
  20.2 8.6 %shard_map.121 = (bf16[32,5120]{1,0:T(8,128)(2,1)S(1)}, bf16[32,5120]{1,0:T(8,128)(2,1)S(1)}, bf16[64,1024]{1,0:T(8,128)(2,1)S(1)}, bf16[64,1024]{1,0:T(8,128)(2...) custom-call(s32[4]{0:T(128)S(1)} %pad_add_fusion._.at_ref, ...), custom_call_target="tpu_custom_call" | custom-call | bytes 1 | tf_op jit(solution)/shard_map/pallas_call | solution.py:432
  28.9 0.2 collective-permute-start.4
  29.1 0.4 collective-permute-start.5
  29.5 1.1 %collective-permute-done.5.other_pull_ref = f32[8,64]{1,0:T(8,128)S(1)} collective-permute-done((f32[8,64]{1,0:T(8,128)S(1)}, f32[8,64]{1,0:T(8,128)S(1)}, u32[]{:S(2)}, u32[]{:S(2)}) %collective-permute-start.5) | collective-permute-done | bytes 2080 | tf_op jit(solution)/shard_map/ppermute | solution.py:26
  30.6 0.0 collective-permute-done.4.other_ref
  30.6 0.6 %shard_map.122 = (bf16[8,5248]{1,0:T(8,128)(2,1)S(1)}, bf16[8,5248]{1,0:T(8,128)(2,1)S(1)}, bf16[8,5248]{1,0:T(8,128)(2,1)S(1)}, bf16[8,5248]{1,0:T(8,128)(2,1)S(1)}) custom-call(s32[4]{0:T(128)S(1)} %pad_add_fusion._.at_ref, bf16[4,8,5120]{2,1,0:T(8,128)(2,1)S(1)} %bitcast.37, bf16[4,8,5120]{2,1,0:T(8,128)(2,1)S(1)} %collective-permute-done.4.other_ref, ...), custom_call_target="tpu_custom_call" | custom-call | bytes 1 | tf_op jit(solution)/shard_map/pallas_call | solution.py:442
  31.2 0.0 collective-permute-done.8
  31.2 1.0 %collective-permute-done.7 = bf16[4,8,5248]{2,1,0:T(8,128)(2,1)S(1)} collective-permute-done((bf16[4,8,5248]{2,1,0:T(8,128)(2,1)S(1)}, bf16[4,8,5248]{2,1,0:T(8,128)(2,1)S(1)}, u32[]{:S(2)}, u32[]{:S(2)}) %collective-permute-start.7) | collective-permute-done | bytes 335904 | tf_op jit(solution)/shard_map/ppermute | solution.py:26
  32.3 0.1 collective-permute-done.6
  32.4 0.0 collective-permute-start.9
  32.4 0.5 collective-permute-start.10
  32.9 0.0 collective-permute-start.11
  32.9 1.4 %collective-permute-start.12 = (bf16[8,5248]{1,0:T(8,128)(2,1)S(1)}, bf16[8,5248]{1,0:T(8,128)(2,1)S(1)}, u32[]{:S(2)}, u32[]{:S(2)}) collective-permute-start(bf16[8,5248]{1,0:T(8,128)(2,1)S(1)} %get-tuple-element.44), channel_id=1, source_target_pairs={{0,2},{1,3},{2,0},{3,1},{4,6},{5,7},{6,4},{7,5},{8,10},{9,11},{10,... | collective-permute-start | bytes 251912 | tf_op jit(solution)/shard_map/ppermute | solution.py:26
  34.3 2.6 %collective-permute-start.13 = (bf16[8,5248]{1,0:T(8,128)(2,1)S(1)}, bf16[8,5248]{1,0:T(8,128)(2,1)S(1)}, u32[]{:S(2)}, u32[]{:S(2)}) collective-permute-start(bf16[8,5248]{1,0:T(8,128)(2,1)S(1)} %get-tuple-element.45), channel_id=1, source_target_pairs={{0,4},{1,5},{2,6},{3,7},{4,0},{5,1},{6,2},{7,3},{8,12},{9,13},{10,... | collective-permute-start | bytes 251912 | tf_op jit(solution)/shard_map/ppermute | solution.py:26
  36.9 0.0 collective-permute-done.9
  36.9 0.6 %collective-permute-start.14 = (bf16[8,5248]{1,0:T(8,128)(2,1)S(1)}, bf16[8,5248]{1,0:T(8,128)(2,1)S(1)}, u32[]{:S(2)}, u32[]{:S(2)}) collective-permute-start(bf16[8,5248]{1,0:T(8,128)(2,1)S(1)} %get-tuple-element.46), channel_id=1, source_target_pairs={{0,6},{1,7},{2,4},{3,5},{4,2},{5,3},{6,0},{7,1},{8,14},{9,15},{10,... | collective-permute-start | bytes 251912 | tf_op jit(solution)/shard_map/ppermute | solution.py:26
  37.5 0.0 collective-permute-done.10
  37.5 0.0 collective-permute-done.11
  37.5 0.0 copy-start
  37.5 5.0 %shard_map.123 = (bf16[256,1024]{1,0:T(8,128)(2,1)S(1)}, bf16[256,1024]{1,0:T(8,128)(2,1)S(1)}, bf16[256,1024]{1,0:T(8,128)(2,1)S(1)}, bf16[2,640,256]{2,1,0:T(8,128)(2,1)S(1)}) custom-call(s32[4]{0:T(128)S(1)} %pad_add_fusion._.at_ref, bf16[32,5248]{1,0:T(8,128)(2,1)S(1)} %bitcast.20, bf16[32,5248]{1,0:T(8,128)(2,1)S(1)} %bitcast.29, ...), custom_call_target="tpu_custom_call" | custom-call | bytes 1 | tf_op jit(solution)/shard_map/pallas_call | solution.py:455
  42.5 0.0 collective-permute-done.12.back_refs_1_
  42.5 1.5 %collective-permute-done.13.back_refs_2_ = bf16[8,5248]{1,0:T(8,128)(2,1)S(1)} collective-permute-done((bf16[8,5248]{1,0:T(8,128)(2,1)S(1)}, bf16[8,5248]{1,0:T(8,128)(2,1)S(1)}, u32[]{:S(2)}, u32[]{:S(2)}) %collective-permute-start.13) | collective-permute-done | bytes 84000 | tf_op jit(solution)/shard_map/ppermute | solution.py:26
  44.0 0.0 collective-permute-done.14.back_refs_3_
  44.0 0.6 %shard_map.124.logit_refs_0_._ = f32[8,64]{1,0:T(8,128)S(1)} custom-call(s32[4]{0:T(128)S(1)} %pad_add_fusion._.at_ref, f32[3,8,64]{2,1,0:T(8,128)S(1)} %get-tuple-element.43.table_ref, bf16[8,5248]{1,0:T(8,128)(2,1)S(1)} %get-tuple-element.39.back_refs_0_, bf16[8,5248]{1,0:T(8,128)(2,1)S(1)} %collective-permute-done.12.back_refs_1_, ...), custom_call_target="tpu_custom_call" | custom-call | bytes 1 | tf_op jit(solution)/shard_map/pallas_call | solution.py:463
  44.6 1.7 %collective-permute-start.17 = (f32[8,64]{1,0:T(8,128)S(1)}, f32[8,64]{1,0:T(8,128)S(1)}, u32[]{:S(2)}, u32[]{:S(2)}) collective-permute-start(f32[8,64]{1,0:T(8,128)S(1)} %shard_map.124.logit_refs_0_._), channel_id=1, source_target_pairs={{0,24},{8,16},{16,8},{24,0},{1,25},{9,17},{17,9},{25,1},{2,26},{10... | collective-permute-start | bytes 6152 | tf_op jit(solution)/shard_map/ppermute | solution.py:26
  46.3 1.3 %collective-permute-start.16 = (f32[8,64]{1,0:T(8,128)S(1)}, f32[8,64]{1,0:T(8,128)S(1)}, u32[]{:S(2)}, u32[]{:S(2)}) collective-permute-start(f32[8,64]{1,0:T(8,128)S(1)} %shard_map.124.logit_refs_0_._), channel_id=1, source_target_pairs={{0,16},{8,24},{16,0},{24,8},{1,17},{9,25},{17,1},{25,9},{2,18},{10... | collective-permute-start | bytes 6152 | tf_op jit(solution)/shard_map/ppermute | solution.py:26
  47.6 0.5 collective-permute-start.15
  48.2 3.6 %shard_map.126 = (f32[640,1024]{1,0:T(8,128)}, f32[640,1024]{1,0:T(8,128)}, f32[640,1024]{1,0:T(8,128)}) custom-call(bf16[2,640,256]{2,1,0:T(8,128)(2,1)S(1)} %get-tuple-element.50._.turned_ref, bf16[256,1024]{1,0:T(8,128)(2,1)S(1)} %get-tuple-element.54.grad_refs_0_, bf16[256,1024]{1,0:T(8,128)(2,1)S(1)} %get-tuple-element.55.grad_refs_1_, ...), custom_call_target="tpu_custom_call" | custom-call | bytes 1 | tf_op jit(solution)/shard_map/pallas_call | solution.py:471
  51.7 0.0 collective-permute-done.17.logit_refs_3_
  51.7 0.0 collective-permute-done.16.logit_refs_2_
  51.8 0.0 collective-permute-done.15.logit_refs_1_
  51.8 0.0 copy-done
  51.8 1.8 %shard_map.125 = (bf16[8,2560]{1,0:T(8,128)(2,1)}, bf16[8,2560]{1,0:T(8,128)(2,1)}, f32[8,2560]{1,0:T(8,128)}) custom-call(s32[4]{0:T(128)S(1)} %pad_add_fusion._.at_ref, bf16[32,5248]{1,0:T(8,128)(2,1)S(1)} %bitcast.21, bf16[32,5248]{1,0:T(8,128)(2,1)S(1)} %bitcast.30, bf16[32,5248]{1,0:T(8,128)(2,1)S(1)} %bitcast.28, bf16[32,5248]{1,0:T(8,128)(2,1)S(1)} %bitcast.26, ...), custom_call_target="tpu_custom_call" | custom-call | bytes 1 | tf_op jit(solution)/shard_map/pallas_call | solution.py:483
  (1 shorter events, 0.0 us)
Async XLA Ops:
  1.5 12.9 %collective-permute-start.2 = (bf16[8,5248]{1,0:T(8,128)(2,1)S(1)}, bf16[8,5248]{1,0:T(8,128)(2,1)S(1)}, u32[]{:S(2)}, u32[]{:S(2)}) collective-permute-start(bf16[8,5248]{1,0:T(8,128)(2,1)S(1)} %shard_map.118.piece_refs_0_), channel_id=1, source_target_pairs={{0,6},{1,7},{2,4},{3,5},{4,2},{5,3},{6,0},{7,1},{8,14},{9,15},{10,... | collective-permute-start | bytes 251912 | tf_op jit(solution)/shard_map/ppermute | solution.py:26
  6.7 7.8 %collective-permute-start.1 = (bf16[8,5248]{1,0:T(8,128)(2,1)S(1)}, bf16[8,5248]{1,0:T(8,128)(2,1)S(1)}, u32[]{:S(2)}, u32[]{:S(2)}) collective-permute-start(bf16[8,5248]{1,0:T(8,128)(2,1)S(1)} %shard_map.118.piece_refs_0_), channel_id=1, source_target_pairs={{0,4},{1,5},{2,6},{3,7},{4,0},{5,1},{6,2},{7,3},{8,12},{9,13},{10,... | collective-permute-start | bytes 251912 | tf_op jit(solution)/shard_map/ppermute | solution.py:26
  6.7 7.8 %collective-permute-start = (bf16[8,5248]{1,0:T(8,128)(2,1)S(1)}, bf16[8,5248]{1,0:T(8,128)(2,1)S(1)}, u32[]{:S(2)}, u32[]{:S(2)}) collective-permute-start(bf16[8,5248]{1,0:T(8,128)(2,1)S(1)} %shard_map.118.piece_refs_0_), channel_id=1, source_target_pairs={{0,2},{1,3},{2,0},{3,1},{4,6},{5,7},{6,4},{7,5},{8,10},{9,11},{10,... | collective-permute-start | bytes 251912 | tf_op jit(solution)/shard_map/ppermute | solution.py:26
  15.0 16.2 %collective-permute-start.8 = (bf16[4,8,5248]{2,1,0:T(8,128)(2,1)S(1)}, bf16[4,8,5248]{2,1,0:T(8,128)(2,1)S(1)}, u32[]{:S(2)}, u32[]{:S(2)}) collective-permute-start(bf16[4,8,5248]{2,1,0:T(8,128)(2,1)S(1)} %shard_map.120), channel_id=1, source_target_pairs={{0,24},{8,16},{16,8},{24,0},{1,25},{9,17},{17,9},{25,1},{2,26},{10... | collective-permute-start | bytes 1007624 | tf_op jit(solution)/shard_map/ppermute | solution.py:26
  17.7 14.6 %collective-permute-start.7 = (bf16[4,8,5248]{2,1,0:T(8,128)(2,1)S(1)}, bf16[4,8,5248]{2,1,0:T(8,128)(2,1)S(1)}, u32[]{:S(2)}, u32[]{:S(2)}) collective-permute-start(bf16[4,8,5248]{2,1,0:T(8,128)(2,1)S(1)} %shard_map.120), channel_id=1, source_target_pairs={{0,16},{8,24},{16,0},{24,8},{1,17},{9,25},{17,1},{25,9},{2,18},{10... | collective-permute-start | bytes 1007624 | tf_op jit(solution)/shard_map/ppermute | solution.py:26
  18.2 14.2 %collective-permute-start.6 = (bf16[4,8,5248]{2,1,0:T(8,128)(2,1)S(1)}, bf16[4,8,5248]{2,1,0:T(8,128)(2,1)S(1)}, u32[]{:S(2)}, u32[]{:S(2)}) collective-permute-start(bf16[4,8,5248]{2,1,0:T(8,128)(2,1)S(1)} %shard_map.120), channel_id=1, source_target_pairs={{0,8},{8,0},{16,24},{24,16},{1,9},{9,1},{17,25},{25,17},{2,10},{10... | collective-permute-start | bytes 1007624 | tf_op jit(solution)/shard_map/ppermute | solution.py:26
  18.6 1.6 %collective-permute-start.3 = (bf16[4,8,5248]{2,1,0:T(8,128)(2,1)S(1)}, bf16[4,8,5248]{2,1,0:T(8,128)(2,1)S(1)}, u32[]{:S(2)}, u32[]{:S(2)}) collective-permute-start(bf16[4,8,5248]{2,1,0:T(8,128)(2,1)S(1)} %shard_map.120), channel_id=1, source_target_pairs={{0,1},{1,0},{2,3},{3,2},{4,5},{5,4},{6,7},{7,6},{8,9},{9,8},{10,11... | collective-permute-start | bytes 1007624 | tf_op jit(solution)/shard_map/ppermute | solution.py:26
  28.9 1.7 %collective-permute-start.4 = (bf16[4,8,5120]{2,1,0:T(8,128)(2,1)S(1)}, bf16[4,8,5120]{2,1,0:T(8,128)(2,1)S(1)}, u32[]{:S(2)}, u32[]{:S(2)}) collective-permute-start(bf16[4,8,5120]{2,1,0:T(8,128)(2,1)S(1)} %bitcast.39), channel_id=1, source_target_pairs={{0,1},{1,0},{2,3},{3,2},{4,5},{5,4},{6,7},{7,6},{8,9},{9,8},{10,11... | collective-permute-start | bytes 983048 | tf_op jit(solution)/shard_map/ppermute | solution.py:26
  29.1 1.5 %collective-permute-start.5 = (f32[8,64]{1,0:T(8,128)S(1)}, f32[8,64]{1,0:T(8,128)S(1)}, u32[]{:S(2)}, u32[]{:S(2)}) collective-permute-start(f32[8,64]{1,0:T(8,128)S(1)} %get-tuple-element.38.pull_ref), channel_id=1, source_target_pairs={{0,1},{1,0},{2,3},{3,2},{4,5},{5,4},{6,7},{7,6},{8,9},{9,8},{10,11... | collective-permute-start | bytes 6152 | tf_op jit(solution)/shard_map/ppermute | solution.py:26
  32.4 4.5 %collective-permute-start.9 = (bf16[4,8,5248]{2,1,0:T(8,128)(2,1)S(1)}, bf16[4,8,5248]{2,1,0:T(8,128)(2,1)S(1)}, u32[]{:S(2)}, u32[]{:S(2)}) collective-permute-start(bf16[4,8,5248]{2,1,0:T(8,128)(2,1)S(1)} %collective-permute-done.6), channel_id=1, source_target_pairs={{0,1},{1,0},{2,3},{3,2},{4,5},{5,4},{6,7},{7,6},{8,9},{9,8},{10,11... | collective-permute-start | bytes 1007624 | tf_op jit(solution)/shard_map/ppermute | solution.py:26
  32.4 5.1 %collective-permute-start.10 = (bf16[4,8,5248]{2,1,0:T(8,128)(2,1)S(1)}, bf16[4,8,5248]{2,1,0:T(8,128)(2,1)S(1)}, u32[]{:S(2)}, u32[]{:S(2)}) collective-permute-start(bf16[4,8,5248]{2,1,0:T(8,128)(2,1)S(1)} %collective-permute-done.7), channel_id=1, source_target_pairs={{0,1},{1,0},{2,3},{3,2},{4,5},{5,4},{6,7},{7,6},{8,9},{9,8},{10,11... | collective-permute-start | bytes 1007624 | tf_op jit(solution)/shard_map/ppermute | solution.py:26
  32.9 4.6 %collective-permute-start.11 = (bf16[4,8,5248]{2,1,0:T(8,128)(2,1)S(1)}, bf16[4,8,5248]{2,1,0:T(8,128)(2,1)S(1)}, u32[]{:S(2)}, u32[]{:S(2)}) collective-permute-start(bf16[4,8,5248]{2,1,0:T(8,128)(2,1)S(1)} %collective-permute-done.8), channel_id=1, source_target_pairs={{0,1},{1,0},{2,3},{3,2},{4,5},{5,4},{6,7},{7,6},{8,9},{9,8},{10,11... | collective-permute-start | bytes 1007624 | tf_op jit(solution)/shard_map/ppermute | solution.py:26
  32.9 9.6 %collective-permute-start.12 = (bf16[8,5248]{1,0:T(8,128)(2,1)S(1)}, bf16[8,5248]{1,0:T(8,128)(2,1)S(1)}, u32[]{:S(2)}, u32[]{:S(2)}) collective-permute-start(bf16[8,5248]{1,0:T(8,128)(2,1)S(1)} %get-tuple-element.44), channel_id=1, source_target_pairs={{0,2},{1,3},{2,0},{3,1},{4,6},{5,7},{6,4},{7,5},{8,10},{9,11},{10,... | collective-permute-start | bytes 251912 | tf_op jit(solution)/shard_map/ppermute | solution.py:26
  34.3 9.8 %collective-permute-start.13 = (bf16[8,5248]{1,0:T(8,128)(2,1)S(1)}, bf16[8,5248]{1,0:T(8,128)(2,1)S(1)}, u32[]{:S(2)}, u32[]{:S(2)}) collective-permute-start(bf16[8,5248]{1,0:T(8,128)(2,1)S(1)} %get-tuple-element.45), channel_id=1, source_target_pairs={{0,4},{1,5},{2,6},{3,7},{4,0},{5,1},{6,2},{7,3},{8,12},{9,13},{10,... | collective-permute-start | bytes 251912 | tf_op jit(solution)/shard_map/ppermute | solution.py:26
  36.9 7.1 %collective-permute-start.14 = (bf16[8,5248]{1,0:T(8,128)(2,1)S(1)}, bf16[8,5248]{1,0:T(8,128)(2,1)S(1)}, u32[]{:S(2)}, u32[]{:S(2)}) collective-permute-start(bf16[8,5248]{1,0:T(8,128)(2,1)S(1)} %get-tuple-element.46), channel_id=1, source_target_pairs={{0,6},{1,7},{2,4},{3,5},{4,2},{5,3},{6,0},{7,1},{8,14},{9,15},{10,... | collective-permute-start | bytes 251912 | tf_op jit(solution)/shard_map/ppermute | solution.py:26
  37.5 14.3 %copy-start = (f32[2560,8]{0,1:T(8,128)S(1)}, f32[2560,8]{0,1:T(8,128)}, u32[]{:S(2)}) copy-start(f32[2560,8]{0,1:T(8,128)} %param.9) | copy-start | bytes 245764
  44.6 7.1 %collective-permute-start.17 = (f32[8,64]{1,0:T(8,128)S(1)}, f32[8,64]{1,0:T(8,128)S(1)}, u32[]{:S(2)}, u32[]{:S(2)}) collective-permute-start(f32[8,64]{1,0:T(8,128)S(1)} %shard_map.124.logit_refs_0_._), channel_id=1, source_target_pairs={{0,24},{8,16},{16,8},{24,0},{1,25},{9,17},{17,9},{25,1},{2,26},{10... | collective-permute-start | bytes 6152 | tf_op jit(solution)/shard_map/ppermute | solution.py:26
  46.3 5.4 %collective-permute-start.16 = (f32[8,64]{1,0:T(8,128)S(1)}, f32[8,64]{1,0:T(8,128)S(1)}, u32[]{:S(2)}, u32[]{:S(2)}) collective-permute-start(f32[8,64]{1,0:T(8,128)S(1)} %shard_map.124.logit_refs_0_._), channel_id=1, source_target_pairs={{0,16},{8,24},{16,0},{24,8},{1,17},{9,25},{17,1},{25,9},{2,18},{10... | collective-permute-start | bytes 6152 | tf_op jit(solution)/shard_map/ppermute | solution.py:26
  47.6 4.1 %collective-permute-start.15 = (f32[8,64]{1,0:T(8,128)S(1)}, f32[8,64]{1,0:T(8,128)S(1)}, u32[]{:S(2)}, u32[]{:S(2)}) collective-permute-start(f32[8,64]{1,0:T(8,128)S(1)} %shard_map.124.logit_refs_0_._), channel_id=1, source_target_pairs={{0,8},{8,0},{16,24},{24,16},{1,9},{9,1},{17,25},{25,17},{2,10},{10... | collective-permute-start | bytes 6152 | tf_op jit(solution)/shard_map/ppermute | solution.py:26

commit v8 on v7

--- a/solution.py
+++ b/solution.py
@@ -77,11 +77,15 @@
     )
 
 
-def hidden_step(at, x, slot_gate, w_gate_ref, w_up_ref, w_down_ref):
+def hidden_dots(start, x, w_gate_ref, w_up_ref, w_down_ref):
     features = w_gate_ref.shape[0]
+    at = pl.ds(start, STEP)
     gate_pre = dot(x[:, :features], w_gate_ref[:, at])
     up_pre = dot(x[:, :features], w_up_ref[:, at])
-    raw = dot(x[:, features : 2 * features], w_down_ref[:, at])
+    return gate_pre, up_pre, dot(x[:, features : 2 * features], w_down_ref[:, at])
+
+
+def hidden_grads(gate_pre, up_pre, raw, slot_gate):
     sigma = 1.0 / (1.0 + jnp.exp(-gate_pre))
     silu = gate_pre * sigma
     hidden = silu * up_pre
@@ -134,6 +138,8 @@
     experts = parts_ref.shape[0] // 3
     core = at_ref[0]
     place_rows(x_ref, 0, core, mine_ref, theirs_ref)
+    weights = (w_gate_ref, w_up_ref, w_down_ref)
+    dots = hidden_dots(0, x_ref, *weights)
     affinity, denominator, gates = gate_tables(x_ref, parts_ref, experts)
     table_ref[0] = affinity
     table_ref[1] = gates
@@ -142,7 +148,10 @@
     pulls = jnp.zeros(slot_gate.shape, F32)
     for start in range(0, hidden_units, STEP):
         at = pl.ds(start, STEP)
-        grads, pulled = hidden_step(at, x_ref, slot_gate, w_gate_ref, w_up_ref, w_down_ref)
+        now = dots
+        if start + STEP < hidden_units:
+            dots = hidden_dots(start + STEP, x_ref, *weights)
+        grads, pulled = hidden_grads(*now, slot_gate)
         gate_grad_ref[:, at], up_grad_ref[:, at], gated_ref[:, at] = grads
         pulls += sum(pulled[:, lane : lane + LANES] for lane in range(0, STEP, LANES))
     ones = jnp.ones((pull_ref.shape[0], LANES), F32)
@@ -198,13 +207,29 @@
     out_ref[...] = (pulls - mean_pull) / denominator * affinity * (1.0 - affinity)
 
 
+def send_weights(start, turned_ref, grad_refs, target_refs, out_refs, sems):
+    at = pl.ds(start, STEP)
+    copies = []
+    for j, (grad_ref, out_ref, target_ref) in enumerate(zip(grad_refs, out_refs, target_refs)):
+        here = pl.ds(start % out_ref.shape[1], STEP)
+        out_ref[:, here] = dot(turned_ref[j // 2], grad_ref[:, at])
+        copy = pltpu.make_async_copy(
+            out_ref.at[:, here], target_ref.at[:, at], sems.at[start % out_ref.shape[1] // STEP, j]
+        )
+        copy.start()
+        copies.append(copy)
+    return copies
+
+
 def far_kernel(
     at_ref, mine_refs, theirs_refs, parts_ref, w_gate_ref, w_up_ref, w_down_ref, own_refs,
-    gate_grad_ref, up_grad_ref, gated_ref, turned_ref, x_ref,
+    gate_grad_ref, up_grad_ref, gated_ref, turned_ref, x_ref, gate_ref, up_ref, down_ref,
+    out_refs, sems,
 ):
     features, hidden_units = w_gate_ref.shape
     experts = parts_ref.shape[0] // 3
     grad_refs = (gate_grad_ref, up_grad_ref, gated_ref)
+    target_refs = (gate_ref, up_ref, down_ref)
     portion = turned_ref.shape[1]
     group_rows = own_refs[0].shape[0]
     for m, (mine_ref, theirs_ref) in enumerate(zip(mine_refs, theirs_refs)):
@@ -215,75 +240,75 @@
             at = pl.ds(pl.multiple_of(half * features + first + row, LANES), LANES)
             turned_ref[half, row : row + LANES, :] = x_ref[:, at].T
     far = x_ref.at[group_rows:, :]
+    weights = (w_gate_ref, w_up_ref, w_down_ref)
+    dots = hidden_dots(0, far, *weights)
     slot_gate = slot_gates(gate_tables(far, parts_ref, experts)[2], at_ref[1])
+    copies = []
     for start in range(0, hidden_units, STEP):
         at = pl.ds(start, STEP)
-        grads, _ = hidden_step(at, far, slot_gate, w_gate_ref, w_up_ref, w_down_ref)
+        now = dots
+        if start + STEP < hidden_units:
+            dots = hidden_dots(start + STEP, far, *weights)
+        grads, _ = hidden_grads(*now, slot_gate)
         for grad_ref, own_ref, grad in zip(grad_refs, own_refs, grads):
             grad_ref[:group_rows, at] = own_ref[:, at]
             grad_ref[group_rows:, at] = grad
-
-
-def weight_kernel(turned_ref, grad_refs, _, gate_ref, up_ref, down_ref, out_refs, sems):
-    target_refs = (gate_ref, up_ref, down_ref)
-    copies = []
-    for step, start in enumerate(range(0, grad_refs[0].shape[1], STEP)):
-        at = pl.ds(start, STEP)
-        for j, (grad_ref, out_ref, target_ref) in enumerate(
-            zip(grad_refs, out_refs, target_refs)
-        ):
-            out_ref[:, at] = dot(turned_ref[j // 2], grad_ref[:, at])
-            copy = pltpu.make_async_copy(
-                out_ref.at[:, at], target_ref.at[:, at], sems.at[step, j]
-            )
-            copy.start()
-            copies.append(copy)
+        if start < out_refs[0].shape[1]:
+            copies += send_weights(start, turned_ref, grad_refs, target_refs, out_refs, sems)
     for copy in copies:
         copy.wait()
 
 
+def weight_kernel(
+    turned_ref, grad_refs, _, begun_refs, gate_ref, up_ref, down_ref, out_refs, sems
+):
+    hidden_units = grad_refs[0].shape[1]
+    count = out_refs[0].shape[1]
+    copies = []
+    for start in range(hidden_units - count, hidden_units, STEP):
+        copies += send_weights(
+            start, turned_ref, grad_refs, (gate_ref, up_ref, down_ref), out_refs, sems
+        )
+    for copy in copies:
+        copy.wait()
+
+
 def last_kernel(
-    at_ref, mine_refs, theirs_refs, logit_refs, router_ref, back_refs,
-    mixed_ref, tokens_ref, router_grad_ref, x_ref,
+    at_ref, x_ref, logit_refs, router_ref, back_refs, mixed_ref, tokens_ref, router_grad_ref
 ):
     experts, features = router_ref.shape
-    count = mixed_ref.shape[0]
-    chips = len(back_refs)
-    grads = logit_refs[0][...]
-    shape = (count, grads.shape[1])
-    row = lax.broadcasted_iota(jnp.int32, shape, 0) + (at_ref[0] * chips + at_ref[3]) * count
-    own = (lax.broadcasted_iota(jnp.int32, shape, 1) == row).astype(F32)
-    own_grads = lax.dot_general(own, grads, LAST, precision=HIGHEST, preferred_element_type=F32)
-    back = jnp.dot(own_grads, router_ref[...], precision=HIGHEST, preferred_element_type=F32)
-    summed = sum(ref[...].astype(F32) for ref in back_refs)
-    mixed_ref[...] = summed[:, :features].astype(BF16)
-    tokens_ref[...] = (summed[:, features : 2 * features] + back).astype(BF16)
+    group_rows = x_ref.shape[0] // len(logit_refs)
+    parts = [jnp.concatenate(parts_of(ref[...]), axis=0).astype(BF16) for ref in logit_refs]
     totals = []
-    group_rows = grads.shape[1]
-    for m, (mine_ref, theirs_ref) in enumerate(zip(mine_refs, theirs_refs)):
-        place_rows(
-            x_ref,
-            m * group_rows,
-            at_ref[0],
-            mine_ref.at[:, :features],
-            theirs_ref.at[:, :features],
-        )
-    for m, logit_ref in enumerate(logit_refs):
-        stacked = jnp.concatenate(parts_of(logit_ref[...]), axis=0).astype(BF16)
-        total = dot(stacked, x_ref[m * group_rows : (m + 1) * group_rows, :])
+    for m, part in enumerate(parts):
+        total = dot(part, x_ref[m * group_rows : (m + 1) * group_rows, :features])
         totals.append(total[2 * experts :] + total[experts : 2 * experts] + total[:experts])
     while len(totals) > 1:
         totals = [totals[i] + totals[i + 1] for i in range(0, len(totals), 2)]
     router_grad_ref[...] = totals[0]
-
-
-def call(kernel, out_shape, in_specs, out_specs, scratch=(), limit=4):
+    count = mixed_ref.shape[0]
+    shape = (count, group_rows)
+    place = at_ref[0] * len(back_refs) + at_ref[3]
+    row = lax.broadcasted_iota(jnp.int32, shape, 0) + place * count
+    own = (lax.broadcasted_iota(jnp.int32, shape, 1) == row).astype(BF16)
+    own_grads = dot(own, parts[0], LAST)
+    back = jnp.zeros((count, features), F32)
+    for e in range(experts):
+        column = sum(own_grads[:, i + e : i + e + 1] for i in range(0, 3 * experts, experts))
+        back += column * router_ref[e : e + 1, :]
+    summed = sum(ref[...].astype(F32) for ref in back_refs)
+    mixed_ref[...] = summed[:, :features].astype(BF16)
+    tokens_ref[...] = (summed[:, features : 2 * features] + back).astype(BF16)
+
+
+def call(kernel, out_shape, in_specs, out_specs, scratch=(), limit=4, aliases={}):
     return pl.pallas_call(
         kernel,
         out_shape=out_shape,
         in_specs=in_specs,
         out_specs=out_specs,
         scratch_shapes=scratch,
+        input_output_aliases=aliases,
         compiler_params=pltpu.CompilerParams(vmem_limit_bytes=limit << 20),
         cost_estimate=pl.CostEstimate(flops=0, bytes_accessed=1, transcendentals=0),
     )
@@ -452,14 +477,22 @@
     mine, theirs = [[x.reshape(half, width) for x in xs] for xs in (mine, theirs)]
 
     count = groups * group_rows
-    *grads, turned = call(
+    begun = hidden_units // (2 * STEP) * STEP
+    in_vmem = [pltpu.VMEM((count, hidden_units), BF16)] * 3
+    *outs, grad_gate, grad_up, grad_down = call(
         far_kernel,
-        [pltpu.VMEM((count, hidden_units), BF16)] * 3 + [pltpu.VMEM((2, portion, count), BF16)],
+        in_vmem
+        + [pltpu.VMEM((2, portion, count), BF16), pltpu.VMEM((count, width), BF16)]
+        + [pltpu.HBM((portion, hidden_units), F32)] * 3,
         [IN_SMEM, [IN_VMEM] * groups, [IN_VMEM] * groups] + [IN_VMEM] * 4 + [[IN_VMEM] * 3],
-        [IN_VMEM] * 4,
-        [pltpu.VMEM((count, width), BF16)],
-        12,
+        [IN_VMEM] * 5 + [in_hbm_spec] * 3,
+        [
+            [pltpu.VMEM((portion, begun), F32)] * 3,
+            pltpu.SemaphoreType.DMA((begun // STEP, 3)),
+        ],
+        16,
     )(at, mine, theirs, parts, *weights, own)
+    *grads, turned, x = outs
     logit = call(
         logit_kernel,
         small,
@@ -467,28 +500,26 @@
         IN_VMEM,
     )(at, tables, back, turned)
     logits = [logit] + [swap(logit, "dp", m) for m in range(1, groups)]
-    result = jax.ShapeDtypeStruct((portion, hidden_units), F32)
+    rest = hidden_units - begun
     grad_gate, grad_up, grad_down = call(
         weight_kernel,
-        [result] * 3,
-        [IN_VMEM, [IN_VMEM] * 3, pl.BlockSpec(memory_space=pl.ANY)],
-        [pl.BlockSpec(memory_space=pl.ANY)] * 3,
+        [pltpu.HBM((portion, hidden_units), F32)] * 3,
+        [IN_VMEM, [IN_VMEM] * 3, pl.BlockSpec(memory_space=pl.ANY), [in_hbm_spec] * 3],
+        [in_hbm_spec] * 3,
         [
-            [pltpu.VMEM((portion, hidden_units), F32)] * 3,
-            pltpu.SemaphoreType.DMA((hidden_units // STEP, 3)),
+            [pltpu.VMEM((portion, rest), F32)] * 3,
+            pltpu.SemaphoreType.DMA((rest // STEP, 3)),
         ],
-        12,
-    )(turned, grads, logit)
+        16,
+        {5: 0, 6: 1, 7: 2},
+    )(turned, grads, logit, [grad_gate, grad_up, grad_down])
     rows = jax.ShapeDtypeStruct((tok_count, features), BF16)
     mixed, grad_tokens, router_grad = call(
         last_kernel,
         [rows] * 2 + [jax.ShapeDtypeStruct((experts, features), F32)],
-        [IN_SMEM]
-        + [[IN_VMEM] * groups] * 3
-        + [IN_VMEM, [IN_VMEM] * chips],
+        [IN_SMEM, IN_VMEM, [IN_VMEM] * groups, IN_VMEM, [IN_VMEM] * chips],
         [IN_VMEM] * 3,
-        [pltpu.VMEM((count, features), BF16)],
-    )(at, mine, theirs, logits, router_t, back)
+    )(at, x, logits, router_t, back)
     return (mixed, grad_tokens, router_grad.T, grad_gate, grad_up, grad_down)
 
 

time: 53.8 us -> 53.2 us (0.989)
  Pallas kernels: 27.8 us -> 27.1 us
  transfers between devices with their start and end apart: 18 -> 18, of which waited for: 5 -> 6; matrix products, arithmetic and copies ran while one was open for 2% -> 2% of each run, Pallas kernels for 45% -> 44%
where the time goes in v8:
time: 53.2 us; the launch traced here: 52.9 us
  Pallas kernels  27.1 us (51%)
  starting transfers between devices  18.5 us (35%)
  waiting for transfers between devices  5.53 us (10%)
  other arithmetic  0.99 us (2%)
  between operations  0.78 us (1%)
    ppermute x18, starting transfers between devices, swap(): return lax.ppermute(x, axis, [(i, i ^ mask) for i in range(count)])  18.5 us
    pallas_call x1, Pallas kernels, kernels_plan(): call(own_kernel, [rows] * 2 + [grad] * 3 + [small, jax.ShapeDtypeStruct((...  8.51 us
    pallas_call x1, Pallas kernels, kernels_plan(): call(load_kernel, weight_kinds, [IN_SMEM] + [in_hbm_spec] * 3, [IN_VMEM]...  6.11 us
    pallas_call x1, Pallas kernels, kernels_plan(): call(far_kernel, in_vmem + [pltpu.VMEM((2, portion, count), BF16), pltpu....  5.78 us
    ppermute x18, waiting for transfers between devices, swap(): return lax.ppermute(x, axis, [(i, i ^ mask) for i in range(count)])  5.53 us
    pallas_call x1, Pallas kernels, kernels_plan(): call(weight_kernel, [pltpu.HBM((portion, hidden_units), F32)] * 3, [IN_VM...  2.3 us
    pallas_call x1, Pallas kernels, kernels_plan(): call(last_kernel, [rows] * 2 + [jax.ShapeDtypeStruct((experts, features),...  1.72 us
  transfers between devices with their start and end apart: 18, of which 6 were waited for; matrix products, arithmetic and copies ran while one was open for 2% of the time, Pallas kernels for 44%

profile of v8, /device:TPU:0, one launch (start us, length us, event | category | flops | bytes accessed | tf_op | source)
XLA Modules:
  0.0 52.9 jit_solution(6939187566898800527)
XLA Ops:
  0.6 0.9 %shard_map.118.piece_refs_0_ = bf16[8,5248]{1,0:T(8,128)(2,1)S(1)} custom-call(bf16[8,2560]{1,0:T(8,128)(2,1)} %tokens_hbm.1, bf16[8,2560]{1,0:T(8,128)(2,1)} %cot_hbm.1, s32[8,6]{1,0:T(8,128)} %routes_hbm.1), custom_call_target="tpu_custom_call" | custom-call | bytes 1 | tf_op jit(solution)/shard_map/pallas_call | solution.py:431
  1.5 5.1 %collective-permute-start.2 = (bf16[8,5248]{1,0:T(8,128)(2,1)S(1)}, bf16[8,5248]{1,0:T(8,128)(2,1)S(1)}, u32[]{:S(2)}, u32[]{:S(2)}) collective-permute-start(bf16[8,5248]{1,0:T(8,128)(2,1)S(1)} %shard_map.118.piece_refs_0_), channel_id=1, source_target_pairs={{0,6},{1,7},{2,4},{3,5},{4,2},{5,3},{6,0},{7,1},{8,14},{9,15},{10,... | collective-permute-start | bytes 251912 | tf_op jit(solution)/shard_map/ppermute | solution.py:26
  6.7 0.0 collective-permute-start.1
  6.7 0.6 %collective-permute-start = (bf16[8,5248]{1,0:T(8,128)(2,1)S(1)}, bf16[8,5248]{1,0:T(8,128)(2,1)S(1)}, u32[]{:S(2)}, u32[]{:S(2)}) collective-permute-start(bf16[8,5248]{1,0:T(8,128)(2,1)S(1)} %shard_map.118.piece_refs_0_), channel_id=1, source_target_pairs={{0,2},{1,3},{2,0},{3,1},{4,6},{5,7},{6,4},{7,5},{8,10},{9,11},{10,... | collective-permute-start | bytes 251912 | tf_op jit(solution)/shard_map/ppermute | solution.py:26
  7.3 0.9 %reduce-precision_convert_fusion.1 = (bf16[8,2560]{1,0:T(8,128)(2,1)S(1)}, bf16[8,2560]{1,0:T(8,128)(2,1)S(1)}, bf16[8,2560]{1,0:T(8,128)(2,1)S(1)}) fusion(f32[2560,8]{0,1:T(8,128)} %param.9), kind=kLoop, calls=%fused_computation.4 | loop fusion | flops 163840 | bytes 204800 | tf_op jit(solution)/shard_map/convert_element_type | solution.py:37
  8.2 0.1 pad_add_fusion._.at_ref
  8.3 6.1 %shard_map.119 = (bf16[2560,1024]{1,0:T(8,128)(2,1)S(1)}, bf16[2560,1024]{1,0:T(8,128)(2,1)S(1)}, bf16[2560,1024]{1,0:T(8,128)(2,1)S(1)}) custom-call(s32[4]{0:T(128)S(1)} %pad_add_fusion._.at_ref, bf16[2560,1024]{1,0:T(8,128)(2,1)} %refs_0_.1, bf16[2560,1024]{1,0:T(8,128)(2,1)} %refs_1_.1, bf16[2560,1024]{1,0:T(8,128)(2,1)} %refs_2_.1), custom_call_target="tpu_custom_call" | custom-call | bytes 1 | tf_op jit(solution)/shard_map/pallas_call | solution.py:439
  14.4 0.0 collective-permute-done.2.piece_refs_3_
  14.4 0.0 collective-permute-done.1.piece_refs_2_
  14.5 0.0 collective-permute-done.piece_refs_1_
  14.5 0.6 %shard_map.120 = bf16[4,8,5248]{2,1,0:T(8,128)(2,1)S(1)} custom-call(s32[4]{0:T(128)S(1)} %pad_add_fusion._.at_ref, bf16[8,5248]{1,0:T(8,128)(2,1)S(1)} %shard_map.118.piece_refs_0_, bf16[8,5248]{1,0:T(8,128)(2,1)S(1)} %collective-permute-done.piece_refs_1_, bf16[8,5248]{1,0:T(8,128)(2,1)S(1)} %collective-permute-done.1.piece_refs_2_, ...), custom_call_target="tpu_custom_call" | custom-call | bytes 1 | tf_op jit(solution)/shard_map/pallas_call | solution.py:446
  15.0 2.7 %collective-permute-start.8 = (bf16[4,8,5248]{2,1,0:T(8,128)(2,1)S(1)}, bf16[4,8,5248]{2,1,0:T(8,128)(2,1)S(1)}, u32[]{:S(2)}, u32[]{:S(2)}) collective-permute-start(bf16[4,8,5248]{2,1,0:T(8,128)(2,1)S(1)} %shard_map.120), channel_id=1, source_target_pairs={{0,24},{8,16},{16,8},{24,0},{1,25},{9,17},{17,9},{25,1},{2,26},{10... | collective-permute-start | bytes 1007624 | tf_op jit(solution)/shard_map/ppermute | solution.py:26
  17.7 0.5 collective-permute-start.7
  18.2 0.4 collective-permute-start.6
  18.6 0.0 collective-permute-start.3
  18.6 1.6 %collective-permute-done.3 = bf16[4,8,5248]{2,1,0:T(8,128)(2,1)S(1)} collective-permute-done((bf16[4,8,5248]{2,1,0:T(8,128)(2,1)S(1)}, bf16[4,8,5248]{2,1,0:T(8,128)(2,1)S(1)}, u32[]{:S(2)}, u32[]{:S(2)}) %collective-permute-start.3) | collective-permute-done | bytes 335904 | tf_op jit(solution)/shard_map/ppermute | solution.py:26
  20.2 8.5 %shard_map.121 = (bf16[32,5120]{1,0:T(8,128)(2,1)S(1)}, bf16[32,5120]{1,0:T(8,128)(2,1)S(1)}, bf16[64,1024]{1,0:T(8,128)(2,1)S(1)}, bf16[64,1024]{1,0:T(8,128)(2...) custom-call(s32[4]{0:T(128)S(1)} %pad_add_fusion._.at_ref, ...), custom_call_target="tpu_custom_call" | custom-call | bytes 1 | tf_op jit(solution)/shard_map/pallas_call | solution.py:457
  28.8 0.2 collective-permute-start.4
  29.0 0.4 collective-permute-start.5
  29.3 1.1 %collective-permute-done.5.other_pull_ref = f32[8,64]{1,0:T(8,128)S(1)} collective-permute-done((f32[8,64]{1,0:T(8,128)S(1)}, f32[8,64]{1,0:T(8,128)S(1)}, u32[]{:S(2)}, u32[]{:S(2)}) %collective-permute-start.5) | collective-permute-done | bytes 2080 | tf_op jit(solution)/shard_map/ppermute | solution.py:26
  30.5 0.0 collective-permute-done.4.other_ref
  30.5 0.6 %shard_map.122 = (bf16[8,5248]{1,0:T(8,128)(2,1)S(1)}, bf16[8,5248]{1,0:T(8,128)(2,1)S(1)}, bf16[8,5248]{1,0:T(8,128)(2,1)S(1)}, bf16[8,5248]{1,0:T(8,128)(2,1)S(1)}) custom-call(s32[4]{0:T(128)S(1)} %pad_add_fusion._.at_ref, bf16[4,8,5120]{2,1,0:T(8,128)(2,1)S(1)} %bitcast.29, bf16[4,8,5120]{2,1,0:T(8,128)(2,1)S(1)} %collective-permute-done.4.other_ref, ...), custom_call_target="tpu_custom_call" | custom-call | bytes 1 | tf_op jit(solution)/shard_map/pallas_call | solution.py:467
  31.1 0.0 collective-permute-done.8
  31.1 1.2 %collective-permute-done.7 = bf16[4,8,5248]{2,1,0:T(8,128)(2,1)S(1)} collective-permute-done((bf16[4,8,5248]{2,1,0:T(8,128)(2,1)S(1)}, bf16[4,8,5248]{2,1,0:T(8,128)(2,1)S(1)}, u32[]{:S(2)}, u32[]{:S(2)}) %collective-permute-start.7) | collective-permute-done | bytes 335904 | tf_op jit(solution)/shard_map/ppermute | solution.py:26
  32.3 0.1 collective-permute-done.6
  32.4 0.0 collective-permute-start.9
  32.4 0.5 collective-permute-start.10
  32.9 0.0 collective-permute-start.11
  32.9 1.4 %collective-permute-start.12 = (bf16[8,5248]{1,0:T(8,128)(2,1)S(1)}, bf16[8,5248]{1,0:T(8,128)(2,1)S(1)}, u32[]{:S(2)}, u32[]{:S(2)}) collective-permute-start(bf16[8,5248]{1,0:T(8,128)(2,1)S(1)} %get-tuple-element.52), channel_id=1, source_target_pairs={{0,2},{1,3},{2,0},{3,1},{4,6},{5,7},{6,4},{7,5},{8,10},{9,11},{10,... | collective-permute-start | bytes 251912 | tf_op jit(solution)/shard_map/ppermute | solution.py:26
  34.3 2.6 %collective-permute-start.13 = (bf16[8,5248]{1,0:T(8,128)(2,1)S(1)}, bf16[8,5248]{1,0:T(8,128)(2,1)S(1)}, u32[]{:S(2)}, u32[]{:S(2)}) collective-permute-start(bf16[8,5248]{1,0:T(8,128)(2,1)S(1)} %get-tuple-element.53), channel_id=1, source_target_pairs={{0,4},{1,5},{2,6},{3,7},{4,0},{5,1},{6,2},{7,3},{8,12},{9,13},{10,... | collective-permute-start | bytes 251912 | tf_op jit(solution)/shard_map/ppermute | solution.py:26
  36.9 0.0 collective-permute-done.9
  36.9 0.6 %collective-permute-start.14 = (bf16[8,5248]{1,0:T(8,128)(2,1)S(1)}, bf16[8,5248]{1,0:T(8,128)(2,1)S(1)}, u32[]{:S(2)}, u32[]{:S(2)}) collective-permute-start(bf16[8,5248]{1,0:T(8,128)(2,1)S(1)} %get-tuple-element.54), channel_id=1, source_target_pairs={{0,6},{1,7},{2,4},{3,5},{4,2},{5,3},{6,0},{7,1},{8,14},{9,15},{10,... | collective-permute-start | bytes 251912 | tf_op jit(solution)/shard_map/ppermute | solution.py:26
  37.5 0.0 collective-permute-done.10
  37.5 0.0 collective-permute-done.11
  37.5 5.8 %shard_map.123 = (bf16[256,1024]{1,0:T(8,128)(2,1)S(1)}, bf16[256,1024]{1,0:T(8,128)(2,1)S(1)}, bf16[256,1024]{1,0:T(8,128)(2,1)S(1)}, bf16[2,640,256]{2,1,0:T(8...) custom-call(s32[4]{0:T(128)S(1)} %pad_add_fusion._.at_ref, ...), custom_call_target="tpu_custom_call" | custom-call | bytes 1 | tf_op jit(solution)/shard_map/pallas_call | solution.py:482
  43.3 0.0 collective-permute-done.12.back_refs_1_
  43.3 0.7 %collective-permute-done.13.back_refs_2_ = bf16[8,5248]{1,0:T(8,128)(2,1)S(1)} collective-permute-done((bf16[8,5248]{1,0:T(8,128)(2,1)S(1)}, bf16[8,5248]{1,0:T(8,128)(2,1)S(1)}, u32[]{:S(2)}, u32[]{:S(2)}) %collective-permute-start.13) | collective-permute-done | bytes 84000 | tf_op jit(solution)/shard_map/ppermute | solution.py:26
  44.0 0.0 collective-permute-done.14.back_refs_3_
  44.0 0.6 %shard_map.124.logit_refs_0_._ = f32[8,64]{1,0:T(8,128)S(1)} custom-call(s32[4]{0:T(128)S(1)} %pad_add_fusion._.at_ref, f32[3,8,64]{2,1,0:T(8,128)S(1)} %get-tuple-element.51.table_ref, bf16[8,5248]{1,0:T(8,128)(2,1)S(1)} %get-tuple-element.43.back_refs_0_, bf16[8,5248]{1,0:T(8,128)(2,1)S(1)} %collective-permute-done.12.back_refs_1_, ...), custom_call_target="tpu_custom_call" | custom-call | bytes 1 | tf_op jit(solution)/shard_map/pallas_call | solution.py:496
  44.6 1.7 %collective-permute-start.17 = (f32[8,64]{1,0:T(8,128)S(1)}, f32[8,64]{1,0:T(8,128)S(1)}, u32[]{:S(2)}, u32[]{:S(2)}) collective-permute-start(f32[8,64]{1,0:T(8,128)S(1)} %shard_map.124.logit_refs_0_._), channel_id=1, source_target_pairs={{0,24},{8,16},{16,8},{24,0},{1,25},{9,17},{17,9},{25,1},{2,26},{10... | collective-permute-start | bytes 6152 | tf_op jit(solution)/shard_map/ppermute | solution.py:26
  46.3 1.3 %collective-permute-start.16 = (f32[8,64]{1,0:T(8,128)S(1)}, f32[8,64]{1,0:T(8,128)S(1)}, u32[]{:S(2)}, u32[]{:S(2)}) collective-permute-start(f32[8,64]{1,0:T(8,128)S(1)} %shard_map.124.logit_refs_0_._), channel_id=1, source_target_pairs={{0,16},{8,24},{16,0},{24,8},{1,17},{9,25},{17,1},{25,9},{2,18},{10... | collective-permute-start | bytes 6152 | tf_op jit(solution)/shard_map/ppermute | solution.py:26
  47.6 0.5 %collective-permute-start.15 = (f32[8,64]{1,0:T(8,128)S(1)}, f32[8,64]{1,0:T(8,128)S(1)}, u32[]{:S(2)}, u32[]{:S(2)}) collective-permute-start(f32[8,64]{1,0:T(8,128)S(1)} %shard_map.124.logit_refs_0_._), channel_id=1, source_target_pairs={{0,8},{8,0},{16,24},{24,16},{1,9},{9,1},{17,25},{25,17},{2,10},{10... | collective-permute-start | bytes 6152 | tf_op jit(solution)/shard_map/ppermute | solution.py:26
  48.2 0.0 copy-start
  48.2 2.3 %shard_map.126 = (f32[640,1024]{1,0:T(8,128)}, f32[640,1024]{1,0:T(8,128)}, f32[640,1024]{1,0:T(8,128)}) custom-call(bf16[2,640,256]{2,1,0:T(8,128)(2,1)S(1)} %get-tuple-element.55._.turned_ref, bf16[256,1024]{1,0:T(8,128)(2,1)S(1)} %get-tuple-element.59.grad_refs_0_, ...), custom_call_target="tpu_custom_call", output_to_operand_aliasing={{0}: (5, {}), {1}: (6, {}), {2}: (7, {})} | custom-call | bytes 1 | tf_op jit(solution)/shard_map/pallas_call | solution.py:504
  50.5 0.0 collective-permute-done.17.logit_refs_3_
  50.5 0.0 collective-permute-done.16.logit_refs_2_
  50.5 0.7 %collective-permute-done.15.logit_refs_1_ = f32[8,64]{1,0:T(8,128)S(1)} collective-permute-done((f32[8,64]{1,0:T(8,128)S(1)}, f32[8,64]{1,0:T(8,128)S(1)}, u32[]{:S(2)}, u32[]{:S(2)}) %collective-permute-start.15) | collective-permute-done | bytes 2080 | tf_op jit(solution)/shard_map/ppermute | solution.py:26
  51.2 0.0 copy-done
  51.2 1.7 %shard_map.125 = (bf16[8,2560]{1,0:T(8,128)(2,1)}, bf16[8,2560]{1,0:T(8,128)(2,1)}, f32[8,2560]{1,0:T(8,128)}) custom-call(s32[4]{0:T(128)S(1)} %pad_add_fusion._.at_ref, bf16[256,5248]{1,0:T(8,128)(2,1)S(1)} %get-tuple-element.50.x_ref, f32[8,64]{1,0:T(8,128)S(1)} %shard_map.124.logit_refs_0_._, f32[8,64]{1,0:T(8,128)S(1)} %collective-permute-done.15.logit_refs_1_, ...), custom_call_target="tpu_custom_call" | custom-call | bytes 1 | tf_op jit(solution)/shard_map/pallas_call | solution.py:517
  (1 shorter events, 0.0 us)
Async XLA Ops:
  1.5 12.9 %collective-permute-start.2 = (bf16[8,5248]{1,0:T(8,128)(2,1)S(1)}, bf16[8,5248]{1,0:T(8,128)(2,1)S(1)}, u32[]{:S(2)}, u32[]{:S(2)}) collective-permute-start(bf16[8,5248]{1,0:T(8,128)(2,1)S(1)} %shard_map.118.piece_refs_0_), channel_id=1, source_target_pairs={{0,6},{1,7},{2,4},{3,5},{4,2},{5,3},{6,0},{7,1},{8,14},{9,15},{10,... | collective-permute-start | bytes 251912 | tf_op jit(solution)/shard_map/ppermute | solution.py:26
  6.7 7.8 %collective-permute-start.1 = (bf16[8,5248]{1,0:T(8,128)(2,1)S(1)}, bf16[8,5248]{1,0:T(8,128)(2,1)S(1)}, u32[]{:S(2)}, u32[]{:S(2)}) collective-permute-start(bf16[8,5248]{1,0:T(8,128)(2,1)S(1)} %shard_map.118.piece_refs_0_), channel_id=1, source_target_pairs={{0,4},{1,5},{2,6},{3,7},{4,0},{5,1},{6,2},{7,3},{8,12},{9,13},{10,... | collective-permute-start | bytes 251912 | tf_op jit(solution)/shard_map/ppermute | solution.py:26
  6.7 7.8 %collective-permute-start = (bf16[8,5248]{1,0:T(8,128)(2,1)S(1)}, bf16[8,5248]{1,0:T(8,128)(2,1)S(1)}, u32[]{:S(2)}, u32[]{:S(2)}) collective-permute-start(bf16[8,5248]{1,0:T(8,128)(2,1)S(1)} %shard_map.118.piece_refs_0_), channel_id=1, source_target_pairs={{0,2},{1,3},{2,0},{3,1},{4,6},{5,7},{6,4},{7,5},{8,10},{9,11},{10,... | collective-permute-start | bytes 251912 | tf_op jit(solution)/shard_map/ppermute | solution.py:26
  15.0 16.1 %collective-permute-start.8 = (bf16[4,8,5248]{2,1,0:T(8,128)(2,1)S(1)}, bf16[4,8,5248]{2,1,0:T(8,128)(2,1)S(1)}, u32[]{:S(2)}, u32[]{:S(2)}) collective-permute-start(bf16[4,8,5248]{2,1,0:T(8,128)(2,1)S(1)} %shard_map.120), channel_id=1, source_target_pairs={{0,24},{8,16},{16,8},{24,0},{1,25},{9,17},{17,9},{25,1},{2,26},{10... | collective-permute-start | bytes 1007624 | tf_op jit(solution)/shard_map/ppermute | solution.py:26
  17.7 14.6 %collective-permute-start.7 = (bf16[4,8,5248]{2,1,0:T(8,128)(2,1)S(1)}, bf16[4,8,5248]{2,1,0:T(8,128)(2,1)S(1)}, u32[]{:S(2)}, u32[]{:S(2)}) collective-permute-start(bf16[4,8,5248]{2,1,0:T(8,128)(2,1)S(1)} %shard_map.120), channel_id=1, source_target_pairs={{0,16},{8,24},{16,0},{24,8},{1,17},{9,25},{17,1},{25,9},{2,18},{10... | collective-permute-start | bytes 1007624 | tf_op jit(solution)/shard_map/ppermute | solution.py:26
  18.2 14.2 %collective-permute-start.6 = (bf16[4,8,5248]{2,1,0:T(8,128)(2,1)S(1)}, bf16[4,8,5248]{2,1,0:T(8,128)(2,1)S(1)}, u32[]{:S(2)}, u32[]{:S(2)}) collective-permute-start(bf16[4,8,5248]{2,1,0:T(8,128)(2,1)S(1)} %shard_map.120), channel_id=1, source_target_pairs={{0,8},{8,0},{16,24},{24,16},{1,9},{9,1},{17,25},{25,17},{2,10},{10... | collective-permute-start | bytes 1007624 | tf_op jit(solution)/shard_map/ppermute | solution.py:26
  18.6 1.6 %collective-permute-start.3 = (bf16[4,8,5248]{2,1,0:T(8,128)(2,1)S(1)}, bf16[4,8,5248]{2,1,0:T(8,128)(2,1)S(1)}, u32[]{:S(2)}, u32[]{:S(2)}) collective-permute-start(bf16[4,8,5248]{2,1,0:T(8,128)(2,1)S(1)} %shard_map.120), channel_id=1, source_target_pairs={{0,1},{1,0},{2,3},{3,2},{4,5},{5,4},{6,7},{7,6},{8,9},{9,8},{10,11... | collective-permute-start | bytes 1007624 | tf_op jit(solution)/shard_map/ppermute | solution.py:26
  28.8 1.7 %collective-permute-start.4 = (bf16[4,8,5120]{2,1,0:T(8,128)(2,1)S(1)}, bf16[4,8,5120]{2,1,0:T(8,128)(2,1)S(1)}, u32[]{:S(2)}, u32[]{:S(2)}) collective-permute-start(bf16[4,8,5120]{2,1,0:T(8,128)(2,1)S(1)} %bitcast.31), channel_id=1, source_target_pairs={{0,1},{1,0},{2,3},{3,2},{4,5},{5,4},{6,7},{7,6},{8,9},{9,8},{10,11... | collective-permute-start | bytes 983048 | tf_op jit(solution)/shard_map/ppermute | solution.py:26
  29.0 1.5 %collective-permute-start.5 = (f32[8,64]{1,0:T(8,128)S(1)}, f32[8,64]{1,0:T(8,128)S(1)}, u32[]{:S(2)}, u32[]{:S(2)}) collective-permute-start(f32[8,64]{1,0:T(8,128)S(1)} %get-tuple-element.42.pull_ref), channel_id=1, source_target_pairs={{0,1},{1,0},{2,3},{3,2},{4,5},{5,4},{6,7},{7,6},{8,9},{9,8},{10,11... | collective-permute-start | bytes 6152 | tf_op jit(solution)/shard_map/ppermute | solution.py:26
  32.4 4.5 %collective-permute-start.9 = (bf16[4,8,5248]{2,1,0:T(8,128)(2,1)S(1)}, bf16[4,8,5248]{2,1,0:T(8,128)(2,1)S(1)}, u32[]{:S(2)}, u32[]{:S(2)}) collective-permute-start(bf16[4,8,5248]{2,1,0:T(8,128)(2,1)S(1)} %collective-permute-done.6), channel_id=1, source_target_pairs={{0,1},{1,0},{2,3},{3,2},{4,5},{5,4},{6,7},{7,6},{8,9},{9,8},{10,11... | collective-permute-start | bytes 1007624 | tf_op jit(solution)/shard_map/ppermute | solution.py:26
  32.4 5.1 %collective-permute-start.10 = (bf16[4,8,5248]{2,1,0:T(8,128)(2,1)S(1)}, bf16[4,8,5248]{2,1,0:T(8,128)(2,1)S(1)}, u32[]{:S(2)}, u32[]{:S(2)}) collective-permute-start(bf16[4,8,5248]{2,1,0:T(8,128)(2,1)S(1)} %collective-permute-done.7), channel_id=1, source_target_pairs={{0,1},{1,0},{2,3},{3,2},{4,5},{5,4},{6,7},{7,6},{8,9},{9,8},{10,11... | collective-permute-start | bytes 1007624 | tf_op jit(solution)/shard_map/ppermute | solution.py:26
  32.9 4.6 %collective-permute-start.11 = (bf16[4,8,5248]{2,1,0:T(8,128)(2,1)S(1)}, bf16[4,8,5248]{2,1,0:T(8,128)(2,1)S(1)}, u32[]{:S(2)}, u32[]{:S(2)}) collective-permute-start(bf16[4,8,5248]{2,1,0:T(8,128)(2,1)S(1)} %collective-permute-done.8), channel_id=1, source_target_pairs={{0,1},{1,0},{2,3},{3,2},{4,5},{5,4},{6,7},{7,6},{8,9},{9,8},{10,11... | collective-permute-start | bytes 1007624 | tf_op jit(solution)/shard_map/ppermute | solution.py:26
  32.9 10.4 %collective-permute-start.12 = (bf16[8,5248]{1,0:T(8,128)(2,1)S(1)}, bf16[8,5248]{1,0:T(8,128)(2,1)S(1)}, u32[]{:S(2)}, u32[]{:S(2)}) collective-permute-start(bf16[8,5248]{1,0:T(8,128)(2,1)S(1)} %get-tuple-element.52), channel_id=1, source_target_pairs={{0,2},{1,3},{2,0},{3,1},{4,6},{5,7},{6,4},{7,5},{8,10},{9,11},{10,... | collective-permute-start | bytes 251912 | tf_op jit(solution)/shard_map/ppermute | solution.py:26
  34.3 9.8 %collective-permute-start.13 = (bf16[8,5248]{1,0:T(8,128)(2,1)S(1)}, bf16[8,5248]{1,0:T(8,128)(2,1)S(1)}, u32[]{:S(2)}, u32[]{:S(2)}) collective-permute-start(bf16[8,5248]{1,0:T(8,128)(2,1)S(1)} %get-tuple-element.53), channel_id=1, source_target_pairs={{0,4},{1,5},{2,6},{3,7},{4,0},{5,1},{6,2},{7,3},{8,12},{9,13},{10,... | collective-permute-start | bytes 251912 | tf_op jit(solution)/shard_map/ppermute | solution.py:26
  36.9 7.1 %collective-permute-start.14 = (bf16[8,5248]{1,0:T(8,128)(2,1)S(1)}, bf16[8,5248]{1,0:T(8,128)(2,1)S(1)}, u32[]{:S(2)}, u32[]{:S(2)}) collective-permute-start(bf16[8,5248]{1,0:T(8,128)(2,1)S(1)} %get-tuple-element.54), channel_id=1, source_target_pairs={{0,6},{1,7},{2,4},{3,5},{4,2},{5,3},{6,0},{7,1},{8,14},{9,15},{10,... | collective-permute-start | bytes 251912 | tf_op jit(solution)/shard_map/ppermute | solution.py:26
  44.6 5.9 %collective-permute-start.17 = (f32[8,64]{1,0:T(8,128)S(1)}, f32[8,64]{1,0:T(8,128)S(1)}, u32[]{:S(2)}, u32[]{:S(2)}) collective-permute-start(f32[8,64]{1,0:T(8,128)S(1)} %shard_map.124.logit_refs_0_._), channel_id=1, source_target_pairs={{0,24},{8,16},{16,8},{24,0},{1,25},{9,17},{17,9},{25,1},{2,26},{10... | collective-permute-start | bytes 6152 | tf_op jit(solution)/shard_map/ppermute | solution.py:26
  46.3 4.2 %collective-permute-start.16 = (f32[8,64]{1,0:T(8,128)S(1)}, f32[8,64]{1,0:T(8,128)S(1)}, u32[]{:S(2)}, u32[]{:S(2)}) collective-permute-start(f32[8,64]{1,0:T(8,128)S(1)} %shard_map.124.logit_refs_0_._), channel_id=1, source_target_pairs={{0,16},{8,24},{16,0},{24,8},{1,17},{9,25},{17,1},{25,9},{2,18},{10... | collective-permute-start | bytes 6152 | tf_op jit(solution)/shard_map/ppermute | solution.py:26
  47.6 3.6 %collective-permute-start.15 = (f32[8,64]{1,0:T(8,128)S(1)}, f32[8,64]{1,0:T(8,128)S(1)}, u32[]{:S(2)}, u32[]{:S(2)}) collective-permute-start(f32[8,64]{1,0:T(8,128)S(1)} %shard_map.124.logit_refs_0_._), channel_id=1, source_target_pairs={{0,8},{8,0},{16,24},{24,16},{1,9},{9,1},{17,25},{25,17},{2,10},{10... | collective-permute-start | bytes 6152 | tf_op jit(solution)/shard_map/ppermute | solution.py:26
  48.2 3.1 %copy-start = (f32[2560,8]{0,1:T(8,128)S(1)}, f32[2560,8]{0,1:T(8,128)}, u32[]{:S(2)}) copy-start(f32[2560,8]{0,1:T(8,128)} %param.9) | copy-start | bytes 245764

commit v9 on v8

--- a/solution.py
+++ b/solution.py
@@ -422,7 +422,6 @@
     portion = features // groups
     at = jnp.stack([me % 2, me, lax.axis_index("dp"), me // 2]).astype(jnp.int32)
     router_t = router.T
-    parts = jnp.concatenate(three_parts(router_t), axis=0)
     weight_kinds = [pltpu.VMEM(w.shape, w.dtype) for w in (w_gate, w_up, w_down)]
     small = jax.ShapeDtypeStruct((experts, group_rows), F32)
     in_hbm_spec = pl.BlockSpec(memory_space=pltpu.HBM)
@@ -451,6 +450,8 @@
     )(at, pieces, weights[0])
     mine = [by_chip] + [swap(by_chip, "dp", m) for m in range(1, groups)]
     theirs = swap(by_chip, "expert", 1)
+    _, late_router = lax.optimization_barrier([by_chip, router_t])
+    parts = jnp.concatenate(three_parts(late_router), axis=0)
 
     rows = jax.ShapeDtypeStruct((half, 2 * features), BF16)
     grad = jax.ShapeDtypeStruct((group_rows, hidden_units), BF16)

time: 53.2 us -> 52.2 us (0.981)
  other arithmetic: 0.99 us -> 0.11 us
    convert_element_type x1, other arithmetic: 0.91 us -> 0.02 us  [three_parts(): parts.append(part.astype(BF16))]
  transfers between devices with their start and end apart: 18 -> 18, of which waited for: 6 -> 7; matrix products, arithmetic and copies ran while one was open for 2% -> 0% of each run, Pallas kernels for 44% -> 45%
where the time goes in v9:
time: 52.2 us; the launch traced here: 52 us
  Pallas kernels  27.1 us (52%)
  starting transfers between devices  18.3 us (35%)
  waiting for transfers between devices  5.75 us (11%)
  between operations  0.76 us (1%)
    ppermute x18, starting transfers between devices, swap(): return lax.ppermute(x, axis, [(i, i ^ mask) for i in range(count)])  18.3 us
    pallas_call x1, Pallas kernels, kernels_plan(): call(own_kernel, [rows] * 2 + [grad] * 3 + [small, jax.ShapeDtypeStruct((...  8.5 us
    pallas_call x1, Pallas kernels, kernels_plan(): call(load_kernel, weight_kinds, [IN_SMEM] + [in_hbm_spec] * 3, [IN_VMEM]...  6.11 us
    pallas_call x1, Pallas kernels, kernels_plan(): call(far_kernel, in_vmem + [pltpu.VMEM((2, portion, count), BF16), pltpu....  5.78 us
    ppermute x18, waiting for transfers between devices, swap(): return lax.ppermute(x, axis, [(i, i ^ mask) for i in range(count)])  5.75 us
    pallas_call x1, Pallas kernels, kernels_plan(): call(weight_kernel, [pltpu.HBM((portion, hidden_units), F32)] * 3, [IN_VM...  2.3 us
    pallas_call x1, Pallas kernels, kernels_plan(): call(last_kernel, [rows] * 2 + [jax.ShapeDtypeStruct((experts, features),...  1.72 us
  transfers between devices with their start and end apart: 18, of which 7 were waited for; matrix products, arithmetic and copies ran while one was open for 0% of the time, Pallas kernels for 45%

profile of v9, /device:TPU:0, one launch (start us, length us, event | category | flops | bytes accessed | tf_op | source)
XLA Modules:
  0.0 52.0 jit_solution(15664513726761309600)
XLA Ops:
  0.6 0.9 %shard_map.118.piece_refs_0_ = bf16[8,5248]{1,0:T(8,128)(2,1)S(1)} custom-call(bf16[8,2560]{1,0:T(8,128)(2,1)} %tokens_hbm.1, bf16[8,2560]{1,0:T(8,128)(2,1)} %cot_hbm.1, s32[8,6]{1,0:T(8,128)} %routes_hbm.1), custom_call_target="tpu_custom_call" | custom-call | bytes 1 | tf_op jit(solution)/shard_map/pallas_call | solution.py:430
  1.5 5.1 %collective-permute-start.2 = (bf16[8,5248]{1,0:T(8,128)(2,1)S(1)}, bf16[8,5248]{1,0:T(8,128)(2,1)S(1)}, u32[]{:S(2)}, u32[]{:S(2)}) collective-permute-start(bf16[8,5248]{1,0:T(8,128)(2,1)S(1)} %shard_map.118.piece_refs_0_), channel_id=1, source_target_pairs={{0,6},{1,7},{2,4},{3,5},{4,2},{5,3},{6,0},{7,1},{8,14},{9,15},{10,... | collective-permute-start | bytes 251912 | tf_op jit(solution)/shard_map/ppermute | solution.py:26
  6.7 0.0 collective-permute-start.1
  6.7 0.6 %collective-permute-start = (bf16[8,5248]{1,0:T(8,128)(2,1)S(1)}, bf16[8,5248]{1,0:T(8,128)(2,1)S(1)}, u32[]{:S(2)}, u32[]{:S(2)}) collective-permute-start(bf16[8,5248]{1,0:T(8,128)(2,1)S(1)} %shard_map.118.piece_refs_0_), channel_id=1, source_target_pairs={{0,2},{1,3},{2,0},{3,1},{4,6},{5,7},{6,4},{7,5},{8,10},{9,11},{10,... | collective-permute-start | bytes 251912 | tf_op jit(solution)/shard_map/ppermute | solution.py:26
  7.3 0.1 pad_add_fusion._.at_ref
  7.4 6.1 %shard_map.119 = (bf16[2560,1024]{1,0:T(8,128)(2,1)S(1)}, bf16[2560,1024]{1,0:T(8,128)(2,1)S(1)}, bf16[2560,1024]{1,0:T(8,128)(2,1)S(1)}) custom-call(s32[4]{0:T(128)S(1)} %pad_add_fusion._.at_ref, bf16[2560,1024]{1,0:T(8,128)(2,1)} %refs_0_.1, bf16[2560,1024]{1,0:T(8,128)(2,1)} %refs_1_.1, bf16[2560,1024]{1,0:T(8,128)(2,1)} %refs_2_.1), custom_call_target="tpu_custom_call" | custom-call | bytes 1 | tf_op jit(solution)/shard_map/pallas_call | solution.py:438
  13.5 0.0 collective-permute-done.2.piece_refs_3_
  13.5 0.2 collective-permute-done.1.piece_refs_2_
  13.7 0.0 collective-permute-done.piece_refs_1_
  13.7 0.0 copy-start
  13.7 0.6 %shard_map.120 = bf16[4,8,5248]{2,1,0:T(8,128)(2,1)S(1)} custom-call(s32[4]{0:T(128)S(1)} %pad_add_fusion._.at_ref, bf16[8,5248]{1,0:T(8,128)(2,1)S(1)} %shard_map.118.piece_refs_0_, bf16[8,5248]{1,0:T(8,128)(2,1)S(1)} %collective-permute-done.piece_refs_1_, bf16[8,5248]{1,0:T(8,128)(2,1)S(1)} %collective-permute-done.1.piece_refs_2_, ...), custom_call_target="tpu_custom_call" | custom-call | bytes 1 | tf_op jit(solution)/shard_map/pallas_call | solution.py:445
  14.3 2.5 %collective-permute-start.8 = (bf16[4,8,5248]{2,1,0:T(8,128)(2,1)S(1)}, bf16[4,8,5248]{2,1,0:T(8,128)(2,1)S(1)}, u32[]{:S(2)}, u32[]{:S(2)}) collective-permute-start(bf16[4,8,5248]{2,1,0:T(8,128)(2,1)S(1)} %shard_map.120), channel_id=1, source_target_pairs={{0,24},{8,16},{16,8},{24,0},{1,25},{9,17},{17,9},{25,1},{2,26},{10... | collective-permute-start | bytes 1007624 | tf_op jit(solution)/shard_map/ppermute | solution.py:26
  16.8 0.5 collective-permute-start.7
  17.3 0.5 %collective-permute-start.6 = (bf16[4,8,5248]{2,1,0:T(8,128)(2,1)S(1)}, bf16[4,8,5248]{2,1,0:T(8,128)(2,1)S(1)}, u32[]{:S(2)}, u32[]{:S(2)}) collective-permute-start(bf16[4,8,5248]{2,1,0:T(8,128)(2,1)S(1)} %shard_map.120), channel_id=1, source_target_pairs={{0,8},{8,0},{16,24},{24,16},{1,9},{9,1},{17,25},{25,17},{2,10},{10... | collective-permute-start | bytes 1007624 | tf_op jit(solution)/shard_map/ppermute | solution.py:26
  17.8 0.0 collective-permute-start.3
  17.8 0.0 copy-done
  17.9 1.6 %collective-permute-done.3 = bf16[4,8,5248]{2,1,0:T(8,128)(2,1)S(1)} collective-permute-done((bf16[4,8,5248]{2,1,0:T(8,128)(2,1)S(1)}, bf16[4,8,5248]{2,1,0:T(8,128)(2,1)S(1)}, u32[]{:S(2)}, u32[]{:S(2)}) %collective-permute-start.3) | collective-permute-done | bytes 335904 | tf_op jit(solution)/shard_map/ppermute | solution.py:26
  19.5 8.5 %shard_map.121 = (bf16[32,5120]{1,0:T(8,128)(2,1)S(1)}, bf16[32,5120]{1,0:T(8,128)(2,1)S(1)}, bf16[64,1024]{1,0:T(8,128)(2,1)S(1)}, bf16[64,1024]{1,0:T(8,128)(2...) custom-call(s32[4]{0:T(128)S(1)} %pad_add_fusion._.at_ref, ...), custom_call_target="tpu_custom_call" | custom-call | bytes 1 | tf_op jit(solution)/shard_map/pallas_call | solution.py:458
  28.0 0.2 collective-permute-start.4
  28.2 0.4 collective-permute-start.5
  28.6 1.1 %collective-permute-done.5.other_pull_ref = f32[8,64]{1,0:T(8,128)S(1)} collective-permute-done((f32[8,64]{1,0:T(8,128)S(1)}, f32[8,64]{1,0:T(8,128)S(1)}, u32[]{:S(2)}, u32[]{:S(2)}) %collective-permute-start.5) | collective-permute-done | bytes 2080 | tf_op jit(solution)/shard_map/ppermute | solution.py:26
  29.7 0.0 collective-permute-done.4.other_ref
  29.7 0.6 %shard_map.122 = (bf16[8,5248]{1,0:T(8,128)(2,1)S(1)}, bf16[8,5248]{1,0:T(8,128)(2,1)S(1)}, bf16[8,5248]{1,0:T(8,128)(2,1)S(1)}, bf16[8,5248]{1,0:T(8,128)(2,1)S(1)}) custom-call(s32[4]{0:T(128)S(1)} %pad_add_fusion._.at_ref, bf16[4,8,5120]{2,1,0:T(8,128)(2,1)S(1)} %bitcast.26, bf16[4,8,5120]{2,1,0:T(8,128)(2,1)S(1)} %collective-permute-done.4.other_ref, ...), custom_call_target="tpu_custom_call" | custom-call | bytes 1 | tf_op jit(solution)/shard_map/pallas_call | solution.py:468
  30.3 0.0 collective-permute-done.8
  30.3 1.2 %collective-permute-done.7 = bf16[4,8,5248]{2,1,0:T(8,128)(2,1)S(1)} collective-permute-done((bf16[4,8,5248]{2,1,0:T(8,128)(2,1)S(1)}, bf16[4,8,5248]{2,1,0:T(8,128)(2,1)S(1)}, u32[]{:S(2)}, u32[]{:S(2)}) %collective-permute-start.7) | collective-permute-done | bytes 335904 | tf_op jit(solution)/shard_map/ppermute | solution.py:26
  31.5 0.2 collective-permute-done.6
  31.7 0.0 collective-permute-start.9
  31.7 0.5 collective-permute-start.10
  32.2 0.0 collective-permute-start.11
  32.2 1.1 %collective-permute-start.12 = (bf16[8,5248]{1,0:T(8,128)(2,1)S(1)}, bf16[8,5248]{1,0:T(8,128)(2,1)S(1)}, u32[]{:S(2)}, u32[]{:S(2)}) collective-permute-start(bf16[8,5248]{1,0:T(8,128)(2,1)S(1)} %get-tuple-element.54), channel_id=1, source_target_pairs={{0,2},{1,3},{2,0},{3,1},{4,6},{5,7},{6,4},{7,5},{8,10},{9,11},{10,... | collective-permute-start | bytes 251912 | tf_op jit(solution)/shard_map/ppermute | solution.py:26
  33.4 2.6 %collective-permute-start.13 = (bf16[8,5248]{1,0:T(8,128)(2,1)S(1)}, bf16[8,5248]{1,0:T(8,128)(2,1)S(1)}, u32[]{:S(2)}, u32[]{:S(2)}) collective-permute-start(bf16[8,5248]{1,0:T(8,128)(2,1)S(1)} %get-tuple-element.55), channel_id=1, source_target_pairs={{0,4},{1,5},{2,6},{3,7},{4,0},{5,1},{6,2},{7,3},{8,12},{9,13},{10,... | collective-permute-start | bytes 251912 | tf_op jit(solution)/shard_map/ppermute | solution.py:26
  36.0 0.0 collective-permute-done.9
  36.0 0.6 %collective-permute-start.14 = (bf16[8,5248]{1,0:T(8,128)(2,1)S(1)}, bf16[8,5248]{1,0:T(8,128)(2,1)S(1)}, u32[]{:S(2)}, u32[]{:S(2)}) collective-permute-start(bf16[8,5248]{1,0:T(8,128)(2,1)S(1)} %get-tuple-element.56), channel_id=1, source_target_pairs={{0,6},{1,7},{2,4},{3,5},{4,2},{5,3},{6,0},{7,1},{8,14},{9,15},{10,... | collective-permute-start | bytes 251912 | tf_op jit(solution)/shard_map/ppermute | solution.py:26
  36.6 0.0 collective-permute-done.10
  36.6 0.0 collective-permute-done.11
  36.6 5.8 %shard_map.123 = (bf16[256,1024]{1,0:T(8,128)(2,1)S(1)}, bf16[256,1024]{1,0:T(8,128)(2,1)S(1)}, bf16[256,1024]{1,0:T(8,128)(2,1)S(1)}, bf16[2,640,256]{2,1,0:T(8...) custom-call(s32[4]{0:T(128)S(1)} %pad_add_fusion._.at_ref, ...), custom_call_target="tpu_custom_call" | custom-call | bytes 1 | tf_op jit(solution)/shard_map/pallas_call | solution.py:483
  42.4 0.0 collective-permute-done.12.back_refs_1_
  42.4 0.7 %collective-permute-done.13.back_refs_2_ = bf16[8,5248]{1,0:T(8,128)(2,1)S(1)} collective-permute-done((bf16[8,5248]{1,0:T(8,128)(2,1)S(1)}, bf16[8,5248]{1,0:T(8,128)(2,1)S(1)}, u32[]{:S(2)}, u32[]{:S(2)}) %collective-permute-start.13) | collective-permute-done | bytes 84000 | tf_op jit(solution)/shard_map/ppermute | solution.py:26
  43.1 0.0 collective-permute-done.14.back_refs_3_
  43.1 0.6 %shard_map.124.logit_refs_0_._ = f32[8,64]{1,0:T(8,128)S(1)} custom-call(s32[4]{0:T(128)S(1)} %pad_add_fusion._.at_ref, f32[3,8,64]{2,1,0:T(8,128)S(1)} %get-tuple-element.53.table_ref, bf16[8,5248]{1,0:T(8,128)(2,1)S(1)} %get-tuple-element.45.back_refs_0_, bf16[8,5248]{1,0:T(8,128)(2,1)S(1)} %collective-permute-done.12.back_refs_1_, ...), custom_call_target="tpu_custom_call" | custom-call | bytes 1 | tf_op jit(solution)/shard_map/pallas_call | solution.py:497
  43.7 1.7 %collective-permute-start.17 = (f32[8,64]{1,0:T(8,128)S(1)}, f32[8,64]{1,0:T(8,128)S(1)}, u32[]{:S(2)}, u32[]{:S(2)}) collective-permute-start(f32[8,64]{1,0:T(8,128)S(1)} %shard_map.124.logit_refs_0_._), channel_id=1, source_target_pairs={{0,24},{8,16},{16,8},{24,0},{1,25},{9,17},{17,9},{25,1},{2,26},{10... | collective-permute-start | bytes 6152 | tf_op jit(solution)/shard_map/ppermute | solution.py:26
  45.4 1.3 %collective-permute-start.16 = (f32[8,64]{1,0:T(8,128)S(1)}, f32[8,64]{1,0:T(8,128)S(1)}, u32[]{:S(2)}, u32[]{:S(2)}) collective-permute-start(f32[8,64]{1,0:T(8,128)S(1)} %shard_map.124.logit_refs_0_._), channel_id=1, source_target_pairs={{0,16},{8,24},{16,0},{24,8},{1,17},{9,25},{17,1},{25,9},{2,18},{10... | collective-permute-start | bytes 6152 | tf_op jit(solution)/shard_map/ppermute | solution.py:26
  46.7 0.5 %collective-permute-start.15 = (f32[8,64]{1,0:T(8,128)S(1)}, f32[8,64]{1,0:T(8,128)S(1)}, u32[]{:S(2)}, u32[]{:S(2)}) collective-permute-start(f32[8,64]{1,0:T(8,128)S(1)} %shard_map.124.logit_refs_0_._), channel_id=1, source_target_pairs={{0,8},{8,0},{16,24},{24,16},{1,9},{9,1},{17,25},{25,17},{2,10},{10... | collective-permute-start | bytes 6152 | tf_op jit(solution)/shard_map/ppermute | solution.py:26
  47.2 2.3 %shard_map.126 = (f32[640,1024]{1,0:T(8,128)}, f32[640,1024]{1,0:T(8,128)}, f32[640,1024]{1,0:T(8,128)}) custom-call(bf16[2,640,256]{2,1,0:T(8,128)(2,1)S(1)} %get-tuple-element.57._.turned_ref, bf16[256,1024]{1,0:T(8,128)(2,1)S(1)} %get-tuple-element.61.grad_refs_0_, ...), custom_call_target="tpu_custom_call", output_to_operand_aliasing={{0}: (5, {}), {1}: (6, {}), {2}: (7, {})} | custom-call | bytes 1 | tf_op jit(solution)/shard_map/pallas_call | solution.py:505
  49.6 0.0 collective-permute-done.17.logit_refs_3_
  49.6 0.0 collective-permute-done.16.logit_refs_2_
  49.6 0.7 %collective-permute-done.15.logit_refs_1_ = f32[8,64]{1,0:T(8,128)S(1)} collective-permute-done((f32[8,64]{1,0:T(8,128)S(1)}, f32[8,64]{1,0:T(8,128)S(1)}, u32[]{:S(2)}, u32[]{:S(2)}) %collective-permute-start.15) | collective-permute-done | bytes 2080 | tf_op jit(solution)/shard_map/ppermute | solution.py:26
  50.3 1.7 %shard_map.125 = (bf16[8,2560]{1,0:T(8,128)(2,1)}, bf16[8,2560]{1,0:T(8,128)(2,1)}, f32[8,2560]{1,0:T(8,128)}) custom-call(s32[4]{0:T(128)S(1)} %pad_add_fusion._.at_ref, bf16[256,5248]{1,0:T(8,128)(2,1)S(1)} %get-tuple-element.52.x_ref, f32[8,64]{1,0:T(8,128)S(1)} %shard_map.124.logit_refs_0_._, f32[8,64]{1,0:T(8,128)S(1)} %collective-permute-done.15.logit_refs_1_, ...), custom_call_target="tpu_custom_call" | custom-call | bytes 1 | tf_op jit(solution)/shard_map/pallas_call | solution.py:518
  (2 shorter events, 0.0 us)
Async XLA Ops:
  1.5 12.0 %collective-permute-start.2 = (bf16[8,5248]{1,0:T(8,128)(2,1)S(1)}, bf16[8,5248]{1,0:T(8,128)(2,1)S(1)}, u32[]{:S(2)}, u32[]{:S(2)}) collective-permute-start(bf16[8,5248]{1,0:T(8,128)(2,1)S(1)} %shard_map.118.piece_refs_0_), channel_id=1, source_target_pairs={{0,6},{1,7},{2,4},{3,5},{4,2},{5,3},{6,0},{7,1},{8,14},{9,15},{10,... | collective-permute-start | bytes 251912 | tf_op jit(solution)/shard_map/ppermute | solution.py:26
  6.7 7.0 %collective-permute-start.1 = (bf16[8,5248]{1,0:T(8,128)(2,1)S(1)}, bf16[8,5248]{1,0:T(8,128)(2,1)S(1)}, u32[]{:S(2)}, u32[]{:S(2)}) collective-permute-start(bf16[8,5248]{1,0:T(8,128)(2,1)S(1)} %shard_map.118.piece_refs_0_), channel_id=1, source_target_pairs={{0,4},{1,5},{2,6},{3,7},{4,0},{5,1},{6,2},{7,3},{8,12},{9,13},{10,... | collective-permute-start | bytes 251912 | tf_op jit(solution)/shard_map/ppermute | solution.py:26
  6.7 7.0 %collective-permute-start = (bf16[8,5248]{1,0:T(8,128)(2,1)S(1)}, bf16[8,5248]{1,0:T(8,128)(2,1)S(1)}, u32[]{:S(2)}, u32[]{:S(2)}) collective-permute-start(bf16[8,5248]{1,0:T(8,128)(2,1)S(1)} %shard_map.118.piece_refs_0_), channel_id=1, source_target_pairs={{0,2},{1,3},{2,0},{3,1},{4,6},{5,7},{6,4},{7,5},{8,10},{9,11},{10,... | collective-permute-start | bytes 251912 | tf_op jit(solution)/shard_map/ppermute | solution.py:26
  13.7 4.1 %copy-start = (f32[2560,8]{0,1:T(8,128)S(1)}, f32[2560,8]{0,1:T(8,128)}, u32[]{:S(2)}) copy-start(f32[2560,8]{0,1:T(8,128)} %param.9) | copy-start | bytes 245764
  14.3 16.0 %collective-permute-start.8 = (bf16[4,8,5248]{2,1,0:T(8,128)(2,1)S(1)}, bf16[4,8,5248]{2,1,0:T(8,128)(2,1)S(1)}, u32[]{:S(2)}, u32[]{:S(2)}) collective-permute-start(bf16[4,8,5248]{2,1,0:T(8,128)(2,1)S(1)} %shard_map.120), channel_id=1, source_target_pairs={{0,24},{8,16},{16,8},{24,0},{1,25},{9,17},{17,9},{25,1},{2,26},{10... | collective-permute-start | bytes 1007624 | tf_op jit(solution)/shard_map/ppermute | solution.py:26
  16.8 14.7 %collective-permute-start.7 = (bf16[4,8,5248]{2,1,0:T(8,128)(2,1)S(1)}, bf16[4,8,5248]{2,1,0:T(8,128)(2,1)S(1)}, u32[]{:S(2)}, u32[]{:S(2)}) collective-permute-start(bf16[4,8,5248]{2,1,0:T(8,128)(2,1)S(1)} %shard_map.120), channel_id=1, source_target_pairs={{0,16},{8,24},{16,0},{24,8},{1,17},{9,25},{17,1},{25,9},{2,18},{10... | collective-permute-start | bytes 1007624 | tf_op jit(solution)/shard_map/ppermute | solution.py:26
  17.3 14.4 %collective-permute-start.6 = (bf16[4,8,5248]{2,1,0:T(8,128)(2,1)S(1)}, bf16[4,8,5248]{2,1,0:T(8,128)(2,1)S(1)}, u32[]{:S(2)}, u32[]{:S(2)}) collective-permute-start(bf16[4,8,5248]{2,1,0:T(8,128)(2,1)S(1)} %shard_map.120), channel_id=1, source_target_pairs={{0,8},{8,0},{16,24},{24,16},{1,9},{9,1},{17,25},{25,17},{2,10},{10... | collective-permute-start | bytes 1007624 | tf_op jit(solution)/shard_map/ppermute | solution.py:26
  17.8 1.6 %collective-permute-start.3 = (bf16[4,8,5248]{2,1,0:T(8,128)(2,1)S(1)}, bf16[4,8,5248]{2,1,0:T(8,128)(2,1)S(1)}, u32[]{:S(2)}, u32[]{:S(2)}) collective-permute-start(bf16[4,8,5248]{2,1,0:T(8,128)(2,1)S(1)} %shard_map.120), channel_id=1, source_target_pairs={{0,1},{1,0},{2,3},{3,2},{4,5},{5,4},{6,7},{7,6},{8,9},{9,8},{10,11... | collective-permute-start | bytes 1007624 | tf_op jit(solution)/shard_map/ppermute | solution.py:26
  28.0 1.7 %collective-permute-start.4 = (bf16[4,8,5120]{2,1,0:T(8,128)(2,1)S(1)}, bf16[4,8,5120]{2,1,0:T(8,128)(2,1)S(1)}, u32[]{:S(2)}, u32[]{:S(2)}) collective-permute-start(bf16[4,8,5120]{2,1,0:T(8,128)(2,1)S(1)} %bitcast.29), channel_id=1, source_target_pairs={{0,1},{1,0},{2,3},{3,2},{4,5},{5,4},{6,7},{7,6},{8,9},{9,8},{10,11... | collective-permute-start | bytes 983048 | tf_op jit(solution)/shard_map/ppermute | solution.py:26
  28.2 1.5 %collective-permute-start.5 = (f32[8,64]{1,0:T(8,128)S(1)}, f32[8,64]{1,0:T(8,128)S(1)}, u32[]{:S(2)}, u32[]{:S(2)}) collective-permute-start(f32[8,64]{1,0:T(8,128)S(1)} %get-tuple-element.44.pull_ref), channel_id=1, source_target_pairs={{0,1},{1,0},{2,3},{3,2},{4,5},{5,4},{6,7},{7,6},{8,9},{9,8},{10,11... | collective-permute-start | bytes 6152 | tf_op jit(solution)/shard_map/ppermute | solution.py:26
  31.7 4.3 %collective-permute-start.9 = (bf16[4,8,5248]{2,1,0:T(8,128)(2,1)S(1)}, bf16[4,8,5248]{2,1,0:T(8,128)(2,1)S(1)}, u32[]{:S(2)}, u32[]{:S(2)}) collective-permute-start(bf16[4,8,5248]{2,1,0:T(8,128)(2,1)S(1)} %collective-permute-done.6), channel_id=1, source_target_pairs={{0,1},{1,0},{2,3},{3,2},{4,5},{5,4},{6,7},{7,6},{8,9},{9,8},{10,11... | collective-permute-start | bytes 1007624 | tf_op jit(solution)/shard_map/ppermute | solution.py:26
  31.7 4.9 %collective-permute-start.10 = (bf16[4,8,5248]{2,1,0:T(8,128)(2,1)S(1)}, bf16[4,8,5248]{2,1,0:T(8,128)(2,1)S(1)}, u32[]{:S(2)}, u32[]{:S(2)}) collective-permute-start(bf16[4,8,5248]{2,1,0:T(8,128)(2,1)S(1)} %collective-permute-done.7), channel_id=1, source_target_pairs={{0,1},{1,0},{2,3},{3,2},{4,5},{5,4},{6,7},{7,6},{8,9},{9,8},{10,11... | collective-permute-start | bytes 1007624 | tf_op jit(solution)/shard_map/ppermute | solution.py:26
  32.2 4.4 %collective-permute-start.11 = (bf16[4,8,5248]{2,1,0:T(8,128)(2,1)S(1)}, bf16[4,8,5248]{2,1,0:T(8,128)(2,1)S(1)}, u32[]{:S(2)}, u32[]{:S(2)}) collective-permute-start(bf16[4,8,5248]{2,1,0:T(8,128)(2,1)S(1)} %collective-permute-done.8), channel_id=1, source_target_pairs={{0,1},{1,0},{2,3},{3,2},{4,5},{5,4},{6,7},{7,6},{8,9},{9,8},{10,11... | collective-permute-start | bytes 1007624 | tf_op jit(solution)/shard_map/ppermute | solution.py:26
  32.2 10.2 %collective-permute-start.12 = (bf16[8,5248]{1,0:T(8,128)(2,1)S(1)}, bf16[8,5248]{1,0:T(8,128)(2,1)S(1)}, u32[]{:S(2)}, u32[]{:S(2)}) collective-permute-start(bf16[8,5248]{1,0:T(8,128)(2,1)S(1)} %get-tuple-element.54), channel_id=1, source_target_pairs={{0,2},{1,3},{2,0},{3,1},{4,6},{5,7},{6,4},{7,5},{8,10},{9,11},{10,... | collective-permute-start | bytes 251912 | tf_op jit(solution)/shard_map/ppermute | solution.py:26
  33.4 9.8 %collective-permute-start.13 = (bf16[8,5248]{1,0:T(8,128)(2,1)S(1)}, bf16[8,5248]{1,0:T(8,128)(2,1)S(1)}, u32[]{:S(2)}, u32[]{:S(2)}) collective-permute-start(bf16[8,5248]{1,0:T(8,128)(2,1)S(1)} %get-tuple-element.55), channel_id=1, source_target_pairs={{0,4},{1,5},{2,6},{3,7},{4,0},{5,1},{6,2},{7,3},{8,12},{9,13},{10,... | collective-permute-start | bytes 251912 | tf_op jit(solution)/shard_map/ppermute | solution.py:26
  36.0 7.1 %collective-permute-start.14 = (bf16[8,5248]{1,0:T(8,128)(2,1)S(1)}, bf16[8,5248]{1,0:T(8,128)(2,1)S(1)}, u32[]{:S(2)}, u32[]{:S(2)}) collective-permute-start(bf16[8,5248]{1,0:T(8,128)(2,1)S(1)} %get-tuple-element.56), channel_id=1, source_target_pairs={{0,6},{1,7},{2,4},{3,5},{4,2},{5,3},{6,0},{7,1},{8,14},{9,15},{10,... | collective-permute-start | bytes 251912 | tf_op jit(solution)/shard_map/ppermute | solution.py:26
  43.7 5.9 %collective-permute-start.17 = (f32[8,64]{1,0:T(8,128)S(1)}, f32[8,64]{1,0:T(8,128)S(1)}, u32[]{:S(2)}, u32[]{:S(2)}) collective-permute-start(f32[8,64]{1,0:T(8,128)S(1)} %shard_map.124.logit_refs_0_._), channel_id=1, source_target_pairs={{0,24},{8,16},{16,8},{24,0},{1,25},{9,17},{17,9},{25,1},{2,26},{10... | collective-permute-start | bytes 6152 | tf_op jit(solution)/shard_map/ppermute | solution.py:26
  45.4 4.2 %collective-permute-start.16 = (f32[8,64]{1,0:T(8,128)S(1)}, f32[8,64]{1,0:T(8,128)S(1)}, u32[]{:S(2)}, u32[]{:S(2)}) collective-permute-start(f32[8,64]{1,0:T(8,128)S(1)} %shard_map.124.logit_refs_0_._), channel_id=1, source_target_pairs={{0,16},{8,24},{16,0},{24,8},{1,17},{9,25},{17,1},{25,9},{2,18},{10... | collective-permute-start | bytes 6152 | tf_op jit(solution)/shard_map/ppermute | solution.py:26
  46.7 3.6 %collective-permute-start.15 = (f32[8,64]{1,0:T(8,128)S(1)}, f32[8,64]{1,0:T(8,128)S(1)}, u32[]{:S(2)}, u32[]{:S(2)}) collective-permute-start(f32[8,64]{1,0:T(8,128)S(1)} %shard_map.124.logit_refs_0_._), channel_id=1, source_target_pairs={{0,8},{8,0},{16,24},{24,16},{1,9},{9,1},{17,25},{25,17},{2,10},{10... | collective-permute-start | bytes 6152 | tf_op jit(solution)/shard_map/ppermute | solution.py:26

commit v10 on v9

--- a/solution.py
+++ b/solution.py
@@ -109,19 +109,20 @@
 
 def message_kernel(tokens_hbm, cot_hbm, routes_hbm, out_ref, tokens_ref, cot_ref, routes_ref, sems):
     count, features = tokens_ref.shape
-    pairs = ((tokens_hbm, tokens_ref), (cot_hbm, cot_ref), (routes_hbm, routes_ref))
+    pairs = ((routes_hbm, routes_ref), (tokens_hbm, tokens_ref), (cot_hbm, cot_ref))
     copies = [pltpu.make_async_copy(*pair, sems.at[i]) for i, pair in enumerate(pairs)]
     for copy in copies:
         copy.start()
-    for copy in copies:
-        copy.wait()
-    out_ref[:, :features] = tokens_ref[...]
-    out_ref[:, features : 2 * features] = cot_ref[...]
+    copies[0].wait()
     ids = lax.broadcasted_iota(jnp.int32, (count, LANES), 1)
     picked = jnp.zeros((count, LANES), F32)
     for k in range(routes_ref.shape[1]):
         picked += (routes_ref[:, k : k + 1] == ids).astype(F32)
     out_ref[:, 2 * features :] = picked.astype(BF16)
+    copies[1].wait()
+    out_ref[:, :features] = tokens_ref[...]
+    copies[2].wait()
+    out_ref[:, features : 2 * features] = cot_ref[...]
 
 
 def order_kernel(at_ref, piece_refs, _, out_ref):

time: 52.2 us -> 52.2 us (level)
  no operation moved by 1% of the time
where the time goes in v10:
time: 52.2 us; the launch traced here: 52 us
  Pallas kernels  27 us (52%)
  starting transfers between devices  18.3 us (35%)
  waiting for transfers between devices  5.75 us (11%)
  between operations  0.76 us (1%)
    ppermute x18, starting transfers between devices, swap(): return lax.ppermute(x, axis, [(i, i ^ mask) for i in range(count)])  18.3 us
    pallas_call x1, Pallas kernels, kernels_plan(): call(own_kernel, [rows] * 2 + [grad] * 3 + [small, jax.ShapeDtypeStruct((...  8.5 us
    pallas_call x1, Pallas kernels, kernels_plan(): call(load_kernel, weight_kinds, [IN_SMEM] + [in_hbm_spec] * 3, [IN_VMEM]...  6.11 us
    pallas_call x1, Pallas kernels, kernels_plan(): call(far_kernel, in_vmem + [pltpu.VMEM((2, portion, count), BF16), pltpu....  5.78 us
    ppermute x18, waiting for transfers between devices, swap(): return lax.ppermute(x, axis, [(i, i ^ mask) for i in range(count)])  5.75 us
    pallas_call x1, Pallas kernels, kernels_plan(): call(weight_kernel, [pltpu.HBM((portion, hidden_units), F32)] * 3, [IN_VM...  2.3 us
    pallas_call x1, Pallas kernels, kernels_plan(): call(last_kernel, [rows] * 2 + [jax.ShapeDtypeStruct((experts, features),...  1.71 us
  transfers between devices with their start and end apart: 18, of which 7 were waited for; matrix products, arithmetic and copies ran while one was open for 0% of the time, Pallas kernels for 45%

profile of v10, /device:TPU:0, one launch (start us, length us, event | category | flops | bytes accessed | tf_op | source)
XLA Modules:
  0.0 52.0 jit_solution(17614808340802673656)
XLA Ops:
  0.6 0.8 %shard_map.118.piece_refs_0_ = bf16[8,5248]{1,0:T(8,128)(2,1)S(1)} custom-call(bf16[8,2560]{1,0:T(8,128)(2,1)} %tokens_hbm.1, bf16[8,2560]{1,0:T(8,128)(2,1)} %cot_hbm.1, s32[8,6]{1,0:T(8,128)} %routes_hbm.1), custom_call_target="tpu_custom_call" | custom-call | bytes 1 | tf_op jit(solution)/shard_map/pallas_call | solution.py:431
  1.5 5.1 %collective-permute-start.2 = (bf16[8,5248]{1,0:T(8,128)(2,1)S(1)}, bf16[8,5248]{1,0:T(8,128)(2,1)S(1)}, u32[]{:S(2)}, u32[]{:S(2)}) collective-permute-start(bf16[8,5248]{1,0:T(8,128)(2,1)S(1)} %shard_map.118.piece_refs_0_), channel_id=1, source_target_pairs={{0,6},{1,7},{2,4},{3,5},{4,2},{5,3},{6,0},{7,1},{8,14},{9,15},{10,... | collective-permute-start | bytes 251912 | tf_op jit(solution)/shard_map/ppermute | solution.py:26
  6.6 0.0 collective-permute-start.1
  6.6 0.6 %collective-permute-start = (bf16[8,5248]{1,0:T(8,128)(2,1)S(1)}, bf16[8,5248]{1,0:T(8,128)(2,1)S(1)}, u32[]{:S(2)}, u32[]{:S(2)}) collective-permute-start(bf16[8,5248]{1,0:T(8,128)(2,1)S(1)} %shard_map.118.piece_refs_0_), channel_id=1, source_target_pairs={{0,2},{1,3},{2,0},{3,1},{4,6},{5,7},{6,4},{7,5},{8,10},{9,11},{10,... | collective-permute-start | bytes 251912 | tf_op jit(solution)/shard_map/ppermute | solution.py:26
  7.2 0.1 pad_add_fusion._.at_ref
  7.3 6.1 %shard_map.119 = (bf16[2560,1024]{1,0:T(8,128)(2,1)S(1)}, bf16[2560,1024]{1,0:T(8,128)(2,1)S(1)}, bf16[2560,1024]{1,0:T(8,128)(2,1)S(1)}) custom-call(s32[4]{0:T(128)S(1)} %pad_add_fusion._.at_ref, bf16[2560,1024]{1,0:T(8,128)(2,1)} %refs_0_.1, bf16[2560,1024]{1,0:T(8,128)(2,1)} %refs_1_.1, bf16[2560,1024]{1,0:T(8,128)(2,1)} %refs_2_.1), custom_call_target="tpu_custom_call" | custom-call | bytes 1 | tf_op jit(solution)/shard_map/pallas_call | solution.py:439
  13.4 0.0 collective-permute-done.2.piece_refs_3_
  13.5 0.2 collective-permute-done.1.piece_refs_2_
  13.6 0.0 collective-permute-done.piece_refs_1_
  13.6 0.0 copy-start
  13.6 0.6 %shard_map.120 = bf16[4,8,5248]{2,1,0:T(8,128)(2,1)S(1)} custom-call(s32[4]{0:T(128)S(1)} %pad_add_fusion._.at_ref, bf16[8,5248]{1,0:T(8,128)(2,1)S(1)} %shard_map.118.piece_refs_0_, bf16[8,5248]{1,0:T(8,128)(2,1)S(1)} %collective-permute-done.piece_refs_1_, bf16[8,5248]{1,0:T(8,128)(2,1)S(1)} %collective-permute-done.1.piece_refs_2_, ...), custom_call_target="tpu_custom_call" | custom-call | bytes 1 | tf_op jit(solution)/shard_map/pallas_call | solution.py:446
  14.2 2.5 %collective-permute-start.8 = (bf16[4,8,5248]{2,1,0:T(8,128)(2,1)S(1)}, bf16[4,8,5248]{2,1,0:T(8,128)(2,1)S(1)}, u32[]{:S(2)}, u32[]{:S(2)}) collective-permute-start(bf16[4,8,5248]{2,1,0:T(8,128)(2,1)S(1)} %shard_map.120), channel_id=1, source_target_pairs={{0,24},{8,16},{16,8},{24,0},{1,25},{9,17},{17,9},{25,1},{2,26},{10... | collective-permute-start | bytes 1007624 | tf_op jit(solution)/shard_map/ppermute | solution.py:26
  16.7 0.5 collective-permute-start.7
  17.2 0.5 %collective-permute-start.6 = (bf16[4,8,5248]{2,1,0:T(8,128)(2,1)S(1)}, bf16[4,8,5248]{2,1,0:T(8,128)(2,1)S(1)}, u32[]{:S(2)}, u32[]{:S(2)}) collective-permute-start(bf16[4,8,5248]{2,1,0:T(8,128)(2,1)S(1)} %shard_map.120), channel_id=1, source_target_pairs={{0,8},{8,0},{16,24},{24,16},{1,9},{9,1},{17,25},{25,17},{2,10},{10... | collective-permute-start | bytes 1007624 | tf_op jit(solution)/shard_map/ppermute | solution.py:26
  17.8 0.0 collective-permute-start.3
  17.8 0.0 copy-done
  17.8 1.6 %collective-permute-done.3 = bf16[4,8,5248]{2,1,0:T(8,128)(2,1)S(1)} collective-permute-done((bf16[4,8,5248]{2,1,0:T(8,128)(2,1)S(1)}, bf16[4,8,5248]{2,1,0:T(8,128)(2,1)S(1)}, u32[]{:S(2)}, u32[]{:S(2)}) %collective-permute-start.3) | collective-permute-done | bytes 335904 | tf_op jit(solution)/shard_map/ppermute | solution.py:26
  19.4 8.5 %shard_map.121 = (bf16[32,5120]{1,0:T(8,128)(2,1)S(1)}, bf16[32,5120]{1,0:T(8,128)(2,1)S(1)}, bf16[64,1024]{1,0:T(8,128)(2,1)S(1)}, bf16[64,1024]{1,0:T(8,128)(2...) custom-call(s32[4]{0:T(128)S(1)} %pad_add_fusion._.at_ref, ...), custom_call_target="tpu_custom_call" | custom-call | bytes 1 | tf_op jit(solution)/shard_map/pallas_call | solution.py:459
  27.9 0.2 collective-permute-start.4
  28.1 0.4 collective-permute-start.5
  28.5 1.1 %collective-permute-done.5.other_pull_ref = f32[8,64]{1,0:T(8,128)S(1)} collective-permute-done((f32[8,64]{1,0:T(8,128)S(1)}, f32[8,64]{1,0:T(8,128)S(1)}, u32[]{:S(2)}, u32[]{:S(2)}) %collective-permute-start.5) | collective-permute-done | bytes 2080 | tf_op jit(solution)/shard_map/ppermute | solution.py:26
  29.6 0.0 collective-permute-done.4.other_ref
  29.6 0.6 %shard_map.122 = (bf16[8,5248]{1,0:T(8,128)(2,1)S(1)}, bf16[8,5248]{1,0:T(8,128)(2,1)S(1)}, bf16[8,5248]{1,0:T(8,128)(2,1)S(1)}, bf16[8,5248]{1,0:T(8,128)(2,1)S(1)}) custom-call(s32[4]{0:T(128)S(1)} %pad_add_fusion._.at_ref, bf16[4,8,5120]{2,1,0:T(8,128)(2,1)S(1)} %bitcast.26, bf16[4,8,5120]{2,1,0:T(8,128)(2,1)S(1)} %collective-permute-done.4.other_ref, ...), custom_call_target="tpu_custom_call" | custom-call | bytes 1 | tf_op jit(solution)/shard_map/pallas_call | solution.py:469
  30.3 0.0 collective-permute-done.8
  30.3 1.2 %collective-permute-done.7 = bf16[4,8,5248]{2,1,0:T(8,128)(2,1)S(1)} collective-permute-done((bf16[4,8,5248]{2,1,0:T(8,128)(2,1)S(1)}, bf16[4,8,5248]{2,1,0:T(8,128)(2,1)S(1)}, u32[]{:S(2)}, u32[]{:S(2)}) %collective-permute-start.7) | collective-permute-done | bytes 335904 | tf_op jit(solution)/shard_map/ppermute | solution.py:26
  31.4 0.2 collective-permute-done.6
  31.7 0.0 collective-permute-start.9
  31.7 0.5 collective-permute-start.10
  32.2 0.0 collective-permute-start.11
  32.2 1.1 %collective-permute-start.12 = (bf16[8,5248]{1,0:T(8,128)(2,1)S(1)}, bf16[8,5248]{1,0:T(8,128)(2,1)S(1)}, u32[]{:S(2)}, u32[]{:S(2)}) collective-permute-start(bf16[8,5248]{1,0:T(8,128)(2,1)S(1)} %get-tuple-element.54), channel_id=1, source_target_pairs={{0,2},{1,3},{2,0},{3,1},{4,6},{5,7},{6,4},{7,5},{8,10},{9,11},{10,... | collective-permute-start | bytes 251912 | tf_op jit(solution)/shard_map/ppermute | solution.py:26
  33.3 2.6 %collective-permute-start.13 = (bf16[8,5248]{1,0:T(8,128)(2,1)S(1)}, bf16[8,5248]{1,0:T(8,128)(2,1)S(1)}, u32[]{:S(2)}, u32[]{:S(2)}) collective-permute-start(bf16[8,5248]{1,0:T(8,128)(2,1)S(1)} %get-tuple-element.55), channel_id=1, source_target_pairs={{0,4},{1,5},{2,6},{3,7},{4,0},{5,1},{6,2},{7,3},{8,12},{9,13},{10,... | collective-permute-start | bytes 251912 | tf_op jit(solution)/shard_map/ppermute | solution.py:26
  35.9 0.0 collective-permute-done.9
  35.9 0.6 %collective-permute-start.14 = (bf16[8,5248]{1,0:T(8,128)(2,1)S(1)}, bf16[8,5248]{1,0:T(8,128)(2,1)S(1)}, u32[]{:S(2)}, u32[]{:S(2)}) collective-permute-start(bf16[8,5248]{1,0:T(8,128)(2,1)S(1)} %get-tuple-element.56), channel_id=1, source_target_pairs={{0,6},{1,7},{2,4},{3,5},{4,2},{5,3},{6,0},{7,1},{8,14},{9,15},{10,... | collective-permute-start | bytes 251912 | tf_op jit(solution)/shard_map/ppermute | solution.py:26
  36.6 0.0 collective-permute-done.10
  36.6 0.0 collective-permute-done.11
  36.6 5.8 %shard_map.123 = (bf16[256,1024]{1,0:T(8,128)(2,1)S(1)}, bf16[256,1024]{1,0:T(8,128)(2,1)S(1)}, bf16[256,1024]{1,0:T(8,128)(2,1)S(1)}, bf16[2,640,256]{2,1,0:T(8...) custom-call(s32[4]{0:T(128)S(1)} %pad_add_fusion._.at_ref, ...), custom_call_target="tpu_custom_call" | custom-call | bytes 1 | tf_op jit(solution)/shard_map/pallas_call | solution.py:484
  42.4 0.0 collective-permute-done.12.back_refs_1_
  42.4 0.7 %collective-permute-done.13.back_refs_2_ = bf16[8,5248]{1,0:T(8,128)(2,1)S(1)} collective-permute-done((bf16[8,5248]{1,0:T(8,128)(2,1)S(1)}, bf16[8,5248]{1,0:T(8,128)(2,1)S(1)}, u32[]{:S(2)}, u32[]{:S(2)}) %collective-permute-start.13) | collective-permute-done | bytes 84000 | tf_op jit(solution)/shard_map/ppermute | solution.py:26
  43.1 0.0 collective-permute-done.14.back_refs_3_
  43.1 0.6 %shard_map.124.logit_refs_0_._ = f32[8,64]{1,0:T(8,128)S(1)} custom-call(s32[4]{0:T(128)S(1)} %pad_add_fusion._.at_ref, f32[3,8,64]{2,1,0:T(8,128)S(1)} %get-tuple-element.53.table_ref, bf16[8,5248]{1,0:T(8,128)(2,1)S(1)} %get-tuple-element.45.back_refs_0_, bf16[8,5248]{1,0:T(8,128)(2,1)S(1)} %collective-permute-done.12.back_refs_1_, ...), custom_call_target="tpu_custom_call" | custom-call | bytes 1 | tf_op jit(solution)/shard_map/pallas_call | solution.py:498
  43.6 1.7 %collective-permute-start.17 = (f32[8,64]{1,0:T(8,128)S(1)}, f32[8,64]{1,0:T(8,128)S(1)}, u32[]{:S(2)}, u32[]{:S(2)}) collective-permute-start(f32[8,64]{1,0:T(8,128)S(1)} %shard_map.124.logit_refs_0_._), channel_id=1, source_target_pairs={{0,24},{8,16},{16,8},{24,0},{1,25},{9,17},{17,9},{25,1},{2,26},{10... | collective-permute-start | bytes 6152 | tf_op jit(solution)/shard_map/ppermute | solution.py:26
  45.3 1.3 %collective-permute-start.16 = (f32[8,64]{1,0:T(8,128)S(1)}, f32[8,64]{1,0:T(8,128)S(1)}, u32[]{:S(2)}, u32[]{:S(2)}) collective-permute-start(f32[8,64]{1,0:T(8,128)S(1)} %shard_map.124.logit_refs_0_._), channel_id=1, source_target_pairs={{0,16},{8,24},{16,0},{24,8},{1,17},{9,25},{17,1},{25,9},{2,18},{10... | collective-permute-start | bytes 6152 | tf_op jit(solution)/shard_map/ppermute | solution.py:26
  46.6 0.5 %collective-permute-start.15 = (f32[8,64]{1,0:T(8,128)S(1)}, f32[8,64]{1,0:T(8,128)S(1)}, u32[]{:S(2)}, u32[]{:S(2)}) collective-permute-start(f32[8,64]{1,0:T(8,128)S(1)} %shard_map.124.logit_refs_0_._), channel_id=1, source_target_pairs={{0,8},{8,0},{16,24},{24,16},{1,9},{9,1},{17,25},{25,17},{2,10},{10... | collective-permute-start | bytes 6152 | tf_op jit(solution)/shard_map/ppermute | solution.py:26
  47.2 2.3 %shard_map.126 = (f32[640,1024]{1,0:T(8,128)}, f32[640,1024]{1,0:T(8,128)}, f32[640,1024]{1,0:T(8,128)}) custom-call(bf16[2,640,256]{2,1,0:T(8,128)(2,1)S(1)} %get-tuple-element.57._.turned_ref, bf16[256,1024]{1,0:T(8,128)(2,1)S(1)} %get-tuple-element.61.grad_refs_0_, ...), custom_call_target="tpu_custom_call", output_to_operand_aliasing={{0}: (5, {}), {1}: (6, {}), {2}: (7, {})} | custom-call | bytes 1 | tf_op jit(solution)/shard_map/pallas_call | solution.py:506
  49.5 0.0 collective-permute-done.17.logit_refs_3_
  49.5 0.0 collective-permute-done.16.logit_refs_2_
  49.5 0.7 %collective-permute-done.15.logit_refs_1_ = f32[8,64]{1,0:T(8,128)S(1)} collective-permute-done((f32[8,64]{1,0:T(8,128)S(1)}, f32[8,64]{1,0:T(8,128)S(1)}, u32[]{:S(2)}, u32[]{:S(2)}) %collective-permute-start.15) | collective-permute-done | bytes 2080 | tf_op jit(solution)/shard_map/ppermute | solution.py:26
  50.3 1.7 %shard_map.125 = (bf16[8,2560]{1,0:T(8,128)(2,1)}, bf16[8,2560]{1,0:T(8,128)(2,1)}, f32[8,2560]{1,0:T(8,128)}) custom-call(s32[4]{0:T(128)S(1)} %pad_add_fusion._.at_ref, bf16[256,5248]{1,0:T(8,128)(2,1)S(1)} %get-tuple-element.52.x_ref, f32[8,64]{1,0:T(8,128)S(1)} %shard_map.124.logit_refs_0_._, f32[8,64]{1,0:T(8,128)S(1)} %collective-permute-done.15.logit_refs_1_, ...), custom_call_target="tpu_custom_call" | custom-call | bytes 1 | tf_op jit(solution)/shard_map/pallas_call | solution.py:519
  (2 shorter events, 0.0 us)
Async XLA Ops:
  1.5 12.0 %collective-permute-start.2 = (bf16[8,5248]{1,0:T(8,128)(2,1)S(1)}, bf16[8,5248]{1,0:T(8,128)(2,1)S(1)}, u32[]{:S(2)}, u32[]{:S(2)}) collective-permute-start(bf16[8,5248]{1,0:T(8,128)(2,1)S(1)} %shard_map.118.piece_refs_0_), channel_id=1, source_target_pairs={{0,6},{1,7},{2,4},{3,5},{4,2},{5,3},{6,0},{7,1},{8,14},{9,15},{10,... | collective-permute-start | bytes 251912 | tf_op jit(solution)/shard_map/ppermute | solution.py:26
  6.6 7.0 %collective-permute-start.1 = (bf16[8,5248]{1,0:T(8,128)(2,1)S(1)}, bf16[8,5248]{1,0:T(8,128)(2,1)S(1)}, u32[]{:S(2)}, u32[]{:S(2)}) collective-permute-start(bf16[8,5248]{1,0:T(8,128)(2,1)S(1)} %shard_map.118.piece_refs_0_), channel_id=1, source_target_pairs={{0,4},{1,5},{2,6},{3,7},{4,0},{5,1},{6,2},{7,3},{8,12},{9,13},{10,... | collective-permute-start | bytes 251912 | tf_op jit(solution)/shard_map/ppermute | solution.py:26
  6.6 7.0 %collective-permute-start = (bf16[8,5248]{1,0:T(8,128)(2,1)S(1)}, bf16[8,5248]{1,0:T(8,128)(2,1)S(1)}, u32[]{:S(2)}, u32[]{:S(2)}) collective-permute-start(bf16[8,5248]{1,0:T(8,128)(2,1)S(1)} %shard_map.118.piece_refs_0_), channel_id=1, source_target_pairs={{0,2},{1,3},{2,0},{3,1},{4,6},{5,7},{6,4},{7,5},{8,10},{9,11},{10,... | collective-permute-start | bytes 251912 | tf_op jit(solution)/shard_map/ppermute | solution.py:26
  13.6 4.1 %copy-start = (f32[2560,8]{0,1:T(8,128)S(1)}, f32[2560,8]{0,1:T(8,128)}, u32[]{:S(2)}) copy-start(f32[2560,8]{0,1:T(8,128)} %param.9) | copy-start | bytes 245764
  14.2 16.0 %collective-permute-start.8 = (bf16[4,8,5248]{2,1,0:T(8,128)(2,1)S(1)}, bf16[4,8,5248]{2,1,0:T(8,128)(2,1)S(1)}, u32[]{:S(2)}, u32[]{:S(2)}) collective-permute-start(bf16[4,8,5248]{2,1,0:T(8,128)(2,1)S(1)} %shard_map.120), channel_id=1, source_target_pairs={{0,24},{8,16},{16,8},{24,0},{1,25},{9,17},{17,9},{25,1},{2,26},{10... | collective-permute-start | bytes 1007624 | tf_op jit(solution)/shard_map/ppermute | solution.py:26
  16.7 14.7 %collective-permute-start.7 = (bf16[4,8,5248]{2,1,0:T(8,128)(2,1)S(1)}, bf16[4,8,5248]{2,1,0:T(8,128)(2,1)S(1)}, u32[]{:S(2)}, u32[]{:S(2)}) collective-permute-start(bf16[4,8,5248]{2,1,0:T(8,128)(2,1)S(1)} %shard_map.120), channel_id=1, source_target_pairs={{0,16},{8,24},{16,0},{24,8},{1,17},{9,25},{17,1},{25,9},{2,18},{10... | collective-permute-start | bytes 1007624 | tf_op jit(solution)/shard_map/ppermute | solution.py:26
  17.2 14.4 %collective-permute-start.6 = (bf16[4,8,5248]{2,1,0:T(8,128)(2,1)S(1)}, bf16[4,8,5248]{2,1,0:T(8,128)(2,1)S(1)}, u32[]{:S(2)}, u32[]{:S(2)}) collective-permute-start(bf16[4,8,5248]{2,1,0:T(8,128)(2,1)S(1)} %shard_map.120), channel_id=1, source_target_pairs={{0,8},{8,0},{16,24},{24,16},{1,9},{9,1},{17,25},{25,17},{2,10},{10... | collective-permute-start | bytes 1007624 | tf_op jit(solution)/shard_map/ppermute | solution.py:26
  17.8 1.6 %collective-permute-start.3 = (bf16[4,8,5248]{2,1,0:T(8,128)(2,1)S(1)}, bf16[4,8,5248]{2,1,0:T(8,128)(2,1)S(1)}, u32[]{:S(2)}, u32[]{:S(2)}) collective-permute-start(bf16[4,8,5248]{2,1,0:T(8,128)(2,1)S(1)} %shard_map.120), channel_id=1, source_target_pairs={{0,1},{1,0},{2,3},{3,2},{4,5},{5,4},{6,7},{7,6},{8,9},{9,8},{10,11... | collective-permute-start | bytes 1007624 | tf_op jit(solution)/shard_map/ppermute | solution.py:26
  27.9 1.7 %collective-permute-start.4 = (bf16[4,8,5120]{2,1,0:T(8,128)(2,1)S(1)}, bf16[4,8,5120]{2,1,0:T(8,128)(2,1)S(1)}, u32[]{:S(2)}, u32[]{:S(2)}) collective-permute-start(bf16[4,8,5120]{2,1,0:T(8,128)(2,1)S(1)} %bitcast.29), channel_id=1, source_target_pairs={{0,1},{1,0},{2,3},{3,2},{4,5},{5,4},{6,7},{7,6},{8,9},{9,8},{10,11... | collective-permute-start | bytes 983048 | tf_op jit(solution)/shard_map/ppermute | solution.py:26
  28.1 1.5 %collective-permute-start.5 = (f32[8,64]{1,0:T(8,128)S(1)}, f32[8,64]{1,0:T(8,128)S(1)}, u32[]{:S(2)}, u32[]{:S(2)}) collective-permute-start(f32[8,64]{1,0:T(8,128)S(1)} %get-tuple-element.44.pull_ref), channel_id=1, source_target_pairs={{0,1},{1,0},{2,3},{3,2},{4,5},{5,4},{6,7},{7,6},{8,9},{9,8},{10,11... | collective-permute-start | bytes 6152 | tf_op jit(solution)/shard_map/ppermute | solution.py:26
  31.7 4.3 %collective-permute-start.9 = (bf16[4,8,5248]{2,1,0:T(8,128)(2,1)S(1)}, bf16[4,8,5248]{2,1,0:T(8,128)(2,1)S(1)}, u32[]{:S(2)}, u32[]{:S(2)}) collective-permute-start(bf16[4,8,5248]{2,1,0:T(8,128)(2,1)S(1)} %collective-permute-done.6), channel_id=1, source_target_pairs={{0,1},{1,0},{2,3},{3,2},{4,5},{5,4},{6,7},{7,6},{8,9},{9,8},{10,11... | collective-permute-start | bytes 1007624 | tf_op jit(solution)/shard_map/ppermute | solution.py:26
  31.7 4.9 %collective-permute-start.10 = (bf16[4,8,5248]{2,1,0:T(8,128)(2,1)S(1)}, bf16[4,8,5248]{2,1,0:T(8,128)(2,1)S(1)}, u32[]{:S(2)}, u32[]{:S(2)}) collective-permute-start(bf16[4,8,5248]{2,1,0:T(8,128)(2,1)S(1)} %collective-permute-done.7), channel_id=1, source_target_pairs={{0,1},{1,0},{2,3},{3,2},{4,5},{5,4},{6,7},{7,6},{8,9},{9,8},{10,11... | collective-permute-start | bytes 1007624 | tf_op jit(solution)/shard_map/ppermute | solution.py:26
  32.2 4.4 %collective-permute-start.11 = (bf16[4,8,5248]{2,1,0:T(8,128)(2,1)S(1)}, bf16[4,8,5248]{2,1,0:T(8,128)(2,1)S(1)}, u32[]{:S(2)}, u32[]{:S(2)}) collective-permute-start(bf16[4,8,5248]{2,1,0:T(8,128)(2,1)S(1)} %collective-permute-done.8), channel_id=1, source_target_pairs={{0,1},{1,0},{2,3},{3,2},{4,5},{5,4},{6,7},{7,6},{8,9},{9,8},{10,11... | collective-permute-start | bytes 1007624 | tf_op jit(solution)/shard_map/ppermute | solution.py:26
  32.2 10.2 %collective-permute-start.12 = (bf16[8,5248]{1,0:T(8,128)(2,1)S(1)}, bf16[8,5248]{1,0:T(8,128)(2,1)S(1)}, u32[]{:S(2)}, u32[]{:S(2)}) collective-permute-start(bf16[8,5248]{1,0:T(8,128)(2,1)S(1)} %get-tuple-element.54), channel_id=1, source_target_pairs={{0,2},{1,3},{2,0},{3,1},{4,6},{5,7},{6,4},{7,5},{8,10},{9,11},{10,... | collective-permute-start | bytes 251912 | tf_op jit(solution)/shard_map/ppermute | solution.py:26
  33.3 9.8 %collective-permute-start.13 = (bf16[8,5248]{1,0:T(8,128)(2,1)S(1)}, bf16[8,5248]{1,0:T(8,128)(2,1)S(1)}, u32[]{:S(2)}, u32[]{:S(2)}) collective-permute-start(bf16[8,5248]{1,0:T(8,128)(2,1)S(1)} %get-tuple-element.55), channel_id=1, source_target_pairs={{0,4},{1,5},{2,6},{3,7},{4,0},{5,1},{6,2},{7,3},{8,12},{9,13},{10,... | collective-permute-start | bytes 251912 | tf_op jit(solution)/shard_map/ppermute | solution.py:26
  35.9 7.1 %collective-permute-start.14 = (bf16[8,5248]{1,0:T(8,128)(2,1)S(1)}, bf16[8,5248]{1,0:T(8,128)(2,1)S(1)}, u32[]{:S(2)}, u32[]{:S(2)}) collective-permute-start(bf16[8,5248]{1,0:T(8,128)(2,1)S(1)} %get-tuple-element.56), channel_id=1, source_target_pairs={{0,6},{1,7},{2,4},{3,5},{4,2},{5,3},{6,0},{7,1},{8,14},{9,15},{10,... | collective-permute-start | bytes 251912 | tf_op jit(solution)/shard_map/ppermute | solution.py:26
  43.6 5.9 %collective-permute-start.17 = (f32[8,64]{1,0:T(8,128)S(1)}, f32[8,64]{1,0:T(8,128)S(1)}, u32[]{:S(2)}, u32[]{:S(2)}) collective-permute-start(f32[8,64]{1,0:T(8,128)S(1)} %shard_map.124.logit_refs_0_._), channel_id=1, source_target_pairs={{0,24},{8,16},{16,8},{24,0},{1,25},{9,17},{17,9},{25,1},{2,26},{10... | collective-permute-start | bytes 6152 | tf_op jit(solution)/shard_map/ppermute | solution.py:26
  45.3 4.2 %collective-permute-start.16 = (f32[8,64]{1,0:T(8,128)S(1)}, f32[8,64]{1,0:T(8,128)S(1)}, u32[]{:S(2)}, u32[]{:S(2)}) collective-permute-start(f32[8,64]{1,0:T(8,128)S(1)} %shard_map.124.logit_refs_0_._), channel_id=1, source_target_pairs={{0,16},{8,24},{16,0},{24,8},{1,17},{9,25},{17,1},{25,9},{2,18},{10... | collective-permute-start | bytes 6152 | tf_op jit(solution)/shard_map/ppermute | solution.py:26
  46.6 3.6 %collective-permute-start.15 = (f32[8,64]{1,0:T(8,128)S(1)}, f32[8,64]{1,0:T(8,128)S(1)}, u32[]{:S(2)}, u32[]{:S(2)}) collective-permute-start(f32[8,64]{1,0:T(8,128)S(1)} %shard_map.124.logit_refs_0_._), channel_id=1, source_target_pairs={{0,8},{8,0},{16,24},{24,16},{1,9},{9,1},{17,25},{25,17},{2,10},{10... | collective-permute-start | bytes 6152 | tf_op jit(solution)/shard_map/ppermute | solution.py:26
